TPU v7x, 32 devices: a whole 2x2x4 slice. The times are simulated.
32 devices in a mesh: grid: 8 (over z, y), band: 4 (over x, core).
Axes of the slice: x: 2, y: 2, z: 4, core: 2. Of those that a mesh axis runs over, the one named last changes fastest.
Arguments:
- orbitals: bfloat16 [4096, 4096], P(('band', 'grid')), may hold values from -6 to 6
- w_first: bfloat16 [4096, 1024], P(('band', 'grid')), may hold values from -0.09375 to 0.09375
- w_second: bfloat16 [4096, 1024], P(('band', 'grid')), may hold values from -0.09375 to 0.09375
- pivots: int32 [8, 4, 256], P('grid'), may hold values from 0 to 511, as said below
Outputs:
- chosen: bfloat16 [1024, 256], replicated
- quality: float32 [8, 256], P('grid')
Inputs may be any that keep to these rules, and one draw needn't show every extreme that they name: Each list pivots[g, r, :] holds distinct values below 512 and contains 2 * 256 - 1; indices g that agree in all bits from bit r upward have equal lists in round r.
All inputs are finite; a program needn't handle non-finite values.
Results may differ from a plain program's by a relative error of at most 0.0026.
Values may be sent and summed in bfloat16 or wider, within the bound.
No kernel may reach another device: no remote copies, remote signals or barrier semaphores. Data moves between devices by JAX's collectives and lax.ppermute only.
A program may use at most 64 MiB of HBM per device.

v0:
```python
import jax
import jax.numpy as jnp
from jax import lax
from jax.sharding import PartitionSpec as P

ridge = 0.1


def partner(block, axis, bit):
    count = lax.axis_size(axis)
    route = []
    for low in range(count):
        high = low | 1 << bit
        if high != low and high < count:
            route += [(low, high), (high, low)]
    return lax.ppermute(block, axis, route)


def log_pivots(chosen):
    count_rows = chosen.shape[0]
    gram_product = lax.dot_general(
        chosen, chosen, (((0,), (0,)), ((), ())), preferred_element_type=jnp.float32
    )
    gram_product = gram_product / count_rows + ridge * jnp.eye(chosen.shape[1], dtype=jnp.float32)
    cholesky_factor = jnp.linalg.cholesky(gram_product)
    return jnp.log(jnp.diagonal(cholesky_factor))


def local(orbitals, w_first, w_second, pivots):
    regrouped = lax.all_to_all(orbitals, "grid", split_axis=1, concat_axis=0, tiled=True)
    contract = (((0,), (0,)), ((), ()))
    whole_first, whole_second = (
        lax.all_gather(w_first, "grid", axis=0, tiled=True),
        lax.all_gather(w_second, "grid", axis=0, tiled=True),
    )
    sketch_first = lax.dot_general(
        whole_first, regrouped, contract, preferred_element_type=jnp.float32
    )
    sketch_second = lax.dot_general(
        whole_second, regrouped, contract, preferred_element_type=jnp.float32
    )
    first_share_part, share_second = (
        lax.psum_scatter(sketch_first, "band", scatter_dimension=1, tiled=True),
        lax.psum_scatter(sketch_second, "band", scatter_dimension=1, tiled=True),
    )
    share_products = (first_share_part * share_second).astype(jnp.bfloat16)
    pair_products = lax.all_gather(share_products, "band", axis=1, tiled=True)
    order = pivots[0]
    chosen = jnp.take(pair_products, order[0], axis=1)
    quality = log_pivots(chosen)
    sections = lax.axis_size("grid").bit_length() - 1
    for section in range(1, sections + 1):
        partner_cols = partner(chosen, "grid", section - 1)
        upper_flag = lax.axis_index("grid") >> section - 1 & 1 == 1
        lower_set = jnp.where(upper_flag, partner_cols, chosen)
        upper_set = jnp.where(upper_flag, chosen, partner_cols)
        merged = jnp.concatenate([lower_set, upper_set], axis=1)
        chosen = jnp.take(merged, order[section], axis=1)
        quality = quality + log_pivots(chosen)
    return (chosen, quality[None, :])


def solution(mesh):
    in_specs = (
        P(("band", "grid"), None),
        P(("band", "grid"), None),
        P(("band", "grid"), None),
        P("grid", None, None),
    )
    out_specs = (P(), P("grid", None))
    return jax.shard_map(local, mesh=mesh, in_specs=in_specs, out_specs=out_specs, check_vma=False)
```

profile of v0, /device:TPU:0, one launch (start us, length us, event | category | flops | bytes accessed | tf_op | source)
XLA Modules:
  0.0 386.7 jit_solution(8141706302817574253)
XLA Ops:
  7.2 0.7 all-gather.4.cloned.1.call-update
  7.9 0.7 all-gather.6.cloned.1.call-update
  8.7 1.6 copy.26
  10.3 41.3 %all_to_all.19 = bf16[128,8,512]{0,2,1:T(8,128)(2,1)S(1)} all-to-all(bf16[128,8,512]{0,2,1:T(8,128)(2,1)S(1)} %bitcast.92), channel_id=1, replica_groups=mesh['grid'=8,'band'=4] {'grid'}, dimensions={1} | all-to-all | bytes 2097152 | tf_op jit(solution)/shard_map/all_to_all | solution.py:30
  51.6 0.5 copy.27
  52.1 20.4 %all-gather.4.cloned.1.call-done = bf16[1024,1024]{1,0:T(8,128)(2,1)} async-done(((bf16[128,1024]{1,0:T(8,128)(2,1)}), bf16[1024,1024]{1,0:T(8,128)(2,1)}) %all-gather.4.cloned.1.call-update) | async-done | bytes 2097168 | tf_op jit(solution)/shard_map/all_gather | solution.py:33
  72.6 4.2 %fusion.21 = f32[1024,512]{1,0:T(8,128)} fusion(bf16[1024,1024]{1,0:T(8,128)(2,1)} %all-gather.4.cloned.1.call-done, bf16[1024,512]{1,0:T(8,128)(2,1)S(1)} %bitcast.93), kind=kOutput, calls=%fused_computation.105 | convolution fusion | flops 1073741824 | bytes 5242880 | tf_op jit(solution)/shard_map/dot_general | solution.py:36
  76.9 45.6 %all-gather.6.cloned.1.call-done = bf16[1024,1024]{1,0:T(8,128)(2,1)} async-done(((bf16[128,1024]{1,0:T(8,128)(2,1)}), bf16[1024,1024]{1,0:T(8,128)(2,1)}) %all-gather.6.cloned.1.call-update) | async-done | bytes 2097168 | tf_op jit(solution)/shard_map/all_gather | solution.py:34
  122.5 4.2 %fusion.22 = f32[1024,512]{1,0:T(8,128)} fusion(bf16[1024,1024]{1,0:T(8,128)(2,1)} %all-gather.6.cloned.1.call-done, bf16[1024,512]{1,0:T(8,128)(2,1)S(1)} %bitcast.94), kind=kOutput, calls=%fused_computation.106 | convolution fusion | flops 1073741824 | bytes 5242880 | tf_op jit(solution)/shard_map/dot_general | solution.py:39
  126.8 0.6 copy-done
  127.4 27.5 %reduce-scatter.3.cloned.1.call-done = f32[1024,128]{1,0:T(8,128)} async-done(((f32[1024,512]{1,0:T(8,128)}), f32[1024,128]{1,0:T(8,128)}) %reduce-scatter.3.cloned.1.call-update) | async-done | bytes 524304 | tf_op jit(solution)/shard_map/reduce_scatter | solution.py:43
  155.0 34.0 %reduce-scatter.5.cloned.1.call-done = f32[1024,128]{1,0:T(8,128)} async-done(((f32[1024,512]{1,0:T(8,128)}), f32[1024,128]{1,0:T(8,128)}) %reduce-scatter.5.cloned.1.call-update) | async-done | bytes 524304 | tf_op jit(solution)/shard_map/reduce_scatter | solution.py:44
  189.0 2.0 multiply_convert_fusion
  191.1 16.9 %all-gather.8.cloned.1.call-done = bf16[1024,512]{1,0:T(8,128)(2,1)} async-done(((bf16[1024,128]{1,0:T(8,128)(2,1)}), bf16[1024,512]{1,0:T(8,128)(2,1)}) %all-gather.8.cloned.1.call-update) | async-done | bytes 1048592 | tf_op jit(solution)/shard_map/all_gather | solution.py:47
  208.0 1.9 copy.28
  209.9 1.2 gather_fusion.4
  211.2 1.5 collective-permute-start
  212.7 0.3 fusion
  213.3 11.7 %cholesky.214 = f32[128,128]{1,0:T(8,128)S(1)} custom-call(f32[128,128]{1,0:T(8,128)S(1)} %cholesky.346), custom_call_target="Cholesky" | custom-call | tf_op jit(solution)/shard_map/jit(cholesky)/cholesky | solution.py:25
  225.0 9.8 %custom-call.19 = f32[1,128,128]{1,2,0:T(8,128)S(1)} custom-call(f32[1,128,128]{2,1,0:T(8,128)S(1)} %get-tuple-element.19), custom_call_target="InvertDiagBlocksLowerTriangular" | custom-call | tf_op jit(solution)/shard_map/jit(cholesky)/cholesky | solution.py:25
  235.3 11.7 %cholesky.231 = f32[128,128]{1,0:T(8,128)S(1)} custom-call(f32[128,128]{1,0:T(8,128)S(1)} %convolution_subtract_fusion.3), custom_call_target="Cholesky" | custom-call | tf_op jit(solution)/shard_map/jit(cholesky)/cholesky | solution.py:25
  247.1 0.6 compare_reduce_fusion.6
  249.1 2.5 gather_fusion
  251.8 1.2 gather_fusion.5
  253.1 1.6 collective-permute-start.1
  254.7 0.3 fusion.1
  255.2 11.7 %cholesky.248 = f32[128,128]{1,0:T(8,128)S(1)} custom-call(f32[128,128]{1,0:T(8,128)S(1)} %cholesky.349), custom_call_target="Cholesky" | custom-call | tf_op jit(solution)/shard_map/jit(cholesky)/cholesky | solution.py:25
  267.0 9.8 %custom-call.20 = f32[1,128,128]{1,2,0:T(8,128)S(1)} custom-call(f32[1,128,128]{2,1,0:T(8,128)S(1)} %get-tuple-element.23), custom_call_target="InvertDiagBlocksLowerTriangular" | custom-call | tf_op jit(solution)/shard_map/jit(cholesky)/cholesky | solution.py:25
  277.3 11.7 %cholesky.265 = f32[128,128]{1,0:T(8,128)S(1)} custom-call(f32[128,128]{1,0:T(8,128)S(1)} %convolution_subtract_fusion.2), custom_call_target="Cholesky" | custom-call | tf_op jit(solution)/shard_map/jit(cholesky)/cholesky | solution.py:25
  289.0 0.6 compare_reduce_fusion.4
  291.0 2.6 gather_fusion.1
  293.8 1.2 gather_fusion.6
  295.1 2.5 collective-permute-start.2
  298.1 11.7 %cholesky.282 = f32[128,128]{1,0:T(8,128)S(1)} custom-call(f32[128,128]{1,0:T(8,128)S(1)} %cholesky.352), custom_call_target="Cholesky" | custom-call | tf_op jit(solution)/shard_map/jit(cholesky)/cholesky | solution.py:25
  309.9 9.8 %custom-call.21 = f32[1,128,128]{1,2,0:T(8,128)S(1)} custom-call(f32[1,128,128]{2,1,0:T(8,128)S(1)} %get-tuple-element.27), custom_call_target="InvertDiagBlocksLowerTriangular" | custom-call | tf_op jit(solution)/shard_map/jit(cholesky)/cholesky | solution.py:25
  320.2 11.7 %cholesky.299 = f32[128,128]{1,0:T(8,128)S(1)} custom-call(f32[128,128]{1,0:T(8,128)S(1)} %convolution_subtract_fusion.1), custom_call_target="Cholesky" | custom-call | tf_op jit(solution)/shard_map/jit(cholesky)/cholesky | solution.py:25
  331.9 0.6 compare_reduce_fusion.3
  332.6 0.6 compare_reduce_fusion.2
  334.5 2.6 gather_fusion.2
  337.4 1.2 gather_fusion.7
  338.7 1.0 copy.37
  340.2 11.7 %cholesky.316 = f32[128,128]{1,0:T(8,128)S(1)} custom-call(f32[128,128]{1,0:T(8,128)S(1)} %cholesky.355), custom_call_target="Cholesky" | custom-call | tf_op jit(solution)/shard_map/jit(cholesky)/cholesky | solution.py:25
  352.0 9.8 %custom-call.22 = f32[1,128,128]{1,2,0:T(8,128)S(1)} custom-call(f32[1,128,128]{2,1,0:T(8,128)S(1)} %get-tuple-element.31), custom_call_target="InvertDiagBlocksLowerTriangular" | custom-call | tf_op jit(solution)/shard_map/jit(cholesky)/cholesky | solution.py:25
  362.3 11.7 %cholesky.333 = f32[128,128]{1,0:T(8,128)S(1)} custom-call(f32[128,128]{1,0:T(8,128)S(1)} %convolution_subtract_fusion), custom_call_target="Cholesky" | custom-call | tf_op jit(solution)/shard_map/jit(cholesky)/cholesky | solution.py:25
  374.0 0.6 compare_reduce_fusion.1
  374.7 0.7 compare_reduce_fusion
  376.8 2.3 gather_fusion.3
  379.1 0.6 log_add_fusion
  (73 shorter events, 5.1 us)
Async XLA Ops:
  7.2 65.4 %all-gather.4.cloned.1.call-start = ((), (), s32[]{:S(2)}) async-start(), calls=%async_computation.3 | async-start | bytes 2359296 | tf_op jit(solution)/shard_map/all_gather | solution.py:33
  7.9 114.6 %all-gather.6.cloned.1.call-start = ((), (), s32[]{:S(2)}) async-start(), calls=%async_computation.5 | async-start | bytes 2359296 | tf_op jit(solution)/shard_map/all_gather | solution.py:34
  8.6 146.3 %reduce-scatter.3.cloned.1.call-start = ((), (), s32[]{:S(2)}) async-start(), calls=%async_computation.4 | async-start | bytes 2621440 | tf_op jit(solution)/shard_map/reduce_scatter | solution.py:43
  76.8 112.1 %reduce-scatter.5.cloned.1.call-start = ((), (), s32[]{:S(2)}) async-start(), calls=%async_computation.6 | async-start | bytes 2621440 | tf_op jit(solution)/shard_map/reduce_scatter | solution.py:44
  126.7 0.7 copy-start
  126.7 81.2 %all-gather.8.cloned.1.call-start = ((), (), s32[]{:S(2)}) async-start(), calls=%async_computation.7 | async-start | bytes 1310720 | tf_op jit(solution)/shard_map/all_gather | solution.py:47
  211.2 40.4 %collective-permute-start = (bf16[1024,256]{0,1:T(8,128)(2,1)S(1)}, bf16[1024,256]{0,1:T(8,128)(2,1)S(1)}, u32[]{:S(2)}, u32[]{:S(2)}) collective-permute-start(bf16[1024,256]{0,1:T(8,128)(2,1)S(1)} %select_bitcast_fusion.3), channel_id=1, source_target_pairs={{0,4},{4,0},{8,12},{12,8},{16,20},{20,16},{24,28},{28,24},{1,5},{5... | collective-permute-start | bytes 1572872 | tf_op jit(solution)/shard_map/ppermute | solution.py:16
  253.1 40.5 %collective-permute-start.1 = (bf16[1024,256]{0,1:T(8,128)(2,1)S(1)}, bf16[1024,256]{0,1:T(8,128)(2,1)S(1)}, u32[]{:S(2)}, u32[]{:S(2)}) collective-permute-start(bf16[1024,256]{0,1:T(8,128)(2,1)S(1)} %select_bitcast_fusion.2), channel_id=1, source_target_pairs={{0,8},{8,0},{4,12},{12,4},{16,24},{24,16},{20,28},{28,20},{1,9},{9... | collective-permute-start | bytes 1572872 | tf_op jit(solution)/shard_map/ppermute | solution.py:16
  295.1 42.0 %collective-permute-start.2 = (bf16[1024,256]{0,1:T(8,128)(2,1)S(1)}, bf16[1024,256]{0,1:T(8,128)(2,1)S(1)}, u32[]{:S(2)}, u32[]{:S(2)}) collective-permute-start(bf16[1024,256]{0,1:T(8,128)(2,1)S(1)} %select_bitcast_fusion.1), channel_id=1, source_target_pairs={{0,16},{16,0},{4,20},{20,4},{8,24},{24,8},{12,28},{28,12},{1,17},{... | collective-permute-start | bytes 1572872 | tf_op jit(solution)/shard_map/ppermute | solution.py:16
Sparse Core Ops, SparseCore 0:
  10.1 62.3 all-gather.3
  74.7 47.7 all-gather.5
  125.0 29.8 reduce-scatter.2
  157.5 31.4 reduce-scatter.4
  191.1 16.8 all-gather.7
where the time goes:
time: 390 us; the launch traced here: 387 us
  waiting for transfers between devices  146 us (37%)
  other arithmetic  141 us (36%)
  blocking collectives  41.3 us (11%)
  local copies, waits for them, and re-layouts  21 us (5%)
  between operations  20 us (5%)
  matrix products  11.7 us (3%)
  starting transfers between devices  5.76 us (1%)
    another operation x26, other arithmetic, log_pivots(): cholesky_factor = jnp.linalg.cholesky(gram_product)  137 us
    all_gather x1, waiting for transfers between devices, local(): lax.all_gather(w_second, 'grid', axis=0, tiled=True)  45.6 us
    all_to_all x1, blocking collectives, local(): lax.all_to_all(orbitals, 'grid', split_axis=1, concat_axis=0, tiled=True)  41.3 us
    reduce_scatter x1, waiting for transfers between devices, local(): lax.psum_scatter(sketch_second, 'band', scatter_dimension=1, tiled=True)  34 us
    reduce_scatter x1, waiting for transfers between devices, local(): lax.psum_scatter(sketch_first, 'band', scatter_dimension=1, tiled=True)  27.5 us
    all_gather x1, waiting for transfers between devices, local(): lax.all_gather(w_first, 'grid', axis=0, tiled=True)  20.4 us
    all_gather x1, waiting for transfers between devices, local(): pair_products = lax.all_gather(share_products, 'band', axis=1, tiled=True)  16.9 us
    gather x4, local copies, waits for them, and re-layouts, log_pivots(): return jnp.log(jnp.diagonal(cholesky_factor))  10 us
  transfers between devices with their start and end apart: 8, of which 5 were waited for; matrix products, arithmetic and copies ran while one was open for 32% of the time, Pallas kernels for 0%

commit v1 on v0

v1 whole, which is shorter than its diff:
```python
import functools

import jax
import jax.numpy as jnp
from jax import lax
from jax.experimental import pallas as pl
from jax.experimental.pallas import tpu as pltpu
from jax.sharding import PartitionSpec as P

ridge = 0.1
f32, bf16, f16 = jnp.float32, jnp.bfloat16, jnp.float16
step = 8
column_dims = (((0,), (0,)), ((), ()))


def bits_of(count):
    return count.bit_length() - 1


def exchange(block, axis, delta):
    count = lax.axis_size(axis)
    return lax.ppermute(block, axis, [(i, i ^ delta) for i in range(count)])


def reversed_bits(value, bits):
    out = 0
    for t in range(bits):
        out = out | ((value >> t) & 1) << (bits - 1 - t)
    return out


def select_kernel(where_ref, pivots_ref, orbitals_ref, out_ref):
    order = pivots_ref[0]
    width, kept = orbitals_ref.shape[1], order.shape[1]
    one_hot = (lax.broadcasted_iota(jnp.int32, (width, kept), 0) == order).astype(f32).astype(bf16)
    out_ref[0] = jnp.dot(orbitals_ref[...], one_hot, preferred_element_type=f32).astype(bf16)


def select_points(orbitals, orders, here):
    groups, _, kept = orders.shape
    rows, points = orbitals.shape
    width = points // groups
    high = bits_of(groups) - 1
    return pl.pallas_call(
        select_kernel,
        grid_spec=pltpu.PrefetchScalarGridSpec(
            num_scalar_prefetch=1,
            grid=(groups,),
            in_specs=[
                pl.BlockSpec((1, 1, kept), lambda d, w: (d, 0, 0)),
                pl.BlockSpec((rows, width), lambda d, w: (0, w[0] ^ d)),
            ],
            out_specs=pl.BlockSpec((1, rows, kept), lambda d, w: (d & 1, 0, reversed_bits(d >> 1, high))),
        ),
        out_shape=jax.ShapeDtypeStruct((2, rows, groups // 2 * kept), bf16),
    )(here[None], orders, orbitals)


def split3(v):
    a = v.astype(bf16)
    rest = v - a.astype(f32)
    b = rest.astype(bf16)
    c = (rest - b.astype(f32)).astype(bf16)
    return a, b, c


def pivots_kernel(sets, *refs):
    cands, out_ref, grams = refs[:sets], refs[sets], refs[sets + 1 :]
    rows, n = cands[0].shape
    diagonal = lax.broadcasted_iota(jnp.int32, (n, n), 0) == lax.broadcasted_iota(jnp.int32, (n, n), 1)
    shift = jnp.where(diagonal, f32(ridge), f32(0))
    for cand, gram in zip(cands, grams):
        product = lax.dot_general(cand[...], cand[...], column_dims, preferred_element_type=f32)
        gram[...] = product * f32(1 / rows) + shift
    out_ref[...] = jnp.zeros_like(out_ref)
    sublane = lax.broadcasted_iota(jnp.int32, (step, n), 0)
    lane = lax.broadcasted_iota(jnp.int32, (step, n), 1)
    below = lax.broadcasted_iota(jnp.int32, (step, 1), 0)

    def panel(k, carry):
        first = pl.multiple_of(k * step, step)
        on_diagonal = lane == first + sublane
        for q, gram in enumerate(grams):
            block = gram[pl.ds(first, step), :]
            corner = [
                jnp.sum(jnp.where(on_diagonal, block[i : i + 1, :], 0.0), axis=1, keepdims=True) for i in range(step)
            ]
            heads, inverses = [], []
            for j in range(step):
                head = corner[j][j : j + 1, :]
                inverse = 1.0 / head
                factor = jnp.where(below > j, corner[j] * inverse, 0.0)
                block = block - factor * block[j : j + 1, :]
                for c in range(j + 1, step):
                    corner[c] = corner[c] - factor * corner[c][j : j + 1, :]
                heads.append(head)
                inverses.append(inverse)
            column = jnp.concatenate(heads, axis=0)
            out_ref[q : q + 1, :] += jnp.sum(jnp.where(on_diagonal, column, 0.0), axis=0, keepdims=True)
            u1, u2, u3 = split3(block)
            v1, v2, v3 = split3(block * jnp.concatenate(inverses, axis=0))
            left = jnp.concatenate([v1, v1, v2, v2, v1, v3], axis=0)
            right = jnp.concatenate([u1, u2, u1, u2, u3, u1], axis=0)
            gram[...] -= lax.dot_general(left, right, column_dims, preferred_element_type=f32)
        return carry

    lax.fori_loop(0, n // step, panel, 0)
    out_ref[...] = 0.5 * jnp.log(out_ref[...])


def log_pivots(cands):
    sets, (rows, n) = len(cands), cands[0].shape
    return pl.pallas_call(
        functools.partial(pivots_kernel, sets),
        out_shape=jax.ShapeDtypeStruct((sets, n), f32),
        in_specs=[pl.BlockSpec(memory_space=pltpu.VMEM)] * sets,
        out_specs=pl.BlockSpec(memory_space=pltpu.VMEM),
        scratch_shapes=[pltpu.VMEM((n, n), f32)] * sets,
        compiler_params=pltpu.CompilerParams(vmem_limit_bytes=40 << 20),
    )(*cands)


def half_of(block, upper):
    size = block.shape[-1] // 2
    return lax.dynamic_slice_in_dim(block, upper * size, size, axis=block.ndim - 1)


def pack(block):
    block = block.reshape(-1, block.shape[-1])
    exponent = jnp.ceil(jnp.log2(jnp.maximum(jnp.max(jnp.abs(block)), f32(1e-30))))
    codes = (block * jnp.exp2(14.0 - exponent)).astype(f16)
    tag = jnp.full((16, codes.shape[-1]), exponent, f32).astype(f16)
    return jnp.concatenate([codes, tag], axis=0)


def unpack(codes, shape):
    return codes[:-16].astype(f32).reshape(shape) * jnp.exp2(codes[-1, 0].astype(f32) - 14.0)


def local(orbitals, w_first, w_second, pivots):
    here, place = lax.axis_index("grid"), lax.axis_index("band")
    grid_bits, band_bits = bits_of(lax.axis_size("grid")), bits_of(lax.axis_size("band"))
    order = pivots[0]
    kept = order.shape[1]

    orders = order[:1][None]
    for t in range(grid_bits):
        orders = jnp.concatenate([orders, exchange(orders, "grid", 1 << t)], axis=0)

    mixing = [jnp.stack([w_first, w_second])]
    for t in reversed(range(1, band_bits)):
        upper = place >> t & 1
        got = [exchange(half_of(m, 1 - upper), "band", 1 << t) for m in mixing]
        mixing = [half_of(m, upper) for m in mixing] + got
    mixing = mixing + [exchange(m, "grid", 1) for m in mixing]
    mixing = jnp.concatenate(mixing, axis=1)

    picked = select_points(orbitals, orders, here)
    own, got = picked[0], exchange(picked[1], "grid", 1)
    rows = [own]
    far = [got]
    for t in reversed(range(1, band_bits)):
        rows = rows + [exchange(m, "band", 1 << t) for m in rows]
        far = far + [exchange(m, "band", 1 << t) for m in far]
    rows = jnp.concatenate(rows + far, axis=0)

    mixes, points = [half_of(mixing, place & 1)], [rows]
    mixes.append(exchange(half_of(mixing, 1 - (place & 1)), "band", 1))
    points.append(exchange(rows, "band", 1))
    mixes, points = jnp.concatenate(mixes, axis=1), jnp.concatenate(points, axis=0)

    def partial(columns):
        return jnp.stack([lax.dot_general(m, columns, column_dims, preferred_element_type=f32) for m in mixes])

    size = points.shape[1]
    if grid_bits > 1:
        size = size // 2
        got = exchange(pack(partial(points[:, size:])), "grid", 2)
        sketch = partial(points[:, :size])
        sketch = sketch + unpack(got, sketch.shape)
    else:
        sketch = partial(points)
    for t in range(2, grid_bits):
        size = size // 2
        got = exchange(pack(sketch[..., size:]), "grid", 1 << t)
        sketch = sketch[..., :size]
        sketch = sketch + unpack(got, sketch.shape)
    chosen = (sketch[0] * sketch[1]).astype(bf16)

    def over_band(block):
        for t in reversed(range(band_bits)):
            got = exchange(block, "band", 1 << t)
            upper = place >> t & 1 == 1
            count = 1 << (band_bits - 1 - t)
            share = block.reshape((count, -1) + block.shape[1:])
            other = got.reshape(share.shape)
            low, high = jnp.where(upper, other, share), jnp.where(upper, share, other)
            block = jnp.concatenate([low, high], axis=1).reshape((-1,) + block.shape[1:])
        return block

    cands = [over_band(chosen)]
    index = lax.broadcasted_iota(jnp.int32, (kept, kept), 0)
    for section in range(1, grid_bits + 1):
        got = exchange(chosen, "grid", 1 << section - 1)
        upper = here >> section - 1 & 1
        mine = (index == order[section] - upper * kept).astype(bf16)
        other = (index == order[section] - (1 - upper) * kept).astype(bf16)
        chosen = jnp.dot(chosen, mine, preferred_element_type=f32) + jnp.dot(got, other, preferred_element_type=f32)
        chosen = chosen.astype(bf16)
        cands.append(over_band(chosen))
    quality = jnp.sum(log_pivots(cands), axis=0, keepdims=True)
    return cands[-1], quality


def solution(mesh):
    in_specs = (
        P(("band", "grid"), None),
        P(("band", "grid"), None),
        P(("band", "grid"), None),
        P("grid", None, None),
    )
    out_specs = (P(), P("grid", None))
    return jax.shard_map(local, mesh=mesh, in_specs=in_specs, out_specs=out_specs, check_vma=False)
```

time: 390 us -> 130 us (0.33)
  other arithmetic: 141 us -> 5.79 us
  waiting for transfers between devices: 146 us -> 57.2 us
  blocking collectives: 41.3 us -> 0 us
  Pallas kernels: 0 us -> 27.6 us
  starting transfers between devices: 5.76 us -> 29.7 us
  local copies, waits for them, and re-layouts: 21 us -> 2.52 us
  between operations: 20 us -> 4.09 us
  matrix products: 11.7 us -> 3.03 us
    another operation x26 -> x1, other arithmetic: 137 us -> 0.04 us  [local(): mixing = [jnp.stack([w_first, w_second])]]
    all_gather x3 -> x0, waiting for transfers between devices: 82.9 us -> none  [the longest x1 45.6 us: local(): lax.all_gather(w_second, 'grid', axis=0, tiled=True)]
    reduce_scatter x2 -> x0, waiting for transfers between devices: 61.5 us -> none  [the longest x1 34 us: local(): lax.psum_scatter(sketch_second, 'band', scatter_dimension=1, tiled=True)]
    ppermute x3 -> x24, waiting for transfers between devices: 0.01 us -> 57.2 us  [exchange(): return lax.ppermute(block, axis, [(i, i ^ delta) for i in range(count)])]
    all_to_all x1 -> x0, blocking collectives: 41.3 us -> none  [local(): lax.all_to_all(orbitals, 'grid', split_axis=1, concat_axis=0, tiled=True)]
    pallas_call x0 -> x2, Pallas kernels: none -> 27.6 us  [the longest x1 21.8 us: log_pivots(): pl.pallas_call(functools.partial(pivots_kernel, sets), out_shape=jax.Shap...]
    ppermute x3 -> x24, starting transfers between devices: 5.56 us -> 29.7 us  [exchange(): return lax.ppermute(block, axis, [(i, i ^ delta) for i in range(count)])]
    gather x8 -> x0, local copies, waits for them, and re-layouts: 14.7 us -> none  [the longest x4 10 us: log_pivots(): return jnp.log(jnp.diagonal(cholesky_factor))]
  transfers between devices with their start and end apart: 8 -> 24, of which waited for: 5 -> 16; matrix products, arithmetic and copies ran while one was open for 32% -> 3% of each run, Pallas kernels for 0% -> 0%
where the time goes in v1:
time: 130 us
  waiting for transfers between devices  57.2 us (44%)
  starting transfers between devices  29.7 us (23%)
  Pallas kernels  27.6 us (21%)
  other arithmetic  5.79 us (4%)
  between operations  4.09 us (3%)
  matrix products  3.03 us (2%)
  local copies, waits for them, and re-layouts  2.52 us (2%)
    ppermute x24, waiting for transfers between devices, exchange(): return lax.ppermute(block, axis, [(i, i ^ delta) for i in range(count)])  57.2 us
    ppermute x24, starting transfers between devices, exchange(): return lax.ppermute(block, axis, [(i, i ^ delta) for i in range(count)])  29.7 us
    pallas_call x1, Pallas kernels, log_pivots(): pl.pallas_call(functools.partial(pivots_kernel, sets), out_shape=jax.Shap...  21.8 us
    pallas_call x1, Pallas kernels, select_points(): pl.pallas_call(select_kernel, grid_spec=pltpu.PrefetchScalarGridSpec(num_...  5.8 us
  transfers between devices with their start and end apart: 24, of which 16 were waited for; matrix products, arithmetic and copies ran while one was open for 3% of the time, Pallas kernels for 0%

profile of v1, /device:TPU:0, one launch (start us, length us, event | category | flops | bytes accessed | tf_op | source)
XLA Modules:
  0.0 129.8 jit_solution(11808036352741847730)
XLA Ops:
  0.7 0.8 slice_subtract_fusion
  1.5 3.0 %collective-permute-start.4 = (s32[1,1,256]{2,1,0:T(1,128)S(1)}, s32[1,1,256]{2,1,0:T(1,128)S(1)}, u32[]{:S(2)}, u32[]{:S(2)}) collective-permute-start(s32[1,1,256]{2,1,0:T(1,128)S(1)} %get-tuple-element.36), channel_id=1, source_target_pairs={{0,4},{4,0},{8,12},{12,8},{16,20},{20,16},{24,28},{28,24},{1,5},{5... | collective-permute-start | bytes 3080 | tf_op jit(solution)/shard_map/ppermute | solution.py:22
  4.5 1.5 %collective-permute-done.4 = s32[1,1,256]{2,1,0:T(1,128)S(1)} collective-permute-done((s32[1,1,256]{2,1,0:T(1,128)S(1)}, s32[1,1,256]{2,1,0:T(1,128)S(1)}, u32[]{:S(2)}, u32[]{:S(2)}) %collective-permute-start.4) | collective-permute-done | bytes 1056 | tf_op jit(solution)/shard_map/ppermute | solution.py:22
  6.1 2.1 %collective-permute-start.5 = (s32[2,1,256]{2,1,0:T(1,128)S(1)}, s32[2,1,256]{2,1,0:T(1,128)S(1)}, u32[]{:S(2)}, u32[]{:S(2)}) collective-permute-start(s32[2,1,256]{2,1,0:T(1,128)S(1)} %pad_add_fusion.2), channel_id=1, source_target_pairs={{0,8},{4,12},{8,0},{12,4},{16,24},{20,28},{24,16},{28,20},{1,9},{5... | collective-permute-start | bytes 6152 | tf_op jit(solution)/shard_map/ppermute | solution.py:22
  8.2 1.6 %collective-permute-done.5 = s32[2,1,256]{2,1,0:T(1,128)S(1)} collective-permute-done((s32[2,1,256]{2,1,0:T(1,128)S(1)}, s32[2,1,256]{2,1,0:T(1,128)S(1)}, u32[]{:S(2)}, u32[]{:S(2)}) %collective-permute-start.5) | collective-permute-done | bytes 2080 | tf_op jit(solution)/shard_map/ppermute | solution.py:22
  9.7 3.0 %collective-permute-start.6 = (s32[4,1,256]{2,1,0:T(1,128)S(1)}, s32[4,1,256]{2,1,0:T(1,128)S(1)}, u32[]{:S(2)}, u32[]{:S(2)}) collective-permute-start(s32[4,1,256]{2,1,0:T(1,128)S(1)} %pad_add_fusion.1), channel_id=1, source_target_pairs={{0,16},{4,20},{8,24},{12,28},{16,0},{20,4},{24,8},{28,12},{1,17},{... | collective-permute-start | bytes 12296 | tf_op jit(solution)/shard_map/ppermute | solution.py:22
  12.8 1.6 %collective-permute-done.6 = s32[4,1,256]{2,1,0:T(1,128)S(1)} collective-permute-done((s32[4,1,256]{2,1,0:T(1,128)S(1)}, s32[4,1,256]{2,1,0:T(1,128)S(1)}, u32[]{:S(2)}, u32[]{:S(2)}) %collective-permute-start.6) | collective-permute-done | bytes 4128 | tf_op jit(solution)/shard_map/ppermute | solution.py:22
  14.3 0.6 pad_add_fusion.pivots_ref
  14.9 5.8 %shard_map.59 = bf16[2,128,1024]{2,1,0:T(8,128)(2,1)} custom-call(s32[1]{0:T(128)} %bitcast.3.where_ref, s32[8,1,256]{2,1,0:T(1,128)} %pad_add_fusion.pivots_ref, bf16[128,4096]{1,0:T(8,128)(2,1)} %orbitals_ref.1), custom_call_target="tpu_custom_call" | custom-call | tf_op jit(solution)/shard_map/pallas_call | solution.py:44
  20.7 1.1 slice_bitcast_fusion
  21.8 1.9 %collective-permute-start.8 = (bf16[128,1024]{1,0:T(8,128)(2,1)S(1)}, bf16[128,1024]{1,0:T(8,128)(2,1)S(1)}, u32[]{:S(2)}, u32[]{:S(2)}) collective-permute-start(bf16[128,1024]{1,0:T(8,128)(2,1)S(1)} %get-tuple-element.14), channel_id=1, source_target_pairs={{0,4},{4,0},{8,12},{12,8},{16,20},{20,16},{24,28},{28,24},{1,5},{5... | collective-permute-start | bytes 786440 | tf_op jit(solution)/shard_map/ppermute | solution.py:22
  23.8 1.6 %collective-permute-start = (bf16[2,128,512]{2,1,0:T(8,128)(2,1)S(1)}, bf16[2,128,512]{2,1,0:T(8,128)(2,1)S(1)}, u32[]{:S(2)}, u32[]{:S(2)}) collective-permute-start(bf16[2,128,512]{2,1,0:T(8,128)(2,1)S(1)} %get-tuple-element.13), channel_id=1, source_target_pairs={{0,2},{1,3},{2,0},{3,1},{4,6},{5,7},{6,4},{7,5},{8,10},{9,11},{10,... | collective-permute-start | bytes 786440 | tf_op jit(solution)/shard_map/ppermute | solution.py:22
  25.3 0.5 collective-permute-start.7
  25.8 2.9 %collective-permute-done.8 = bf16[128,1024]{1,0:T(8,128)(2,1)S(1)} collective-permute-done((bf16[128,1024]{1,0:T(8,128)(2,1)S(1)}, bf16[128,1024]{1,0:T(8,128)(2,1)S(1)}, u32[]{:S(2)}, u32[]{:S(2)}) %collective-permute-start.8) | collective-permute-done | bytes 262176 | tf_op jit(solution)/shard_map/ppermute | solution.py:22
  28.8 3.3 %collective-permute-start.9 = (bf16[128,1024]{1,0:T(8,128)(2,1)S(1)}, bf16[128,1024]{1,0:T(8,128)(2,1)S(1)}, u32[]{:S(2)}, u32[]{:S(2)}) collective-permute-start(bf16[128,1024]{1,0:T(8,128)(2,1)S(1)} %collective-permute-done.8), channel_id=1, source_target_pairs={{0,2},{1,3},{2,0},{3,1},{4,6},{5,7},{6,4},{7,5},{8,10},{9,11},{10,... | collective-permute-start | bytes 786440 | tf_op jit(solution)/shard_map/ppermute | solution.py:22
  32.0 1.5 %collective-permute-start.1 = (bf16[2,128,512]{2,1,0:T(8,128)(2,1)S(1)}, bf16[2,128,512]{2,1,0:T(8,128)(2,1)}, u32[]{:S(2)}, u32[]{:S(2)}) collective-permute-start(bf16[2,128,512]{2,1,0:T(8,128)(2,1)S(1)} %get-tuple-element.12), channel_id=1, source_target_pairs={{0,4},{4,0},{8,12},{12,8},{16,20},{20,16},{24,28},{28,24},{1,5},{5... | collective-permute-start | bytes 786440 | tf_op jit(solution)/shard_map/ppermute | solution.py:22
  33.5 0.6 collective-permute-start.2
  34.1 2.5 %collective-permute-done.7 = bf16[128,1024]{1,0:T(8,128)(2,1)S(1)} collective-permute-done((bf16[128,1024]{1,0:T(8,128)(2,1)S(1)}, bf16[128,1024]{1,0:T(8,128)(2,1)S(1)}, u32[]{:S(2)}, u32[]{:S(2)}) %collective-permute-start.7) | collective-permute-done | bytes 262176 | tf_op jit(solution)/shard_map/ppermute | solution.py:22
  36.6 2.8 %collective-permute-done.9 = bf16[128,1024]{1,0:T(8,128)(2,1)S(1)} collective-permute-done((bf16[128,1024]{1,0:T(8,128)(2,1)S(1)}, bf16[128,1024]{1,0:T(8,128)(2,1)S(1)}, u32[]{:S(2)}, u32[]{:S(2)}) %collective-permute-start.9) | collective-permute-done | bytes 262176 | tf_op jit(solution)/shard_map/ppermute | solution.py:22
  39.6 1.8 %collective-permute-done.2 = bf16[2,128,512]{2,1,0:T(8,128)(2,1)} collective-permute-done((bf16[2,128,512]{2,1,0:T(8,128)(2,1)S(1)}, bf16[2,128,512]{2,1,0:T(8,128)(2,1)}, u32[]{:S(2)}, u32[]{:S(2)}) %collective-permute-start.2) | collective-permute-done | bytes 262176 | tf_op jit(solution)/shard_map/ppermute | solution.py:22
  41.3 1.1 pad_maximum_fusion
  42.8 1.7 %collective-permute-done.3 = bf16[2,512,256]{2,1,0:T(8,128)(2,1)S(1)} collective-permute-done((bf16[2,512,256]{2,1,0:T(8,128)(2,1)S(1)}, bf16[2,512,256]{2,1,0:T(8,128)(2,1)S(1)}, u32[]{:S(2)}, u32[]{:S(2)}) %collective-permute-start.3) | collective-permute-done | bytes 524320 | tf_op jit(solution)/shard_map/ppermute | solution.py:22
  44.5 0.5 convolution_bitcast_fusion.1
  45.0 0.5 convolution_bitcast_fusion
  45.5 0.7 abs_reduce_fusion
  47.2 1.6 %collective-permute-start.11 = (f16[528,512]{1,0:T(8,128)(2,1)S(1)}, f16[528,512]{1,0:T(8,128)(2,1)S(1)}, u32[]{:S(2)}, u32[]{:S(2)}) collective-permute-start(f16[528,512]{1,0:T(8,128)(2,1)S(1)} %concatenate.61), channel_id=1, source_target_pairs={{0,8},{4,12},{8,0},{12,4},{16,24},{20,28},{24,16},{28,20},{1,9},{5... | collective-permute-start | bytes 1622024 | tf_op jit(solution)/shard_map/ppermute | solution.py:22
  48.8 0.5 convolution_bitcast_fusion.2
  49.3 0.5 convolution_bitcast_fusion.3
  49.8 11.8 %collective-permute-done.11 = f16[528,512]{1,0:T(8,128)(2,1)S(1)} collective-permute-done((f16[528,512]{1,0:T(8,128)(2,1)S(1)}, f16[528,512]{1,0:T(8,128)(2,1)S(1)}, u32[]{:S(2)}, u32[]{:S(2)}) %collective-permute-start.11) | collective-permute-done | bytes 540704 | tf_op jit(solution)/shard_map/ppermute | solution.py:22
  61.6 0.5 slice.76
  63.2 0.7 abs_reduce_fusion.1
  64.7 2.6 %collective-permute-start.12 = (f16[528,256]{1,0:T(8,128)(2,1)S(1)}, f16[528,256]{1,0:T(8,128)(2,1)S(1)}, u32[]{:S(2)}, u32[]{:S(2)}) collective-permute-start(f16[528,256]{1,0:T(8,128)(2,1)S(1)} %concatenate.62), channel_id=1, source_target_pairs={{0,16},{4,20},{8,24},{12,28},{16,0},{20,4},{24,8},{28,12},{1,17},{... | collective-permute-start | bytes 811016 | tf_op jit(solution)/shard_map/ppermute | solution.py:22
  67.3 11.8 %collective-permute-done.12 = f16[528,256]{1,0:T(8,128)(2,1)S(1)} collective-permute-done((f16[528,256]{1,0:T(8,128)(2,1)S(1)}, f16[528,256]{1,0:T(8,128)(2,1)S(1)}, u32[]{:S(2)}, u32[]{:S(2)}) %collective-permute-start.12) | collective-permute-done | bytes 270368 | tf_op jit(solution)/shard_map/ppermute | solution.py:22
  79.1 0.5 slice.80
  80.5 1.5 %collective-permute-start.13 = (bf16[256,256]{1,0:T(8,128)(2,1)S(1)}, bf16[256,256]{1,0:T(8,128)(2,1)S(1)}, u32[]{:S(2)}, u32[]{:S(2)}) collective-permute-start(bf16[256,256]{1,0:T(8,128)(2,1)S(1)} %fusion.16), channel_id=1, source_target_pairs={{0,4},{4,0},{8,12},{12,8},{16,20},{20,16},{24,28},{28,24},{1,5},{5... | collective-permute-start | bytes 393224 | tf_op jit(solution)/shard_map/ppermute | solution.py:22
  82.4 3.2 %collective-permute-done.13 = bf16[256,256]{1,0:T(8,128)(2,1)S(1)} collective-permute-done((bf16[256,256]{1,0:T(8,128)(2,1)S(1)}, bf16[256,256]{1,0:T(8,128)(2,1)S(1)}, u32[]{:S(2)}, u32[]{:S(2)}) %collective-permute-start.13) | collective-permute-done | bytes 131104 | tf_op jit(solution)/shard_map/ppermute | solution.py:22
  85.8 0.3 collective-permute-start.20
  86.0 1.1 collective-permute-start.14
  87.2 0.7 collective-permute-done.18
  88.2 2.8 %collective-permute-done.14 = bf16[256,256]{1,0:T(8,128)(2,1)S(1)} collective-permute-done((bf16[256,256]{1,0:T(8,128)(2,1)S(1)}, bf16[256,256]{1,0:T(8,128)(2,1)S(1)}, u32[]{:S(2)}, u32[]{:S(2)}) %collective-permute-start.14) | collective-permute-done | bytes 131104 | tf_op jit(solution)/shard_map/ppermute | solution.py:22
  91.2 1.9 %collective-permute-start.22 = (bf16[256,256]{1,0:T(8,128)(2,1)S(1)}, bf16[256,256]{1,0:T(8,128)(2,1)S(1)}, u32[]{:S(2)}, u32[]{:S(2)}) collective-permute-start(bf16[256,256]{1,0:T(8,128)(2,1)S(1)} %fusion.1), channel_id=1, source_target_pairs={{0,2},{1,3},{2,0},{3,1},{4,6},{5,7},{6,4},{7,5},{8,10},{9,11},{10,... | collective-permute-start | bytes 393224 | tf_op jit(solution)/shard_map/ppermute | solution.py:22
  93.1 2.4 %collective-permute-start.15 = (bf16[256,256]{1,0:T(8,128)(2,1)S(1)}, bf16[256,256]{1,0:T(8,128)(2,1)S(1)}, u32[]{:S(2)}, u32[]{:S(2)}) collective-permute-start(bf16[256,256]{1,0:T(8,128)(2,1)S(1)} %fusion.1), channel_id=1, source_target_pairs={{0,16},{4,20},{8,24},{12,28},{16,0},{20,4},{24,8},{28,12},{1,17},{... | collective-permute-start | bytes 393224 | tf_op jit(solution)/shard_map/ppermute | solution.py:22
  95.9 4.5 %collective-permute-done.15 = bf16[256,256]{1,0:T(8,128)(2,1)S(1)} collective-permute-done((bf16[256,256]{1,0:T(8,128)(2,1)S(1)}, bf16[256,256]{1,0:T(8,128)(2,1)S(1)}, u32[]{:S(2)}, u32[]{:S(2)}) %collective-permute-start.15) | collective-permute-done | bytes 131104 | tf_op jit(solution)/shard_map/ppermute | solution.py:22
  100.6 0.3 collective-permute-start.16
  101.0 4.6 %collective-permute-done.16 = bf16[256,256]{1,0:T(8,128)(2,1)S(1)} collective-permute-done((bf16[256,256]{1,0:T(8,128)(2,1)S(1)}, bf16[256,256]{1,0:T(8,128)(2,1)S(1)}, u32[]{:S(2)}, u32[]{:S(2)}) %collective-permute-start.16) | collective-permute-done | bytes 131104 | tf_op jit(solution)/shard_map/ppermute | solution.py:22
  106.0 1.3 %collective-permute-done.17 = bf16[512,256]{1,0:T(8,128)(2,1)S(1)} collective-permute-done((bf16[512,256]{1,0:T(8,128)(2,1)S(1)}, bf16[512,256]{1,0:T(8,128)(2,1)S(1)}, u32[]{:S(2)}, u32[]{:S(2)}) %collective-permute-start.17) | collective-permute-done | bytes 262176 | tf_op jit(solution)/shard_map/ppermute | solution.py:22
  107.5 21.8 %shard_map.60 = f32[4,256]{1,0:T(4,128)S(1)} custom-call(bf16[1024,256]{1,0:T(8,128)(2,1)S(1)} %bitcast.88, bf16[1024,256]{1,0:T(8,128)(2,1)S(1)} %bitcast.85, bf16[1024,256]{1,0:T(8,128)(2,1)S(1)} %bitcast.84, bf16[1024,256]{1,0:T(8,128)(2,1)S(1)} %bitcast.86), custom_call_target="tpu_custom_call" | custom-call | tf_op jit(solution)/shard_map/pallas_call | solution.py:113
  129.3 0.6 reduce_sum.9
  (74 shorter events, 3.6 us)
Async XLA Ops:
  0.6 23.1 %copy-start.4 = (bf16[128,1024]{1,0:T(8,128)(2,1)S(1)}, bf16[128,1024]{1,0:T(8,128)(2,1)}, u32[]{:S(2)}) copy-start(bf16[128,1024]{1,0:T(8,128)(2,1)} %param.5) | copy-start | bytes 786436
  0.6 23.1 %copy-start.5 = (bf16[128,1024]{1,0:T(8,128)(2,1)S(1)}, bf16[128,1024]{1,0:T(8,128)(2,1)}, u32[]{:S(2)}) copy-start(bf16[128,1024]{1,0:T(8,128)(2,1)} %param.6) | copy-start | bytes 786436
  1.5 4.6 %collective-permute-start.4 = (s32[1,1,256]{2,1,0:T(1,128)S(1)}, s32[1,1,256]{2,1,0:T(1,128)S(1)}, u32[]{:S(2)}, u32[]{:S(2)}) collective-permute-start(s32[1,1,256]{2,1,0:T(1,128)S(1)} %get-tuple-element.36), channel_id=1, source_target_pairs={{0,4},{4,0},{8,12},{12,8},{16,20},{20,16},{24,28},{28,24},{1,5},{5... | collective-permute-start | bytes 3080 | tf_op jit(solution)/shard_map/ppermute | solution.py:22
  6.1 3.6 %collective-permute-start.5 = (s32[2,1,256]{2,1,0:T(1,128)S(1)}, s32[2,1,256]{2,1,0:T(1,128)S(1)}, u32[]{:S(2)}, u32[]{:S(2)}) collective-permute-start(s32[2,1,256]{2,1,0:T(1,128)S(1)} %pad_add_fusion.2), channel_id=1, source_target_pairs={{0,8},{4,12},{8,0},{12,4},{16,24},{20,28},{24,16},{28,20},{1,9},{5... | collective-permute-start | bytes 6152 | tf_op jit(solution)/shard_map/ppermute | solution.py:22
  9.7 4.6 %collective-permute-start.6 = (s32[4,1,256]{2,1,0:T(1,128)S(1)}, s32[4,1,256]{2,1,0:T(1,128)S(1)}, u32[]{:S(2)}, u32[]{:S(2)}) collective-permute-start(s32[4,1,256]{2,1,0:T(1,128)S(1)} %pad_add_fusion.1), channel_id=1, source_target_pairs={{0,16},{4,20},{8,24},{12,28},{16,0},{20,4},{24,8},{28,12},{1,17},{... | collective-permute-start | bytes 12296 | tf_op jit(solution)/shard_map/ppermute | solution.py:22
  21.8 7.0 %collective-permute-start.8 = (bf16[128,1024]{1,0:T(8,128)(2,1)S(1)}, bf16[128,1024]{1,0:T(8,128)(2,1)S(1)}, u32[]{:S(2)}, u32[]{:S(2)}) collective-permute-start(bf16[128,1024]{1,0:T(8,128)(2,1)S(1)} %get-tuple-element.14), channel_id=1, source_target_pairs={{0,4},{4,0},{8,12},{12,8},{16,20},{20,16},{24,28},{28,24},{1,5},{5... | collective-permute-start | bytes 786440 | tf_op jit(solution)/shard_map/ppermute | solution.py:22
  23.8 9.8 %collective-permute-start = (bf16[2,128,512]{2,1,0:T(8,128)(2,1)S(1)}, bf16[2,128,512]{2,1,0:T(8,128)(2,1)S(1)}, u32[]{:S(2)}, u32[]{:S(2)}) collective-permute-start(bf16[2,128,512]{2,1,0:T(8,128)(2,1)S(1)} %get-tuple-element.13), channel_id=1, source_target_pairs={{0,2},{1,3},{2,0},{3,1},{4,6},{5,7},{6,4},{7,5},{8,10},{9,11},{10,... | collective-permute-start | bytes 786440 | tf_op jit(solution)/shard_map/ppermute | solution.py:22
  25.3 11.3 %collective-permute-start.7 = (bf16[128,1024]{1,0:T(8,128)(2,1)S(1)}, bf16[128,1024]{1,0:T(8,128)(2,1)S(1)}, u32[]{:S(2)}, u32[]{:S(2)}) collective-permute-start(bf16[128,1024]{1,0:T(8,128)(2,1)S(1)} %get-tuple-element.15), channel_id=1, source_target_pairs={{0,2},{1,3},{2,0},{3,1},{4,6},{5,7},{6,4},{7,5},{8,10},{9,11},{10,... | collective-permute-start | bytes 786440 | tf_op jit(solution)/shard_map/ppermute | solution.py:22
  28.8 10.6 %collective-permute-start.9 = (bf16[128,1024]{1,0:T(8,128)(2,1)S(1)}, bf16[128,1024]{1,0:T(8,128)(2,1)S(1)}, u32[]{:S(2)}, u32[]{:S(2)}) collective-permute-start(bf16[128,1024]{1,0:T(8,128)(2,1)S(1)} %collective-permute-done.8), channel_id=1, source_target_pairs={{0,2},{1,3},{2,0},{3,1},{4,6},{5,7},{6,4},{7,5},{8,10},{9,11},{10,... | collective-permute-start | bytes 786440 | tf_op jit(solution)/shard_map/ppermute | solution.py:22
  32.0 7.5 %collective-permute-start.1 = (bf16[2,128,512]{2,1,0:T(8,128)(2,1)S(1)}, bf16[2,128,512]{2,1,0:T(8,128)(2,1)}, u32[]{:S(2)}, u32[]{:S(2)}) collective-permute-start(bf16[2,128,512]{2,1,0:T(8,128)(2,1)S(1)} %get-tuple-element.12), channel_id=1, source_target_pairs={{0,4},{4,0},{8,12},{12,8},{16,20},{20,16},{24,28},{28,24},{1,5},{5... | collective-permute-start | bytes 786440 | tf_op jit(solution)/shard_map/ppermute | solution.py:22
  33.5 7.8 %collective-permute-start.2 = (bf16[2,128,512]{2,1,0:T(8,128)(2,1)S(1)}, bf16[2,128,512]{2,1,0:T(8,128)(2,1)}, u32[]{:S(2)}, u32[]{:S(2)}) collective-permute-start(bf16[2,128,512]{2,1,0:T(8,128)(2,1)S(1)} %collective-permute-done), channel_id=1, source_target_pairs={{0,4},{4,0},{8,12},{12,8},{16,20},{20,16},{24,28},{28,24},{1,5},{5... | collective-permute-start | bytes 786440 | tf_op jit(solution)/shard_map/ppermute | solution.py:22
  39.4 3.3 %collective-permute-start.10 = (bf16[512,1024]{1,0:T(8,128)(2,1)S(1)}, bf16[512,1024]{1,0:T(8,128)(2,1)S(1)}, u32[]{:S(2)}, u32[]{:S(2)}) collective-permute-start(bf16[512,1024]{1,0:T(8,128)(2,1)S(1)} %pad_maximum_fusion.1), channel_id=1, source_target_pairs={{0,1},{1,0},{2,3},{3,2},{4,5},{5,4},{6,7},{7,6},{8,9},{9,8},{10,11... | collective-permute-start | bytes 3145736 | tf_op jit(solution)/shard_map/ppermute | solution.py:22
  39.5 3.1 %copy-start.1 = (bf16[2,128,1024]{2,1,0:T(8,128)(2,1)S(1)}, bf16[2,128,1024]{2,1,0:T(8,128)(2,1)}, u32[]{:S(2)}) copy-start(bf16[2,128,1024]{2,1,0:T(8,128)(2,1)} %shard_map.59) | copy-start | bytes 1572868
  42.5 2.5 %copy-start.2 = (bf16[2,512,256]{2,1,0:T(8,128)(2,1)}, bf16[2,512,256]{2,1,0:T(8,128)(2,1)S(1)}, u32[]{:S(2)}) copy-start(bf16[2,512,256]{2,1,0:T(8,128)(2,1)S(1)} %get-tuple-element.2) | copy-start | bytes 1572868
  42.5 2.0 %collective-permute-start.3 = (bf16[2,512,256]{2,1,0:T(8,128)(2,1)S(1)}, bf16[2,512,256]{2,1,0:T(8,128)(2,1)S(1)}, u32[]{:S(2)}, u32[]{:S(2)}) collective-permute-start(bf16[2,512,256]{2,1,0:T(8,128)(2,1)S(1)} %get-tuple-element.3), channel_id=1, source_target_pairs={{0,1},{1,0},{2,3},{3,2},{4,5},{5,4},{6,7},{7,6},{8,9},{9,8},{10,11... | collective-permute-start | bytes 1572872 | tf_op jit(solution)/shard_map/ppermute | solution.py:22
  42.8 2.6 %copy-start.6 = (bf16[1024,1024]{1,0:T(8,128)(2,1)}, bf16[1024,1024]{1,0:T(8,128)(2,1)S(1)}, u32[]{:S(2)}) copy-start(bf16[1024,1024]{1,0:T(8,128)(2,1)S(1)} %constant_dynamic-update-slice_fusion) | copy-start | bytes 6291460
  44.5 1.0 copy-start.8
  45.5 3.3 %copy-start.3 = (bf16[2,512,256]{2,1,0:T(8,128)(2,1)S(1)}, bf16[2,512,256]{2,1,0:T(8,128)(2,1)}, u32[]{:S(2)}) copy-start(bf16[2,512,256]{2,1,0:T(8,128)(2,1)} %copy-done.2) | copy-start | bytes 1572868
  46.2 2.7 %copy-start.9 = (bf16[2,512,256]{2,1,0:T(8,128)(2,1)S(1)}, bf16[2,512,256]{2,1,0:T(8,128)(2,1)}, u32[]{:S(2)}) copy-start(bf16[2,512,256]{2,1,0:T(8,128)(2,1)} %copy-done.8) | copy-start | bytes 1572868
  47.0 1.9 %copy-start.7 = (bf16[1024,1024]{1,0:T(8,128)(2,1)S(1)}, bf16[1024,1024]{1,0:T(8,128)(2,1)}, u32[]{:S(2)}) copy-start(bf16[1024,1024]{1,0:T(8,128)(2,1)} %copy-done.6) | copy-start | bytes 6291460
  47.2 14.4 %collective-permute-start.11 = (f16[528,512]{1,0:T(8,128)(2,1)S(1)}, f16[528,512]{1,0:T(8,128)(2,1)S(1)}, u32[]{:S(2)}, u32[]{:S(2)}) collective-permute-start(f16[528,512]{1,0:T(8,128)(2,1)S(1)} %concatenate.61), channel_id=1, source_target_pairs={{0,8},{4,12},{8,0},{12,4},{16,24},{20,28},{24,16},{28,20},{1,9},{5... | collective-permute-start | bytes 1622024 | tf_op jit(solution)/shard_map/ppermute | solution.py:22
  64.7 14.4 %collective-permute-start.12 = (f16[528,256]{1,0:T(8,128)(2,1)S(1)}, f16[528,256]{1,0:T(8,128)(2,1)S(1)}, u32[]{:S(2)}, u32[]{:S(2)}) collective-permute-start(f16[528,256]{1,0:T(8,128)(2,1)S(1)} %concatenate.62), channel_id=1, source_target_pairs={{0,16},{4,20},{8,24},{12,28},{16,0},{20,4},{24,8},{28,12},{1,17},{... | collective-permute-start | bytes 811016 | tf_op jit(solution)/shard_map/ppermute | solution.py:22
  80.5 5.0 %collective-permute-start.13 = (bf16[256,256]{1,0:T(8,128)(2,1)S(1)}, bf16[256,256]{1,0:T(8,128)(2,1)S(1)}, u32[]{:S(2)}, u32[]{:S(2)}) collective-permute-start(bf16[256,256]{1,0:T(8,128)(2,1)S(1)} %fusion.16), channel_id=1, source_target_pairs={{0,4},{4,0},{8,12},{12,8},{16,20},{20,16},{24,28},{28,24},{1,5},{5... | collective-permute-start | bytes 393224 | tf_op jit(solution)/shard_map/ppermute | solution.py:22
  82.1 5.8 %collective-permute-start.18 = (bf16[256,256]{1,0:T(8,128)(2,1)S(1)}, bf16[256,256]{1,0:T(8,128)(2,1)S(1)}, u32[]{:S(2)}, u32[]{:S(2)}) collective-permute-start(bf16[256,256]{1,0:T(8,128)(2,1)S(1)} %fusion.16), channel_id=1, source_target_pairs={{0,2},{1,3},{2,0},{3,1},{4,6},{5,7},{6,4},{7,5},{8,10},{9,11},{10,... | collective-permute-start | bytes 393224 | tf_op jit(solution)/shard_map/ppermute | solution.py:22
  85.8 9.8 %collective-permute-start.20 = (bf16[256,256]{1,0:T(8,128)(2,1)S(1)}, bf16[256,256]{1,0:T(8,128)(2,1)S(1)}, u32[]{:S(2)}, u32[]{:S(2)}) collective-permute-start(bf16[256,256]{1,0:T(8,128)(2,1)S(1)} %fusion), channel_id=1, source_target_pairs={{0,2},{1,3},{2,0},{3,1},{4,6},{5,7},{6,4},{7,5},{8,10},{9,11},{10,... | collective-permute-start | bytes 393224 | tf_op jit(solution)/shard_map/ppermute | solution.py:22
  86.0 5.0 %collective-permute-start.14 = (bf16[256,256]{1,0:T(8,128)(2,1)S(1)}, bf16[256,256]{1,0:T(8,128)(2,1)S(1)}, u32[]{:S(2)}, u32[]{:S(2)}) collective-permute-start(bf16[256,256]{1,0:T(8,128)(2,1)S(1)} %fusion), channel_id=1, source_target_pairs={{0,8},{4,12},{8,0},{12,4},{16,24},{20,28},{24,16},{28,20},{1,9},{5... | collective-permute-start | bytes 393224 | tf_op jit(solution)/shard_map/ppermute | solution.py:22
  87.9 18.1 %collective-permute-start.19 = (bf16[512,256]{1,0:T(8,128)(2,1)S(1)}, bf16[512,256]{1,0:T(8,128)(2,1)S(1)}, u32[]{:S(2)}, u32[]{:S(2)}) collective-permute-start(bf16[512,256]{1,0:T(8,128)(2,1)S(1)} %get-tuple-element.24), channel_id=1, source_target_pairs={{0,1},{1,0},{2,3},{3,2},{4,5},{5,4},{6,7},{7,6},{8,9},{9,8},{10,11... | collective-permute-start | bytes 786440 | tf_op jit(solution)/shard_map/ppermute | solution.py:22
  91.2 9.6 %collective-permute-start.22 = (bf16[256,256]{1,0:T(8,128)(2,1)S(1)}, bf16[256,256]{1,0:T(8,128)(2,1)S(1)}, u32[]{:S(2)}, u32[]{:S(2)}) collective-permute-start(bf16[256,256]{1,0:T(8,128)(2,1)S(1)} %fusion.1), channel_id=1, source_target_pairs={{0,2},{1,3},{2,0},{3,1},{4,6},{5,7},{6,4},{7,5},{8,10},{9,11},{10,... | collective-permute-start | bytes 393224 | tf_op jit(solution)/shard_map/ppermute | solution.py:22
  93.1 7.3 %collective-permute-start.15 = (bf16[256,256]{1,0:T(8,128)(2,1)S(1)}, bf16[256,256]{1,0:T(8,128)(2,1)S(1)}, u32[]{:S(2)}, u32[]{:S(2)}) collective-permute-start(bf16[256,256]{1,0:T(8,128)(2,1)S(1)} %fusion.1), channel_id=1, source_target_pairs={{0,16},{4,20},{8,24},{12,28},{16,0},{20,4},{24,8},{28,12},{1,17},{... | collective-permute-start | bytes 393224 | tf_op jit(solution)/shard_map/ppermute | solution.py:22
  95.6 10.2 %collective-permute-start.21 = (bf16[512,256]{1,0:T(8,128)(2,1)S(1)}, bf16[512,256]{1,0:T(8,128)(2,1)S(1)}, u32[]{:S(2)}, u32[]{:S(2)}) collective-permute-start(bf16[512,256]{1,0:T(8,128)(2,1)S(1)} %get-tuple-element.20), channel_id=1, source_target_pairs={{0,1},{1,0},{2,3},{3,2},{4,5},{5,4},{6,7},{7,6},{8,9},{9,8},{10,11... | collective-permute-start | bytes 786440 | tf_op jit(solution)/shard_map/ppermute | solution.py:22
  100.6 5.0 %collective-permute-start.16 = (bf16[256,256]{1,0:T(8,128)(2,1)S(1)}, bf16[256,256]{1,0:T(8,128)(2,1)S(1)}, u32[]{:S(2)}, u32[]{:S(2)}) collective-permute-start(bf16[256,256]{1,0:T(8,128)(2,1)S(1)} %fusion.2), channel_id=1, source_target_pairs={{0,2},{1,3},{2,0},{3,1},{4,6},{5,7},{6,4},{7,5},{8,10},{9,11},{10,... | collective-permute-start | bytes 393224 | tf_op jit(solution)/shard_map/ppermute | solution.py:22
  100.9 4.9 %collective-permute-start.23 = (bf16[512,256]{1,0:T(8,128)(2,1)S(1)}, bf16[512,256]{1,0:T(8,128)(2,1)S(1)}, u32[]{:S(2)}, u32[]{:S(2)}) collective-permute-start(bf16[512,256]{1,0:T(8,128)(2,1)S(1)} %get-tuple-element.16), channel_id=1, source_target_pairs={{0,1},{1,0},{2,3},{3,2},{4,5},{5,4},{6,7},{7,6},{8,9},{9,8},{10,11... | collective-permute-start | bytes 786440 | tf_op jit(solution)/shard_map/ppermute | solution.py:22
  105.7 1.6 %collective-permute-start.17 = (bf16[512,256]{1,0:T(8,128)(2,1)S(1)}, bf16[512,256]{1,0:T(8,128)(2,1)S(1)}, u32[]{:S(2)}, u32[]{:S(2)}) collective-permute-start(bf16[512,256]{1,0:T(8,128)(2,1)S(1)} %get-tuple-element.28), channel_id=1, source_target_pairs={{0,1},{1,0},{2,3},{3,2},{4,5},{5,4},{6,7},{7,6},{8,9},{9,8},{10,11... | collective-permute-start | bytes 786440 | tf_op jit(solution)/shard_map/ppermute | solution.py:22
  107.5 22.4 %copy-start = (bf16[2,512,256]{2,1,0:T(8,128)(2,1)}, bf16[2,512,256]{2,1,0:T(8,128)(2,1)S(1)}, u32[]{:S(2)}) copy-start(bf16[2,512,256]{2,1,0:T(8,128)(2,1)S(1)} %pad_maximum_fusion.4) | copy-start | bytes 1572868

commit v2 on v1

v2 whole, which is shorter than its diff:
```python
import functools

import jax
import jax.numpy as jnp
from jax import lax
from jax.experimental import pallas as pl
from jax.experimental.pallas import tpu as pltpu
from jax.sharding import PartitionSpec as P

ridge = 0.1
f32, bf16, f16 = jnp.float32, jnp.bfloat16, jnp.float16
step, height, lanes = 8, 32, 128
column_dims = (((0,), (0,)), ((), ()))


def bits_of(count):
    return count.bit_length() - 1


def exchange(block, axis, delta):
    count = lax.axis_size(axis)
    return lax.ppermute(block, axis, [(i, i ^ delta) for i in range(count)])


def reversed_bits(value, bits):
    out = 0
    for t in range(bits):
        out = out | ((value >> t) & 1) << (bits - 1 - t)
    return out


def select_kernel(where_ref, orders_ref, orbitals_ref, out_ref):
    kept = orders_ref.shape[2]
    width = orbitals_ref.shape[1] // 2
    index = lax.broadcasted_iota(jnp.int32, (width, kept), 0)
    for j in range(2):
        side = where_ref[0] & 1 ^ j
        one_hot = (index == orders_ref[side]).astype(f32).astype(bf16)
        columns = orbitals_ref[:, j * width : (j + 1) * width]
        out_ref[side, 0] = jnp.dot(columns, one_hot, preferred_element_type=f32).astype(bf16)


def select_points(orbitals, orders, here):
    groups, _, kept = orders.shape
    rows, points = orbitals.shape
    high = bits_of(groups) - 1
    parts = 2 if high else 1
    per_part = groups // 2 // parts

    def out_block(k, w):
        place = reversed_bits(k, high)
        return (0, place // per_part, 0, place % per_part)

    return pl.pallas_call(
        select_kernel,
        grid_spec=pltpu.PrefetchScalarGridSpec(
            num_scalar_prefetch=1,
            grid=(groups // 2,),
            in_specs=[
                pl.BlockSpec((2, 1, kept), lambda k, w: (k, 0, 0)),
                pl.BlockSpec((rows, 2 * points // groups), lambda k, w: (0, w[0] >> 1 ^ k)),
            ],
            out_specs=pl.BlockSpec((2, 1, rows, kept), out_block),
        ),
        out_shape=jax.ShapeDtypeStruct((2, parts, rows, per_part * kept), bf16),
    )(here[None], orders, orbitals)


def split3(v):
    a = v.astype(bf16)
    rest = v - a.astype(f32)
    b = rest.astype(bf16)
    c = (rest - b.astype(f32)).astype(bf16)
    return a, b, c


def eliminate(block, first):
    width = block.shape[1]
    lane = lax.broadcasted_iota(jnp.int32, (1, width), 1)
    on_diagonal = lax.broadcasted_iota(jnp.int32, (step, width), 1) - lax.broadcasted_iota(
        jnp.int32, (step, width), 0
    )
    done, scaled, diagonal = [], [], 0.0
    for corner in range(0, block.shape[0], step):
        below = lax.broadcasted_iota(jnp.int32, (block.shape[0], 1), 0)
        start = first + corner
        columns = [jnp.sum(jnp.where(lane == start + j, block, 0.0), axis=1, keepdims=True) for j in range(step)]
        heads, inverses = [], []
        for j in range(step):
            head = columns[j][j : j + 1, :]
            inverse = 1.0 / head
            factor = jnp.where(below > j, columns[j] * inverse, 0.0)
            block = block - factor * block[j : j + 1, :]
            for c in range(j + 1, step):
                columns[c] = columns[c] - factor * columns[c][j : j + 1, :]
            heads.append(head)
            inverses.append(inverse)
        heads = jnp.concatenate(heads, axis=0)
        diagonal = diagonal + jnp.sum(jnp.where(on_diagonal == start, heads, 0.0), axis=0, keepdims=True)
        done.append(block[:step])
        scaled.append(block[:step] * jnp.concatenate(inverses, axis=0))
        block = block[step:]
    return jnp.concatenate(done, axis=0), jnp.concatenate(scaled, axis=0), diagonal


def outer(scaled, rows):
    u1, u2, u3 = split3(rows)
    v1, v2, v3 = split3(scaled)
    left = jnp.concatenate([v1, v1, v2, v2, v1, v3], axis=0)
    right = jnp.concatenate([u1, u2, u1, u2, u3, u1], axis=0)
    return lax.dot_general(left, right, column_dims, preferred_element_type=f32)


def pivots_kernel(sets, *refs):
    cands, out_ref, grams = refs[:sets], refs[sets], refs[sets + 1 :]
    rows, n = cands[0].shape
    diagonal = lax.broadcasted_iota(jnp.int32, (n, n), 0) == lax.broadcasted_iota(jnp.int32, (n, n), 1)
    shift = jnp.where(diagonal, f32(ridge), f32(0))
    for cand, gram in zip(cands, grams):
        product = lax.dot_general(cand[...], cand[...], column_dims, preferred_element_type=f32)
        gram[...] = product * f32(1 / rows) + shift
    out_ref[...] = jnp.zeros_like(out_ref)
    for base in range(0, n, lanes):

        def panel(k, carry, base=base):
            first = pl.multiple_of(k * height, height)
            parts = [eliminate(gram[pl.ds(base + first, height), base:], first) for gram in grams]
            for q, (done, scaled, diagonal) in enumerate(parts):
                out_ref[q : q + 1, base:] += diagonal
                grams[q][base:, base:] -= outer(scaled, done)
            return carry

        lax.fori_loop(0, min(lanes, n - base) // height, panel, 0)
    out_ref[...] = 0.5 * jnp.log(out_ref[...])


def log_pivots(cands):
    sets, (rows, n) = len(cands), cands[0].shape
    return pl.pallas_call(
        functools.partial(pivots_kernel, sets),
        out_shape=jax.ShapeDtypeStruct((sets, n), f32),
        in_specs=[pl.BlockSpec(memory_space=pltpu.VMEM)] * sets,
        out_specs=pl.BlockSpec(memory_space=pltpu.VMEM),
        scratch_shapes=[pltpu.VMEM((n, n), f32)] * sets,
        compiler_params=pltpu.CompilerParams(vmem_limit_bytes=40 << 20),
    )(*cands)


def half_of(block, upper):
    size = block.shape[-1] // 2
    return lax.dynamic_slice_in_dim(block, upper * size, size, axis=block.ndim - 1)


def pack(block):
    block = block.reshape(-1, block.shape[-1])
    exponent = jnp.ceil(jnp.log2(jnp.maximum(jnp.max(jnp.abs(block)), f32(1e-30))))
    codes = (block * jnp.exp2(14.0 - exponent)).astype(f16)
    tag = jnp.full((16, codes.shape[-1]), exponent, f32).astype(f16)
    return jnp.concatenate([codes, tag], axis=0)


def unpack(codes, shape):
    return codes[:-16].astype(f32).reshape(shape) * jnp.exp2(codes[-1, 0].astype(f32) - 14.0)


def local(orbitals, w_first, w_second, pivots):
    here, place = lax.axis_index("grid"), lax.axis_index("band")
    grid_bits, band_bits = bits_of(lax.axis_size("grid")), bits_of(lax.axis_size("band"))
    order = pivots[0]
    kept = order.shape[1]

    mixing = [jnp.stack([w_first, w_second])]
    for t in reversed(range(1, band_bits)):
        upper = place >> t & 1
        got = [exchange(half_of(m, 1 - upper), "band", 1 << t) for m in mixing]
        mixing = [half_of(m, upper) for m in mixing] + got
    near = exchange(mixing[0], "grid", 1)

    orders = order[:1][None]
    for t in range(grid_bits):
        if t == grid_bits - 1:
            orders, mixing, near = lax.optimization_barrier((orders, mixing, near))
        orders = jnp.concatenate([orders, exchange(orders, "grid", 1 << t)], axis=0)
    mixing = jnp.concatenate(mixing + [near] + [exchange(m, "grid", 1) for m in mixing[1:]], axis=1)
    mixes = jnp.concatenate(
        [half_of(mixing, place & 1), exchange(half_of(mixing, 1 - (place & 1)), "band", 1)], axis=1
    )

    picked = select_points(orbitals, orders, here)
    picked, mixing = lax.optimization_barrier((picked, mixing))
    parts = []
    for part in reversed(range(picked.shape[1])):
        own, far = [picked[0, part]], [exchange(picked[1, part], "grid", 1)]
        for t in reversed(range(1, band_bits)):
            own = own + [exchange(m, "band", 1 << t) for m in own]
            far = far + [exchange(m, "band", 1 << t) for m in far]
        rows = jnp.concatenate(own + far, axis=0)
        parts.append(jnp.concatenate([rows, exchange(rows, "band", 1)], axis=0))

    def partial(columns):
        return jnp.stack([lax.dot_general(m, columns, column_dims, preferred_element_type=f32) for m in mixes])

    def swap(block, bit):
        return unpack(exchange(pack(block), "grid", 1 << bit), block.shape)

    def halves(block, bit):
        if bit + 1 >= grid_bits:
            return [block]
        size = block.shape[-1] // 2
        return [block[..., :size], block[..., size:]]

    if len(parts) > 1:
        go = [partial(columns) for columns in halves(parts[0], 1)]
        stay = [partial(columns) for columns in halves(parts[1], 1)]
        for t in range(1, grid_bits):
            got = [swap(block, t) for block in reversed(go)]
            total = [block + other for block, other in zip(stay, reversed(got))]
            if len(total) > 1:
                stay, go = halves(total[0], t + 1), halves(total[1], t + 1)
        sketch = total[0]
    else:
        sketch = partial(parts[0])
    chosen = (sketch[0] * sketch[1]).astype(bf16)

    def over_band(block):
        for t in reversed(range(band_bits)):
            got = exchange(block, "band", 1 << t)
            upper = place >> t & 1 == 1
            count = 1 << (band_bits - 1 - t)
            share = block.reshape((count, -1) + block.shape[1:])
            other = got.reshape(share.shape)
            low, high = jnp.where(upper, other, share), jnp.where(upper, share, other)
            block = jnp.concatenate([low, high], axis=1).reshape((-1,) + block.shape[1:])
        return block

    cands = [over_band(chosen)]
    index = lax.broadcasted_iota(jnp.int32, (kept, kept), 0)
    for section in range(1, grid_bits + 1):
        got = exchange(chosen, "grid", 1 << section - 1)
        upper = here >> section - 1 & 1
        mine = (index == order[section] - upper * kept).astype(bf16)
        other = (index == order[section] - (1 - upper) * kept).astype(bf16)
        chosen = jnp.dot(chosen, mine, preferred_element_type=f32) + jnp.dot(got, other, preferred_element_type=f32)
        chosen = chosen.astype(bf16)
        cands.append(over_band(chosen))
    quality = jnp.sum(log_pivots(cands), axis=0, keepdims=True)
    return cands[-1], quality


def solution(mesh):
    in_specs = (
        P(("band", "grid"), None),
        P(("band", "grid"), None),
        P(("band", "grid"), None),
        P("grid", None, None),
    )
    out_specs = (P(), P("grid", None))
    return jax.shard_map(local, mesh=mesh, in_specs=in_specs, out_specs=out_specs, check_vma=False)
```

time: 130 us -> 115 us (0.88)
  Pallas kernels: 27.6 us -> 15.7 us
  waiting for transfers between devices: 57.2 us -> 46.9 us
  local copies, waits for them, and re-layouts: 2.52 us -> 5.15 us
  matrix products: 3.03 us -> 4.91 us
  between operations: 4.09 us -> 5.51 us
  starting transfers between devices: 29.7 us -> 31 us
    ppermute x24 -> x29, waiting for transfers between devices: 57.2 us -> 46.9 us  [exchange(): return lax.ppermute(block, axis, [(i, i ^ delta) for i in range(count)])]
    pallas_call x1, Pallas kernels: 21.8 us -> 12 us  [log_pivots(): pl.pallas_call(functools.partial(pivots_kernel, sets), out_shape=jax.Shap...]
    unnamed x24 -> x20, local copies, waits for them, and re-layouts: 0.12 us -> 3.24 us
    pallas_call x1, Pallas kernels: 5.8 us -> 3.75 us  [select_points(): pl.pallas_call(select_kernel, grid_spec=pltpu.PrefetchScalarGridSpec(num_...]
    dot_general x4 -> x8, matrix products: 1.84 us -> 3.73 us  [partial(): lax.dot_general(m, columns, column_dims, preferred_element_type=f32)]
    ppermute x24 -> x29, starting transfers between devices: 29.7 us -> 31 us  [exchange(): return lax.ppermute(block, axis, [(i, i ^ delta) for i in range(count)])]
  transfers between devices with their start and end apart: 24 -> 29, of which waited for: 16 -> 15; matrix products, arithmetic and copies ran while one was open for 3% -> 6% of each run, Pallas kernels for 0% -> 3%
where the time goes in v2:
time: 115 us
  waiting for transfers between devices  46.9 us (41%)
  starting transfers between devices  31 us (27%)
  Pallas kernels  15.7 us (14%)
  between operations  5.51 us (5%)
  other arithmetic  5.4 us (5%)
  local copies, waits for them, and re-layouts  5.15 us (4%)
  matrix products  4.91 us (4%)
    ppermute x29, waiting for transfers between devices, exchange(): return lax.ppermute(block, axis, [(i, i ^ delta) for i in range(count)])  46.9 us
    ppermute x29, starting transfers between devices, exchange(): return lax.ppermute(block, axis, [(i, i ^ delta) for i in range(count)])  31 us
    pallas_call x1, Pallas kernels, log_pivots(): pl.pallas_call(functools.partial(pivots_kernel, sets), out_shape=jax.Shap...  12 us
    pallas_call x1, Pallas kernels, select_points(): pl.pallas_call(select_kernel, grid_spec=pltpu.PrefetchScalarGridSpec(num_...  3.75 us
    dot_general x8, matrix products, partial(): lax.dot_general(m, columns, column_dims, preferred_element_type=f32)  3.73 us
    unnamed x20, local copies, waits for them, and re-layouts  3.24 us
  transfers between devices with their start and end apart: 29, of which 15 were waited for; matrix products, arithmetic and copies ran while one was open for 6% of the time, Pallas kernels for 3%

profile of v2, /device:TPU:0, one launch (start us, length us, event | category | flops | bytes accessed | tf_op | source)
XLA Modules:
  0.0 114.6 jit_solution(2590102446491665380)
XLA Ops:
  0.6 1.1 fusion.15
  1.8 3.0 %collective-permute-start.2 = (bf16[2,128,512]{2,1,0:T(8,128)(2,1)S(1)}, bf16[2,128,512]{2,1,0:T(8,128)(2,1)S(1)}, u32[]{:S(2)}, u32[]{:S(2)}) collective-permute-start(bf16[2,128,512]{2,1,0:T(8,128)(2,1)S(1)} %get-tuple-element.30), channel_id=1, source_target_pairs={{0,2},{1,3},{2,0},{3,1},{4,6},{5,7},{6,4},{7,5},{8,10},{9,11},{10,... | collective-permute-start | bytes 786440 | tf_op jit(solution)/shard_map/ppermute | solution.py:22
  4.8 1.5 %collective-permute-start.3 = (bf16[2,128,512]{2,1,0:T(8,128)(2,1)S(1)}, bf16[2,128,512]{2,1,0:T(8,128)(2,1)S(1)}, u32[]{:S(2)}, u32[]{:S(2)}) collective-permute-start(bf16[2,128,512]{2,1,0:T(8,128)(2,1)S(1)} %get-tuple-element.7), channel_id=1, source_target_pairs={{0,4},{4,0},{8,12},{12,8},{16,20},{20,16},{24,28},{28,24},{1,5},{5... | collective-permute-start | bytes 786440 | tf_op jit(solution)/shard_map/ppermute | solution.py:22
  6.3 0.7 copy-done.4
  7.0 0.6 collective-permute-start
  7.6 5.0 %collective-permute-done = s32[1,1,256]{2,1,0:T(1,128)S(1)} collective-permute-done((s32[1,1,256]{2,1,0:T(1,128)S(1)}, s32[1,1,256]{2,1,0:T(1,128)S(1)}, u32[]{:S(2)}, u32[]{:S(2)}) %collective-permute-start) | collective-permute-done | bytes 1056 | tf_op jit(solution)/shard_map/ppermute | solution.py:22
  12.6 1.6 %collective-permute-start.1 = (s32[2,1,256]{2,1,0:T(1,128)S(1)}, s32[2,1,256]{2,1,0:T(1,128)S(1)}, u32[]{:S(2)}, u32[]{:S(2)}) collective-permute-start(s32[2,1,256]{2,1,0:T(1,128)S(1)} %pad_add_fusion.2), channel_id=1, source_target_pairs={{0,8},{4,12},{8,0},{12,4},{16,24},{20,28},{24,16},{28,20},{1,9},{5... | collective-permute-start | bytes 6152 | tf_op jit(solution)/shard_map/ppermute | solution.py:22
  14.2 2.0 %collective-permute-done.1 = s32[2,1,256]{2,1,0:T(1,128)S(1)} collective-permute-done((s32[2,1,256]{2,1,0:T(1,128)S(1)}, s32[2,1,256]{2,1,0:T(1,128)S(1)}, u32[]{:S(2)}, u32[]{:S(2)}) %collective-permute-start.1) | collective-permute-done | bytes 2080 | tf_op jit(solution)/shard_map/ppermute | solution.py:22
  16.2 1.6 %collective-permute-start.4 = (bf16[2,128,512]{2,1,0:T(8,128)(2,1)S(1)}, bf16[2,128,512]{2,1,0:T(8,128)(2,1)S(1)}, u32[]{:S(2)}, u32[]{:S(2)}) collective-permute-start(bf16[2,128,512]{2,1,0:T(8,128)(2,1)S(1)} %collective-permute-done.2), channel_id=1, source_target_pairs={{0,4},{4,0},{8,12},{12,8},{16,20},{20,16},{24,28},{28,24},{1,5},{5... | collective-permute-start | bytes 786440 | tf_op jit(solution)/shard_map/ppermute | solution.py:22
  17.8 2.7 %collective-permute-start.6 = (s32[4,1,256]{2,1,0:T(1,128)S(1)}, s32[4,1,256]{2,1,0:T(1,128)S(1)}, u32[]{:S(2)}, u32[]{:S(2)}) collective-permute-start(s32[4,1,256]{2,1,0:T(1,128)S(1)} %pad_add_fusion.1), channel_id=1, source_target_pairs={{0,16},{4,20},{8,24},{12,28},{16,0},{20,4},{24,8},{28,12},{1,17},{... | collective-permute-start | bytes 12296 | tf_op jit(solution)/shard_map/ppermute | solution.py:22
  20.5 1.9 %collective-permute-done.6 = s32[4,1,256]{2,1,0:T(1,128)S(1)} collective-permute-done((s32[4,1,256]{2,1,0:T(1,128)S(1)}, s32[4,1,256]{2,1,0:T(1,128)S(1)}, u32[]{:S(2)}, u32[]{:S(2)}) %collective-permute-start.6) | collective-permute-done | bytes 4128 | tf_op jit(solution)/shard_map/ppermute | solution.py:22
  22.4 0.6 pad_add_fusion.orders_ref
  23.0 3.7 %shard_map.59 = bf16[2,2,128,512]{3,2,1,0:T(8,128)(2,1)} custom-call(s32[1]{0:T(128)} %bitcast.3.where_ref, s32[8,1,256]{2,1,0:T(1,128)} %pad_add_fusion.orders_ref, bf16[128,4096]{1,0:T(8,128)(2,1)} %orbitals_ref.1), custom_call_target="tpu_custom_call" | custom-call | tf_op jit(solution)/shard_map/pallas_call | solution.py:54
  27.0 0.9 copy-done.1
  27.9 0.6 collective-permute-start.7
  28.8 1.7 %collective-permute-start.11 = (bf16[128,512]{1,0:T(8,128)(2,1)S(1)}, bf16[128,512]{1,0:T(8,128)(2,1)S(1)}, u32[]{:S(2)}, u32[]{:S(2)}) collective-permute-start(bf16[128,512]{1,0:T(8,128)(2,1)S(1)} %get-tuple-element.25), channel_id=1, source_target_pairs={{0,2},{1,3},{2,0},{3,1},{4,6},{5,7},{6,4},{7,5},{8,10},{9,11},{10,... | collective-permute-start | bytes 393224 | tf_op jit(solution)/shard_map/ppermute | solution.py:22
  30.5 1.5 %collective-permute-start.12 = (bf16[128,512]{1,0:T(8,128)(2,1)S(1)}, bf16[128,512]{1,0:T(8,128)(2,1)S(1)}, u32[]{:S(2)}, u32[]{:S(2)}) collective-permute-start(bf16[128,512]{1,0:T(8,128)(2,1)S(1)} %get-tuple-element.24), channel_id=1, source_target_pairs={{0,4},{4,0},{8,12},{12,8},{16,20},{20,16},{24,28},{28,24},{1,5},{5... | collective-permute-start | bytes 393224 | tf_op jit(solution)/shard_map/ppermute | solution.py:22
  32.0 2.7 %collective-permute-done.8 = bf16[128,512]{1,0:T(8,128)(2,1)S(1)} collective-permute-done((bf16[128,512]{1,0:T(8,128)(2,1)S(1)}, bf16[128,512]{1,0:T(8,128)(2,1)S(1)}, u32[]{:S(2)}, u32[]{:S(2)}) %collective-permute-start.8) | collective-permute-done | bytes 131104 | tf_op jit(solution)/shard_map/ppermute | solution.py:22
  34.7 1.5 %collective-permute-start.9 = (bf16[128,512]{1,0:T(8,128)(2,1)S(1)}, bf16[128,512]{1,0:T(8,128)(2,1)S(1)}, u32[]{:S(2)}, u32[]{:S(2)}) collective-permute-start(bf16[128,512]{1,0:T(8,128)(2,1)S(1)} %collective-permute-done.8), channel_id=1, source_target_pairs={{0,2},{1,3},{2,0},{3,1},{4,6},{5,7},{6,4},{7,5},{8,10},{9,11},{10,... | collective-permute-start | bytes 393224 | tf_op jit(solution)/shard_map/ppermute | solution.py:22
  36.2 1.4 %collective-permute-start.13 = (bf16[128,512]{1,0:T(8,128)(2,1)S(1)}, bf16[128,512]{1,0:T(8,128)(2,1)S(1)}, u32[]{:S(2)}, u32[]{:S(2)}) collective-permute-start(bf16[128,512]{1,0:T(8,128)(2,1)S(1)} %collective-permute-done.12), channel_id=1, source_target_pairs={{0,2},{1,3},{2,0},{3,1},{4,6},{5,7},{6,4},{7,5},{8,10},{9,11},{10,... | collective-permute-start | bytes 393224 | tf_op jit(solution)/shard_map/ppermute | solution.py:22
  37.5 2.5 %collective-permute-done.9 = bf16[128,512]{1,0:T(8,128)(2,1)S(1)} collective-permute-done((bf16[128,512]{1,0:T(8,128)(2,1)S(1)}, bf16[128,512]{1,0:T(8,128)(2,1)S(1)}, u32[]{:S(2)}, u32[]{:S(2)}) %collective-permute-start.9) | collective-permute-done | bytes 131104 | tf_op jit(solution)/shard_map/ppermute | solution.py:22
  40.1 1.3 %collective-permute-done.13 = bf16[128,512]{1,0:T(8,128)(2,1)S(1)} collective-permute-done((bf16[128,512]{1,0:T(8,128)(2,1)S(1)}, bf16[128,512]{1,0:T(8,128)(2,1)S(1)}, u32[]{:S(2)}, u32[]{:S(2)}) %collective-permute-start.13) | collective-permute-done | bytes 131104 | tf_op jit(solution)/shard_map/ppermute | solution.py:22
  44.8 0.6 abs_reduce_fusion.1
  46.2 0.6 abs_reduce_fusion.2
  47.7 1.6 %collective-permute-start.16 = (f16[528,256]{1,0:T(8,128)(2,1)S(1)}, f16[528,256]{1,0:T(8,128)(2,1)S(1)}, u32[]{:S(2)}, u32[]{:S(2)}) collective-permute-start(f16[528,256]{1,0:T(8,128)(2,1)S(1)} %concatenate.73), channel_id=1, source_target_pairs={{0,8},{4,12},{8,0},{12,4},{16,24},{20,28},{24,16},{28,20},{1,9},{5... | collective-permute-start | bytes 811016 | tf_op jit(solution)/shard_map/ppermute | solution.py:22
  49.5 0.5 collective-permute-start.15
  50.0 0.5 copy-done.3
  50.9 6.2 %collective-permute-done.16 = f16[528,256]{1,0:T(8,128)(2,1)S(1)} collective-permute-done((f16[528,256]{1,0:T(8,128)(2,1)S(1)}, f16[528,256]{1,0:T(8,128)(2,1)S(1)}, u32[]{:S(2)}, u32[]{:S(2)}) %collective-permute-start.16) | collective-permute-done | bytes 270368 | tf_op jit(solution)/shard_map/ppermute | solution.py:22
  58.3 0.7 abs_reduce_fusion
  59.9 2.6 %collective-permute-start.17 = (f16[528,256]{1,0:T(8,128)(2,1)S(1)}, f16[528,256]{1,0:T(8,128)(2,1)S(1)}, u32[]{:S(2)}, u32[]{:S(2)}) collective-permute-start(f16[528,256]{1,0:T(8,128)(2,1)S(1)} %concatenate.74), channel_id=1, source_target_pairs={{0,16},{4,20},{8,24},{12,28},{16,0},{20,4},{24,8},{28,12},{1,17},{... | collective-permute-start | bytes 811016 | tf_op jit(solution)/shard_map/ppermute | solution.py:22
  62.5 1.4 %convolution_bitcast_fusion.7 = f32[1,256,256]{2,1,0:T(8,128)S(1)} fusion(bf16[1024,256]{1,0:T(8,128)(2,1)S(1)} %get-tuple-element.12, bf16[1024,512]{1,0:T(8,128)(2,1)} %copy-done.2), kind=kOutput, calls=%fused_computation.10 | convolution fusion | flops 134217728 | bytes 1310720 | tf_op jit(solution)/shard_map/dot_general | solution.py:201
  63.9 0.5 slice.90
  65.2 8.4 %collective-permute-done.17 = f16[528,256]{1,0:T(8,128)(2,1)S(1)} collective-permute-done((f16[528,256]{1,0:T(8,128)(2,1)S(1)}, f16[528,256]{1,0:T(8,128)(2,1)S(1)}, u32[]{:S(2)}, u32[]{:S(2)}) %collective-permute-start.17) | collective-permute-done | bytes 270368 | tf_op jit(solution)/shard_map/ppermute | solution.py:22
  75.0 1.4 %collective-permute-start.23 = (bf16[256,256]{1,0:T(8,128)(2,1)S(1)}, bf16[256,256]{1,0:T(8,128)(2,1)S(1)}, u32[]{:S(2)}, u32[]{:S(2)}) collective-permute-start(bf16[256,256]{1,0:T(8,128)(2,1)S(1)} %fusion.21), channel_id=1, source_target_pairs={{0,2},{1,3},{2,0},{3,1},{4,6},{5,7},{6,4},{7,5},{8,10},{9,11},{10,... | collective-permute-start | bytes 393224 | tf_op jit(solution)/shard_map/ppermute | solution.py:22
  76.4 0.7 collective-permute-start.18
  77.3 4.0 %collective-permute-done.18 = bf16[256,256]{1,0:T(8,128)(2,1)S(1)} collective-permute-done((bf16[256,256]{1,0:T(8,128)(2,1)S(1)}, bf16[256,256]{1,0:T(8,128)(2,1)S(1)}, u32[]{:S(2)}, u32[]{:S(2)}) %collective-permute-start.18) | collective-permute-done | bytes 131104 | tf_op jit(solution)/shard_map/ppermute | solution.py:22
  81.6 0.9 collective-permute-start.19
  82.4 0.7 collective-permute-start.25
  83.5 3.1 %collective-permute-done.19 = bf16[256,256]{1,0:T(8,128)(2,1)S(1)} collective-permute-done((bf16[256,256]{1,0:T(8,128)(2,1)S(1)}, bf16[256,256]{1,0:T(8,128)(2,1)S(1)}, u32[]{:S(2)}, u32[]{:S(2)}) %collective-permute-start.19) | collective-permute-done | bytes 131104 | tf_op jit(solution)/shard_map/ppermute | solution.py:22
  86.8 2.2 %collective-permute-start.20 = (bf16[256,256]{1,0:T(8,128)(2,1)S(1)}, bf16[256,256]{1,0:T(8,128)(2,1)S(1)}, u32[]{:S(2)}, u32[]{:S(2)}) collective-permute-start(bf16[256,256]{1,0:T(8,128)(2,1)S(1)} %fusion.1), channel_id=1, source_target_pairs={{0,16},{4,20},{8,24},{12,28},{16,0},{20,4},{24,8},{28,12},{1,17},{... | collective-permute-start | bytes 393224 | tf_op jit(solution)/shard_map/ppermute | solution.py:22
  89.0 0.7 collective-permute-start.27
  90.0 4.1 %collective-permute-done.20 = bf16[256,256]{1,0:T(8,128)(2,1)S(1)} collective-permute-done((bf16[256,256]{1,0:T(8,128)(2,1)S(1)}, bf16[256,256]{1,0:T(8,128)(2,1)S(1)}, u32[]{:S(2)}, u32[]{:S(2)}) %collective-permute-start.20) | collective-permute-done | bytes 131104 | tf_op jit(solution)/shard_map/ppermute | solution.py:22
  94.4 1.3 %collective-permute-start.21 = (bf16[256,256]{1,0:T(8,128)(2,1)S(1)}, bf16[256,256]{1,0:T(8,128)(2,1)S(1)}, u32[]{:S(2)}, u32[]{:S(2)}) collective-permute-start(bf16[256,256]{1,0:T(8,128)(2,1)S(1)} %fusion.2), channel_id=1, source_target_pairs={{0,2},{1,3},{2,0},{3,1},{4,6},{5,7},{6,4},{7,5},{8,10},{9,11},{10,... | collective-permute-start | bytes 393224 | tf_op jit(solution)/shard_map/ppermute | solution.py:22
  95.8 3.6 %collective-permute-done.21 = bf16[256,256]{1,0:T(8,128)(2,1)S(1)} collective-permute-done((bf16[256,256]{1,0:T(8,128)(2,1)S(1)}, bf16[256,256]{1,0:T(8,128)(2,1)S(1)}, u32[]{:S(2)}, u32[]{:S(2)}) %collective-permute-start.21) | collective-permute-done | bytes 131104 | tf_op jit(solution)/shard_map/ppermute | solution.py:22
  99.7 1.3 %collective-permute-done.22 = bf16[512,256]{1,0:T(8,128)(2,1)S(1)} collective-permute-done((bf16[512,256]{1,0:T(8,128)(2,1)S(1)}, bf16[512,256]{1,0:T(8,128)(2,1)S(1)}, u32[]{:S(2)}, u32[]{:S(2)}) %collective-permute-start.22) | collective-permute-done | bytes 262176 | tf_op jit(solution)/shard_map/ppermute | solution.py:22
  101.2 0.7 copy-done
  102.0 12.0 %shard_map.60 = f32[4,256]{1,0:T(4,128)S(1)} custom-call(bf16[1024,256]{1,0:T(8,128)(2,1)S(1)} %bitcast.113, bf16[1024,256]{1,0:T(8,128)(2,1)S(1)} %bitcast.109, bf16[1024,256]{1,0:T(8,128)(2,1)S(1)} %bitcast.110, bf16[1024,256]{1,0:T(8,128)(2,1)S(1)} %bitcast.111), custom_call_target="tpu_custom_call" | custom-call | tf_op jit(solution)/shard_map/pallas_call | solution.py:139
  114.0 0.6 reduce_sum.9
  (91 shorter events, 8.1 us)
Async XLA Ops:
  1.8 14.4 %collective-permute-start.2 = (bf16[2,128,512]{2,1,0:T(8,128)(2,1)S(1)}, bf16[2,128,512]{2,1,0:T(8,128)(2,1)S(1)}, u32[]{:S(2)}, u32[]{:S(2)}) collective-permute-start(bf16[2,128,512]{2,1,0:T(8,128)(2,1)S(1)} %get-tuple-element.30), channel_id=1, source_target_pairs={{0,2},{1,3},{2,0},{3,1},{4,6},{5,7},{6,4},{7,5},{8,10},{9,11},{10,... | collective-permute-start | bytes 786440 | tf_op jit(solution)/shard_map/ppermute | solution.py:22
  4.8 11.4 %collective-permute-start.3 = (bf16[2,128,512]{2,1,0:T(8,128)(2,1)S(1)}, bf16[2,128,512]{2,1,0:T(8,128)(2,1)S(1)}, u32[]{:S(2)}, u32[]{:S(2)}) collective-permute-start(bf16[2,128,512]{2,1,0:T(8,128)(2,1)S(1)} %get-tuple-element.7), channel_id=1, source_target_pairs={{0,4},{4,0},{8,12},{12,8},{16,20},{20,16},{24,28},{28,24},{1,5},{5... | collective-permute-start | bytes 786440 | tf_op jit(solution)/shard_map/ppermute | solution.py:22
  6.3 0.7 copy-start.4
  7.0 5.6 %collective-permute-start = (s32[1,1,256]{2,1,0:T(1,128)S(1)}, s32[1,1,256]{2,1,0:T(1,128)S(1)}, u32[]{:S(2)}, u32[]{:S(2)}) collective-permute-start(s32[1,1,256]{2,1,0:T(1,128)S(1)} %get-tuple-element.52), channel_id=1, source_target_pairs={{0,4},{4,0},{8,12},{12,8},{16,20},{20,16},{24,28},{28,24},{1,5},{5... | collective-permute-start | bytes 3080 | tf_op jit(solution)/shard_map/ppermute | solution.py:22
  12.6 3.6 %collective-permute-start.1 = (s32[2,1,256]{2,1,0:T(1,128)S(1)}, s32[2,1,256]{2,1,0:T(1,128)S(1)}, u32[]{:S(2)}, u32[]{:S(2)}) collective-permute-start(s32[2,1,256]{2,1,0:T(1,128)S(1)} %pad_add_fusion.2), channel_id=1, source_target_pairs={{0,8},{4,12},{8,0},{12,4},{16,24},{20,28},{24,16},{28,20},{1,9},{5... | collective-permute-start | bytes 6152 | tf_op jit(solution)/shard_map/ppermute | solution.py:22
  16.2 10.5 %collective-permute-start.4 = (bf16[2,128,512]{2,1,0:T(8,128)(2,1)S(1)}, bf16[2,128,512]{2,1,0:T(8,128)(2,1)S(1)}, u32[]{:S(2)}, u32[]{:S(2)}) collective-permute-start(bf16[2,128,512]{2,1,0:T(8,128)(2,1)S(1)} %collective-permute-done.2), channel_id=1, source_target_pairs={{0,4},{4,0},{8,12},{12,8},{16,20},{20,16},{24,28},{28,24},{1,5},{5... | collective-permute-start | bytes 786440 | tf_op jit(solution)/shard_map/ppermute | solution.py:22
  17.8 4.6 %collective-permute-start.6 = (s32[4,1,256]{2,1,0:T(1,128)S(1)}, s32[4,1,256]{2,1,0:T(1,128)S(1)}, u32[]{:S(2)}, u32[]{:S(2)}) collective-permute-start(s32[4,1,256]{2,1,0:T(1,128)S(1)} %pad_add_fusion.1), channel_id=1, source_target_pairs={{0,16},{4,20},{8,24},{12,28},{16,0},{20,4},{24,8},{28,12},{1,17},{... | collective-permute-start | bytes 12296 | tf_op jit(solution)/shard_map/ppermute | solution.py:22
  26.8 1.0 copy-start.1
  26.9 14.7 %collective-permute-start.5 = (bf16[2,512,256]{2,1,0:T(8,128)(2,1)S(1)}, bf16[2,512,256]{2,1,0:T(8,128)(2,1)S(1)}, u32[]{:S(2)}, u32[]{:S(2)}) collective-permute-start(bf16[2,512,256]{2,1,0:T(8,128)(2,1)S(1)} %get-tuple-element.15), channel_id=1, source_target_pairs={{0,1},{1,0},{2,3},{3,2},{4,5},{5,4},{6,7},{7,6},{8,9},{9,8},{10,11... | collective-permute-start | bytes 1572872 | tf_op jit(solution)/shard_map/ppermute | solution.py:22
  27.9 8.3 %collective-permute-start.7 = (bf16[128,512]{1,0:T(8,128)(2,1)S(1)}, bf16[128,512]{1,0:T(8,128)(2,1)S(1)}, u32[]{:S(2)}, u32[]{:S(2)}) collective-permute-start(bf16[128,512]{1,0:T(8,128)(2,1)S(1)} %get-tuple-element.27), channel_id=1, source_target_pairs={{0,2},{1,3},{2,0},{3,1},{4,6},{5,7},{6,4},{7,5},{8,10},{9,11},{10,... | collective-permute-start | bytes 393224 | tf_op jit(solution)/shard_map/ppermute | solution.py:22
  28.5 6.2 %collective-permute-start.8 = (bf16[128,512]{1,0:T(8,128)(2,1)S(1)}, bf16[128,512]{1,0:T(8,128)(2,1)S(1)}, u32[]{:S(2)}, u32[]{:S(2)}) collective-permute-start(bf16[128,512]{1,0:T(8,128)(2,1)S(1)} %get-tuple-element.26), channel_id=1, source_target_pairs={{0,4},{4,0},{8,12},{12,8},{16,20},{20,16},{24,28},{28,24},{1,5},{5... | collective-permute-start | bytes 393224 | tf_op jit(solution)/shard_map/ppermute | solution.py:22
  28.8 8.7 %collective-permute-start.11 = (bf16[128,512]{1,0:T(8,128)(2,1)S(1)}, bf16[128,512]{1,0:T(8,128)(2,1)S(1)}, u32[]{:S(2)}, u32[]{:S(2)}) collective-permute-start(bf16[128,512]{1,0:T(8,128)(2,1)S(1)} %get-tuple-element.25), channel_id=1, source_target_pairs={{0,2},{1,3},{2,0},{3,1},{4,6},{5,7},{6,4},{7,5},{8,10},{9,11},{10,... | collective-permute-start | bytes 393224 | tf_op jit(solution)/shard_map/ppermute | solution.py:22
  30.5 5.7 %collective-permute-start.12 = (bf16[128,512]{1,0:T(8,128)(2,1)S(1)}, bf16[128,512]{1,0:T(8,128)(2,1)S(1)}, u32[]{:S(2)}, u32[]{:S(2)}) collective-permute-start(bf16[128,512]{1,0:T(8,128)(2,1)S(1)} %get-tuple-element.24), channel_id=1, source_target_pairs={{0,4},{4,0},{8,12},{12,8},{16,20},{20,16},{24,28},{28,24},{1,5},{5... | collective-permute-start | bytes 393224 | tf_op jit(solution)/shard_map/ppermute | solution.py:22
  34.7 5.3 %collective-permute-start.9 = (bf16[128,512]{1,0:T(8,128)(2,1)S(1)}, bf16[128,512]{1,0:T(8,128)(2,1)S(1)}, u32[]{:S(2)}, u32[]{:S(2)}) collective-permute-start(bf16[128,512]{1,0:T(8,128)(2,1)S(1)} %collective-permute-done.8), channel_id=1, source_target_pairs={{0,2},{1,3},{2,0},{3,1},{4,6},{5,7},{6,4},{7,5},{8,10},{9,11},{10,... | collective-permute-start | bytes 393224 | tf_op jit(solution)/shard_map/ppermute | solution.py:22
  36.2 5.2 %collective-permute-start.13 = (bf16[128,512]{1,0:T(8,128)(2,1)S(1)}, bf16[128,512]{1,0:T(8,128)(2,1)S(1)}, u32[]{:S(2)}, u32[]{:S(2)}) collective-permute-start(bf16[128,512]{1,0:T(8,128)(2,1)S(1)} %collective-permute-done.12), channel_id=1, source_target_pairs={{0,2},{1,3},{2,0},{3,1},{4,6},{5,7},{6,4},{7,5},{8,10},{9,11},{10,... | collective-permute-start | bytes 393224 | tf_op jit(solution)/shard_map/ppermute | solution.py:22
  40.0 2.0 %collective-permute-start.10 = (bf16[512,512]{1,0:T(8,128)(2,1)S(1)}, bf16[512,512]{1,0:T(8,128)(2,1)S(1)}, u32[]{:S(2)}, u32[]{:S(2)}) collective-permute-start(bf16[512,512]{1,0:T(8,128)(2,1)S(1)} %pad_maximum_fusion.1), channel_id=1, source_target_pairs={{0,1},{1,0},{2,3},{3,2},{4,5},{5,4},{6,7},{7,6},{8,9},{9,8},{10,11... | collective-permute-start | bytes 1572872 | tf_op jit(solution)/shard_map/ppermute | solution.py:22
  41.5 2.0 %collective-permute-start.14 = (bf16[512,512]{1,0:T(8,128)(2,1)S(1)}, bf16[512,512]{1,0:T(8,128)(2,1)S(1)}, u32[]{:S(2)}, u32[]{:S(2)}) collective-permute-start(bf16[512,512]{1,0:T(8,128)(2,1)S(1)} %pad_maximum_fusion.2), channel_id=1, source_target_pairs={{0,1},{1,0},{2,3},{3,2},{4,5},{5,4},{6,7},{7,6},{8,9},{9,8},{10,11... | collective-permute-start | bytes 1572872 | tf_op jit(solution)/shard_map/ppermute | solution.py:22
  42.1 1.0 copy-start.2
  47.7 9.4 %collective-permute-start.16 = (f16[528,256]{1,0:T(8,128)(2,1)S(1)}, f16[528,256]{1,0:T(8,128)(2,1)S(1)}, u32[]{:S(2)}, u32[]{:S(2)}) collective-permute-start(f16[528,256]{1,0:T(8,128)(2,1)S(1)} %concatenate.73), channel_id=1, source_target_pairs={{0,8},{4,12},{8,0},{12,4},{16,24},{20,28},{24,16},{28,20},{1,9},{5... | collective-permute-start | bytes 811016 | tf_op jit(solution)/shard_map/ppermute | solution.py:22
  49.3 1.2 %copy-start.3 = (bf16[1024,512]{1,0:T(8,128)(2,1)S(1)}, bf16[1024,512]{1,0:T(8,128)(2,1)}, u32[]{:S(2)}) copy-start(bf16[1024,512]{1,0:T(8,128)(2,1)} %copy-done.2) | copy-start | bytes 3145732
  49.5 14.4 %collective-permute-start.15 = (f16[528,256]{1,0:T(8,128)(2,1)S(1)}, f16[528,256]{1,0:T(8,128)(2,1)S(1)}, u32[]{:S(2)}, u32[]{:S(2)}) collective-permute-start(f16[528,256]{1,0:T(8,128)(2,1)S(1)} %concatenate.72), channel_id=1, source_target_pairs={{0,8},{4,12},{8,0},{12,4},{16,24},{20,28},{24,16},{28,20},{1,9},{5... | collective-permute-start | bytes 811016 | tf_op jit(solution)/shard_map/ppermute | solution.py:22
  59.9 13.7 %collective-permute-start.17 = (f16[528,256]{1,0:T(8,128)(2,1)S(1)}, f16[528,256]{1,0:T(8,128)(2,1)S(1)}, u32[]{:S(2)}, u32[]{:S(2)}) collective-permute-start(f16[528,256]{1,0:T(8,128)(2,1)S(1)} %concatenate.74), channel_id=1, source_target_pairs={{0,16},{4,20},{8,24},{12,28},{16,0},{20,4},{24,8},{28,12},{1,17},{... | collective-permute-start | bytes 811016 | tf_op jit(solution)/shard_map/ppermute | solution.py:22
  75.0 8.1 %collective-permute-start.23 = (bf16[256,256]{1,0:T(8,128)(2,1)S(1)}, bf16[256,256]{1,0:T(8,128)(2,1)S(1)}, u32[]{:S(2)}, u32[]{:S(2)}) collective-permute-start(bf16[256,256]{1,0:T(8,128)(2,1)S(1)} %fusion.21), channel_id=1, source_target_pairs={{0,2},{1,3},{2,0},{3,1},{4,6},{5,7},{6,4},{7,5},{8,10},{9,11},{10,... | collective-permute-start | bytes 393224 | tf_op jit(solution)/shard_map/ppermute | solution.py:22
  76.4 5.0 %collective-permute-start.18 = (bf16[256,256]{1,0:T(8,128)(2,1)S(1)}, bf16[256,256]{1,0:T(8,128)(2,1)S(1)}, u32[]{:S(2)}, u32[]{:S(2)}) collective-permute-start(bf16[256,256]{1,0:T(8,128)(2,1)S(1)} %fusion.21), channel_id=1, source_target_pairs={{0,4},{4,0},{8,12},{12,8},{16,20},{20,16},{24,28},{28,24},{1,5},{5... | collective-permute-start | bytes 393224 | tf_op jit(solution)/shard_map/ppermute | solution.py:22
  81.6 5.0 %collective-permute-start.19 = (bf16[256,256]{1,0:T(8,128)(2,1)S(1)}, bf16[256,256]{1,0:T(8,128)(2,1)S(1)}, u32[]{:S(2)}, u32[]{:S(2)}) collective-permute-start(bf16[256,256]{1,0:T(8,128)(2,1)S(1)} %fusion), channel_id=1, source_target_pairs={{0,8},{4,12},{8,0},{12,4},{16,24},{20,28},{24,16},{28,20},{1,9},{5... | collective-permute-start | bytes 393224 | tf_op jit(solution)/shard_map/ppermute | solution.py:22
  82.4 7.3 %collective-permute-start.25 = (bf16[256,256]{1,0:T(8,128)(2,1)S(1)}, bf16[256,256]{1,0:T(8,128)(2,1)S(1)}, u32[]{:S(2)}, u32[]{:S(2)}) collective-permute-start(bf16[256,256]{1,0:T(8,128)(2,1)S(1)} %fusion), channel_id=1, source_target_pairs={{0,2},{1,3},{2,0},{3,1},{4,6},{5,7},{6,4},{7,5},{8,10},{9,11},{10,... | collective-permute-start | bytes 393224 | tf_op jit(solution)/shard_map/ppermute | solution.py:22
  83.2 16.6 %collective-permute-start.24 = (bf16[512,256]{1,0:T(8,128)(2,1)S(1)}, bf16[512,256]{1,0:T(8,128)(2,1)S(1)}, u32[]{:S(2)}, u32[]{:S(2)}) collective-permute-start(bf16[512,256]{1,0:T(8,128)(2,1)S(1)} %get-tuple-element.40), channel_id=1, source_target_pairs={{0,1},{1,0},{2,3},{3,2},{4,5},{5,4},{6,7},{7,6},{8,9},{9,8},{10,11... | collective-permute-start | bytes 786440 | tf_op jit(solution)/shard_map/ppermute | solution.py:22
  86.8 7.3 %collective-permute-start.20 = (bf16[256,256]{1,0:T(8,128)(2,1)S(1)}, bf16[256,256]{1,0:T(8,128)(2,1)S(1)}, u32[]{:S(2)}, u32[]{:S(2)}) collective-permute-start(bf16[256,256]{1,0:T(8,128)(2,1)S(1)} %fusion.1), channel_id=1, source_target_pairs={{0,16},{4,20},{8,24},{12,28},{16,0},{20,4},{24,8},{28,12},{1,17},{... | collective-permute-start | bytes 393224 | tf_op jit(solution)/shard_map/ppermute | solution.py:22
  89.0 6.6 %collective-permute-start.27 = (bf16[256,256]{1,0:T(8,128)(2,1)S(1)}, bf16[256,256]{1,0:T(8,128)(2,1)S(1)}, u32[]{:S(2)}, u32[]{:S(2)}) collective-permute-start(bf16[256,256]{1,0:T(8,128)(2,1)S(1)} %fusion.1), channel_id=1, source_target_pairs={{0,2},{1,3},{2,0},{3,1},{4,6},{5,7},{6,4},{7,5},{8,10},{9,11},{10,... | collective-permute-start | bytes 393224 | tf_op jit(solution)/shard_map/ppermute | solution.py:22
  89.8 9.8 %collective-permute-start.26 = (bf16[512,256]{1,0:T(8,128)(2,1)S(1)}, bf16[512,256]{1,0:T(8,128)(2,1)S(1)}, u32[]{:S(2)}, u32[]{:S(2)}) collective-permute-start(bf16[512,256]{1,0:T(8,128)(2,1)S(1)} %get-tuple-element.36), channel_id=1, source_target_pairs={{0,1},{1,0},{2,3},{3,2},{4,5},{5,4},{6,7},{7,6},{8,9},{9,8},{10,11... | collective-permute-start | bytes 786440 | tf_op jit(solution)/shard_map/ppermute | solution.py:22
  94.4 5.0 %collective-permute-start.21 = (bf16[256,256]{1,0:T(8,128)(2,1)S(1)}, bf16[256,256]{1,0:T(8,128)(2,1)S(1)}, u32[]{:S(2)}, u32[]{:S(2)}) collective-permute-start(bf16[256,256]{1,0:T(8,128)(2,1)S(1)} %fusion.2), channel_id=1, source_target_pairs={{0,2},{1,3},{2,0},{3,1},{4,6},{5,7},{6,4},{7,5},{8,10},{9,11},{10,... | collective-permute-start | bytes 393224 | tf_op jit(solution)/shard_map/ppermute | solution.py:22
  95.7 3.8 %collective-permute-start.28 = (bf16[512,256]{1,0:T(8,128)(2,1)S(1)}, bf16[512,256]{1,0:T(8,128)(2,1)S(1)}, u32[]{:S(2)}, u32[]{:S(2)}) collective-permute-start(bf16[512,256]{1,0:T(8,128)(2,1)S(1)} %get-tuple-element.32), channel_id=1, source_target_pairs={{0,1},{1,0},{2,3},{3,2},{4,5},{5,4},{6,7},{7,6},{8,9},{9,8},{10,11... | collective-permute-start | bytes 786440 | tf_op jit(solution)/shard_map/ppermute | solution.py:22
  99.5 1.6 %collective-permute-start.22 = (bf16[512,256]{1,0:T(8,128)(2,1)S(1)}, bf16[512,256]{1,0:T(8,128)(2,1)S(1)}, u32[]{:S(2)}, u32[]{:S(2)}) collective-permute-start(bf16[512,256]{1,0:T(8,128)(2,1)S(1)} %get-tuple-element.44), channel_id=1, source_target_pairs={{0,1},{1,0},{2,3},{3,2},{4,5},{5,4},{6,7},{7,6},{8,9},{9,8},{10,11... | collective-permute-start | bytes 786440 | tf_op jit(solution)/shard_map/ppermute | solution.py:22
  101.2 0.8 copy-start

commit v3 on v2

--- a/solution.py
+++ b/solution.py
@@ -10,6 +10,7 @@
 ridge = 0.1
 f32, bf16, f16 = jnp.float32, jnp.bfloat16, jnp.float16
 step, height, lanes = 8, 32, 128
+top, tag_rows = 14.0, 16
 column_dims = (((0,), (0,)), ((), ()))
 
 
@@ -29,41 +30,28 @@
     return out
 
 
-def select_kernel(where_ref, orders_ref, orbitals_ref, out_ref):
-    kept = orders_ref.shape[2]
-    width = orbitals_ref.shape[1] // 2
-    index = lax.broadcasted_iota(jnp.int32, (width, kept), 0)
-    for j in range(2):
-        side = where_ref[0] & 1 ^ j
-        one_hot = (index == orders_ref[side]).astype(f32).astype(bf16)
-        columns = orbitals_ref[:, j * width : (j + 1) * width]
-        out_ref[side, 0] = jnp.dot(columns, one_hot, preferred_element_type=f32).astype(bf16)
-
-
-def select_points(orbitals, orders, here):
-    groups, _, kept = orders.shape
-    rows, points = orbitals.shape
-    high = bits_of(groups) - 1
-    parts = 2 if high else 1
-    per_part = groups // 2 // parts
-
-    def out_block(k, w):
-        place = reversed_bits(k, high)
-        return (0, place // per_part, 0, place % per_part)
-
+def pick_kernel(blocks_ref, orders_ref, array_ref, out_ref):
+    index = lax.broadcasted_iota(jnp.int32, (array_ref.shape[1], orders_ref.shape[2]), 0)
+    one_hot = (index == orders_ref[0]).astype(f32).astype(bf16)
+    out_ref[...] = jnp.dot(array_ref[...], one_hot, preferred_element_type=f32).astype(bf16)
+
+
+def pick(array, orders, blocks, width):
+    count, _, kept = orders.shape
+    rows = array.shape[0]
     return pl.pallas_call(
-        select_kernel,
+        pick_kernel,
         grid_spec=pltpu.PrefetchScalarGridSpec(
             num_scalar_prefetch=1,
-            grid=(groups // 2,),
+            grid=(count,),
             in_specs=[
-                pl.BlockSpec((2, 1, kept), lambda k, w: (k, 0, 0)),
-                pl.BlockSpec((rows, 2 * points // groups), lambda k, w: (0, w[0] >> 1 ^ k)),
+                pl.BlockSpec((1, 1, kept), lambda i, w: (i, 0, 0)),
+                pl.BlockSpec((rows, width), lambda i, w: (0, w[i])),
             ],
-            out_specs=pl.BlockSpec((2, 1, rows, kept), out_block),
+            out_specs=pl.BlockSpec((rows, kept), lambda i, w: (0, i)),
         ),
-        out_shape=jax.ShapeDtypeStruct((2, parts, rows, per_part * kept), bf16),
-    )(here[None], orders, orbitals)
+        out_shape=jax.ShapeDtypeStruct((rows, count * kept), bf16),
+    )(blocks, orders, array)
 
 
 def split3(v):
@@ -147,80 +135,125 @@
 
 
 def half_of(block, upper):
-    size = block.shape[-1] // 2
-    return lax.dynamic_slice_in_dim(block, upper * size, size, axis=block.ndim - 1)
-
-
-def pack(block):
-    block = block.reshape(-1, block.shape[-1])
-    exponent = jnp.ceil(jnp.log2(jnp.maximum(jnp.max(jnp.abs(block)), f32(1e-30))))
-    codes = (block * jnp.exp2(14.0 - exponent)).astype(f16)
-    tag = jnp.full((16, codes.shape[-1]), exponent, f32).astype(f16)
-    return jnp.concatenate([codes, tag], axis=0)
-
-
-def unpack(codes, shape):
-    return codes[:-16].astype(f32).reshape(shape) * jnp.exp2(codes[-1, 0].astype(f32) - 14.0)
+    size = block.shape[1] // 2
+    return lax.dynamic_slice_in_dim(block, upper * size, size, axis=1)
+
+
+def sketch_kernel(mode, dots, plain, coded, *refs):
+    refs, out_ref = refs[:-1], refs[-1]
+    total = 0.0
+    if dots:
+        mix_ref, refs = refs[0], refs[1:]
+        start = 0
+        for points_ref in refs[:dots]:
+            rows = points_ref.shape[0]
+            total += jnp.dot(mix_ref[:, start : start + rows], points_ref[...], preferred_element_type=f32)
+            start += rows
+    for term in refs[dots : dots + plain]:
+        total += term[...]
+    for codes in refs[dots + plain :]:
+        size = codes.shape[0] - tag_rows
+        total += codes[:size, :] * jnp.exp2(codes[size : size + 1, :] - top)
+    size = total.shape[0]
+    if mode == "code":
+        largest = jnp.maximum(jnp.max(jnp.abs(total), axis=(0, 1), keepdims=True), f32(1e-30))
+        exponent = jnp.ceil(jnp.log2(largest))
+        out_ref[:size, :] = total * jnp.exp2(top - exponent)
+        out_ref[size:, :] = jnp.broadcast_to(exponent, (tag_rows, total.shape[1]))
+    elif mode == "keep":
+        out_ref[...] = total
+    else:
+        out_ref[...] = (total[: size // 2] * total[size // 2 :]).astype(bf16)
+
+
+def sketch(mode, mix, points, plain, coded):
+    size, columns = mix.shape[0], (points + plain + coded)[0].shape[1]
+    rows, kind = {"code": (size + tag_rows, f32), "keep": (size, f32), "multiply": (size // 2, bf16)}[mode]
+    operands = ([mix] + points if points else []) + plain + coded
+    return pl.pallas_call(
+        functools.partial(sketch_kernel, mode, len(points), len(plain), len(coded)),
+        out_shape=jax.ShapeDtypeStruct((rows, columns), kind),
+        in_specs=[pl.BlockSpec(memory_space=pltpu.VMEM)] * len(operands),
+        out_specs=pl.BlockSpec(memory_space=pltpu.VMEM),
+        compiler_params=pltpu.CompilerParams(vmem_limit_bytes=48 << 20),
+    )(*operands)
+
+
+def halves(block):
+    size = (block[0] + block[1])[0].shape[1] // 2
+    return [[[a[:, :size] for a in b] for b in block], [[a[:, size:] for a in b] for b in block]]
 
 
 def local(orbitals, w_first, w_second, pivots):
     here, place = lax.axis_index("grid"), lax.axis_index("band")
-    grid_bits, band_bits = bits_of(lax.axis_size("grid")), bits_of(lax.axis_size("band"))
+    groups = lax.axis_size("grid")
+    grid_bits, band_bits = bits_of(groups), bits_of(lax.axis_size("band"))
     order = pivots[0]
     kept = order.shape[1]
-
-    mixing = [jnp.stack([w_first, w_second])]
+    width = orbitals.shape[1] // groups
+
+    parts = 2 if grid_bits > 1 else 1
+    count = groups // 2 // parts
+    places = [[reversed_bits(p * count + i, grid_bits - 1) for i in range(count)] for p in range(parts)]
+    raw = [
+        lax.dynamic_slice_in_dim(orbitals, (here ^ 2 * k + 1) * width, width, axis=1) for k in places[-1]
+    ]
+    raw = exchange(jnp.concatenate(raw, axis=1), "grid", 1)
+
+    mixing = [jnp.stack([w_first.T, w_second.T])]
     for t in reversed(range(1, band_bits)):
         upper = place >> t & 1
         got = [exchange(half_of(m, 1 - upper), "band", 1 << t) for m in mixing]
         mixing = [half_of(m, upper) for m in mixing] + got
-    near = exchange(mixing[0], "grid", 1)
 
     orders = order[:1][None]
-    for t in range(grid_bits):
+    near = mixing[0]
+    for t in reversed(range(1, grid_bits)):
+        orders = jnp.stack([orders, exchange(orders, "grid", 1 << t)], axis=1).reshape((-1,) + orders.shape[1:])
         if t == grid_bits - 1:
-            orders, mixing, near = lax.optimization_barrier((orders, mixing, near))
-        orders = jnp.concatenate([orders, exchange(orders, "grid", 1 << t)], axis=0)
-    mixing = jnp.concatenate(mixing + [near] + [exchange(m, "grid", 1) for m in mixing[1:]], axis=1)
-    mixes = jnp.concatenate(
-        [half_of(mixing, place & 1), exchange(half_of(mixing, 1 - (place & 1)), "band", 1)], axis=1
-    )
-
-    picked = select_points(orbitals, orders, here)
-    picked, mixing = lax.optimization_barrier((picked, mixing))
-    parts = []
-    for part in reversed(range(picked.shape[1])):
-        own, far = [picked[0, part]], [exchange(picked[1, part], "grid", 1)]
+            orders, near = lax.optimization_barrier((orders, near))
+    near = exchange(near, "grid", 1)
+    lists = [jnp.stack([orders[k] for k in p]) for p in places]
+
+    def over_bands(block):
+        blocks = [block]
         for t in reversed(range(1, band_bits)):
-            own = own + [exchange(m, "band", 1 << t) for m in own]
-            far = far + [exchange(m, "band", 1 << t) for m in far]
-        rows = jnp.concatenate(own + far, axis=0)
-        parts.append(jnp.concatenate([rows, exchange(rows, "band", 1)], axis=0))
-
-    def partial(columns):
-        return jnp.stack([lax.dot_general(m, columns, column_dims, preferred_element_type=f32) for m in mixes])
+            blocks = blocks + [exchange(m, "band", 1 << t) for m in blocks]
+        return blocks
+
+    def names(p, side):
+        return jnp.stack([here ^ 2 * k + side for k in places[p]])
+
+    gathered = {}
+    for p in reversed(range(parts)):
+        own = over_bands(pick(orbitals, lists[p], names(p, 0), width))
+        if p == parts - 1:
+            far = pick(raw, lists[p], jnp.arange(count, dtype=jnp.int32), width)
+        else:
+            others = exchange(lists[p], "grid", 1)
+            far = exchange(pick(orbitals, others, names(p, 1), width), "grid", 1)
+        rows = jnp.concatenate(own + over_bands(far), axis=0)
+        gathered[p] = [rows, exchange(rows, "band", 1)]
+
+    mixing = jnp.concatenate(mixing + [near] + [exchange(m, "grid", 1) for m in mixing[1:]], axis=2)
+    mixes = [half_of(mixing, place & 1), exchange(half_of(mixing, 1 - (place & 1)), "band", 1)]
+    mix = jnp.concatenate(mixes, axis=2)
+    mix = mix.reshape(-1, mix.shape[2])
 
     def swap(block, bit):
-        return unpack(exchange(pack(block), "grid", 1 << bit), block.shape)
-
-    def halves(block, bit):
-        if bit + 1 >= grid_bits:
-            return [block]
-        size = block.shape[-1] // 2
-        return [block[..., :size], block[..., size:]]
-
-    if len(parts) > 1:
-        go = [partial(columns) for columns in halves(parts[0], 1)]
-        stay = [partial(columns) for columns in halves(parts[1], 1)]
-        for t in range(1, grid_bits):
-            got = [swap(block, t) for block in reversed(go)]
-            total = [block + other for block, other in zip(stay, reversed(got))]
-            if len(total) > 1:
-                stay, go = halves(total[0], t + 1), halves(total[1], t + 1)
-        sketch = total[0]
+        codes = sketch("code", mix, block[0], [], block[1]).astype(f16)
+        return exchange(codes, "grid", 1 << bit).astype(f32)
+
+    stay = [gathered[0], []]
+    if parts > 1:
+        go = [gathered[1], []]
+        for t in range(1, grid_bits - 1):
+            got = [swap(block, t) for block in reversed(halves(go))]
+            stay, go = [[points, codes + [new]] for (points, codes), new in zip(halves(stay), reversed(got))]
+        kept_sum = sketch("keep", mix, stay[0], [], stay[1])
+        chosen = sketch("multiply", mix, [], [kept_sum], [swap(go, grid_bits - 1)])
     else:
-        sketch = partial(parts[0])
-    chosen = (sketch[0] * sketch[1]).astype(bf16)
+        chosen = sketch("multiply", mix, stay[0], [], [])
 
     def over_band(block):
         for t in reversed(range(band_bits)):

time: 115 us -> 106 us (0.922)
  Pallas kernels: 15.7 us -> 24.8 us
  waiting for transfers between devices: 46.9 us -> 41.6 us
  starting transfers between devices: 31 us -> 26.1 us
  between operations: 5.51 us -> 1.12 us
  matrix products: 4.91 us -> 1.19 us
    pallas_call x1 -> x9, Pallas kernels: 3.75 us -> 12.8 us  [the longest x4 10.5 us: pick(): pl.pallas_call(pick_kernel, grid_spec=pltpu.PrefetchScalarGridSpec(num_sc...]
    ppermute x29, waiting for transfers between devices: 46.9 us -> 41.6 us  [exchange(): return lax.ppermute(block, axis, [(i, i ^ delta) for i in range(count)])]
    ppermute x29, starting transfers between devices: 31 us -> 26.1 us  [exchange(): return lax.ppermute(block, axis, [(i, i ^ delta) for i in range(count)])]
    dot_general x8 -> x0, matrix products: 3.73 us -> none  [partial(): lax.dot_general(m, columns, column_dims, preferred_element_type=f32)]
    unnamed x20 -> x16, local copies, waits for them, and re-layouts: 3.24 us -> 0.73 us
    another operation x3 -> x7, other arithmetic: 1.24 us -> 3.66 us  [the longest x3 1.92 us: names(): return jnp.stack([here ^ 2 * k + side for k in places[p]])]
    reduce_max x3 -> x0, other arithmetic: 1.94 us -> none  [pack(): jnp.max(jnp.abs(block))]
  transfers between devices with their start and end apart: 29 -> 29, of which waited for: 15 -> 13; matrix products, arithmetic and copies ran while one was open for 6% -> 9% of each run, Pallas kernels for 3% -> 12%
where the time goes in v3:
time: 106 us
  waiting for transfers between devices  41.6 us (39%)
  starting transfers between devices  26.1 us (25%)
  Pallas kernels  24.8 us (23%)
  other arithmetic  6.04 us (6%)
  local copies, waits for them, and re-layouts  5.12 us (5%)
  matrix products  1.19 us (1%)
  between operations  1.12 us (1%)
    ppermute x29, waiting for transfers between devices, exchange(): return lax.ppermute(block, axis, [(i, i ^ delta) for i in range(count)])  41.6 us
    ppermute x29, starting transfers between devices, exchange(): return lax.ppermute(block, axis, [(i, i ^ delta) for i in range(count)])  26.1 us
    pallas_call x1, Pallas kernels, log_pivots(): pl.pallas_call(functools.partial(pivots_kernel, sets), out_shape=jax.Shap...  12 us
    pallas_call x4, Pallas kernels, pick(): pl.pallas_call(pick_kernel, grid_spec=pltpu.PrefetchScalarGridSpec(num_sc...  10.5 us
    pallas_call x5, Pallas kernels, sketch(): pl.pallas_call(functools.partial(sketch_kernel, mode, len(points), len(pl...  2.3 us
    slice x4, local copies, waits for them, and re-layouts, halves(): a[:, size:]  2.2 us
  transfers between devices with their start and end apart: 29, of which 13 were waited for; matrix products, arithmetic and copies ran while one was open for 9% of the time, Pallas kernels for 12%

profile of v3, /device:TPU:0, one launch (start us, length us, event | category | flops | bytes accessed | tf_op | source)
XLA Modules:
  0.0 106.0 jit_solution(3944137633441092780)
XLA Ops:
  0.6 1.1 %fusion.4 = (bf16[2,512,128]{1,2,0:T(8,128)(2,1)S(1)}, bf16[2,512,128]{1,2,0:T(8,128)(2,1)S(1)}) fusion(s32[]{:T(128)S(6)} %select_n.116, bf16[1,1024,128]{1,2,0:T(8,128)(2,1)} %bitcast.85, bf16[1,1024,128]{1,2,0:T(8,128)(2,1)} %bitcast.86, s32[]{:T(128)S(6)} %select_n.117), kind=kLoop, calls=%fused_computation.19 | loop fusion | flops 1048576 | bytes 1048584 | tf_op jit(solution)/shard_map/stack | solution.py:203
  1.8 3.0 %collective-permute-start = (bf16[2,512,128]{1,2,0:T(8,128)(2,1)S(1)}, bf16[2,512,128]{1,2,0:T(8,128)(2,1)S(1)}, u32[]{:S(2)}, u32[]{:S(2)}) collective-permute-start(bf16[2,512,128]{1,2,0:T(8,128)(2,1)S(1)} %get-tuple-element.27), channel_id=1, source_target_pairs={{0,2},{1,3},{2,0},{3,1},{4,6},{5,7},{6,4},{7,5},{8,10},{9,11},{10,... | collective-permute-start | bytes 786440 | tf_op jit(solution)/shard_map/ppermute | solution.py:23
  4.8 2.7 %collective-permute-start.1 = (s32[1,1,256]{2,1,0:T(1,128)S(1)}, s32[1,1,256]{2,1,0:T(1,128)S(1)}, u32[]{:S(2)}, u32[]{:S(2)}) collective-permute-start(s32[1,1,256]{2,1,0:T(1,128)S(1)} %get-tuple-element.49), channel_id=1, source_target_pairs={{0,16},{4,20},{8,24},{12,28},{16,0},{20,4},{24,8},{28,12},{1,17},{... | collective-permute-start | bytes 3080 | tf_op jit(solution)/shard_map/ppermute | solution.py:23
  7.5 1.0 constant_dynamic-slice_fusion.1
  8.5 1.6 %collective-permute-start.12 = (bf16[128,1024]{1,0:T(8,128)(2,1)S(1)}, bf16[128,1024]{1,0:T(8,128)(2,1)S(1)}, u32[]{:S(2)}, u32[]{:S(2)}) collective-permute-start(bf16[128,1024]{1,0:T(8,128)(2,1)S(1)} %pad_maximum_fusion.8), channel_id=1, source_target_pairs={{0,4},{4,0},{8,12},{12,8},{16,20},{20,16},{24,28},{28,24},{1,5},{5... | collective-permute-start | bytes 786440 | tf_op jit(solution)/shard_map/ppermute | solution.py:23
  10.1 0.6 pad_add_fusion.4.blocks_ref
  10.7 1.6 %collective-permute-start.5 = (s32[2,1,256]{2,1,0:T(1,128)S(1)}, s32[2,1,256]{2,1,0:T(1,128)S(1)}, u32[]{:S(2)}, u32[]{:S(2)}) collective-permute-start(s32[2,1,256]{2,1,0:T(1,128)S(1)} %add_bitcast_fusion), channel_id=1, source_target_pairs={{0,8},{4,12},{8,0},{12,4},{16,24},{20,28},{24,16},{28,20},{1,9},{5... | collective-permute-start | bytes 6152 | tf_op jit(solution)/shard_map/ppermute | solution.py:23
  12.3 0.6 pad_add_fusion.5.blocks_ref
  13.4 0.9 collective-permute-done.5
  14.3 0.7 collective-permute-start.7
  15.0 1.4 %collective-permute-start.3 = (bf16[2,512,128]{1,2,0:T(8,128)(2,1)S(1)}, bf16[2,512,128]{1,2,0:T(8,128)(2,1)S(1)}, u32[]{:S(2)}, u32[]{:S(2)}) collective-permute-start(bf16[2,512,128]{1,2,0:T(8,128)(2,1)S(1)} %collective-permute-done), channel_id=1, source_target_pairs={{0,4},{4,0},{8,12},{12,8},{16,20},{20,16},{24,28},{28,24},{1,5},{5... | collective-permute-start | bytes 786440 | tf_op jit(solution)/shard_map/ppermute | solution.py:23
  16.4 0.6 pad_add_fusion.2.orders_ref
  17.0 2.6 %shard_map.61 = bf16[128,512]{1,0:T(8,128)(2,1)} custom-call(s32[2]{0:T(128)} %pad_add_fusion.5.blocks_ref, s32[2,1,256]{2,1,0:T(1,128)} %pad_add_fusion.2.orders_ref, bf16[128,4096]{1,0:T(8,128)(2,1)} %array_ref.5), custom_call_target="tpu_custom_call" | custom-call | tf_op jit(solution)/shard_map/pallas_call | solution.py:42
  20.2 3.3 %collective-permute-done.7.orders_ref = s32[2,1,256]{2,1,0:T(1,128)S(1)} collective-permute-done((s32[2,1,256]{2,1,0:T(1,128)S(1)}, s32[2,1,256]{2,1,0:T(1,128)S(1)}, u32[]{:S(2)}, u32[]{:S(2)}) %collective-permute-start.7) | collective-permute-done | bytes 2080 | tf_op jit(solution)/shard_map/ppermute | solution.py:23
  23.5 0.6 copy-done.7
  24.0 2.6 %shard_map.60 = bf16[128,512]{1,0:T(8,128)(2,1)} custom-call(s32[2]{0:T(128)} %pad_add_fusion.4.blocks_ref, s32[2,1,256]{2,1,0:T(1,128)} %copy-done.7, bf16[128,4096]{1,0:T(8,128)(2,1)} %array_ref.5), custom_call_target="tpu_custom_call" | custom-call | tf_op jit(solution)/shard_map/pallas_call | solution.py:42
  26.7 1.5 %collective-permute-start.8 = (bf16[128,512]{1,0:T(8,128)(2,1)}, bf16[128,512]{1,0:T(8,128)(2,1)S(1)}, u32[]{:S(2)}, u32[]{:S(2)}) collective-permute-start(bf16[128,512]{1,0:T(8,128)(2,1)} %shard_map.60), channel_id=1, source_target_pairs={{0,4},{4,0},{8,12},{12,8},{16,20},{20,16},{24,28},{28,24},{1,5},{5... | collective-permute-start | bytes 393224 | tf_op jit(solution)/shard_map/ppermute | solution.py:23
  28.2 0.6 iota.18.blocks_ref
  28.9 2.6 %shard_map.62 = bf16[128,512]{1,0:T(8,128)(2,1)} custom-call(s32[2]{0:T(128)} %iota.18.blocks_ref, s32[2,1,256]{2,1,0:T(1,128)} %pad_add_fusion.2.orders_ref, bf16[128,1024]{1,0:T(8,128)(2,1)} %copy-done.4), custom_call_target="tpu_custom_call" | custom-call | tf_op jit(solution)/shard_map/pallas_call | solution.py:42
  32.1 0.7 pad_add_fusion.3.blocks_ref
  32.7 2.6 %shard_map.59 = bf16[128,512]{1,0:T(8,128)(2,1)} custom-call(s32[2]{0:T(128)} %pad_add_fusion.3.blocks_ref, s32[2,1,256]{2,1,0:T(1,128)} %copy-done.5, bf16[128,4096]{1,0:T(8,128)(2,1)} %array_ref.5), custom_call_target="tpu_custom_call" | custom-call | tf_op jit(solution)/shard_map/pallas_call | solution.py:42
  35.4 1.5 %collective-permute-start.6 = (bf16[128,512]{1,0:T(8,128)(2,1)}, bf16[128,512]{1,0:T(8,128)(2,1)S(1)}, u32[]{:S(2)}, u32[]{:S(2)}) collective-permute-start(bf16[128,512]{1,0:T(8,128)(2,1)} %shard_map.59), channel_id=1, source_target_pairs={{0,2},{1,3},{2,0},{3,1},{4,6},{5,7},{6,4},{7,5},{8,10},{9,11},{10,... | collective-permute-start | bytes 393224 | tf_op jit(solution)/shard_map/ppermute | solution.py:23
  37.4 0.7 collective-permute-done.13
  38.4 0.5 collective-permute-start.4
  39.0 1.6 %collective-permute-done.6 = bf16[128,512]{1,0:T(8,128)(2,1)S(1)} collective-permute-done((bf16[128,512]{1,0:T(8,128)(2,1)}, bf16[128,512]{1,0:T(8,128)(2,1)S(1)}, u32[]{:S(2)}, u32[]{:S(2)}) %collective-permute-start.6) | collective-permute-done | bytes 131104 | tf_op jit(solution)/shard_map/ppermute | solution.py:23
  40.6 1.4 %collective-permute-done.9 = bf16[128,512]{1,0:T(8,128)(2,1)S(1)} collective-permute-done((bf16[128,512]{1,0:T(8,128)(2,1)S(1)}, bf16[128,512]{1,0:T(8,128)(2,1)S(1)}, u32[]{:S(2)}, u32[]{:S(2)}) %collective-permute-start.9) | collective-permute-done | bytes 131104 | tf_op jit(solution)/shard_map/ppermute | solution.py:23
  42.0 0.8 pad_maximum_fusion.2
  43.5 0.6 shard_map.65
  44.2 1.6 %collective-permute-start.16 = (f16[528,256]{1,0:T(8,128)(2,1)S(1)}, f16[528,256]{1,0:T(8,128)(2,1)S(1)}, u32[]{:S(2)}, u32[]{:S(2)}) collective-permute-start(f16[528,256]{1,0:T(8,128)(2,1)S(1)} %convert_element_type.35), channel_id=1, source_target_pairs={{0,8},{4,12},{8,0},{12,4},{16,24},{20,28},{24,16},{28,20},{1,9},{5... | collective-permute-start | bytes 811016 | tf_op jit(solution)/shard_map/ppermute | solution.py:23
  45.8 1.1 %fusion.21 = (bf16[512,256]{1,0:T(8,128)(2,1)S(1)}, bf16[512,256]{1,0:T(8,128)(2,1)S(1)}) fusion(bf16[512,512]{1,0:T(8,128)(2,1)} %pad_maximum_fusion.2), kind=kLoop, calls=%fused_computation.81 | loop fusion | bytes 1048576 | tf_op jit(solution)/shard_map/slice | solution.py:184
  46.9 1.1 %fusion.20 = (bf16[512,256]{1,0:T(8,128)(2,1)S(1)}, bf16[512,256]{1,0:T(8,128)(2,1)S(1)}) fusion(bf16[512,512]{1,0:T(8,128)(2,1)} %collective-permute-done.10), kind=kLoop, calls=%fused_computation.80 | loop fusion | bytes 1048576 | tf_op jit(solution)/shard_map/slice | solution.py:184
  48.0 0.6 shard_map.63
  49.1 4.4 %collective-permute-done.16 = f16[528,256]{1,0:T(8,128)(2,1)S(1)} collective-permute-done((f16[528,256]{1,0:T(8,128)(2,1)S(1)}, f16[528,256]{1,0:T(8,128)(2,1)S(1)}, u32[]{:S(2)}, u32[]{:S(2)}) %collective-permute-start.16) | collective-permute-done | bytes 270368 | tf_op jit(solution)/shard_map/ppermute | solution.py:23
  53.6 0.6 shard_map.66
  54.4 6.0 %collective-permute-done.15 = f16[528,256]{1,0:T(8,128)(2,1)S(1)} collective-permute-done((f16[528,256]{1,0:T(8,128)(2,1)S(1)}, f16[528,256]{1,0:T(8,128)(2,1)S(1)}, u32[]{:S(2)}, u32[]{:S(2)}) %collective-permute-start.15) | collective-permute-done | bytes 270368 | tf_op jit(solution)/shard_map/ppermute | solution.py:23
  60.9 7.9 %collective-permute-done.17 = f16[528,256]{1,0:T(8,128)(2,1)S(1)} collective-permute-done((f16[528,256]{1,0:T(8,128)(2,1)S(1)}, f16[528,256]{1,0:T(8,128)(2,1)S(1)}, u32[]{:S(2)}, u32[]{:S(2)}) %collective-permute-start.17) | collective-permute-done | bytes 270368 | tf_op jit(solution)/shard_map/ppermute | solution.py:23
  68.9 0.6 collective-permute-start.18
  69.4 1.5 %collective-permute-start.23 = (bf16[256,256]{1,0:T(8,128)(2,1)S(1)}, bf16[256,256]{1,0:T(8,128)(2,1)S(1)}, u32[]{:S(2)}, u32[]{:S(2)}) collective-permute-start(bf16[256,256]{1,0:T(8,128)(2,1)S(1)} %shard_map.67), channel_id=1, source_target_pairs={{0,2},{1,3},{2,0},{3,1},{4,6},{5,7},{6,4},{7,5},{8,10},{9,11},{10,... | collective-permute-start | bytes 393224 | tf_op jit(solution)/shard_map/ppermute | solution.py:23
  70.9 3.0 %collective-permute-done.18 = bf16[256,256]{1,0:T(8,128)(2,1)S(1)} collective-permute-done((bf16[256,256]{1,0:T(8,128)(2,1)S(1)}, bf16[256,256]{1,0:T(8,128)(2,1)S(1)}, u32[]{:S(2)}, u32[]{:S(2)}) %collective-permute-start.18) | collective-permute-done | bytes 131104 | tf_op jit(solution)/shard_map/ppermute | solution.py:23
  74.4 1.6 %collective-permute-start.25 = (bf16[256,256]{1,0:T(8,128)(2,1)S(1)}, bf16[256,256]{1,0:T(8,128)(2,1)S(1)}, u32[]{:S(2)}, u32[]{:S(2)}) collective-permute-start(bf16[256,256]{1,0:T(8,128)(2,1)S(1)} %fusion), channel_id=1, source_target_pairs={{0,2},{1,3},{2,0},{3,1},{4,6},{5,7},{6,4},{7,5},{8,10},{9,11},{10,... | collective-permute-start | bytes 393224 | tf_op jit(solution)/shard_map/ppermute | solution.py:23
  76.3 3.0 %collective-permute-done.19 = bf16[256,256]{1,0:T(8,128)(2,1)S(1)} collective-permute-done((bf16[256,256]{1,0:T(8,128)(2,1)S(1)}, bf16[256,256]{1,0:T(8,128)(2,1)S(1)}, u32[]{:S(2)}, u32[]{:S(2)}) %collective-permute-start.19) | collective-permute-done | bytes 131104 | tf_op jit(solution)/shard_map/ppermute | solution.py:23
  79.6 1.6 %collective-permute-start.27 = (bf16[256,256]{1,0:T(8,128)(2,1)S(1)}, bf16[256,256]{1,0:T(8,128)(2,1)S(1)}, u32[]{:S(2)}, u32[]{:S(2)}) collective-permute-start(bf16[256,256]{1,0:T(8,128)(2,1)S(1)} %fusion.1), channel_id=1, source_target_pairs={{0,2},{1,3},{2,0},{3,1},{4,6},{5,7},{6,4},{7,5},{8,10},{9,11},{10,... | collective-permute-start | bytes 393224 | tf_op jit(solution)/shard_map/ppermute | solution.py:23
  81.5 4.8 %collective-permute-done.20 = bf16[256,256]{1,0:T(8,128)(2,1)S(1)} collective-permute-done((bf16[256,256]{1,0:T(8,128)(2,1)S(1)}, bf16[256,256]{1,0:T(8,128)(2,1)S(1)}, u32[]{:S(2)}, u32[]{:S(2)}) %collective-permute-start.20) | collective-permute-done | bytes 131104 | tf_op jit(solution)/shard_map/ppermute | solution.py:23
  86.5 1.6 %collective-permute-start.21 = (bf16[256,256]{1,0:T(8,128)(2,1)S(1)}, bf16[256,256]{1,0:T(8,128)(2,1)S(1)}, u32[]{:S(2)}, u32[]{:S(2)}) collective-permute-start(bf16[256,256]{1,0:T(8,128)(2,1)S(1)} %fusion.2), channel_id=1, source_target_pairs={{0,2},{1,3},{2,0},{3,1},{4,6},{5,7},{6,4},{7,5},{8,10},{9,11},{10,... | collective-permute-start | bytes 393224 | tf_op jit(solution)/shard_map/ppermute | solution.py:23
  88.2 3.3 %collective-permute-done.21 = bf16[256,256]{1,0:T(8,128)(2,1)S(1)} collective-permute-done((bf16[256,256]{1,0:T(8,128)(2,1)S(1)}, bf16[256,256]{1,0:T(8,128)(2,1)S(1)}, u32[]{:S(2)}, u32[]{:S(2)}) %collective-permute-start.21) | collective-permute-done | bytes 131104 | tf_op jit(solution)/shard_map/ppermute | solution.py:23
  91.9 1.3 %collective-permute-done.22 = bf16[512,256]{1,0:T(8,128)(2,1)S(1)} collective-permute-done((bf16[512,256]{1,0:T(8,128)(2,1)S(1)}, bf16[512,256]{1,0:T(8,128)(2,1)S(1)}, u32[]{:S(2)}, u32[]{:S(2)}) %collective-permute-start.22) | collective-permute-done | bytes 262176 | tf_op jit(solution)/shard_map/ppermute | solution.py:23
  93.4 12.0 %shard_map.68 = f32[4,256]{1,0:T(4,128)S(1)} custom-call(bf16[1024,256]{1,0:T(8,128)(2,1)S(1)} %bitcast.80, bf16[1024,256]{1,0:T(8,128)(2,1)S(1)} %bitcast.76, bf16[1024,256]{1,0:T(8,128)(2,1)S(1)} %bitcast.77, bf16[1024,256]{1,0:T(8,128)(2,1)S(1)} %bitcast.78), custom_call_target="tpu_custom_call" | custom-call | tf_op jit(solution)/shard_map/pallas_call | solution.py:127
  105.4 0.6 reduce_sum.9
  (86 shorter events, 6.8 us)
Async XLA Ops:
  0.6 4.2 %copy-start.6 = (s32[1,4,256]{2,1,0:T(4,128)S(1)}, s32[1,4,256]{2,1,0:T(4,128)}, u32[]{:S(2)}) copy-start(s32[1,4,256]{2,1,0:T(4,128)} %param.7) | copy-start | bytes 12292
  1.8 13.2 %collective-permute-start = (bf16[2,512,128]{1,2,0:T(8,128)(2,1)S(1)}, bf16[2,512,128]{1,2,0:T(8,128)(2,1)S(1)}, u32[]{:S(2)}, u32[]{:S(2)}) collective-permute-start(bf16[2,512,128]{1,2,0:T(8,128)(2,1)S(1)} %get-tuple-element.27), channel_id=1, source_target_pairs={{0,2},{1,3},{2,0},{3,1},{4,6},{5,7},{6,4},{7,5},{8,10},{9,11},{10,... | collective-permute-start | bytes 786440 | tf_op jit(solution)/shard_map/ppermute | solution.py:23
  4.8 5.9 %collective-permute-start.1 = (s32[1,1,256]{2,1,0:T(1,128)S(1)}, s32[1,1,256]{2,1,0:T(1,128)S(1)}, u32[]{:S(2)}, u32[]{:S(2)}) collective-permute-start(s32[1,1,256]{2,1,0:T(1,128)S(1)} %get-tuple-element.49), channel_id=1, source_target_pairs={{0,16},{4,20},{8,24},{12,28},{16,0},{20,4},{24,8},{28,12},{1,17},{... | collective-permute-start | bytes 3080 | tf_op jit(solution)/shard_map/ppermute | solution.py:23
  8.5 19.7 %collective-permute-start.12 = (bf16[128,1024]{1,0:T(8,128)(2,1)S(1)}, bf16[128,1024]{1,0:T(8,128)(2,1)S(1)}, u32[]{:S(2)}, u32[]{:S(2)}) collective-permute-start(bf16[128,1024]{1,0:T(8,128)(2,1)S(1)} %pad_maximum_fusion.8), channel_id=1, source_target_pairs={{0,4},{4,0},{8,12},{12,8},{16,20},{20,16},{24,28},{28,24},{1,5},{5... | collective-permute-start | bytes 786440 | tf_op jit(solution)/shard_map/ppermute | solution.py:23
  10.7 3.6 %collective-permute-start.5 = (s32[2,1,256]{2,1,0:T(1,128)S(1)}, s32[2,1,256]{2,1,0:T(1,128)S(1)}, u32[]{:S(2)}, u32[]{:S(2)}) collective-permute-start(s32[2,1,256]{2,1,0:T(1,128)S(1)} %add_bitcast_fusion), channel_id=1, source_target_pairs={{0,8},{4,12},{8,0},{12,4},{16,24},{20,28},{24,16},{28,20},{1,9},{5... | collective-permute-start | bytes 6152 | tf_op jit(solution)/shard_map/ppermute | solution.py:23
  12.9 25.4 %collective-permute-start.2 = (bf16[2,512,128]{1,2,0:T(8,128)(2,1)S(1)}, bf16[2,512,128]{1,2,0:T(8,128)(2,1)S(1)}, u32[]{:S(2)}, u32[]{:S(2)}) collective-permute-start(bf16[2,512,128]{1,2,0:T(8,128)(2,1)S(1)} %get-tuple-element.4), channel_id=1, source_target_pairs={{0,4},{4,0},{8,12},{12,8},{16,20},{20,16},{24,28},{28,24},{1,5},{5... | collective-permute-start | bytes 786440 | tf_op jit(solution)/shard_map/ppermute | solution.py:23
  14.3 12.4 %copy-start.5 = (s32[2,1,256]{2,1,0:T(1,128)}, s32[2,1,256]{2,1,0:T(1,128)S(1)}, u32[]{:S(2)}) copy-start(s32[2,1,256]{2,1,0:T(1,128)S(1)} %pad_add_fusion.1.orders_ref) | copy-start | bytes 6148
  14.3 9.1 %collective-permute-start.7 = (s32[2,1,256]{2,1,0:T(1,128)S(1)}, s32[2,1,256]{2,1,0:T(1,128)S(1)}, u32[]{:S(2)}, u32[]{:S(2)}) collective-permute-start(s32[2,1,256]{2,1,0:T(1,128)S(1)} %pad_add_fusion.1.orders_ref), channel_id=1, source_target_pairs={{0,4},{4,0},{8,12},{12,8},{16,20},{20,16},{24,28},{28,24},{1,5},{5... | collective-permute-start | bytes 6152 | tf_op jit(solution)/shard_map/ppermute | solution.py:23
  15.0 23.2 %collective-permute-start.3 = (bf16[2,512,128]{1,2,0:T(8,128)(2,1)S(1)}, bf16[2,512,128]{1,2,0:T(8,128)(2,1)S(1)}, u32[]{:S(2)}, u32[]{:S(2)}) collective-permute-start(bf16[2,512,128]{1,2,0:T(8,128)(2,1)S(1)} %collective-permute-done), channel_id=1, source_target_pairs={{0,4},{4,0},{8,12},{12,8},{16,20},{20,16},{24,28},{28,24},{1,5},{5... | collective-permute-start | bytes 786440 | tf_op jit(solution)/shard_map/ppermute | solution.py:23
  19.7 15.7 %collective-permute-start.11 = (bf16[128,512]{1,0:T(8,128)(2,1)}, bf16[128,512]{1,0:T(8,128)(2,1)S(1)}, u32[]{:S(2)}, u32[]{:S(2)}) collective-permute-start(bf16[128,512]{1,0:T(8,128)(2,1)} %shard_map.61), channel_id=1, source_target_pairs={{0,2},{1,3},{2,0},{3,1},{4,6},{5,7},{6,4},{7,5},{8,10},{9,11},{10,... | collective-permute-start | bytes 393224 | tf_op jit(solution)/shard_map/ppermute | solution.py:23
  23.5 0.6 copy-start.7
  26.7 11.5 %copy-start.1 = (bf16[128,512]{1,0:T(8,128)(2,1)S(1)}, bf16[128,512]{1,0:T(8,128)(2,1)}, u32[]{:S(2)}) copy-start(bf16[128,512]{1,0:T(8,128)(2,1)} %shard_map.61) | copy-start | bytes 393220
  26.7 10.2 %collective-permute-start.8 = (bf16[128,512]{1,0:T(8,128)(2,1)}, bf16[128,512]{1,0:T(8,128)(2,1)S(1)}, u32[]{:S(2)}, u32[]{:S(2)}) collective-permute-start(bf16[128,512]{1,0:T(8,128)(2,1)} %shard_map.60), channel_id=1, source_target_pairs={{0,4},{4,0},{8,12},{12,8},{16,20},{20,16},{24,28},{28,24},{1,5},{5... | collective-permute-start | bytes 393224 | tf_op jit(solution)/shard_map/ppermute | solution.py:23
  28.2 0.7 copy-start.4
  31.5 6.6 %copy-start.3 = (bf16[128,512]{1,0:T(8,128)(2,1)S(1)}, bf16[128,512]{1,0:T(8,128)(2,1)}, u32[]{:S(2)}) copy-start(bf16[128,512]{1,0:T(8,128)(2,1)} %shard_map.62) | copy-start | bytes 393220
  31.5 6.6 %collective-permute-start.13 = (bf16[128,512]{1,0:T(8,128)(2,1)}, bf16[128,512]{1,0:T(8,128)(2,1)S(1)}, u32[]{:S(2)}, u32[]{:S(2)}) collective-permute-start(bf16[128,512]{1,0:T(8,128)(2,1)} %shard_map.62), channel_id=1, source_target_pairs={{0,2},{1,3},{2,0},{3,1},{4,6},{5,7},{6,4},{7,5},{8,10},{9,11},{10,... | collective-permute-start | bytes 393224 | tf_op jit(solution)/shard_map/ppermute | solution.py:23
  35.4 5.2 %collective-permute-start.6 = (bf16[128,512]{1,0:T(8,128)(2,1)}, bf16[128,512]{1,0:T(8,128)(2,1)S(1)}, u32[]{:S(2)}, u32[]{:S(2)}) collective-permute-start(bf16[128,512]{1,0:T(8,128)(2,1)} %shard_map.59), channel_id=1, source_target_pairs={{0,2},{1,3},{2,0},{3,1},{4,6},{5,7},{6,4},{7,5},{8,10},{9,11},{10,... | collective-permute-start | bytes 393224 | tf_op jit(solution)/shard_map/ppermute | solution.py:23
  36.9 5.1 %collective-permute-start.9 = (bf16[128,512]{1,0:T(8,128)(2,1)S(1)}, bf16[128,512]{1,0:T(8,128)(2,1)S(1)}, u32[]{:S(2)}, u32[]{:S(2)}) collective-permute-start(bf16[128,512]{1,0:T(8,128)(2,1)S(1)} %collective-permute-done.8), channel_id=1, source_target_pairs={{0,2},{1,3},{2,0},{3,1},{4,6},{5,7},{6,4},{7,5},{8,10},{9,11},{10,... | collective-permute-start | bytes 393224 | tf_op jit(solution)/shard_map/ppermute | solution.py:23
  38.2 4.7 %collective-permute-start.14 = (bf16[512,512]{1,0:T(8,128)(2,1)S(1)}, bf16[512,512]{1,0:T(8,128)(2,1)S(1)}, u32[]{:S(2)}, u32[]{:S(2)}) collective-permute-start(bf16[512,512]{1,0:T(8,128)(2,1)S(1)} %pad_maximum_fusion.3), channel_id=1, source_target_pairs={{0,1},{1,0},{2,3},{3,2},{4,5},{5,4},{6,7},{7,6},{8,9},{9,8},{10,11... | collective-permute-start | bytes 1572872 | tf_op jit(solution)/shard_map/ppermute | solution.py:23
  38.4 3.6 %copy-start.2 = (bf16[128,512]{1,0:T(8,128)(2,1)S(1)}, bf16[128,512]{1,0:T(8,128)(2,1)}, u32[]{:S(2)}) copy-start(bf16[128,512]{1,0:T(8,128)(2,1)} %shard_map.59) | copy-start | bytes 393220
  38.4 4.4 %collective-permute-start.4 = (bf16[2,256,512]{1,2,0:T(8,128)(2,1)S(1)}, bf16[2,256,512]{1,2,0:T(8,128)(2,1)S(1)}, u32[]{:S(2)}, u32[]{:S(2)}) collective-permute-start(bf16[2,256,512]{1,2,0:T(8,128)(2,1)S(1)} %get-tuple-element.9), channel_id=1, source_target_pairs={{0,1},{1,0},{2,3},{3,2},{4,5},{5,4},{6,7},{7,6},{8,9},{9,8},{10,11... | collective-permute-start | bytes 1572872 | tf_op jit(solution)/shard_map/ppermute | solution.py:23
  42.8 4.1 %collective-permute-start.10 = (bf16[512,512]{1,0:T(8,128)(2,1)}, bf16[512,512]{1,0:T(8,128)(2,1)}, u32[]{:S(2)}, u32[]{:S(2)}) collective-permute-start(bf16[512,512]{1,0:T(8,128)(2,1)} %pad_maximum_fusion.2), channel_id=1, source_target_pairs={{0,1},{1,0},{2,3},{3,2},{4,5},{5,4},{6,7},{7,6},{8,9},{9,8},{10,11... | collective-permute-start | bytes 1572872 | tf_op jit(solution)/shard_map/ppermute | solution.py:23
  44.2 9.3 %collective-permute-start.16 = (f16[528,256]{1,0:T(8,128)(2,1)S(1)}, f16[528,256]{1,0:T(8,128)(2,1)S(1)}, u32[]{:S(2)}, u32[]{:S(2)}) collective-permute-start(f16[528,256]{1,0:T(8,128)(2,1)S(1)} %convert_element_type.35), channel_id=1, source_target_pairs={{0,8},{4,12},{8,0},{12,4},{16,24},{20,28},{24,16},{28,20},{1,9},{5... | collective-permute-start | bytes 811016 | tf_op jit(solution)/shard_map/ppermute | solution.py:23
  48.6 11.8 %collective-permute-start.15 = (f16[528,256]{1,0:T(8,128)(2,1)S(1)}, f16[528,256]{1,0:T(8,128)(2,1)S(1)}, u32[]{:S(2)}, u32[]{:S(2)}) collective-permute-start(f16[528,256]{1,0:T(8,128)(2,1)S(1)} %convert_element_type.33), channel_id=1, source_target_pairs={{0,8},{4,12},{8,0},{12,4},{16,24},{20,28},{24,16},{28,20},{1,9},{5... | collective-permute-start | bytes 811016 | tf_op jit(solution)/shard_map/ppermute | solution.py:23
  54.2 14.5 %collective-permute-start.17 = (f16[528,256]{1,0:T(8,128)(2,1)S(1)}, f16[528,256]{1,0:T(8,128)(2,1)S(1)}, u32[]{:S(2)}, u32[]{:S(2)}) collective-permute-start(f16[528,256]{1,0:T(8,128)(2,1)S(1)} %convert_element_type.37), channel_id=1, source_target_pairs={{0,16},{4,20},{8,24},{12,28},{16,0},{20,4},{24,8},{28,12},{1,17},{... | collective-permute-start | bytes 811016 | tf_op jit(solution)/shard_map/ppermute | solution.py:23
  68.9 5.0 %collective-permute-start.18 = (bf16[256,256]{1,0:T(8,128)(2,1)S(1)}, bf16[256,256]{1,0:T(8,128)(2,1)S(1)}, u32[]{:S(2)}, u32[]{:S(2)}) collective-permute-start(bf16[256,256]{1,0:T(8,128)(2,1)S(1)} %shard_map.67), channel_id=1, source_target_pairs={{0,4},{4,0},{8,12},{12,8},{16,20},{20,16},{24,28},{28,24},{1,5},{5... | collective-permute-start | bytes 393224 | tf_op jit(solution)/shard_map/ppermute | solution.py:23
  69.4 6.5 %collective-permute-start.23 = (bf16[256,256]{1,0:T(8,128)(2,1)S(1)}, bf16[256,256]{1,0:T(8,128)(2,1)S(1)}, u32[]{:S(2)}, u32[]{:S(2)}) collective-permute-start(bf16[256,256]{1,0:T(8,128)(2,1)S(1)} %shard_map.67), channel_id=1, source_target_pairs={{0,2},{1,3},{2,0},{3,1},{4,6},{5,7},{6,4},{7,5},{8,10},{9,11},{10,... | collective-permute-start | bytes 393224 | tf_op jit(solution)/shard_map/ppermute | solution.py:23
  74.3 5.0 %collective-permute-start.19 = (bf16[256,256]{1,0:T(8,128)(2,1)S(1)}, bf16[256,256]{1,0:T(8,128)(2,1)S(1)}, u32[]{:S(2)}, u32[]{:S(2)}) collective-permute-start(bf16[256,256]{1,0:T(8,128)(2,1)S(1)} %fusion), channel_id=1, source_target_pairs={{0,8},{4,12},{8,0},{12,4},{16,24},{20,28},{24,16},{28,20},{1,9},{5... | collective-permute-start | bytes 393224 | tf_op jit(solution)/shard_map/ppermute | solution.py:23
  74.4 6.8 %collective-permute-start.25 = (bf16[256,256]{1,0:T(8,128)(2,1)S(1)}, bf16[256,256]{1,0:T(8,128)(2,1)S(1)}, u32[]{:S(2)}, u32[]{:S(2)}) collective-permute-start(bf16[256,256]{1,0:T(8,128)(2,1)S(1)} %fusion), channel_id=1, source_target_pairs={{0,2},{1,3},{2,0},{3,1},{4,6},{5,7},{6,4},{7,5},{8,10},{9,11},{10,... | collective-permute-start | bytes 393224 | tf_op jit(solution)/shard_map/ppermute | solution.py:23
  76.0 15.9 %collective-permute-start.24 = (bf16[512,256]{1,0:T(8,128)(2,1)S(1)}, bf16[512,256]{1,0:T(8,128)(2,1)S(1)}, u32[]{:S(2)}, u32[]{:S(2)}) collective-permute-start(bf16[512,256]{1,0:T(8,128)(2,1)S(1)} %get-tuple-element.36), channel_id=1, source_target_pairs={{0,1},{1,0},{2,3},{3,2},{4,5},{5,4},{6,7},{7,6},{8,9},{9,8},{10,11... | collective-permute-start | bytes 786440 | tf_op jit(solution)/shard_map/ppermute | solution.py:23
  79.5 6.8 %collective-permute-start.20 = (bf16[256,256]{1,0:T(8,128)(2,1)S(1)}, bf16[256,256]{1,0:T(8,128)(2,1)S(1)}, u32[]{:S(2)}, u32[]{:S(2)}) collective-permute-start(bf16[256,256]{1,0:T(8,128)(2,1)S(1)} %fusion.1), channel_id=1, source_target_pairs={{0,16},{4,20},{8,24},{12,28},{16,0},{20,4},{24,8},{28,12},{1,17},{... | collective-permute-start | bytes 393224 | tf_op jit(solution)/shard_map/ppermute | solution.py:23
  79.6 8.5 %collective-permute-start.27 = (bf16[256,256]{1,0:T(8,128)(2,1)S(1)}, bf16[256,256]{1,0:T(8,128)(2,1)S(1)}, u32[]{:S(2)}, u32[]{:S(2)}) collective-permute-start(bf16[256,256]{1,0:T(8,128)(2,1)S(1)} %fusion.1), channel_id=1, source_target_pairs={{0,2},{1,3},{2,0},{3,1},{4,6},{5,7},{6,4},{7,5},{8,10},{9,11},{10,... | collective-permute-start | bytes 393224 | tf_op jit(solution)/shard_map/ppermute | solution.py:23
  81.3 10.5 %collective-permute-start.26 = (bf16[512,256]{1,0:T(8,128)(2,1)S(1)}, bf16[512,256]{1,0:T(8,128)(2,1)S(1)}, u32[]{:S(2)}, u32[]{:S(2)}) collective-permute-start(bf16[512,256]{1,0:T(8,128)(2,1)S(1)} %get-tuple-element.32), channel_id=1, source_target_pairs={{0,1},{1,0},{2,3},{3,2},{4,5},{5,4},{6,7},{7,6},{8,9},{9,8},{10,11... | collective-permute-start | bytes 786440 | tf_op jit(solution)/shard_map/ppermute | solution.py:23
  86.5 5.0 %collective-permute-start.21 = (bf16[256,256]{1,0:T(8,128)(2,1)S(1)}, bf16[256,256]{1,0:T(8,128)(2,1)S(1)}, u32[]{:S(2)}, u32[]{:S(2)}) collective-permute-start(bf16[256,256]{1,0:T(8,128)(2,1)S(1)} %fusion.2), channel_id=1, source_target_pairs={{0,2},{1,3},{2,0},{3,1},{4,6},{5,7},{6,4},{7,5},{8,10},{9,11},{10,... | collective-permute-start | bytes 393224 | tf_op jit(solution)/shard_map/ppermute | solution.py:23
  88.2 3.6 %collective-permute-start.28 = (bf16[512,256]{1,0:T(8,128)(2,1)S(1)}, bf16[512,256]{1,0:T(8,128)(2,1)S(1)}, u32[]{:S(2)}, u32[]{:S(2)}) collective-permute-start(bf16[512,256]{1,0:T(8,128)(2,1)S(1)} %get-tuple-element.28), channel_id=1, source_target_pairs={{0,1},{1,0},{2,3},{3,2},{4,5},{5,4},{6,7},{7,6},{8,9},{9,8},{10,11... | collective-permute-start | bytes 786440 | tf_op jit(solution)/shard_map/ppermute | solution.py:23
  91.6 1.6 %collective-permute-start.22 = (bf16[512,256]{1,0:T(8,128)(2,1)S(1)}, bf16[512,256]{1,0:T(8,128)(2,1)S(1)}, u32[]{:S(2)}, u32[]{:S(2)}) collective-permute-start(bf16[512,256]{1,0:T(8,128)(2,1)S(1)} %get-tuple-element.40), channel_id=1, source_target_pairs={{0,1},{1,0},{2,3},{3,2},{4,5},{5,4},{6,7},{7,6},{8,9},{9,8},{10,11... | collective-permute-start | bytes 786440 | tf_op jit(solution)/shard_map/ppermute | solution.py:23
  93.4 12.1 %copy-start = (bf16[2,512,256]{2,1,0:T(8,128)(2,1)}, bf16[2,512,256]{2,1,0:T(8,128)(2,1)S(1)}, u32[]{:S(2)}) copy-start(bf16[2,512,256]{2,1,0:T(8,128)(2,1)S(1)} %pad_maximum_fusion.4) | copy-start | bytes 1572868

commit v4 on v3

--- a/solution.py
+++ b/solution.py
@@ -30,28 +30,13 @@
     return out
 
 
-def pick_kernel(blocks_ref, orders_ref, array_ref, out_ref):
-    index = lax.broadcasted_iota(jnp.int32, (array_ref.shape[1], orders_ref.shape[2]), 0)
-    one_hot = (index == orders_ref[0]).astype(f32).astype(bf16)
-    out_ref[...] = jnp.dot(array_ref[...], one_hot, preferred_element_type=f32).astype(bf16)
-
-
-def pick(array, orders, blocks, width):
-    count, _, kept = orders.shape
-    rows = array.shape[0]
-    return pl.pallas_call(
-        pick_kernel,
-        grid_spec=pltpu.PrefetchScalarGridSpec(
-            num_scalar_prefetch=1,
-            grid=(count,),
-            in_specs=[
-                pl.BlockSpec((1, 1, kept), lambda i, w: (i, 0, 0)),
-                pl.BlockSpec((rows, width), lambda i, w: (0, w[i])),
-            ],
-            out_specs=pl.BlockSpec((rows, kept), lambda i, w: (0, i)),
-        ),
-        out_shape=jax.ShapeDtypeStruct((rows, count * kept), bf16),
-    )(blocks, orders, array)
+def pick(blocks, lists):
+    out = []
+    for block, listed in zip(blocks, lists):
+        index = lax.broadcasted_iota(jnp.int32, (block.shape[1], listed.shape[0]), 0)
+        one_hot = (index == listed).astype(bf16)
+        out.append(jnp.dot(block, one_hot, preferred_element_type=f32).astype(bf16))
+    return jnp.concatenate(out, axis=1)
 
 
 def split3(v):
@@ -100,7 +85,7 @@
 
 
 def pivots_kernel(sets, *refs):
-    cands, out_ref, grams = refs[:sets], refs[sets], refs[sets + 1 :]
+    cands, total_ref, out_ref, grams = refs[:sets], refs[sets], refs[sets + 1], refs[sets + 2 :]
     rows, n = cands[0].shape
     diagonal = lax.broadcasted_iota(jnp.int32, (n, n), 0) == lax.broadcasted_iota(jnp.int32, (n, n), 1)
     shift = jnp.where(diagonal, f32(ridge), f32(0))
@@ -119,17 +104,17 @@
             return carry
 
         lax.fori_loop(0, min(lanes, n - base) // height, panel, 0)
-    out_ref[...] = 0.5 * jnp.log(out_ref[...])
+    total_ref[...] = jnp.sum(0.5 * jnp.log(out_ref[...]), axis=0, keepdims=True)
 
 
 def log_pivots(cands):
     sets, (rows, n) = len(cands), cands[0].shape
     return pl.pallas_call(
         functools.partial(pivots_kernel, sets),
-        out_shape=jax.ShapeDtypeStruct((sets, n), f32),
+        out_shape=jax.ShapeDtypeStruct((1, n), f32),
         in_specs=[pl.BlockSpec(memory_space=pltpu.VMEM)] * sets,
         out_specs=pl.BlockSpec(memory_space=pltpu.VMEM),
-        scratch_shapes=[pltpu.VMEM((n, n), f32)] * sets,
+        scratch_shapes=[pltpu.VMEM((sets, n), f32)] + [pltpu.VMEM((n, n), f32)] * sets,
         compiler_params=pltpu.CompilerParams(vmem_limit_bytes=40 << 20),
     )(*cands)
 
@@ -139,19 +124,20 @@
     return lax.dynamic_slice_in_dim(block, upper * size, size, axis=1)
 
 
-def sketch_kernel(mode, dots, plain, coded, *refs):
+def sketch_kernel(mode, columns, starts, dots, plain, *refs):
     refs, out_ref = refs[:-1], refs[-1]
     total = 0.0
     if dots:
         mix_ref, refs = refs[0], refs[1:]
-        start = 0
-        for points_ref in refs[:dots]:
-            rows = points_ref.shape[0]
-            total += jnp.dot(mix_ref[:, start : start + rows], points_ref[...], preferred_element_type=f32)
-            start += rows
-    for term in refs[dots : dots + plain]:
+    views = [ref.at[:, start : start + columns] for ref, start in zip(refs, starts)]
+    first = 0
+    for points_ref in views[:dots]:
+        rows = points_ref.shape[0]
+        total += jnp.dot(mix_ref[:, first : first + rows], points_ref[...], preferred_element_type=f32)
+        first += rows
+    for term in views[dots : dots + plain]:
         total += term[...]
-    for codes in refs[dots + plain :]:
+    for codes in views[dots + plain :]:
         size = codes.shape[0] - tag_rows
         total += codes[:size, :] * jnp.exp2(codes[size : size + 1, :] - top)
     size = total.shape[0]
@@ -166,12 +152,14 @@
         out_ref[...] = (total[: size // 2] * total[size // 2 :]).astype(bf16)
 
 
-def sketch(mode, mix, points, plain, coded):
-    size, columns = mix.shape[0], (points + plain + coded)[0].shape[1]
+def sketch(mode, columns, mix, points, plain, coded):
+    size = mix.shape[0]
     rows, kind = {"code": (size + tag_rows, f32), "keep": (size, f32), "multiply": (size // 2, bf16)}[mode]
-    operands = ([mix] + points if points else []) + plain + coded
+    terms = points + plain + coded
+    operands = ([mix] if points else []) + [array for array, _ in terms]
+    starts = [start for _, start in terms]
     return pl.pallas_call(
-        functools.partial(sketch_kernel, mode, len(points), len(plain), len(coded)),
+        functools.partial(sketch_kernel, mode, columns, starts, len(points), len(plain)),
         out_shape=jax.ShapeDtypeStruct((rows, columns), kind),
         in_specs=[pl.BlockSpec(memory_space=pltpu.VMEM)] * len(operands),
         out_specs=pl.BlockSpec(memory_space=pltpu.VMEM),
@@ -180,8 +168,8 @@
 
 
 def halves(block):
-    size = (block[0] + block[1])[0].shape[1] // 2
-    return [[[a[:, :size] for a in b] for b in block], [[a[:, size:] for a in b] for b in block]]
+    size = block[0] // 2
+    return [[size] + [[(a, first + shift) for a, first in terms] for terms in block[1:]] for shift in (0, size)]
 
 
 def local(orbitals, w_first, w_second, pivots):
@@ -192,28 +180,33 @@
     kept = order.shape[1]
     width = orbitals.shape[1] // groups
 
+    orders = order[:1][None]
+    orders = jnp.concatenate([orders, exchange(orders, "grid", 1)], axis=1)
+
     parts = 2 if grid_bits > 1 else 1
     count = groups // 2 // parts
     places = [[reversed_bits(p * count + i, grid_bits - 1) for i in range(count)] for p in range(parts)]
-    raw = [
-        lax.dynamic_slice_in_dim(orbitals, (here ^ 2 * k + 1) * width, width, axis=1) for k in places[-1]
-    ]
-    raw = exchange(jnp.concatenate(raw, axis=1), "grid", 1)
+
+    def blocks_of(p, side):
+        return [
+            lax.dynamic_slice_in_dim(orbitals, (here ^ 2 * k + side) * width, width, axis=1) for k in places[p]
+        ]
+
+    raw = exchange(jnp.concatenate(blocks_of(parts - 1, 1), axis=1), "grid", 1)
 
     mixing = [jnp.stack([w_first.T, w_second.T])]
     for t in reversed(range(1, band_bits)):
         upper = place >> t & 1
-        got = [exchange(half_of(m, 1 - upper), "band", 1 << t) for m in mixing]
-        mixing = [half_of(m, upper) for m in mixing] + got
-
-    orders = order[:1][None]
+        send = [half_of(m, 1 - upper) for m in mixing]
+        orders, send = lax.optimization_barrier((orders, send))
+        mixing = [half_of(m, upper) for m in mixing] + [exchange(m, "band", 1 << t) for m in send]
     near = mixing[0]
     for t in reversed(range(1, grid_bits)):
         orders = jnp.stack([orders, exchange(orders, "grid", 1 << t)], axis=1).reshape((-1,) + orders.shape[1:])
         if t == grid_bits - 1:
             orders, near = lax.optimization_barrier((orders, near))
-    near = exchange(near, "grid", 1)
-    lists = [jnp.stack([orders[k] for k in p]) for p in places]
+    near = [near] + mixing[1:]
+    near = [exchange(m, "grid", 1) for m in near]
 
     def over_bands(block):
         blocks = [block]
@@ -221,39 +214,42 @@
             blocks = blocks + [exchange(m, "band", 1 << t) for m in blocks]
         return blocks
 
-    def names(p, side):
-        return jnp.stack([here ^ 2 * k + side for k in places[p]])
+    def lists_of(p, side):
+        return [orders[k, side] for k in places[p]]
 
     gathered = {}
     for p in reversed(range(parts)):
-        own = over_bands(pick(orbitals, lists[p], names(p, 0), width))
+        own = over_bands(pick(blocks_of(p, 0), lists_of(p, 0)))
         if p == parts - 1:
-            far = pick(raw, lists[p], jnp.arange(count, dtype=jnp.int32), width)
+            far = pick([raw[:, i * width : (i + 1) * width] for i in range(count)], lists_of(p, 0))
+            orders, far = lax.optimization_barrier((orders, far))
         else:
-            others = exchange(lists[p], "grid", 1)
-            far = exchange(pick(orbitals, others, names(p, 1), width), "grid", 1)
+            far = exchange(pick(blocks_of(p, 1), lists_of(p, 1)), "grid", 1)
         rows = jnp.concatenate(own + over_bands(far), axis=0)
         gathered[p] = [rows, exchange(rows, "band", 1)]
 
-    mixing = jnp.concatenate(mixing + [near] + [exchange(m, "grid", 1) for m in mixing[1:]], axis=2)
+    mixing = jnp.concatenate(mixing + near, axis=2)
     mixes = [half_of(mixing, place & 1), exchange(half_of(mixing, 1 - (place & 1)), "band", 1)]
     mix = jnp.concatenate(mixes, axis=2)
     mix = mix.reshape(-1, mix.shape[2])
 
     def swap(block, bit):
-        codes = sketch("code", mix, block[0], [], block[1]).astype(f16)
-        return exchange(codes, "grid", 1 << bit).astype(f32)
-
-    stay = [gathered[0], []]
+        columns, points, codes = block
+        new = sketch("code", columns, mix, points, [], codes).astype(f16)
+        return exchange(new, "grid", 1 << bit).astype(f32), 0
+
+    stay = [count * kept, [(rows, 0) for rows in gathered[0]], []]
     if parts > 1:
-        go = [gathered[1], []]
+        go = [count * kept, [(rows, 0) for rows in gathered[1]], []]
         for t in range(1, grid_bits - 1):
             got = [swap(block, t) for block in reversed(halves(go))]
-            stay, go = [[points, codes + [new]] for (points, codes), new in zip(halves(stay), reversed(got))]
-        kept_sum = sketch("keep", mix, stay[0], [], stay[1])
-        chosen = sketch("multiply", mix, [], [kept_sum], [swap(go, grid_bits - 1)])
+            stay, go = [
+                [columns, points, codes + [new]] for (columns, points, codes), new in zip(halves(stay), reversed(got))
+            ]
+        held = sketch("keep", kept, mix, stay[1], [], stay[2])
+        chosen = sketch("multiply", kept, mix, [], [(held, 0)], [swap(go, grid_bits - 1)])
     else:
-        chosen = sketch("multiply", mix, stay[0], [], [])
+        chosen = sketch("multiply", kept, mix, stay[1], [], [])
 
     def over_band(block):
         for t in reversed(range(band_bits)):
@@ -276,8 +272,7 @@
         chosen = jnp.dot(chosen, mine, preferred_element_type=f32) + jnp.dot(got, other, preferred_element_type=f32)
         chosen = chosen.astype(bf16)
         cands.append(over_band(chosen))
-    quality = jnp.sum(log_pivots(cands), axis=0, keepdims=True)
-    return cands[-1], quality
+    return cands[-1], log_pivots(cands)
 
 
 def solution(mesh):

time: 106 us -> 107 us (level)
  Pallas kernels: 24.8 us -> 14.9 us
  waiting for transfers between devices: 41.6 us -> 50.2 us
  starting transfers between devices: 26.1 us -> 31.9 us
  local copies, waits for them, and re-layouts: 5.12 us -> 1.61 us
  other arithmetic: 6.04 us -> 4.05 us
  matrix products: 1.19 us -> 3.16 us
    pallas_call x9 -> x5, Pallas kernels: 12.8 us -> 2.3 us  [sketch(): pl.pallas_call(functools.partial(sketch_kernel, mode, columns, starts, le...]
    ppermute x29, waiting for transfers between devices: 41.6 us -> 50.2 us  [exchange(): return lax.ppermute(block, axis, [(i, i ^ delta) for i in range(count)])]
    ppermute x29, starting transfers between devices: 26.1 us -> 31.9 us  [exchange(): return lax.ppermute(block, axis, [(i, i ^ delta) for i in range(count)])]
    another operation x5 -> x0, other arithmetic: 2.52 us -> none  [the longest x3 1.92 us: names(): return jnp.stack([here ^ 2 * k + side for k in places[p]])]
    slice x5 -> x2, local copies, waits for them, and re-layouts: 2.21 us -> 0.01 us  [lists_of(): return [orders[k, side] for k in places[p]]]
    dot_general x0 -> x8, matrix products: none -> 1.98 us  [pick(): out.append(jnp.dot(block, one_hot, preferred_element_type=f32).astype(bf16))]
  transfers between devices with their start and end apart: 29 -> 29, of which waited for: 13 -> 16; matrix products, arithmetic and copies ran while one was open for 9% -> 7% of each run, Pallas kernels for 12% -> 2%
where the time goes in v4:
time: 107 us
  waiting for transfers between devices  50.2 us (47%)
  starting transfers between devices  31.9 us (30%)
  Pallas kernels  14.9 us (14%)
  other arithmetic  4.05 us (4%)
  matrix products  3.16 us (3%)
  local copies, waits for them, and re-layouts  1.61 us (2%)
  between operations  1.16 us (1%)
    ppermute x29, waiting for transfers between devices, exchange(): return lax.ppermute(block, axis, [(i, i ^ delta) for i in range(count)])  50.2 us
    ppermute x29, starting transfers between devices, exchange(): return lax.ppermute(block, axis, [(i, i ^ delta) for i in range(count)])  31.9 us
    pallas_call x1, Pallas kernels, log_pivots(): pl.pallas_call(functools.partial(pivots_kernel, sets), out_shape=jax.Shap...  12.6 us
    pallas_call x5, Pallas kernels, sketch(): pl.pallas_call(functools.partial(sketch_kernel, mode, columns, starts, le...  2.3 us
  transfers between devices with their start and end apart: 29, of which 16 were waited for; matrix products, arithmetic and copies ran while one was open for 7% of the time, Pallas kernels for 2%

profile of v4, /device:TPU:0, one launch (start us, length us, event | category | flops | bytes accessed | tf_op | source)
XLA Modules:
  0.0 106.9 jit_solution(15171264082827053732)
XLA Ops:
  0.7 0.8 slice_subtract_fusion
  1.5 3.0 %collective-permute-start = (s32[1,1,256]{2,1,0:T(1,128)S(1)}, s32[1,1,256]{2,1,0:T(1,128)S(1)}, u32[]{:S(2)}, u32[]{:S(2)}) collective-permute-start(s32[1,1,256]{2,1,0:T(1,128)S(1)} %get-tuple-element.54), channel_id=1, source_target_pairs={{0,4},{4,0},{8,12},{12,8},{16,20},{20,16},{24,28},{28,24},{1,5},{5... | collective-permute-start | bytes 3080 | tf_op jit(solution)/shard_map/ppermute | solution.py:23
  4.5 1.1 %fusion.4 = (bf16[2,512,128]{1,2,0:T(8,128)(2,1)S(1)}, bf16[2,512,128]{1,2,0:T(8,128)(2,1)S(1)}) fusion(s32[]{:T(128)S(6)} %select_n.134, bf16[1,1024,128]{1,2,0:T(8,128)(2,1)} %bitcast.81, bf16[1,1024,128]{1,2,0:T(8,128)(2,1)} %bitcast.82, s32[]{:T(128)S(6)} %select_n.135), kind=kLoop, calls=%fused_computation.33 | loop fusion | flops 1048576 | bytes 1048584 | tf_op jit(solution)/shard_map/stack | solution.py:197
  5.7 0.4 collective-permute-done
  6.1 3.1 %collective-permute-start.2 = (s32[1,2,256]{2,1,0:T(2,128)S(1)}, s32[1,2,256]{2,1,0:T(2,128)S(1)}, u32[]{:S(2)}, u32[]{:S(2)}) collective-permute-start(s32[1,2,256]{2,1,0:T(2,128)S(1)} %pad_add_fusion.1), channel_id=1, source_target_pairs={{0,16},{4,20},{8,24},{12,28},{16,0},{20,4},{24,8},{28,12},{1,17},{... | collective-permute-start | bytes 6152 | tf_op jit(solution)/shard_map/ppermute | solution.py:23
  9.2 1.5 %collective-permute-done.2 = s32[1,2,256]{2,1,0:T(2,128)S(1)} collective-permute-done((s32[1,2,256]{2,1,0:T(2,128)S(1)}, s32[1,2,256]{2,1,0:T(2,128)S(1)}, u32[]{:S(2)}, u32[]{:S(2)}) %collective-permute-start.2) | collective-permute-done | bytes 2080 | tf_op jit(solution)/shard_map/ppermute | solution.py:23
  10.7 1.9 %collective-permute-start.6 = (s32[2,2,256]{2,1,0:T(2,128)S(1)}, s32[2,2,256]{2,1,0:T(2,128)S(1)}, u32[]{:S(2)}, u32[]{:S(2)}) collective-permute-start(s32[2,2,256]{2,1,0:T(2,128)S(1)} %add_bitcast_fusion), channel_id=1, source_target_pairs={{0,8},{4,12},{8,0},{12,4},{16,24},{20,28},{24,16},{28,20},{1,9},{5... | collective-permute-start | bytes 12296 | tf_op jit(solution)/shard_map/ppermute | solution.py:23
  12.7 1.6 %collective-permute-start.7 = (bf16[128,1024]{1,0:T(8,128)(2,1)S(1)}, bf16[128,1024]{1,0:T(8,128)(2,1)S(1)}, u32[]{:S(2)}, u32[]{:S(2)}) collective-permute-start(bf16[128,1024]{1,0:T(8,128)(2,1)S(1)} %pad_maximum_fusion.8), channel_id=1, source_target_pairs={{0,4},{4,0},{8,12},{12,8},{16,20},{20,16},{24,28},{28,24},{1,5},{5... | collective-permute-start | bytes 786440 | tf_op jit(solution)/shard_map/ppermute | solution.py:23
  14.3 1.5 %collective-permute-start.1 = (bf16[2,512,128]{1,2,0:T(8,128)(2,1)S(1)}, bf16[2,512,128]{1,2,0:T(8,128)(2,1)S(1)}, u32[]{:S(2)}, u32[]{:S(2)}) collective-permute-start(bf16[2,512,128]{1,2,0:T(8,128)(2,1)S(1)} %get-tuple-element.8), channel_id=1, source_target_pairs={{0,2},{1,3},{2,0},{3,1},{4,6},{5,7},{6,4},{7,5},{8,10},{9,11},{10,... | collective-permute-start | bytes 786440 | tf_op jit(solution)/shard_map/ppermute | solution.py:23
  15.7 0.5 collective-permute-start.3
  16.8 0.6 collective-permute-start.12
  17.4 4.6 %collective-permute-done.7 = bf16[128,1024]{1,0:T(8,128)(2,1)S(1)} collective-permute-done((bf16[128,1024]{1,0:T(8,128)(2,1)S(1)}, bf16[128,1024]{1,0:T(8,128)(2,1)S(1)}, u32[]{:S(2)}, u32[]{:S(2)}) %collective-permute-start.7) | collective-permute-done | bytes 262176 | tf_op jit(solution)/shard_map/ppermute | solution.py:23
  23.0 1.6 %collective-permute-start.9 = (bf16[128,512]{1,0:T(8,128)(2,1)S(1)}, bf16[128,512]{1,0:T(8,128)(2,1)S(1)}, u32[]{:S(2)}, u32[]{:S(2)}) collective-permute-start(bf16[128,512]{1,0:T(8,128)(2,1)S(1)} %pad_maximum_fusion.15), channel_id=1, source_target_pairs={{0,4},{4,0},{8,12},{12,8},{16,20},{20,16},{24,28},{28,24},{1,5},{5... | collective-permute-start | bytes 393224 | tf_op jit(solution)/shard_map/ppermute | solution.py:23
  24.6 1.5 %collective-permute-start.13 = (bf16[128,512]{1,0:T(8,128)(2,1)S(1)}, bf16[128,512]{1,0:T(8,128)(2,1)S(1)}, u32[]{:S(2)}, u32[]{:S(2)}) collective-permute-start(bf16[128,512]{1,0:T(8,128)(2,1)S(1)} %pad_maximum_fusion.13), channel_id=1, source_target_pairs={{0,2},{1,3},{2,0},{3,1},{4,6},{5,7},{6,4},{7,5},{8,10},{9,11},{10,... | collective-permute-start | bytes 393224 | tf_op jit(solution)/shard_map/ppermute | solution.py:23
  26.1 0.5 collective-permute-start.4
  26.9 0.2 convolution_convert_fusion.5
  27.1 0.5 collective-permute-done.3
  27.6 4.9 %collective-permute-done.4 = bf16[2,512,128]{1,2,0:T(8,128)(2,1)S(1)} collective-permute-done((bf16[2,512,128]{1,2,0:T(8,128)(2,1)S(1)}, bf16[2,512,128]{1,2,0:T(8,128)(2,1)S(1)}, u32[]{:S(2)}, u32[]{:S(2)}) %collective-permute-start.4) | collective-permute-done | bytes 262176 | tf_op jit(solution)/shard_map/ppermute | solution.py:23
  32.8 0.5 collective-permute-start.14
  33.4 1.4 %collective-permute-start.8 = (bf16[128,512]{1,0:T(8,128)(2,1)S(1)}, bf16[128,512]{1,0:T(8,128)(2,1)S(1)}, u32[]{:S(2)}, u32[]{:S(2)}) collective-permute-start(bf16[128,512]{1,0:T(8,128)(2,1)S(1)} %pad_maximum_fusion.14), channel_id=1, source_target_pairs={{0,2},{1,3},{2,0},{3,1},{4,6},{5,7},{6,4},{7,5},{8,10},{9,11},{10,... | collective-permute-start | bytes 393224 | tf_op jit(solution)/shard_map/ppermute | solution.py:23
  34.7 0.7 collective-permute-start.10
  35.5 4.3 %collective-permute-done.8 = bf16[128,512]{1,0:T(8,128)(2,1)S(1)} collective-permute-done((bf16[128,512]{1,0:T(8,128)(2,1)S(1)}, bf16[128,512]{1,0:T(8,128)(2,1)S(1)}, u32[]{:S(2)}, u32[]{:S(2)}) %collective-permute-start.8) | collective-permute-done | bytes 131104 | tf_op jit(solution)/shard_map/ppermute | solution.py:23
  39.8 1.9 %collective-permute-done.10 = bf16[128,512]{1,0:T(8,128)(2,1)S(1)} collective-permute-done((bf16[128,512]{1,0:T(8,128)(2,1)S(1)}, bf16[128,512]{1,0:T(8,128)(2,1)S(1)}, u32[]{:S(2)}, u32[]{:S(2)}) %collective-permute-start.10) | collective-permute-done | bytes 131104 | tf_op jit(solution)/shard_map/ppermute | solution.py:23
  41.8 1.1 %pad_maximum_fusion.1 = bf16[2,256,1024]{1,2,0:T(8,128)(2,1)} fusion(bf16[2,256,512]{1,2,0:T(8,128)(2,1)S(1)} %collective-permute-done.5, bf16[2,256,512]{1,2,0:T(8,128)(2,1)S(1)} %get-tuple-element.16), kind=kLoop, calls=%fused_computation.15 | loop fusion | flops 2097152 | bytes 2097152 | tf_op jit(solution)/shard_map/concatenate | solution.py:233
  42.9 1.5 %copy.7 = bf16[2,256,1024]{2,1,0:T(8,128)(2,1)S(1)} copy(bf16[2,256,1024]{1,2,0:T(8,128)(2,1)} %pad_maximum_fusion.1) | data formatting | bytes 2097152 | tf_op jit(solution)/shard_map/concatenate | solution.py:233
  44.4 0.6 shard_map.61
  45.0 0.5 collective-permute-start.16
  45.6 0.6 shard_map.59
  46.2 1.6 %collective-permute-start.15 = (f16[528,256]{1,0:T(8,128)(2,1)S(1)}, f16[528,256]{1,0:T(8,128)(2,1)S(1)}, u32[]{:S(2)}, u32[]{:S(2)}) collective-permute-start(f16[528,256]{1,0:T(8,128)(2,1)S(1)} %convert_element_type.73), channel_id=1, source_target_pairs={{0,8},{4,12},{8,0},{12,4},{16,24},{20,28},{24,16},{28,20},{1,9},{5... | collective-permute-start | bytes 811016 | tf_op jit(solution)/shard_map/ppermute | solution.py:23
  47.9 6.5 %collective-permute-done.16 = f16[528,256]{1,0:T(8,128)(2,1)S(1)} collective-permute-done((f16[528,256]{1,0:T(8,128)(2,1)S(1)}, f16[528,256]{1,0:T(8,128)(2,1)S(1)}, u32[]{:S(2)}, u32[]{:S(2)}) %collective-permute-start.16) | collective-permute-done | bytes 270368 | tf_op jit(solution)/shard_map/ppermute | solution.py:23
  54.4 0.6 shard_map.62
  55.1 2.7 %collective-permute-start.17 = (f16[528,256]{1,0:T(8,128)(2,1)S(1)}, f16[528,256]{1,0:T(8,128)(2,1)S(1)}, u32[]{:S(2)}, u32[]{:S(2)}) collective-permute-start(f16[528,256]{1,0:T(8,128)(2,1)S(1)} %convert_element_type.77), channel_id=1, source_target_pairs={{0,16},{4,20},{8,24},{12,28},{16,0},{20,4},{24,8},{28,12},{1,17},{... | collective-permute-start | bytes 811016 | tf_op jit(solution)/shard_map/ppermute | solution.py:23
  57.7 5.9 %collective-permute-done.15 = f16[528,256]{1,0:T(8,128)(2,1)S(1)} collective-permute-done((f16[528,256]{1,0:T(8,128)(2,1)S(1)}, f16[528,256]{1,0:T(8,128)(2,1)S(1)}, u32[]{:S(2)}, u32[]{:S(2)}) %collective-permute-start.15) | collective-permute-done | bytes 270368 | tf_op jit(solution)/shard_map/ppermute | solution.py:23
  63.7 0.4 shard_map.60.refs_0_
  64.2 5.4 %collective-permute-done.17 = f16[528,256]{1,0:T(8,128)(2,1)S(1)} collective-permute-done((f16[528,256]{1,0:T(8,128)(2,1)S(1)}, f16[528,256]{1,0:T(8,128)(2,1)S(1)}, u32[]{:S(2)}, u32[]{:S(2)}) %collective-permute-start.17) | collective-permute-done | bytes 270368 | tf_op jit(solution)/shard_map/ppermute | solution.py:23
  69.7 1.3 %collective-permute-start.18 = (bf16[256,256]{1,0:T(8,128)(2,1)S(1)}, bf16[256,256]{1,0:T(8,128)(2,1)S(1)}, u32[]{:S(2)}, u32[]{:S(2)}) collective-permute-start(bf16[256,256]{1,0:T(8,128)(2,1)S(1)} %shard_map.63), channel_id=1, source_target_pairs={{0,4},{4,0},{8,12},{12,8},{16,20},{20,16},{24,28},{28,24},{1,5},{5... | collective-permute-start | bytes 393224 | tf_op jit(solution)/shard_map/ppermute | solution.py:23
  71.0 1.5 %collective-permute-start.23 = (bf16[256,256]{1,0:T(8,128)(2,1)S(1)}, bf16[256,256]{1,0:T(8,128)(2,1)S(1)}, u32[]{:S(2)}, u32[]{:S(2)}) collective-permute-start(bf16[256,256]{1,0:T(8,128)(2,1)S(1)} %shard_map.63), channel_id=1, source_target_pairs={{0,2},{1,3},{2,0},{3,1},{4,6},{5,7},{6,4},{7,5},{8,10},{9,11},{10,... | collective-permute-start | bytes 393224 | tf_op jit(solution)/shard_map/ppermute | solution.py:23
  72.5 2.2 %collective-permute-done.18 = bf16[256,256]{1,0:T(8,128)(2,1)S(1)} collective-permute-done((bf16[256,256]{1,0:T(8,128)(2,1)S(1)}, bf16[256,256]{1,0:T(8,128)(2,1)S(1)}, u32[]{:S(2)}, u32[]{:S(2)}) %collective-permute-start.18) | collective-permute-done | bytes 131104 | tf_op jit(solution)/shard_map/ppermute | solution.py:23
  75.2 1.4 %collective-permute-start.25 = (bf16[256,256]{1,0:T(8,128)(2,1)S(1)}, bf16[256,256]{1,0:T(8,128)(2,1)S(1)}, u32[]{:S(2)}, u32[]{:S(2)}) collective-permute-start(bf16[256,256]{1,0:T(8,128)(2,1)S(1)} %fusion), channel_id=1, source_target_pairs={{0,2},{1,3},{2,0},{3,1},{4,6},{5,7},{6,4},{7,5},{8,10},{9,11},{10,... | collective-permute-start | bytes 393224 | tf_op jit(solution)/shard_map/ppermute | solution.py:23
  76.6 0.3 collective-permute-done.23
  77.2 2.9 %collective-permute-done.19 = bf16[256,256]{1,0:T(8,128)(2,1)S(1)} collective-permute-done((bf16[256,256]{1,0:T(8,128)(2,1)S(1)}, bf16[256,256]{1,0:T(8,128)(2,1)S(1)}, u32[]{:S(2)}, u32[]{:S(2)}) %collective-permute-start.19) | collective-permute-done | bytes 131104 | tf_op jit(solution)/shard_map/ppermute | solution.py:23
  80.4 1.1 %collective-permute-start.20 = (bf16[256,256]{1,0:T(8,128)(2,1)S(1)}, bf16[256,256]{1,0:T(8,128)(2,1)S(1)}, u32[]{:S(2)}, u32[]{:S(2)}) collective-permute-start(bf16[256,256]{1,0:T(8,128)(2,1)S(1)} %fusion.1), channel_id=1, source_target_pairs={{0,16},{4,20},{8,24},{12,28},{16,0},{20,4},{24,8},{28,12},{1,17},{... | collective-permute-start | bytes 393224 | tf_op jit(solution)/shard_map/ppermute | solution.py:23
  81.5 1.3 %collective-permute-start.27 = (bf16[256,256]{1,0:T(8,128)(2,1)S(1)}, bf16[256,256]{1,0:T(8,128)(2,1)S(1)}, u32[]{:S(2)}, u32[]{:S(2)}) collective-permute-start(bf16[256,256]{1,0:T(8,128)(2,1)S(1)} %fusion.1), channel_id=1, source_target_pairs={{0,2},{1,3},{2,0},{3,1},{4,6},{5,7},{6,4},{7,5},{8,10},{9,11},{10,... | collective-permute-start | bytes 393224 | tf_op jit(solution)/shard_map/ppermute | solution.py:23
  83.1 4.2 %collective-permute-done.20 = bf16[256,256]{1,0:T(8,128)(2,1)S(1)} collective-permute-done((bf16[256,256]{1,0:T(8,128)(2,1)S(1)}, bf16[256,256]{1,0:T(8,128)(2,1)S(1)}, u32[]{:S(2)}, u32[]{:S(2)}) %collective-permute-start.20) | collective-permute-done | bytes 131104 | tf_op jit(solution)/shard_map/ppermute | solution.py:23
  87.5 1.7 %collective-permute-start.21 = (bf16[256,256]{1,0:T(8,128)(2,1)S(1)}, bf16[256,256]{1,0:T(8,128)(2,1)S(1)}, u32[]{:S(2)}, u32[]{:S(2)}) collective-permute-start(bf16[256,256]{1,0:T(8,128)(2,1)S(1)} %fusion.2), channel_id=1, source_target_pairs={{0,2},{1,3},{2,0},{3,1},{4,6},{5,7},{6,4},{7,5},{8,10},{9,11},{10,... | collective-permute-start | bytes 393224 | tf_op jit(solution)/shard_map/ppermute | solution.py:23
  89.3 3.2 %collective-permute-done.21 = bf16[256,256]{1,0:T(8,128)(2,1)S(1)} collective-permute-done((bf16[256,256]{1,0:T(8,128)(2,1)S(1)}, bf16[256,256]{1,0:T(8,128)(2,1)S(1)}, u32[]{:S(2)}, u32[]{:S(2)}) %collective-permute-start.21) | collective-permute-done | bytes 131104 | tf_op jit(solution)/shard_map/ppermute | solution.py:23
  92.9 1.3 %collective-permute-done.22 = bf16[512,256]{1,0:T(8,128)(2,1)S(1)} collective-permute-done((bf16[512,256]{1,0:T(8,128)(2,1)S(1)}, bf16[512,256]{1,0:T(8,128)(2,1)S(1)}, u32[]{:S(2)}, u32[]{:S(2)}) %collective-permute-start.22) | collective-permute-done | bytes 262176 | tf_op jit(solution)/shard_map/ppermute | solution.py:23
  94.4 12.6 %shard_map.64 = f32[1,256]{1,0:T(1,128)} custom-call(bf16[1024,256]{1,0:T(8,128)(2,1)S(1)} %bitcast.76, bf16[1024,256]{1,0:T(8,128)(2,1)S(1)} %bitcast.72, bf16[1024,256]{1,0:T(8,128)(2,1)S(1)} %bitcast.73, bf16[1024,256]{1,0:T(8,128)(2,1)S(1)} %bitcast.74), custom_call_target="tpu_custom_call" | custom-call | tf_op jit(solution)/shard_map/pallas_call | solution.py:112
  (74 shorter events, 4.6 us)
Async XLA Ops:
  0.6 8.5 %copy-start.1 = (bf16[128,4096]{1,0:T(8,128)(2,1)S(1)}, bf16[128,4096]{1,0:T(8,128)(2,1)}, u32[]{:S(2)}) copy-start(bf16[128,4096]{1,0:T(8,128)(2,1)} %param.4) | copy-start | bytes 3145732
  1.5 4.6 %collective-permute-start = (s32[1,1,256]{2,1,0:T(1,128)S(1)}, s32[1,1,256]{2,1,0:T(1,128)S(1)}, u32[]{:S(2)}, u32[]{:S(2)}) collective-permute-start(s32[1,1,256]{2,1,0:T(1,128)S(1)} %get-tuple-element.54), channel_id=1, source_target_pairs={{0,4},{4,0},{8,12},{12,8},{16,20},{20,16},{24,28},{28,24},{1,5},{5... | collective-permute-start | bytes 3080 | tf_op jit(solution)/shard_map/ppermute | solution.py:23
  6.1 4.7 %collective-permute-start.2 = (s32[1,2,256]{2,1,0:T(2,128)S(1)}, s32[1,2,256]{2,1,0:T(2,128)S(1)}, u32[]{:S(2)}, u32[]{:S(2)}) collective-permute-start(s32[1,2,256]{2,1,0:T(2,128)S(1)} %pad_add_fusion.1), channel_id=1, source_target_pairs={{0,16},{4,20},{8,24},{12,28},{16,0},{20,4},{24,8},{28,12},{1,17},{... | collective-permute-start | bytes 6152 | tf_op jit(solution)/shard_map/ppermute | solution.py:23
  10.7 5.5 %collective-permute-start.6 = (s32[2,2,256]{2,1,0:T(2,128)S(1)}, s32[2,2,256]{2,1,0:T(2,128)S(1)}, u32[]{:S(2)}, u32[]{:S(2)}) collective-permute-start(s32[2,2,256]{2,1,0:T(2,128)S(1)} %add_bitcast_fusion), channel_id=1, source_target_pairs={{0,8},{4,12},{8,0},{12,4},{16,24},{20,28},{24,16},{28,20},{1,9},{5... | collective-permute-start | bytes 12296 | tf_op jit(solution)/shard_map/ppermute | solution.py:23
  12.7 9.3 %collective-permute-start.7 = (bf16[128,1024]{1,0:T(8,128)(2,1)S(1)}, bf16[128,1024]{1,0:T(8,128)(2,1)S(1)}, u32[]{:S(2)}, u32[]{:S(2)}) collective-permute-start(bf16[128,1024]{1,0:T(8,128)(2,1)S(1)} %pad_maximum_fusion.8), channel_id=1, source_target_pairs={{0,4},{4,0},{8,12},{12,8},{16,20},{20,16},{24,28},{28,24},{1,5},{5... | collective-permute-start | bytes 786440 | tf_op jit(solution)/shard_map/ppermute | solution.py:23
  14.3 11.9 %collective-permute-start.1 = (bf16[2,512,128]{1,2,0:T(8,128)(2,1)S(1)}, bf16[2,512,128]{1,2,0:T(8,128)(2,1)S(1)}, u32[]{:S(2)}, u32[]{:S(2)}) collective-permute-start(bf16[2,512,128]{1,2,0:T(8,128)(2,1)S(1)} %get-tuple-element.8), channel_id=1, source_target_pairs={{0,2},{1,3},{2,0},{3,1},{4,6},{5,7},{6,4},{7,5},{8,10},{9,11},{10,... | collective-permute-start | bytes 786440 | tf_op jit(solution)/shard_map/ppermute | solution.py:23
  15.7 11.8 %collective-permute-start.3 = (bf16[2,512,128]{1,2,0:T(8,128)(2,1)S(1)}, bf16[2,512,128]{1,2,0:T(8,128)(2,1)S(1)}, u32[]{:S(2)}, u32[]{:S(2)}) collective-permute-start(bf16[2,512,128]{1,2,0:T(8,128)(2,1)S(1)} %get-tuple-element.10), channel_id=1, source_target_pairs={{0,4},{4,0},{8,12},{12,8},{16,20},{20,16},{24,28},{28,24},{1,5},{5... | collective-permute-start | bytes 786440 | tf_op jit(solution)/shard_map/ppermute | solution.py:23
  16.8 15.9 %collective-permute-start.12 = (bf16[128,512]{1,0:T(8,128)(2,1)S(1)}, bf16[128,512]{1,0:T(8,128)(2,1)S(1)}, u32[]{:S(2)}, u32[]{:S(2)}) collective-permute-start(bf16[128,512]{1,0:T(8,128)(2,1)S(1)} %pad_maximum_fusion.16), channel_id=1, source_target_pairs={{0,2},{1,3},{2,0},{3,1},{4,6},{5,7},{6,4},{7,5},{8,10},{9,11},{10,... | collective-permute-start | bytes 393224 | tf_op jit(solution)/shard_map/ppermute | solution.py:23
  23.0 11.7 %collective-permute-start.9 = (bf16[128,512]{1,0:T(8,128)(2,1)S(1)}, bf16[128,512]{1,0:T(8,128)(2,1)S(1)}, u32[]{:S(2)}, u32[]{:S(2)}) collective-permute-start(bf16[128,512]{1,0:T(8,128)(2,1)S(1)} %pad_maximum_fusion.15), channel_id=1, source_target_pairs={{0,4},{4,0},{8,12},{12,8},{16,20},{20,16},{24,28},{28,24},{1,5},{5... | collective-permute-start | bytes 393224 | tf_op jit(solution)/shard_map/ppermute | solution.py:23
  24.6 8.1 %collective-permute-start.13 = (bf16[128,512]{1,0:T(8,128)(2,1)S(1)}, bf16[128,512]{1,0:T(8,128)(2,1)S(1)}, u32[]{:S(2)}, u32[]{:S(2)}) collective-permute-start(bf16[128,512]{1,0:T(8,128)(2,1)S(1)} %pad_maximum_fusion.13), channel_id=1, source_target_pairs={{0,2},{1,3},{2,0},{3,1},{4,6},{5,7},{6,4},{7,5},{8,10},{9,11},{10,... | collective-permute-start | bytes 393224 | tf_op jit(solution)/shard_map/ppermute | solution.py:23
  26.1 6.4 %collective-permute-start.4 = (bf16[2,512,128]{1,2,0:T(8,128)(2,1)S(1)}, bf16[2,512,128]{1,2,0:T(8,128)(2,1)S(1)}, u32[]{:S(2)}, u32[]{:S(2)}) collective-permute-start(bf16[2,512,128]{1,2,0:T(8,128)(2,1)S(1)} %collective-permute-done.1), channel_id=1, source_target_pairs={{0,4},{4,0},{8,12},{12,8},{16,20},{20,16},{24,28},{28,24},{1,5},{5... | collective-permute-start | bytes 786440 | tf_op jit(solution)/shard_map/ppermute | solution.py:23
  32.7 9.1 %collective-permute-start.5 = (bf16[2,256,512]{1,2,0:T(8,128)(2,1)S(1)}, bf16[2,256,512]{1,2,0:T(8,128)(2,1)S(1)}, u32[]{:S(2)}, u32[]{:S(2)}) collective-permute-start(bf16[2,256,512]{1,2,0:T(8,128)(2,1)S(1)} %get-tuple-element.17), channel_id=1, source_target_pairs={{0,1},{1,0},{2,3},{3,2},{4,5},{5,4},{6,7},{7,6},{8,9},{9,8},{10,11... | collective-permute-start | bytes 1572872 | tf_op jit(solution)/shard_map/ppermute | solution.py:23
  32.8 11.6 %collective-permute-start.14 = (bf16[512,512]{1,0:T(8,128)(2,1)S(1)}, bf16[512,512]{1,0:T(8,128)(2,1)S(1)}, u32[]{:S(2)}, u32[]{:S(2)}) collective-permute-start(bf16[512,512]{1,0:T(8,128)(2,1)S(1)} %pad_maximum_fusion.3.refs_1_), channel_id=1, source_target_pairs={{0,1},{1,0},{2,3},{3,2},{4,5},{5,4},{6,7},{7,6},{8,9},{9,8},{10,11... | collective-permute-start | bytes 1572872 | tf_op jit(solution)/shard_map/ppermute | solution.py:23
  33.4 6.4 %collective-permute-start.8 = (bf16[128,512]{1,0:T(8,128)(2,1)S(1)}, bf16[128,512]{1,0:T(8,128)(2,1)S(1)}, u32[]{:S(2)}, u32[]{:S(2)}) collective-permute-start(bf16[128,512]{1,0:T(8,128)(2,1)S(1)} %pad_maximum_fusion.14), channel_id=1, source_target_pairs={{0,2},{1,3},{2,0},{3,1},{4,6},{5,7},{6,4},{7,5},{8,10},{9,11},{10,... | collective-permute-start | bytes 393224 | tf_op jit(solution)/shard_map/ppermute | solution.py:23
  34.7 7.0 %collective-permute-start.10 = (bf16[128,512]{1,0:T(8,128)(2,1)S(1)}, bf16[128,512]{1,0:T(8,128)(2,1)S(1)}, u32[]{:S(2)}, u32[]{:S(2)}) collective-permute-start(bf16[128,512]{1,0:T(8,128)(2,1)S(1)} %collective-permute-done.9), channel_id=1, source_target_pairs={{0,2},{1,3},{2,0},{3,1},{4,6},{5,7},{6,4},{7,5},{8,10},{9,11},{10,... | collective-permute-start | bytes 393224 | tf_op jit(solution)/shard_map/ppermute | solution.py:23
  41.7 12.7 %collective-permute-start.11 = (bf16[512,512]{1,0:T(8,128)(2,1)S(1)}, bf16[512,512]{1,0:T(8,128)(2,1)S(1)}, u32[]{:S(2)}, u32[]{:S(2)}) collective-permute-start(bf16[512,512]{1,0:T(8,128)(2,1)S(1)} %pad_maximum_fusion.2.refs_1_), channel_id=1, source_target_pairs={{0,1},{1,0},{2,3},{3,2},{4,5},{5,4},{6,7},{7,6},{8,9},{9,8},{10,11... | collective-permute-start | bytes 1572872 | tf_op jit(solution)/shard_map/ppermute | solution.py:23
  45.0 9.3 %collective-permute-start.16 = (f16[528,256]{1,0:T(8,128)(2,1)S(1)}, f16[528,256]{1,0:T(8,128)(2,1)S(1)}, u32[]{:S(2)}, u32[]{:S(2)}) collective-permute-start(f16[528,256]{1,0:T(8,128)(2,1)S(1)} %convert_element_type.75), channel_id=1, source_target_pairs={{0,8},{4,12},{8,0},{12,4},{16,24},{20,28},{24,16},{28,20},{1,9},{5... | collective-permute-start | bytes 811016 | tf_op jit(solution)/shard_map/ppermute | solution.py:23
  46.2 17.5 %collective-permute-start.15 = (f16[528,256]{1,0:T(8,128)(2,1)S(1)}, f16[528,256]{1,0:T(8,128)(2,1)S(1)}, u32[]{:S(2)}, u32[]{:S(2)}) collective-permute-start(f16[528,256]{1,0:T(8,128)(2,1)S(1)} %convert_element_type.73), channel_id=1, source_target_pairs={{0,8},{4,12},{8,0},{12,4},{16,24},{20,28},{24,16},{28,20},{1,9},{5... | collective-permute-start | bytes 811016 | tf_op jit(solution)/shard_map/ppermute | solution.py:23
  55.1 14.5 %collective-permute-start.17 = (f16[528,256]{1,0:T(8,128)(2,1)S(1)}, f16[528,256]{1,0:T(8,128)(2,1)S(1)}, u32[]{:S(2)}, u32[]{:S(2)}) collective-permute-start(f16[528,256]{1,0:T(8,128)(2,1)S(1)} %convert_element_type.77), channel_id=1, source_target_pairs={{0,16},{4,20},{8,24},{12,28},{16,0},{20,4},{24,8},{28,12},{1,17},{... | collective-permute-start | bytes 811016 | tf_op jit(solution)/shard_map/ppermute | solution.py:23
  69.7 5.0 %collective-permute-start.18 = (bf16[256,256]{1,0:T(8,128)(2,1)S(1)}, bf16[256,256]{1,0:T(8,128)(2,1)S(1)}, u32[]{:S(2)}, u32[]{:S(2)}) collective-permute-start(bf16[256,256]{1,0:T(8,128)(2,1)S(1)} %shard_map.63), channel_id=1, source_target_pairs={{0,4},{4,0},{8,12},{12,8},{16,20},{20,16},{24,28},{28,24},{1,5},{5... | collective-permute-start | bytes 393224 | tf_op jit(solution)/shard_map/ppermute | solution.py:23
  71.0 5.9 %collective-permute-start.23 = (bf16[256,256]{1,0:T(8,128)(2,1)S(1)}, bf16[256,256]{1,0:T(8,128)(2,1)S(1)}, u32[]{:S(2)}, u32[]{:S(2)}) collective-permute-start(bf16[256,256]{1,0:T(8,128)(2,1)S(1)} %shard_map.63), channel_id=1, source_target_pairs={{0,2},{1,3},{2,0},{3,1},{4,6},{5,7},{6,4},{7,5},{8,10},{9,11},{10,... | collective-permute-start | bytes 393224 | tf_op jit(solution)/shard_map/ppermute | solution.py:23
  75.1 5.0 %collective-permute-start.19 = (bf16[256,256]{1,0:T(8,128)(2,1)S(1)}, bf16[256,256]{1,0:T(8,128)(2,1)S(1)}, u32[]{:S(2)}, u32[]{:S(2)}) collective-permute-start(bf16[256,256]{1,0:T(8,128)(2,1)S(1)} %fusion), channel_id=1, source_target_pairs={{0,8},{4,12},{8,0},{12,4},{16,24},{20,28},{24,16},{28,20},{1,9},{5... | collective-permute-start | bytes 393224 | tf_op jit(solution)/shard_map/ppermute | solution.py:23
  75.2 7.5 %collective-permute-start.25 = (bf16[256,256]{1,0:T(8,128)(2,1)S(1)}, bf16[256,256]{1,0:T(8,128)(2,1)S(1)}, u32[]{:S(2)}, u32[]{:S(2)}) collective-permute-start(bf16[256,256]{1,0:T(8,128)(2,1)S(1)} %fusion), channel_id=1, source_target_pairs={{0,2},{1,3},{2,0},{3,1},{4,6},{5,7},{6,4},{7,5},{8,10},{9,11},{10,... | collective-permute-start | bytes 393224 | tf_op jit(solution)/shard_map/ppermute | solution.py:23
  77.0 15.9 %collective-permute-start.24 = (bf16[512,256]{1,0:T(8,128)(2,1)S(1)}, bf16[512,256]{1,0:T(8,128)(2,1)S(1)}, u32[]{:S(2)}, u32[]{:S(2)}) collective-permute-start(bf16[512,256]{1,0:T(8,128)(2,1)S(1)} %get-tuple-element.36), channel_id=1, source_target_pairs={{0,1},{1,0},{2,3},{3,2},{4,5},{5,4},{6,7},{7,6},{8,9},{9,8},{10,11... | collective-permute-start | bytes 786440 | tf_op jit(solution)/shard_map/ppermute | solution.py:23
  80.4 6.9 %collective-permute-start.20 = (bf16[256,256]{1,0:T(8,128)(2,1)S(1)}, bf16[256,256]{1,0:T(8,128)(2,1)S(1)}, u32[]{:S(2)}, u32[]{:S(2)}) collective-permute-start(bf16[256,256]{1,0:T(8,128)(2,1)S(1)} %fusion.1), channel_id=1, source_target_pairs={{0,16},{4,20},{8,24},{12,28},{16,0},{20,4},{24,8},{28,12},{1,17},{... | collective-permute-start | bytes 393224 | tf_op jit(solution)/shard_map/ppermute | solution.py:23
  81.5 7.7 %collective-permute-start.27 = (bf16[256,256]{1,0:T(8,128)(2,1)S(1)}, bf16[256,256]{1,0:T(8,128)(2,1)S(1)}, u32[]{:S(2)}, u32[]{:S(2)}) collective-permute-start(bf16[256,256]{1,0:T(8,128)(2,1)S(1)} %fusion.1), channel_id=1, source_target_pairs={{0,2},{1,3},{2,0},{3,1},{4,6},{5,7},{6,4},{7,5},{8,10},{9,11},{10,... | collective-permute-start | bytes 393224 | tf_op jit(solution)/shard_map/ppermute | solution.py:23
  82.8 9.8 %collective-permute-start.26 = (bf16[512,256]{1,0:T(8,128)(2,1)S(1)}, bf16[512,256]{1,0:T(8,128)(2,1)S(1)}, u32[]{:S(2)}, u32[]{:S(2)}) collective-permute-start(bf16[512,256]{1,0:T(8,128)(2,1)S(1)} %get-tuple-element.32), channel_id=1, source_target_pairs={{0,1},{1,0},{2,3},{3,2},{4,5},{5,4},{6,7},{7,6},{8,9},{9,8},{10,11... | collective-permute-start | bytes 786440 | tf_op jit(solution)/shard_map/ppermute | solution.py:23
  87.5 5.0 %collective-permute-start.21 = (bf16[256,256]{1,0:T(8,128)(2,1)S(1)}, bf16[256,256]{1,0:T(8,128)(2,1)S(1)}, u32[]{:S(2)}, u32[]{:S(2)}) collective-permute-start(bf16[256,256]{1,0:T(8,128)(2,1)S(1)} %fusion.2), channel_id=1, source_target_pairs={{0,2},{1,3},{2,0},{3,1},{4,6},{5,7},{6,4},{7,5},{8,10},{9,11},{10,... | collective-permute-start | bytes 393224 | tf_op jit(solution)/shard_map/ppermute | solution.py:23
  89.2 3.5 %collective-permute-start.28 = (bf16[512,256]{1,0:T(8,128)(2,1)S(1)}, bf16[512,256]{1,0:T(8,128)(2,1)S(1)}, u32[]{:S(2)}, u32[]{:S(2)}) collective-permute-start(bf16[512,256]{1,0:T(8,128)(2,1)S(1)} %get-tuple-element.28), channel_id=1, source_target_pairs={{0,1},{1,0},{2,3},{3,2},{4,5},{5,4},{6,7},{7,6},{8,9},{9,8},{10,11... | collective-permute-start | bytes 786440 | tf_op jit(solution)/shard_map/ppermute | solution.py:23
  92.6 1.6 %collective-permute-start.22 = (bf16[512,256]{1,0:T(8,128)(2,1)S(1)}, bf16[512,256]{1,0:T(8,128)(2,1)S(1)}, u32[]{:S(2)}, u32[]{:S(2)}) collective-permute-start(bf16[512,256]{1,0:T(8,128)(2,1)S(1)} %get-tuple-element.40), channel_id=1, source_target_pairs={{0,1},{1,0},{2,3},{3,2},{4,5},{5,4},{6,7},{7,6},{8,9},{9,8},{10,11... | collective-permute-start | bytes 786440 | tf_op jit(solution)/shard_map/ppermute | solution.py:23
  94.3 12.6 %copy-start = (bf16[2,512,256]{2,1,0:T(8,128)(2,1)}, bf16[2,512,256]{2,1,0:T(8,128)(2,1)S(1)}, u32[]{:S(2)}) copy-start(bf16[2,512,256]{2,1,0:T(8,128)(2,1)S(1)} %pad_maximum_fusion.4) | copy-start | bytes 1572868

commit v5 on v4

--- a/solution.py
+++ b/solution.py
@@ -127,14 +127,10 @@
 def sketch_kernel(mode, columns, starts, dots, plain, *refs):
     refs, out_ref = refs[:-1], refs[-1]
     total = 0.0
-    if dots:
-        mix_ref, refs = refs[0], refs[1:]
+    mixes, refs = refs[:dots], refs[dots:]
     views = [ref.at[:, start : start + columns] for ref, start in zip(refs, starts)]
-    first = 0
-    for points_ref in views[:dots]:
-        rows = points_ref.shape[0]
-        total += jnp.dot(mix_ref[:, first : first + rows], points_ref[...], preferred_element_type=f32)
-        first += rows
+    for mix_ref, points_ref in zip(mixes, views):
+        total += jnp.dot(mix_ref[...], points_ref[...], preferred_element_type=f32)
     for term in views[dots : dots + plain]:
         total += term[...]
     for codes in views[dots + plain :]:
@@ -152,11 +148,11 @@
         out_ref[...] = (total[: size // 2] * total[size // 2 :]).astype(bf16)
 
 
-def sketch(mode, columns, mix, points, plain, coded):
-    size = mix.shape[0]
+def sketch(mode, columns, mixes, points, plain, coded):
+    size = mixes[0].shape[0]
     rows, kind = {"code": (size + tag_rows, f32), "keep": (size, f32), "multiply": (size // 2, bf16)}[mode]
     terms = points + plain + coded
-    operands = ([mix] if points else []) + [array for array, _ in terms]
+    operands = mixes[: len(points)] + [array for array, _ in terms]
     starts = [start for _, start in terms]
     return pl.pallas_call(
         functools.partial(sketch_kernel, mode, columns, starts, len(points), len(plain)),
@@ -180,9 +176,6 @@
     kept = order.shape[1]
     width = orbitals.shape[1] // groups
 
-    orders = order[:1][None]
-    orders = jnp.concatenate([orders, exchange(orders, "grid", 1)], axis=1)
-
     parts = 2 if grid_bits > 1 else 1
     count = groups // 2 // parts
     places = [[reversed_bits(p * count + i, grid_bits - 1) for i in range(count)] for p in range(parts)]
@@ -197,14 +190,15 @@
     mixing = [jnp.stack([w_first.T, w_second.T])]
     for t in reversed(range(1, band_bits)):
         upper = place >> t & 1
-        send = [half_of(m, 1 - upper) for m in mixing]
-        orders, send = lax.optimization_barrier((orders, send))
-        mixing = [half_of(m, upper) for m in mixing] + [exchange(m, "band", 1 << t) for m in send]
+        got = [exchange(half_of(m, 1 - upper), "band", 1 << t) for m in mixing]
+        mixing = [half_of(m, upper) for m in mixing] + got
     near = mixing[0]
+
+    orders = order[:1]
     for t in reversed(range(1, grid_bits)):
-        orders = jnp.stack([orders, exchange(orders, "grid", 1 << t)], axis=1).reshape((-1,) + orders.shape[1:])
-        if t == grid_bits - 1:
-            orders, near = lax.optimization_barrier((orders, near))
+        if t == 1:
+            orders, raw, near, mixing = lax.optimization_barrier((orders, raw, near, mixing))
+        orders = jnp.stack([orders, exchange(orders, "grid", 1 << t)], axis=1).reshape(-1, kept)
     near = [near] + mixing[1:]
     near = [exchange(m, "grid", 1) for m in near]
 
@@ -214,28 +208,28 @@
             blocks = blocks + [exchange(m, "band", 1 << t) for m in blocks]
         return blocks
 
-    def lists_of(p, side):
-        return [orders[k, side] for k in places[p]]
+    def lists_of(p):
+        return jnp.stack([orders[k] for k in places[p]])
 
     gathered = {}
     for p in reversed(range(parts)):
-        own = over_bands(pick(blocks_of(p, 0), lists_of(p, 0)))
+        listed = lists_of(p)
+        own = over_bands(pick(blocks_of(p, 0), listed))
         if p == parts - 1:
-            far = pick([raw[:, i * width : (i + 1) * width] for i in range(count)], lists_of(p, 0))
+            far = pick([raw[:, i * width : (i + 1) * width] for i in range(count)], listed)
             orders, far = lax.optimization_barrier((orders, far))
         else:
-            far = exchange(pick(blocks_of(p, 1), lists_of(p, 1)), "grid", 1)
+            far = exchange(pick(blocks_of(p, 1), exchange(listed, "grid", 1)), "grid", 1)
         rows = jnp.concatenate(own + over_bands(far), axis=0)
         gathered[p] = [rows, exchange(rows, "band", 1)]
 
     mixing = jnp.concatenate(mixing + near, axis=2)
     mixes = [half_of(mixing, place & 1), exchange(half_of(mixing, 1 - (place & 1)), "band", 1)]
-    mix = jnp.concatenate(mixes, axis=2)
-    mix = mix.reshape(-1, mix.shape[2])
+    mixes = [m.reshape(-1, m.shape[2]) for m in mixes]
 
     def swap(block, bit):
         columns, points, codes = block
-        new = sketch("code", columns, mix, points, [], codes).astype(f16)
+        new = sketch("code", columns, mixes, points, [], codes).astype(f16)
         return exchange(new, "grid", 1 << bit).astype(f32), 0
 
     stay = [count * kept, [(rows, 0) for rows in gathered[0]], []]
@@ -246,10 +240,10 @@
             stay, go = [
                 [columns, points, codes + [new]] for (columns, points, codes), new in zip(halves(stay), reversed(got))
             ]
-        held = sketch("keep", kept, mix, stay[1], [], stay[2])
-        chosen = sketch("multiply", kept, mix, [], [(held, 0)], [swap(go, grid_bits - 1)])
+        held = sketch("keep", kept, mixes, stay[1], [], stay[2])
+        chosen = sketch("multiply", kept, mixes, [], [(held, 0)], [swap(go, grid_bits - 1)])
     else:
-        chosen = sketch("multiply", kept, mix, stay[1], [], [])
+        chosen = sketch("multiply", kept, mixes, stay[1], [], [])
 
     def over_band(block):
         for t in reversed(range(band_bits)):

time: 107 us -> 107 us (level)
  local copies, waits for them, and re-layouts: 1.61 us -> 8.93 us
  waiting for transfers between devices: 50.2 us -> 45.2 us
  other arithmetic: 4.05 us -> 0.98 us
    ppermute x29, waiting for transfers between devices: 50.2 us -> 45.2 us  [exchange(): return lax.ppermute(block, axis, [(i, i ^ delta) for i in range(count)])]
    unnamed x4 -> x13, local copies, waits for them, and re-layouts: 0.01 us -> 3.64 us
    dynamic_slice x1 -> x2, local copies, waits for them, and re-layouts: 0.08 us -> 2.27 us  [half_of(): return lax.dynamic_slice_in_dim(block, upper * size, size, axis=1)]
    ppermute x0 -> x1, local copies, waits for them, and re-layouts: none -> 1.25 us  [exchange(): return lax.ppermute(block, axis, [(i, i ^ delta) for i in range(count)])]
    concatenate x3 -> x0, other arithmetic: 1.16 us -> none  [the longest x1 1.08 us: local(): mix = jnp.concatenate(mixes, axis=2)]
    another operation x1, other arithmetic: 1.13 us -> 0.04 us  [local(): mixing = [jnp.stack([w_first.T, w_second.T])]]
  transfers between devices with their start and end apart: 29 -> 29, of which waited for: 16 -> 14; matrix products, arithmetic and copies ran while one was open for 7% -> 9% of each run, Pallas kernels for 2% -> 2%
where the time goes in v5:
time: 107 us
  waiting for transfers between devices  45.2 us (42%)
  starting transfers between devices  32.2 us (30%)
  Pallas kernels  14.9 us (14%)
  local copies, waits for them, and re-layouts  8.93 us (8%)
  matrix products  3.17 us (3%)
  between operations  1.14 us (1%)
    ppermute x29, waiting for transfers between devices, exchange(): return lax.ppermute(block, axis, [(i, i ^ delta) for i in range(count)])  45.2 us
    ppermute x29, starting transfers between devices, exchange(): return lax.ppermute(block, axis, [(i, i ^ delta) for i in range(count)])  32.2 us
    pallas_call x1, Pallas kernels, log_pivots(): pl.pallas_call(functools.partial(pivots_kernel, sets), out_shape=jax.Shap...  12.6 us
    unnamed x13, local copies, waits for them, and re-layouts  3.64 us
    pallas_call x5, Pallas kernels, sketch(): pl.pallas_call(functools.partial(sketch_kernel, mode, columns, starts, le...  2.31 us
    dynamic_slice x2, local copies, waits for them, and re-layouts, half_of(): return lax.dynamic_slice_in_dim(block, upper * size, size, axis=1)  2.27 us
  transfers between devices with their start and end apart: 29, of which 14 were waited for; matrix products, arithmetic and copies ran while one was open for 9% of the time, Pallas kernels for 2%

profile of v5, /device:TPU:0, one launch (start us, length us, event | category | flops | bytes accessed | tf_op | source)
XLA Modules:
  0.0 106.5 jit_solution(5867877726154099542)
XLA Ops:
  0.6 1.0 constant_dynamic-slice_fusion.3
  1.7 3.0 %collective-permute-start.1 = (bf16[128,1024]{1,0:T(8,128)(2,1)S(1)}, bf16[128,1024]{1,0:T(8,128)(2,1)S(1)}, u32[]{:S(2)}, u32[]{:S(2)}) collective-permute-start(bf16[128,1024]{1,0:T(8,128)(2,1)S(1)} %pad_maximum_fusion.6), channel_id=1, source_target_pairs={{0,4},{4,0},{8,12},{12,8},{16,20},{20,16},{24,28},{28,24},{1,5},{5... | collective-permute-start | bytes 786440 | tf_op jit(solution)/shard_map/ppermute | solution.py:23
  4.8 1.6 %collective-permute-start.2 = (bf16[2,512,128]{1,2,0:T(8,128)(2,1)S(1)}, bf16[2,512,128]{1,2,0:T(8,128)(2,1)S(1)}, u32[]{:S(2)}, u32[]{:S(2)}) collective-permute-start(bf16[2,512,128]{1,2,0:T(8,128)(2,1)S(1)} %get-tuple-element.28), channel_id=1, source_target_pairs={{0,2},{1,3},{2,0},{3,1},{4,6},{5,7},{6,4},{7,5},{8,10},{9,11},{10,... | collective-permute-start | bytes 786440 | tf_op jit(solution)/shard_map/ppermute | solution.py:23
  6.3 0.7 copy-done.4
  7.0 2.7 %collective-permute-start = (s32[1,256]{1,0:T(1,128)S(1)}, s32[1,256]{1,0:T(1,128)S(1)}, u32[]{:S(2)}, u32[]{:S(2)}) collective-permute-start(s32[1,256]{1,0:T(1,128)S(1)} %get-tuple-element.47), channel_id=1, source_target_pairs={{0,16},{4,20},{8,24},{12,28},{16,0},{20,4},{24,8},{28,12},{1,17},{... | collective-permute-start | bytes 3080 | tf_op jit(solution)/shard_map/ppermute | solution.py:23
  9.7 1.9 %collective-permute-done = s32[1,256]{1,0:T(1,128)S(1)} collective-permute-done((s32[1,256]{1,0:T(1,128)S(1)}, s32[1,256]{1,0:T(1,128)S(1)}, u32[]{:S(2)}, u32[]{:S(2)}) %collective-permute-start) | collective-permute-done | bytes 1056 | tf_op jit(solution)/shard_map/ppermute | solution.py:23
  11.6 1.0 collective-permute-done.2
  12.6 0.8 constant_dynamic-update-slice_fusion.3
  13.4 1.2 %collective-permute-start.4 = (bf16[2,512,128]{1,2,0:T(8,128)(2,1)S(1)}, bf16[2,512,128]{1,2,0:T(8,128)(2,1)S(1)}, u32[]{:S(2)}, u32[]{:S(2)}) collective-permute-start(bf16[2,512,128]{1,2,0:T(8,128)(2,1)S(1)} %collective-permute-done.2), channel_id=1, source_target_pairs={{0,4},{4,0},{8,12},{12,8},{16,20},{20,16},{24,28},{28,24},{1,5},{5... | collective-permute-start | bytes 786440 | tf_op jit(solution)/shard_map/ppermute | solution.py:23
  14.5 1.6 %collective-permute-start.6 = (s32[2,256]{1,0:T(2,128)S(1)}, s32[2,256]{1,0:T(2,128)S(1)}, u32[]{:S(2)}, u32[]{:S(2)}) collective-permute-start(s32[2,256]{1,0:T(2,128)S(1)} %add_bitcast_fusion), channel_id=1, source_target_pairs={{0,8},{4,12},{8,0},{12,4},{16,24},{20,28},{24,16},{28,20},{1,9},{5... | collective-permute-start | bytes 6152 | tf_op jit(solution)/shard_map/ppermute | solution.py:23
  16.1 0.7 constant_dynamic-update-slice_fusion.2
  16.8 0.8 collective-permute-start.3
  18.7 0.9 collective-permute-start.8
  19.6 1.5 %collective-permute-start.13 = (bf16[128,512]{1,0:T(8,128)(2,1)S(1)}, bf16[128,512]{1,0:T(8,128)(2,1)S(1)}, u32[]{:S(2)}, u32[]{:S(2)}) collective-permute-start(bf16[128,512]{1,0:T(8,128)(2,1)S(1)} %pad_maximum_fusion.11), channel_id=1, source_target_pairs={{0,2},{1,3},{2,0},{3,1},{4,6},{5,7},{6,4},{7,5},{8,10},{9,11},{10,... | collective-permute-start | bytes 393224 | tf_op jit(solution)/shard_map/ppermute | solution.py:23
  21.6 0.6 collective-permute-start.12
  22.8 3.1 %collective-permute-done.8 = s32[2,256]{1,0:T(2,128)S(1)} collective-permute-done((s32[2,256]{1,0:T(2,128)S(1)}, s32[2,256]{1,0:T(2,128)S(1)}, u32[]{:S(2)}, u32[]{:S(2)}) %collective-permute-start.8) | collective-permute-done | bytes 2080 | tf_op jit(solution)/shard_map/ppermute | solution.py:23
  26.4 1.6 %collective-permute-start.9 = (bf16[128,512]{1,0:T(8,128)(2,1)S(1)}, bf16[128,512]{1,0:T(8,128)(2,1)S(1)}, u32[]{:S(2)}, u32[]{:S(2)}) collective-permute-start(bf16[128,512]{1,0:T(8,128)(2,1)S(1)} %pad_maximum_fusion.13), channel_id=1, source_target_pairs={{0,4},{4,0},{8,12},{12,8},{16,20},{20,16},{24,28},{28,24},{1,5},{5... | collective-permute-start | bytes 393224 | tf_op jit(solution)/shard_map/ppermute | solution.py:23
  28.1 0.7 constant_dynamic-update-slice_fusion.1
  28.9 0.7 constant_dynamic-update-slice_fusion
  29.6 2.1 %constant_dynamic-slice_fusion = (bf16[2,256,512]{1,2,0:T(8,128)(2,1)}, bf16[2,256,512]{1,2,0:T(8,128)(2,1)S(1)}) fusion(bf16[2,512,512]{1,2,0:T(8,128)(2,1)} %constant_dynamic-update-slice_fusion, s32[]{:T(128)S(6)} %select_n.139, s32[]{:T(128)S(6)} %select_n.138), kind=kLoop, calls=%fused_computation.99 | loop fusion | bytes 2097160 | tf_op jit(solution)/shard_map/dynamic_slice | solution.py:124
  32.1 1.6 %collective-permute-start.7 = (bf16[128,512]{1,0:T(8,128)(2,1)S(1)}, bf16[128,512]{1,0:T(8,128)(2,1)S(1)}, u32[]{:S(2)}, u32[]{:S(2)}) collective-permute-start(bf16[128,512]{1,0:T(8,128)(2,1)S(1)} %pad_maximum_fusion.12), channel_id=1, source_target_pairs={{0,2},{1,3},{2,0},{3,1},{4,6},{5,7},{6,4},{7,5},{8,10},{9,11},{10,... | collective-permute-start | bytes 393224 | tf_op jit(solution)/shard_map/ppermute | solution.py:23
  33.7 0.5 collective-permute-start.10
  34.2 4.3 %collective-permute-done.7 = bf16[128,512]{1,0:T(8,128)(2,1)S(1)} collective-permute-done((bf16[128,512]{1,0:T(8,128)(2,1)S(1)}, bf16[128,512]{1,0:T(8,128)(2,1)S(1)}, u32[]{:S(2)}, u32[]{:S(2)}) %collective-permute-start.7) | collective-permute-done | bytes 131104 | tf_op jit(solution)/shard_map/ppermute | solution.py:23
  38.6 1.9 %collective-permute-done.10 = bf16[128,512]{1,0:T(8,128)(2,1)S(1)} collective-permute-done((bf16[128,512]{1,0:T(8,128)(2,1)S(1)}, bf16[128,512]{1,0:T(8,128)(2,1)S(1)}, u32[]{:S(2)}, u32[]{:S(2)}) %collective-permute-start.10) | collective-permute-done | bytes 131104 | tf_op jit(solution)/shard_map/ppermute | solution.py:23
  40.8 1.3 %copy.9 = bf16[2,256,512]{2,1,0:T(8,128)(2,1)S(1)} copy(bf16[2,256,512]{1,2,0:T(8,128)(2,1)} %collective-permute-done.5) | data formatting | bytes 1048576 | tf_op jit(solution)/shard_map/ppermute | solution.py:23
  42.0 0.6 shard_map.61
  42.7 1.6 %collective-permute-start.16 = (f16[528,256]{1,0:T(8,128)(2,1)S(1)}, f16[528,256]{1,0:T(8,128)(2,1)S(1)}, u32[]{:S(2)}, u32[]{:S(2)}) collective-permute-start(f16[528,256]{1,0:T(8,128)(2,1)S(1)} %convert_element_type.75), channel_id=1, source_target_pairs={{0,8},{4,12},{8,0},{12,4},{16,24},{20,28},{24,16},{28,20},{1,9},{5... | collective-permute-start | bytes 811016 | tf_op jit(solution)/shard_map/ppermute | solution.py:23
  44.4 0.6 shard_map.59
  45.0 0.5 collective-permute-start.15
  45.5 6.5 %collective-permute-done.16 = f16[528,256]{1,0:T(8,128)(2,1)S(1)} collective-permute-done((f16[528,256]{1,0:T(8,128)(2,1)S(1)}, f16[528,256]{1,0:T(8,128)(2,1)S(1)}, u32[]{:S(2)}, u32[]{:S(2)}) %collective-permute-start.16) | collective-permute-done | bytes 270368 | tf_op jit(solution)/shard_map/ppermute | solution.py:23
  52.1 0.6 shard_map.62
  52.8 2.7 %collective-permute-start.17 = (f16[528,256]{1,0:T(8,128)(2,1)S(1)}, f16[528,256]{1,0:T(8,128)(2,1)S(1)}, u32[]{:S(2)}, u32[]{:S(2)}) collective-permute-start(f16[528,256]{1,0:T(8,128)(2,1)S(1)} %convert_element_type.77), channel_id=1, source_target_pairs={{0,16},{4,20},{8,24},{12,28},{16,0},{20,4},{24,8},{28,12},{1,17},{... | collective-permute-start | bytes 811016 | tf_op jit(solution)/shard_map/ppermute | solution.py:23
  55.4 5.9 %collective-permute-done.15 = f16[528,256]{1,0:T(8,128)(2,1)S(1)} collective-permute-done((f16[528,256]{1,0:T(8,128)(2,1)S(1)}, f16[528,256]{1,0:T(8,128)(2,1)S(1)}, u32[]{:S(2)}, u32[]{:S(2)}) %collective-permute-start.15) | collective-permute-done | bytes 270368 | tf_op jit(solution)/shard_map/ppermute | solution.py:23
  61.8 5.4 %collective-permute-done.17 = f16[528,256]{1,0:T(8,128)(2,1)S(1)} collective-permute-done((f16[528,256]{1,0:T(8,128)(2,1)S(1)}, f16[528,256]{1,0:T(8,128)(2,1)S(1)}, u32[]{:S(2)}, u32[]{:S(2)}) %collective-permute-start.17) | collective-permute-done | bytes 270368 | tf_op jit(solution)/shard_map/ppermute | solution.py:23
  67.4 0.6 collective-permute-start.18
  68.0 1.5 %collective-permute-start.23 = (bf16[256,256]{1,0:T(8,128)(2,1)S(1)}, bf16[256,256]{1,0:T(8,128)(2,1)S(1)}, u32[]{:S(2)}, u32[]{:S(2)}) collective-permute-start(bf16[256,256]{1,0:T(8,128)(2,1)S(1)} %shard_map.63), channel_id=1, source_target_pairs={{0,2},{1,3},{2,0},{3,1},{4,6},{5,7},{6,4},{7,5},{8,10},{9,11},{10,... | collective-permute-start | bytes 393224 | tf_op jit(solution)/shard_map/ppermute | solution.py:23
  69.5 3.0 %collective-permute-done.18 = bf16[256,256]{1,0:T(8,128)(2,1)S(1)} collective-permute-done((bf16[256,256]{1,0:T(8,128)(2,1)S(1)}, bf16[256,256]{1,0:T(8,128)(2,1)S(1)}, u32[]{:S(2)}, u32[]{:S(2)}) %collective-permute-start.18) | collective-permute-done | bytes 131104 | tf_op jit(solution)/shard_map/ppermute | solution.py:23
  72.8 0.9 collective-permute-start.19
  73.7 1.5 %collective-permute-start.25 = (bf16[256,256]{1,0:T(8,128)(2,1)S(1)}, bf16[256,256]{1,0:T(8,128)(2,1)S(1)}, u32[]{:S(2)}, u32[]{:S(2)}) collective-permute-start(bf16[256,256]{1,0:T(8,128)(2,1)S(1)} %fusion), channel_id=1, source_target_pairs={{0,2},{1,3},{2,0},{3,1},{4,6},{5,7},{6,4},{7,5},{8,10},{9,11},{10,... | collective-permute-start | bytes 393224 | tf_op jit(solution)/shard_map/ppermute | solution.py:23
  75.5 2.3 %collective-permute-done.19 = bf16[256,256]{1,0:T(8,128)(2,1)S(1)} collective-permute-done((bf16[256,256]{1,0:T(8,128)(2,1)S(1)}, bf16[256,256]{1,0:T(8,128)(2,1)S(1)}, u32[]{:S(2)}, u32[]{:S(2)}) %collective-permute-start.19) | collective-permute-done | bytes 131104 | tf_op jit(solution)/shard_map/ppermute | solution.py:23
  78.1 2.2 %collective-permute-start.20 = (bf16[256,256]{1,0:T(8,128)(2,1)S(1)}, bf16[256,256]{1,0:T(8,128)(2,1)S(1)}, u32[]{:S(2)}, u32[]{:S(2)}) collective-permute-start(bf16[256,256]{1,0:T(8,128)(2,1)S(1)} %fusion.1), channel_id=1, source_target_pairs={{0,16},{4,20},{8,24},{12,28},{16,0},{20,4},{24,8},{28,12},{1,17},{... | collective-permute-start | bytes 393224 | tf_op jit(solution)/shard_map/ppermute | solution.py:23
  80.3 1.5 %collective-permute-start.27 = (bf16[256,256]{1,0:T(8,128)(2,1)S(1)}, bf16[256,256]{1,0:T(8,128)(2,1)S(1)}, u32[]{:S(2)}, u32[]{:S(2)}) collective-permute-start(bf16[256,256]{1,0:T(8,128)(2,1)S(1)} %fusion.1), channel_id=1, source_target_pairs={{0,2},{1,3},{2,0},{3,1},{4,6},{5,7},{6,4},{7,5},{8,10},{9,11},{10,... | collective-permute-start | bytes 393224 | tf_op jit(solution)/shard_map/ppermute | solution.py:23
  82.1 4.0 %collective-permute-done.20 = bf16[256,256]{1,0:T(8,128)(2,1)S(1)} collective-permute-done((bf16[256,256]{1,0:T(8,128)(2,1)S(1)}, bf16[256,256]{1,0:T(8,128)(2,1)S(1)}, u32[]{:S(2)}, u32[]{:S(2)}) %collective-permute-start.20) | collective-permute-done | bytes 131104 | tf_op jit(solution)/shard_map/ppermute | solution.py:23
  86.3 0.9 collective-permute-start.21
  87.3 4.0 %collective-permute-done.21 = bf16[256,256]{1,0:T(8,128)(2,1)S(1)} collective-permute-done((bf16[256,256]{1,0:T(8,128)(2,1)S(1)}, bf16[256,256]{1,0:T(8,128)(2,1)S(1)}, u32[]{:S(2)}, u32[]{:S(2)}) %collective-permute-start.21) | collective-permute-done | bytes 131104 | tf_op jit(solution)/shard_map/ppermute | solution.py:23
  91.7 1.3 %collective-permute-done.22 = bf16[512,256]{1,0:T(8,128)(2,1)S(1)} collective-permute-done((bf16[512,256]{1,0:T(8,128)(2,1)S(1)}, bf16[512,256]{1,0:T(8,128)(2,1)S(1)}, u32[]{:S(2)}, u32[]{:S(2)}) %collective-permute-start.22) | collective-permute-done | bytes 262176 | tf_op jit(solution)/shard_map/ppermute | solution.py:23
  93.2 0.7 copy-done
  93.9 12.6 %shard_map.64 = f32[1,256]{1,0:T(1,128)} custom-call(bf16[1024,256]{1,0:T(8,128)(2,1)S(1)} %bitcast.81, bf16[1024,256]{1,0:T(8,128)(2,1)S(1)} %bitcast.77, bf16[1024,256]{1,0:T(8,128)(2,1)S(1)} %bitcast.78, bf16[1024,256]{1,0:T(8,128)(2,1)S(1)} %bitcast.79), custom_call_target="tpu_custom_call" | custom-call | tf_op jit(solution)/shard_map/pallas_call | solution.py:112
  (85 shorter events, 6.3 us)
Async XLA Ops:
  1.6 3.1 %copy-start.1 = (bf16[128,1024]{1,0:T(8,128)(2,1)S(1)}, bf16[128,1024]{1,0:T(8,128)(2,1)}, u32[]{:S(2)}) copy-start(bf16[128,1024]{1,0:T(8,128)(2,1)} %param.5) | copy-start | bytes 786436
  1.7 3.1 %copy-start.2 = (bf16[128,1024]{1,0:T(8,128)(2,1)S(1)}, bf16[128,1024]{1,0:T(8,128)(2,1)}, u32[]{:S(2)}) copy-start(bf16[128,1024]{1,0:T(8,128)(2,1)} %param.6) | copy-start | bytes 786436
  1.7 9.9 %collective-permute-start.1 = (bf16[128,1024]{1,0:T(8,128)(2,1)S(1)}, bf16[128,1024]{1,0:T(8,128)(2,1)S(1)}, u32[]{:S(2)}, u32[]{:S(2)}) collective-permute-start(bf16[128,1024]{1,0:T(8,128)(2,1)S(1)} %pad_maximum_fusion.6), channel_id=1, source_target_pairs={{0,4},{4,0},{8,12},{12,8},{16,20},{20,16},{24,28},{28,24},{1,5},{5... | collective-permute-start | bytes 786440 | tf_op jit(solution)/shard_map/ppermute | solution.py:23
  4.8 7.8 %collective-permute-start.2 = (bf16[2,512,128]{1,2,0:T(8,128)(2,1)S(1)}, bf16[2,512,128]{1,2,0:T(8,128)(2,1)S(1)}, u32[]{:S(2)}, u32[]{:S(2)}) collective-permute-start(bf16[2,512,128]{1,2,0:T(8,128)(2,1)S(1)} %get-tuple-element.28), channel_id=1, source_target_pairs={{0,2},{1,3},{2,0},{3,1},{4,6},{5,7},{6,4},{7,5},{8,10},{9,11},{10,... | collective-permute-start | bytes 786440 | tf_op jit(solution)/shard_map/ppermute | solution.py:23
  6.3 0.7 copy-start.4
  7.0 4.5 %collective-permute-start = (s32[1,256]{1,0:T(1,128)S(1)}, s32[1,256]{1,0:T(1,128)S(1)}, u32[]{:S(2)}, u32[]{:S(2)}) collective-permute-start(s32[1,256]{1,0:T(1,128)S(1)} %get-tuple-element.47), channel_id=1, source_target_pairs={{0,16},{4,20},{8,24},{12,28},{16,0},{20,4},{24,8},{28,12},{1,17},{... | collective-permute-start | bytes 3080 | tf_op jit(solution)/shard_map/ppermute | solution.py:23
  12.6 8.5 %copy-start.3 = (bf16[128,4096]{1,0:T(8,128)(2,1)S(1)}, bf16[128,4096]{1,0:T(8,128)(2,1)}, u32[]{:S(2)}) copy-start(bf16[128,4096]{1,0:T(8,128)(2,1)} %param.4) | copy-start | bytes 3145732
  13.4 15.5 %collective-permute-start.4 = (bf16[2,512,128]{1,2,0:T(8,128)(2,1)S(1)}, bf16[2,512,128]{1,2,0:T(8,128)(2,1)S(1)}, u32[]{:S(2)}, u32[]{:S(2)}) collective-permute-start(bf16[2,512,128]{1,2,0:T(8,128)(2,1)S(1)} %collective-permute-done.2), channel_id=1, source_target_pairs={{0,4},{4,0},{8,12},{12,8},{16,20},{20,16},{24,28},{28,24},{1,5},{5... | collective-permute-start | bytes 786440 | tf_op jit(solution)/shard_map/ppermute | solution.py:23
  14.5 3.6 %collective-permute-start.6 = (s32[2,256]{1,0:T(2,128)S(1)}, s32[2,256]{1,0:T(2,128)S(1)}, u32[]{:S(2)}, u32[]{:S(2)}) collective-permute-start(s32[2,256]{1,0:T(2,128)S(1)} %add_bitcast_fusion), channel_id=1, source_target_pairs={{0,8},{4,12},{8,0},{12,4},{16,24},{20,28},{24,16},{28,20},{1,9},{5... | collective-permute-start | bytes 6152 | tf_op jit(solution)/shard_map/ppermute | solution.py:23
  16.8 11.3 %collective-permute-start.3 = (bf16[2,512,128]{1,2,0:T(8,128)(2,1)S(1)}, bf16[2,512,128]{1,2,0:T(8,128)(2,1)S(1)}, u32[]{:S(2)}, u32[]{:S(2)}) collective-permute-start(bf16[2,512,128]{1,2,0:T(8,128)(2,1)S(1)} %get-tuple-element.11), channel_id=1, source_target_pairs={{0,4},{4,0},{8,12},{12,8},{16,20},{20,16},{24,28},{28,24},{1,5},{5... | collective-permute-start | bytes 786440 | tf_op jit(solution)/shard_map/ppermute | solution.py:23
  18.7 7.2 %collective-permute-start.8 = (s32[2,256]{1,0:T(2,128)S(1)}, s32[2,256]{1,0:T(2,128)S(1)}, u32[]{:S(2)}, u32[]{:S(2)}) collective-permute-start(s32[2,256]{1,0:T(2,128)S(1)} %pad_add_fusion.1), channel_id=1, source_target_pairs={{0,4},{4,0},{8,12},{12,8},{16,20},{20,16},{24,28},{28,24},{1,5},{5... | collective-permute-start | bytes 6152 | tf_op jit(solution)/shard_map/ppermute | solution.py:23
  19.6 8.4 %collective-permute-start.13 = (bf16[128,512]{1,0:T(8,128)(2,1)S(1)}, bf16[128,512]{1,0:T(8,128)(2,1)S(1)}, u32[]{:S(2)}, u32[]{:S(2)}) collective-permute-start(bf16[128,512]{1,0:T(8,128)(2,1)S(1)} %pad_maximum_fusion.11), channel_id=1, source_target_pairs={{0,2},{1,3},{2,0},{3,1},{4,6},{5,7},{6,4},{7,5},{8,10},{9,11},{10,... | collective-permute-start | bytes 393224 | tf_op jit(solution)/shard_map/ppermute | solution.py:23
  21.6 6.3 %collective-permute-start.12 = (bf16[128,512]{1,0:T(8,128)(2,1)S(1)}, bf16[128,512]{1,0:T(8,128)(2,1)S(1)}, u32[]{:S(2)}, u32[]{:S(2)}) collective-permute-start(bf16[128,512]{1,0:T(8,128)(2,1)S(1)} %pad_maximum_fusion.14), channel_id=1, source_target_pairs={{0,2},{1,3},{2,0},{3,1},{4,6},{5,7},{6,4},{7,5},{8,10},{9,11},{10,... | collective-permute-start | bytes 393224 | tf_op jit(solution)/shard_map/ppermute | solution.py:23
  26.4 7.3 %collective-permute-start.9 = (bf16[128,512]{1,0:T(8,128)(2,1)S(1)}, bf16[128,512]{1,0:T(8,128)(2,1)S(1)}, u32[]{:S(2)}, u32[]{:S(2)}) collective-permute-start(bf16[128,512]{1,0:T(8,128)(2,1)S(1)} %pad_maximum_fusion.13), channel_id=1, source_target_pairs={{0,4},{4,0},{8,12},{12,8},{16,20},{20,16},{24,28},{28,24},{1,5},{5... | collective-permute-start | bytes 393224 | tf_op jit(solution)/shard_map/ppermute | solution.py:23
  28.0 14.0 %collective-permute-start.14 = (bf16[512,512]{1,0:T(8,128)(2,1)S(1)}, bf16[512,512]{1,0:T(8,128)(2,1)S(1)}, u32[]{:S(2)}, u32[]{:S(2)}) collective-permute-start(bf16[512,512]{1,0:T(8,128)(2,1)S(1)} %pad_maximum_fusion.1.refs_2_), channel_id=1, source_target_pairs={{0,1},{1,0},{2,3},{3,2},{4,5},{5,4},{6,7},{7,6},{8,9},{9,8},{10,11... | collective-permute-start | bytes 1572872 | tf_op jit(solution)/shard_map/ppermute | solution.py:23
  31.6 9.1 %collective-permute-start.5 = (bf16[2,256,512]{1,2,0:T(8,128)(2,1)}, bf16[2,256,512]{1,2,0:T(8,128)(2,1)}, u32[]{:S(2)}, u32[]{:S(2)}) collective-permute-start(bf16[2,256,512]{1,2,0:T(8,128)(2,1)} %get-tuple-element.16), channel_id=1, source_target_pairs={{0,1},{1,0},{2,3},{3,2},{4,5},{5,4},{6,7},{7,6},{8,9},{9,8},{10,11... | collective-permute-start | bytes 1572872 | tf_op jit(solution)/shard_map/ppermute | solution.py:23
  32.1 6.4 %collective-permute-start.7 = (bf16[128,512]{1,0:T(8,128)(2,1)S(1)}, bf16[128,512]{1,0:T(8,128)(2,1)S(1)}, u32[]{:S(2)}, u32[]{:S(2)}) collective-permute-start(bf16[128,512]{1,0:T(8,128)(2,1)S(1)} %pad_maximum_fusion.12), channel_id=1, source_target_pairs={{0,2},{1,3},{2,0},{3,1},{4,6},{5,7},{6,4},{7,5},{8,10},{9,11},{10,... | collective-permute-start | bytes 393224 | tf_op jit(solution)/shard_map/ppermute | solution.py:23
  33.7 6.7 %collective-permute-start.10 = (bf16[128,512]{1,0:T(8,128)(2,1)S(1)}, bf16[128,512]{1,0:T(8,128)(2,1)S(1)}, u32[]{:S(2)}, u32[]{:S(2)}) collective-permute-start(bf16[128,512]{1,0:T(8,128)(2,1)S(1)} %collective-permute-done.9), channel_id=1, source_target_pairs={{0,2},{1,3},{2,0},{3,1},{4,6},{5,7},{6,4},{7,5},{8,10},{9,11},{10,... | collective-permute-start | bytes 393224 | tf_op jit(solution)/shard_map/ppermute | solution.py:23
  40.5 11.6 %collective-permute-start.11 = (bf16[512,512]{1,0:T(8,128)(2,1)S(1)}, bf16[512,512]{1,0:T(8,128)(2,1)S(1)}, u32[]{:S(2)}, u32[]{:S(2)}) collective-permute-start(bf16[512,512]{1,0:T(8,128)(2,1)S(1)} %pad_maximum_fusion.refs_2_), channel_id=1, source_target_pairs={{0,1},{1,0},{2,3},{3,2},{4,5},{5,4},{6,7},{7,6},{8,9},{9,8},{10,11... | collective-permute-start | bytes 1572872 | tf_op jit(solution)/shard_map/ppermute | solution.py:23
  42.7 9.3 %collective-permute-start.16 = (f16[528,256]{1,0:T(8,128)(2,1)S(1)}, f16[528,256]{1,0:T(8,128)(2,1)S(1)}, u32[]{:S(2)}, u32[]{:S(2)}) collective-permute-start(f16[528,256]{1,0:T(8,128)(2,1)S(1)} %convert_element_type.75), channel_id=1, source_target_pairs={{0,8},{4,12},{8,0},{12,4},{16,24},{20,28},{24,16},{28,20},{1,9},{5... | collective-permute-start | bytes 811016 | tf_op jit(solution)/shard_map/ppermute | solution.py:23
  45.0 16.3 %collective-permute-start.15 = (f16[528,256]{1,0:T(8,128)(2,1)S(1)}, f16[528,256]{1,0:T(8,128)(2,1)S(1)}, u32[]{:S(2)}, u32[]{:S(2)}) collective-permute-start(f16[528,256]{1,0:T(8,128)(2,1)S(1)} %convert_element_type.73), channel_id=1, source_target_pairs={{0,8},{4,12},{8,0},{12,4},{16,24},{20,28},{24,16},{28,20},{1,9},{5... | collective-permute-start | bytes 811016 | tf_op jit(solution)/shard_map/ppermute | solution.py:23
  52.8 14.5 %collective-permute-start.17 = (f16[528,256]{1,0:T(8,128)(2,1)S(1)}, f16[528,256]{1,0:T(8,128)(2,1)S(1)}, u32[]{:S(2)}, u32[]{:S(2)}) collective-permute-start(f16[528,256]{1,0:T(8,128)(2,1)S(1)} %convert_element_type.77), channel_id=1, source_target_pairs={{0,16},{4,20},{8,24},{12,28},{16,0},{20,4},{24,8},{28,12},{1,17},{... | collective-permute-start | bytes 811016 | tf_op jit(solution)/shard_map/ppermute | solution.py:23
  67.4 5.0 %collective-permute-start.18 = (bf16[256,256]{1,0:T(8,128)(2,1)S(1)}, bf16[256,256]{1,0:T(8,128)(2,1)S(1)}, u32[]{:S(2)}, u32[]{:S(2)}) collective-permute-start(bf16[256,256]{1,0:T(8,128)(2,1)S(1)} %shard_map.63), channel_id=1, source_target_pairs={{0,4},{4,0},{8,12},{12,8},{16,20},{20,16},{24,28},{28,24},{1,5},{5... | collective-permute-start | bytes 393224 | tf_op jit(solution)/shard_map/ppermute | solution.py:23
  68.0 7.2 %collective-permute-start.23 = (bf16[256,256]{1,0:T(8,128)(2,1)S(1)}, bf16[256,256]{1,0:T(8,128)(2,1)S(1)}, u32[]{:S(2)}, u32[]{:S(2)}) collective-permute-start(bf16[256,256]{1,0:T(8,128)(2,1)S(1)} %shard_map.63), channel_id=1, source_target_pairs={{0,2},{1,3},{2,0},{3,1},{4,6},{5,7},{6,4},{7,5},{8,10},{9,11},{10,... | collective-permute-start | bytes 393224 | tf_op jit(solution)/shard_map/ppermute | solution.py:23
  72.8 5.0 %collective-permute-start.19 = (bf16[256,256]{1,0:T(8,128)(2,1)S(1)}, bf16[256,256]{1,0:T(8,128)(2,1)S(1)}, u32[]{:S(2)}, u32[]{:S(2)}) collective-permute-start(bf16[256,256]{1,0:T(8,128)(2,1)S(1)} %fusion), channel_id=1, source_target_pairs={{0,8},{4,12},{8,0},{12,4},{16,24},{20,28},{24,16},{28,20},{1,9},{5... | collective-permute-start | bytes 393224 | tf_op jit(solution)/shard_map/ppermute | solution.py:23
  73.7 8.1 %collective-permute-start.25 = (bf16[256,256]{1,0:T(8,128)(2,1)S(1)}, bf16[256,256]{1,0:T(8,128)(2,1)S(1)}, u32[]{:S(2)}, u32[]{:S(2)}) collective-permute-start(bf16[256,256]{1,0:T(8,128)(2,1)S(1)} %fusion), channel_id=1, source_target_pairs={{0,2},{1,3},{2,0},{3,1},{4,6},{5,7},{6,4},{7,5},{8,10},{9,11},{10,... | collective-permute-start | bytes 393224 | tf_op jit(solution)/shard_map/ppermute | solution.py:23
  75.3 16.4 %collective-permute-start.24 = (bf16[512,256]{1,0:T(8,128)(2,1)S(1)}, bf16[512,256]{1,0:T(8,128)(2,1)S(1)}, u32[]{:S(2)}, u32[]{:S(2)}) collective-permute-start(bf16[512,256]{1,0:T(8,128)(2,1)S(1)} %get-tuple-element.38), channel_id=1, source_target_pairs={{0,1},{1,0},{2,3},{3,2},{4,5},{5,4},{6,7},{7,6},{8,9},{9,8},{10,11... | collective-permute-start | bytes 786440 | tf_op jit(solution)/shard_map/ppermute | solution.py:23
  78.1 8.0 %collective-permute-start.20 = (bf16[256,256]{1,0:T(8,128)(2,1)S(1)}, bf16[256,256]{1,0:T(8,128)(2,1)S(1)}, u32[]{:S(2)}, u32[]{:S(2)}) collective-permute-start(bf16[256,256]{1,0:T(8,128)(2,1)S(1)} %fusion.1), channel_id=1, source_target_pairs={{0,16},{4,20},{8,24},{12,28},{16,0},{20,4},{24,8},{28,12},{1,17},{... | collective-permute-start | bytes 393224 | tf_op jit(solution)/shard_map/ppermute | solution.py:23
  80.3 6.9 %collective-permute-start.27 = (bf16[256,256]{1,0:T(8,128)(2,1)S(1)}, bf16[256,256]{1,0:T(8,128)(2,1)S(1)}, u32[]{:S(2)}, u32[]{:S(2)}) collective-permute-start(bf16[256,256]{1,0:T(8,128)(2,1)S(1)} %fusion.1), channel_id=1, source_target_pairs={{0,2},{1,3},{2,0},{3,1},{4,6},{5,7},{6,4},{7,5},{8,10},{9,11},{10,... | collective-permute-start | bytes 393224 | tf_op jit(solution)/shard_map/ppermute | solution.py:23
  81.8 9.6 %collective-permute-start.26 = (bf16[512,256]{1,0:T(8,128)(2,1)S(1)}, bf16[512,256]{1,0:T(8,128)(2,1)S(1)}, u32[]{:S(2)}, u32[]{:S(2)}) collective-permute-start(bf16[512,256]{1,0:T(8,128)(2,1)S(1)} %get-tuple-element.34), channel_id=1, source_target_pairs={{0,1},{1,0},{2,3},{3,2},{4,5},{5,4},{6,7},{7,6},{8,9},{9,8},{10,11... | collective-permute-start | bytes 786440 | tf_op jit(solution)/shard_map/ppermute | solution.py:23
  86.3 5.0 %collective-permute-start.21 = (bf16[256,256]{1,0:T(8,128)(2,1)S(1)}, bf16[256,256]{1,0:T(8,128)(2,1)S(1)}, u32[]{:S(2)}, u32[]{:S(2)}) collective-permute-start(bf16[256,256]{1,0:T(8,128)(2,1)S(1)} %fusion.2), channel_id=1, source_target_pairs={{0,2},{1,3},{2,0},{3,1},{4,6},{5,7},{6,4},{7,5},{8,10},{9,11},{10,... | collective-permute-start | bytes 393224 | tf_op jit(solution)/shard_map/ppermute | solution.py:23
  87.3 4.2 %collective-permute-start.28 = (bf16[512,256]{1,0:T(8,128)(2,1)S(1)}, bf16[512,256]{1,0:T(8,128)(2,1)S(1)}, u32[]{:S(2)}, u32[]{:S(2)}) collective-permute-start(bf16[512,256]{1,0:T(8,128)(2,1)S(1)} %get-tuple-element.30), channel_id=1, source_target_pairs={{0,1},{1,0},{2,3},{3,2},{4,5},{5,4},{6,7},{7,6},{8,9},{9,8},{10,11... | collective-permute-start | bytes 786440 | tf_op jit(solution)/shard_map/ppermute | solution.py:23
  91.4 1.6 %collective-permute-start.22 = (bf16[512,256]{1,0:T(8,128)(2,1)S(1)}, bf16[512,256]{1,0:T(8,128)(2,1)S(1)}, u32[]{:S(2)}, u32[]{:S(2)}) collective-permute-start(bf16[512,256]{1,0:T(8,128)(2,1)S(1)} %get-tuple-element.42), channel_id=1, source_target_pairs={{0,1},{1,0},{2,3},{3,2},{4,5},{5,4},{6,7},{7,6},{8,9},{9,8},{10,11... | collective-permute-start | bytes 786440 | tf_op jit(solution)/shard_map/ppermute | solution.py:23
  93.1 0.8 copy-start

commit v6 on v5

--- a/solution.py
+++ b/solution.py
@@ -120,42 +120,56 @@
 
 
 def half_of(block, upper):
-    size = block.shape[1] // 2
-    return lax.dynamic_slice_in_dim(block, upper * size, size, axis=1)
-
-
-def sketch_kernel(mode, columns, starts, dots, plain, *refs):
+    size = block.shape[-1] // 2
+    return lax.dynamic_slice_in_dim(block, upper * size, size, axis=block.ndim - 1)
+
+
+def sketch_kernel(mode, which, columns, starts, dots, plain, coded, *refs):
     refs, out_ref = refs[:-1], refs[-1]
-    total = 0.0
     mixes, refs = refs[:dots], refs[dots:]
     views = [ref.at[:, start : start + columns] for ref, start in zip(refs, starts)]
-    for mix_ref, points_ref in zip(mixes, views):
-        total += jnp.dot(mix_ref[...], points_ref[...], preferred_element_type=f32)
-    for term in views[dots : dots + plain]:
-        total += term[...]
-    for codes in views[dots + plain :]:
-        size = codes.shape[0] - tag_rows
-        total += codes[:size, :] * jnp.exp2(codes[size : size + 1, :] - top)
-    size = total.shape[0]
+    points, terms, codes = views[:dots], views[dots : dots + plain], views[dots + plain :]
+    size = (out_ref.shape[0] - tag_rows) // len(which) if mode == "code" else out_ref.shape[0] // len(which)
+    size = out_ref.shape[0] if mode == "multiply" else size
+    totals = []
+    for i in which:
+        total = 0.0
+        for mix_ref, points_ref in zip(mixes, points):
+            total += lax.dot_general(mix_ref[i], points_ref[...], column_dims, preferred_element_type=f32)
+        for term in terms:
+            total += term[i * size : (i + 1) * size, :]
+        first = 0
+        for count in coded:
+            code = codes[first + i] if count > 1 else codes[first]
+            row = 0 if count > 1 else i * size
+            last = code.shape[0] - tag_rows
+            total += code[row : row + size, :] * jnp.exp2(code[last : last + 1, :] - top)
+            first += count
+        totals.append(total)
     if mode == "code":
-        largest = jnp.maximum(jnp.max(jnp.abs(total), axis=(0, 1), keepdims=True), f32(1e-30))
-        exponent = jnp.ceil(jnp.log2(largest))
-        out_ref[:size, :] = total * jnp.exp2(top - exponent)
-        out_ref[size:, :] = jnp.broadcast_to(exponent, (tag_rows, total.shape[1]))
+        largest = functools.reduce(jnp.maximum, [jnp.max(jnp.abs(t), axis=(0, 1), keepdims=True) for t in totals])
+        exponent = jnp.ceil(jnp.log2(jnp.maximum(largest, f32(1e-30))))
+        for j, total in enumerate(totals):
+            out_ref[j * size : (j + 1) * size, :] = total * jnp.exp2(top - exponent)
+        out_ref[len(which) * size :, :] = jnp.broadcast_to(exponent, (tag_rows, columns))
     elif mode == "keep":
-        out_ref[...] = total
+        for j, total in enumerate(totals):
+            out_ref[j * size : (j + 1) * size, :] = total
     else:
-        out_ref[...] = (total[: size // 2] * total[size // 2 :]).astype(bf16)
-
-
-def sketch(mode, columns, mixes, points, plain, coded):
-    size = mixes[0].shape[0]
-    rows, kind = {"code": (size + tag_rows, f32), "keep": (size, f32), "multiply": (size // 2, bf16)}[mode]
-    terms = points + plain + coded
-    operands = mixes[: len(points)] + [array for array, _ in terms]
+        out_ref[...] = (totals[0] * totals[1]).astype(bf16)
+
+
+def sketch(mode, which, block, mixes, plain=()):
+    columns, points, coded = block
+    size = mixes[0].shape[2]
+    shapes = {"code": (len(which) * size + tag_rows, f32), "keep": (len(which) * size, f32), "multiply": (size, bf16)}
+    rows, kind = shapes[mode]
+    terms = list(points) + list(plain) + [term for item in coded for term in item]
+    operands = list(mixes[: len(points)]) + [array for array, _ in terms]
     starts = [start for _, start in terms]
+    counts = [len(item) for item in coded]
     return pl.pallas_call(
-        functools.partial(sketch_kernel, mode, columns, starts, len(points), len(plain)),
+        functools.partial(sketch_kernel, mode, which, columns, starts, len(points), len(plain), counts),
         out_shape=jax.ShapeDtypeStruct((rows, columns), kind),
         in_specs=[pl.BlockSpec(memory_space=pltpu.VMEM)] * len(operands),
         out_specs=pl.BlockSpec(memory_space=pltpu.VMEM),
@@ -164,8 +178,12 @@
 
 
 def halves(block):
-    size = block[0] // 2
-    return [[size] + [[(a, first + shift) for a, first in terms] for terms in block[1:]] for shift in (0, size)]
+    columns, points, coded = block
+    size = columns // 2
+    return [
+        [size, [(a, first + shift) for a, first in points], [[(a, first + shift) for a, first in c] for c in coded]]
+        for shift in (0, size)
+    ]
 
 
 def local(orbitals, w_first, w_second, pivots):
@@ -187,7 +205,7 @@
 
     raw = exchange(jnp.concatenate(blocks_of(parts - 1, 1), axis=1), "grid", 1)
 
-    mixing = [jnp.stack([w_first.T, w_second.T])]
+    mixing = [jnp.stack([w_first, w_second])]
     for t in reversed(range(1, band_bits)):
         upper = place >> t & 1
         got = [exchange(half_of(m, 1 - upper), "band", 1 << t) for m in mixing]
@@ -211,39 +229,47 @@
     def lists_of(p):
         return jnp.stack([orders[k] for k in places[p]])
 
-    gathered = {}
+    def gather(own, far):
+        return jnp.concatenate(over_bands(own) + over_bands(far), axis=0)
+
+    def over_cores(rows):
+        return [(rows, 0), (exchange(rows, "band", 1), 0)]
+
+    def swap(block, bit, sets):
+        codes = [sketch("code", which, block, mixes).astype(f16) for which in sets]
+        return [exchange(code, "grid", 1 << bit) for code in codes]
+
+    picked = {}
     for p in reversed(range(parts)):
         listed = lists_of(p)
-        own = over_bands(pick(blocks_of(p, 0), listed))
+        own = pick(blocks_of(p, 0), listed)
         if p == parts - 1:
             far = pick([raw[:, i * width : (i + 1) * width] for i in range(count)], listed)
-            orders, far = lax.optimization_barrier((orders, far))
+            orders, own, far = lax.optimization_barrier((orders, own, far))
         else:
             far = exchange(pick(blocks_of(p, 1), exchange(listed, "grid", 1)), "grid", 1)
-        rows = jnp.concatenate(own + over_bands(far), axis=0)
-        gathered[p] = [rows, exchange(rows, "band", 1)]
-
-    mixing = jnp.concatenate(mixing + near, axis=2)
+        picked[p] = own, far
+
+    both, each = [(0, 1)], [(0,), (1,)]
+    go = [count * kept, over_cores(gather(*picked[parts - 1])), []]
+    mixing = jnp.concatenate(mixing + near, axis=1)
     mixes = [half_of(mixing, place & 1), exchange(half_of(mixing, 1 - (place & 1)), "band", 1)]
-    mixes = [m.reshape(-1, m.shape[2]) for m in mixes]
-
-    def swap(block, bit):
-        columns, points, codes = block
-        new = sketch("code", columns, mixes, points, [], codes).astype(f16)
-        return exchange(new, "grid", 1 << bit).astype(f32), 0
-
-    stay = [count * kept, [(rows, 0) for rows in gathered[0]], []]
     if parts > 1:
-        go = [count * kept, [(rows, 0) for rows in gathered[1]], []]
-        for t in range(1, grid_bits - 1):
-            got = [swap(block, t) for block in reversed(halves(go))]
-            stay, go = [
-                [columns, points, codes + [new]] for (columns, points, codes), new in zip(halves(stay), reversed(got))
-            ]
-        held = sketch("keep", kept, mixes, stay[1], [], stay[2])
-        chosen = sketch("multiply", kept, mixes, [], [(held, 0)], [swap(go, grid_bits - 1)])
+        stay = None
+        for t in range(1, grid_bits):
+            pieces = halves(go) if t < grid_bits - 1 else [go]
+            coded = [swap(piece, t, each if piece is pieces[-1] else both) for piece in reversed(pieces)]
+            if stay is None:
+                rows = gather(*picked[0])
+                coded[0], rows = lax.optimization_barrier((coded[0], rows))
+                stay = [count * kept, over_cores(rows), []]
+            got = [[(code.astype(f32), 0) for code in codes] for codes in reversed(coded)]
+            if len(pieces) > 1:
+                stay, go = [[n, points, codes + [new]] for (n, points, codes), new in zip(halves(stay), got)]
+        held = sketch("keep", (0, 1), stay, mixes)
+        chosen = sketch("multiply", (0, 1), [kept, [], got], mixes, [(held, 0)])
     else:
-        chosen = sketch("multiply", kept, mixes, stay[1], [], [])
+        chosen = sketch("multiply", (0, 1), go, mixes)
 
     def over_band(block):
         for t in reversed(range(band_bits)):

time: 107 us -> 98.2 us (0.918)
  local copies, waits for them, and re-layouts: 8.93 us -> 1.94 us
  waiting for transfers between devices: 45.2 us -> 43.3 us
    unnamed x13 -> x16, local copies, waits for them, and re-layouts: 3.64 us -> 0.8 us
    dynamic_slice x2 -> x1, local copies, waits for them, and re-layouts: 2.27 us -> 0.08 us  [half_of(): lax.dynamic_slice_in_dim(block, upper * size, size, axis=block.ndim - 1)]
    ppermute x29 -> x31, waiting for transfers between devices: 45.2 us -> 43.3 us  [exchange(): return lax.ppermute(block, axis, [(i, i ^ delta) for i in range(count)])]
    ppermute x1 -> x0, local copies, waits for them, and re-layouts: 1.25 us -> none  [exchange(): return lax.ppermute(block, axis, [(i, i ^ delta) for i in range(count)])]
    pallas_call x5 -> x7, Pallas kernels: 2.31 us -> 3.17 us  [sketch(): pl.pallas_call(functools.partial(sketch_kernel, mode, which, columns, sta...]
    ppermute x29 -> x31, starting transfers between devices: 32.2 us -> 31.8 us  [exchange(): return lax.ppermute(block, axis, [(i, i ^ delta) for i in range(count)])]
  transfers between devices with their start and end apart: 29 -> 31, of which waited for: 14 -> 16; matrix products, arithmetic and copies ran while one was open for 9% -> 4% of each run, Pallas kernels for 2% -> 3%
where the time goes in v6:
time: 98.2 us; the launch traced here: 98.1 us
  waiting for transfers between devices  43.3 us (44%)
  starting transfers between devices  31.8 us (32%)
  Pallas kernels  15.8 us (16%)
  matrix products  3.16 us (3%)
  local copies, waits for them, and re-layouts  1.94 us (2%)
  between operations  1.23 us (1%)
    ppermute x31, waiting for transfers between devices, exchange(): return lax.ppermute(block, axis, [(i, i ^ delta) for i in range(count)])  43.3 us
    ppermute x31, starting transfers between devices, exchange(): return lax.ppermute(block, axis, [(i, i ^ delta) for i in range(count)])  31.8 us
    pallas_call x1, Pallas kernels, log_pivots(): pl.pallas_call(functools.partial(pivots_kernel, sets), out_shape=jax.Shap...  12.6 us
    pallas_call x7, Pallas kernels, sketch(): pl.pallas_call(functools.partial(sketch_kernel, mode, which, columns, sta...  3.17 us
    dot_general x8, matrix products, pick(): out.append(jnp.dot(block, one_hot, preferred_element_type=f32).astype(bf16))  1.97 us
  transfers between devices with their start and end apart: 31, of which 16 were waited for; matrix products, arithmetic and copies ran while one was open for 4% of the time, Pallas kernels for 3%

profile of v6, /device:TPU:0, one launch (start us, length us, event | category | flops | bytes accessed | tf_op | source)
XLA Modules:
  0.0 98.1 jit_solution(9901778566030983906)
XLA Ops:
  0.6 1.0 %constant_dynamic-slice_fusion.3 = (bf16[128,512]{1,0:T(8,128)(2,1)S(1)}, bf16[128,512]{1,0:T(8,128)(2,1)S(1)}) fusion(bf16[128,4096]{1,0:T(8,128)(2,1)} %param.4, s32[]{:T(128)S(6)} %select_n.134, s32[]{:T(128)S(6)} %select_n.135), kind=kLoop, calls=%fused_computation.105 | loop fusion | bytes 524296 | tf_op jit(solution)/shard_map/dynamic_slice | solution.py:203
  1.7 3.0 %collective-permute-start.1 = (bf16[128,1024]{1,0:T(8,128)(2,1)S(1)}, bf16[128,1024]{1,0:T(8,128)(2,1)S(1)}, u32[]{:S(2)}, u32[]{:S(2)}) collective-permute-start(bf16[128,1024]{1,0:T(8,128)(2,1)S(1)} %pad_maximum_fusion.5), channel_id=1, source_target_pairs={{0,4},{4,0},{8,12},{12,8},{16,20},{20,16},{24,28},{28,24},{1,5},{5... | collective-permute-start | bytes 786440 | tf_op jit(solution)/shard_map/ppermute | solution.py:23
  4.8 1.6 %collective-permute-start.2 = (bf16[2,128,512]{2,1,0:T(8,128)(2,1)S(1)}, bf16[2,128,512]{2,1,0:T(8,128)(2,1)S(1)}, u32[]{:S(2)}, u32[]{:S(2)}) collective-permute-start(bf16[2,128,512]{2,1,0:T(8,128)(2,1)S(1)} %get-tuple-element.36), channel_id=1, source_target_pairs={{0,2},{1,3},{2,0},{3,1},{4,6},{5,7},{6,4},{7,5},{8,10},{9,11},{10,... | collective-permute-start | bytes 786440 | tf_op jit(solution)/shard_map/ppermute | solution.py:23
  6.3 0.7 copy-done.4
  7.0 2.7 %collective-permute-start = (s32[1,256]{1,0:T(1,128)S(1)}, s32[1,256]{1,0:T(1,128)S(1)}, u32[]{:S(2)}, u32[]{:S(2)}) collective-permute-start(s32[1,256]{1,0:T(1,128)S(1)} %get-tuple-element.55), channel_id=1, source_target_pairs={{0,16},{4,20},{8,24},{12,28},{16,0},{20,4},{24,8},{28,12},{1,17},{... | collective-permute-start | bytes 3080 | tf_op jit(solution)/shard_map/ppermute | solution.py:23
  9.7 1.9 %collective-permute-done = s32[1,256]{1,0:T(1,128)S(1)} collective-permute-done((s32[1,256]{1,0:T(1,128)S(1)}, s32[1,256]{1,0:T(1,128)S(1)}, u32[]{:S(2)}, u32[]{:S(2)}) %collective-permute-start) | collective-permute-done | bytes 1056 | tf_op jit(solution)/shard_map/ppermute | solution.py:23
  11.6 1.0 %collective-permute-done.2 = bf16[2,128,512]{2,1,0:T(8,128)(2,1)S(1)} collective-permute-done((bf16[2,128,512]{2,1,0:T(8,128)(2,1)S(1)}, bf16[2,128,512]{2,1,0:T(8,128)(2,1)S(1)}, u32[]{:S(2)}, u32[]{:S(2)}) %collective-permute-start.2) | collective-permute-done | bytes 262176 | tf_op jit(solution)/shard_map/ppermute | solution.py:23
  12.6 1.3 %collective-permute-start.4 = (bf16[2,128,512]{2,1,0:T(8,128)(2,1)S(1)}, bf16[2,128,512]{2,1,0:T(8,128)(2,1)S(1)}, u32[]{:S(2)}, u32[]{:S(2)}) collective-permute-start(bf16[2,128,512]{2,1,0:T(8,128)(2,1)S(1)} %collective-permute-done.2), channel_id=1, source_target_pairs={{0,4},{4,0},{8,12},{12,8},{16,20},{20,16},{24,28},{28,24},{1,5},{5... | collective-permute-start | bytes 786440 | tf_op jit(solution)/shard_map/ppermute | solution.py:23
  13.9 1.6 %collective-permute-start.6 = (s32[2,256]{1,0:T(2,128)S(1)}, s32[2,256]{1,0:T(2,128)S(1)}, u32[]{:S(2)}, u32[]{:S(2)}) collective-permute-start(s32[2,256]{1,0:T(2,128)S(1)} %add_bitcast_fusion), channel_id=1, source_target_pairs={{0,8},{4,12},{8,0},{12,4},{16,24},{20,28},{24,16},{28,20},{1,9},{5... | collective-permute-start | bytes 6152 | tf_op jit(solution)/shard_map/ppermute | solution.py:23
  15.5 0.9 collective-permute-start.3
  16.4 1.1 %collective-permute-done.6 = s32[2,256]{1,0:T(2,128)S(1)} collective-permute-done((s32[2,256]{1,0:T(2,128)S(1)}, s32[2,256]{1,0:T(2,128)S(1)}, u32[]{:S(2)}, u32[]{:S(2)}) %collective-permute-start.6) | collective-permute-done | bytes 2080 | tf_op jit(solution)/shard_map/ppermute | solution.py:23
  18.5 1.6 %collective-permute-start.7 = (bf16[128,512]{1,0:T(8,128)(2,1)S(1)}, bf16[128,512]{1,0:T(8,128)(2,1)S(1)}, u32[]{:S(2)}, u32[]{:S(2)}) collective-permute-start(bf16[128,512]{1,0:T(8,128)(2,1)S(1)} %get-tuple-element.18), channel_id=1, source_target_pairs={{0,2},{1,3},{2,0},{3,1},{4,6},{5,7},{6,4},{7,5},{8,10},{9,11},{10,... | collective-permute-start | bytes 393224 | tf_op jit(solution)/shard_map/ppermute | solution.py:23
  20.1 0.5 collective-permute-start.8
  20.7 0.9 collective-permute-start.13
  21.8 3.4 %collective-permute-done.13 = s32[2,256]{1,0:T(2,128)S(1)} collective-permute-done((s32[2,256]{1,0:T(2,128)S(1)}, s32[2,256]{1,0:T(2,128)S(1)}, u32[]{:S(2)}, u32[]{:S(2)}) %collective-permute-start.13) | collective-permute-done | bytes 2080 | tf_op jit(solution)/shard_map/ppermute | solution.py:23
  26.0 0.5 collective-permute-start.5
  26.6 1.6 %collective-permute-start.14 = (bf16[128,512]{1,0:T(8,128)(2,1)S(1)}, bf16[128,512]{1,0:T(8,128)(2,1)S(1)}, u32[]{:S(2)}, u32[]{:S(2)}) collective-permute-start(bf16[128,512]{1,0:T(8,128)(2,1)S(1)} %pad_maximum_fusion.13), channel_id=1, source_target_pairs={{0,4},{4,0},{8,12},{12,8},{16,20},{20,16},{24,28},{28,24},{1,5},{5... | collective-permute-start | bytes 393224 | tf_op jit(solution)/shard_map/ppermute | solution.py:23
  28.4 1.6 %collective-permute-start.12 = (bf16[128,512]{1,0:T(8,128)(2,1)S(1)}, bf16[128,512]{1,0:T(8,128)(2,1)S(1)}, u32[]{:S(2)}, u32[]{:S(2)}) collective-permute-start(bf16[128,512]{1,0:T(8,128)(2,1)S(1)} %pad_maximum_fusion.12), channel_id=1, source_target_pairs={{0,2},{1,3},{2,0},{3,1},{4,6},{5,7},{6,4},{7,5},{8,10},{9,11},{10,... | collective-permute-start | bytes 393224 | tf_op jit(solution)/shard_map/ppermute | solution.py:23
  30.0 2.1 %collective-permute-done.14 = bf16[128,512]{1,0:T(8,128)(2,1)S(1)} collective-permute-done((bf16[128,512]{1,0:T(8,128)(2,1)S(1)}, bf16[128,512]{1,0:T(8,128)(2,1)S(1)}, u32[]{:S(2)}, u32[]{:S(2)}) %collective-permute-start.14) | collective-permute-done | bytes 131104 | tf_op jit(solution)/shard_map/ppermute | solution.py:23
  32.1 1.5 %collective-permute-start.15 = (bf16[128,512]{1,0:T(8,128)(2,1)S(1)}, bf16[128,512]{1,0:T(8,128)(2,1)S(1)}, u32[]{:S(2)}, u32[]{:S(2)}) collective-permute-start(bf16[128,512]{1,0:T(8,128)(2,1)S(1)} %collective-permute-done.14), channel_id=1, source_target_pairs={{0,2},{1,3},{2,0},{3,1},{4,6},{5,7},{6,4},{7,5},{8,10},{9,11},{10,... | collective-permute-start | bytes 393224 | tf_op jit(solution)/shard_map/ppermute | solution.py:23
  33.6 0.5 shard_map.59
  34.1 1.6 %collective-permute-start.10 = (f16[272,256]{1,0:T(8,128)(2,1)S(1)}, f16[272,256]{1,0:T(8,128)(2,1)S(1)}, u32[]{:S(2)}, u32[]{:S(2)}) collective-permute-start(f16[272,256]{1,0:T(8,128)(2,1)S(1)} %convert_element_type.81), channel_id=1, source_target_pairs={{0,8},{4,12},{8,0},{12,4},{16,24},{20,28},{24,16},{28,20},{1,9},{5... | collective-permute-start | bytes 417800 | tf_op jit(solution)/shard_map/ppermute | solution.py:23
  35.8 0.5 shard_map.60
  36.3 0.5 collective-permute-start.11
  37.1 3.4 %collective-permute-done.10 = f16[272,256]{1,0:T(8,128)(2,1)S(1)} collective-permute-done((f16[272,256]{1,0:T(8,128)(2,1)S(1)}, f16[272,256]{1,0:T(8,128)(2,1)S(1)}, u32[]{:S(2)}, u32[]{:S(2)}) %collective-permute-start.10) | collective-permute-done | bytes 139296 | tf_op jit(solution)/shard_map/ppermute | solution.py:23
  40.6 1.5 %collective-permute-done.11 = f16[272,256]{1,0:T(8,128)(2,1)S(1)} collective-permute-done((f16[272,256]{1,0:T(8,128)(2,1)S(1)}, f16[272,256]{1,0:T(8,128)(2,1)S(1)}, u32[]{:S(2)}, u32[]{:S(2)}) %collective-permute-start.11) | collective-permute-done | bytes 139296 | tf_op jit(solution)/shard_map/ppermute | solution.py:23
  42.0 0.6 shard_map.61
  42.8 1.2 %collective-permute-start.17 = (f16[528,256]{1,0:T(8,128)(2,1)S(1)}, f16[528,256]{1,0:T(8,128)(2,1)S(1)}, u32[]{:S(2)}, u32[]{:S(2)}) collective-permute-start(f16[528,256]{1,0:T(8,128)(2,1)S(1)} %convert_element_type.87), channel_id=1, source_target_pairs={{0,8},{4,12},{8,0},{12,4},{16,24},{20,28},{24,16},{28,20},{1,9},{5... | collective-permute-start | bytes 811016 | tf_op jit(solution)/shard_map/ppermute | solution.py:23
  44.1 0.5 shard_map.63
  44.6 2.7 %collective-permute-start.18 = (f16[272,256]{1,0:T(8,128)(2,1)S(1)}, f16[272,256]{1,0:T(8,128)(2,1)S(1)}, u32[]{:S(2)}, u32[]{:S(2)}) collective-permute-start(f16[272,256]{1,0:T(8,128)(2,1)S(1)} %convert_element_type.91), channel_id=1, source_target_pairs={{0,16},{4,20},{8,24},{12,28},{16,0},{20,4},{24,8},{28,12},{1,17},{... | collective-permute-start | bytes 417800 | tf_op jit(solution)/shard_map/ppermute | solution.py:23
  47.2 0.5 shard_map.64
  47.8 0.4 collective-permute-start.19
  48.2 8.9 %collective-permute-done.17 = f16[528,256]{1,0:T(8,128)(2,1)S(1)} collective-permute-done((f16[528,256]{1,0:T(8,128)(2,1)S(1)}, f16[528,256]{1,0:T(8,128)(2,1)S(1)}, u32[]{:S(2)}, u32[]{:S(2)}) %collective-permute-start.17) | collective-permute-done | bytes 270368 | tf_op jit(solution)/shard_map/ppermute | solution.py:23
  57.2 0.5 shard_map.62.refs_0_
  57.7 2.7 %collective-permute-done.19 = f16[272,256]{1,0:T(8,128)(2,1)S(1)} collective-permute-done((f16[272,256]{1,0:T(8,128)(2,1)S(1)}, f16[272,256]{1,0:T(8,128)(2,1)S(1)}, u32[]{:S(2)}, u32[]{:S(2)}) %collective-permute-start.19) | collective-permute-done | bytes 139296 | tf_op jit(solution)/shard_map/ppermute | solution.py:23
  60.5 1.6 %collective-permute-start.20 = (bf16[256,256]{1,0:T(8,128)(2,1)S(1)}, bf16[256,256]{1,0:T(8,128)(2,1)S(1)}, u32[]{:S(2)}, u32[]{:S(2)}) collective-permute-start(bf16[256,256]{1,0:T(8,128)(2,1)S(1)} %shard_map.65), channel_id=1, source_target_pairs={{0,4},{4,0},{8,12},{12,8},{16,20},{20,16},{24,28},{28,24},{1,5},{5... | collective-permute-start | bytes 393224 | tf_op jit(solution)/shard_map/ppermute | solution.py:23
  62.0 0.5 collective-permute-start.25
  62.6 2.9 %collective-permute-done.20 = bf16[256,256]{1,0:T(8,128)(2,1)S(1)} collective-permute-done((bf16[256,256]{1,0:T(8,128)(2,1)S(1)}, bf16[256,256]{1,0:T(8,128)(2,1)S(1)}, u32[]{:S(2)}, u32[]{:S(2)}) %collective-permute-start.20) | collective-permute-done | bytes 131104 | tf_op jit(solution)/shard_map/ppermute | solution.py:23
  66.2 0.5 collective-permute-start.27
  66.7 0.5 collective-permute-done.25
  67.5 3.4 %collective-permute-done.21 = bf16[256,256]{1,0:T(8,128)(2,1)S(1)} collective-permute-done((bf16[256,256]{1,0:T(8,128)(2,1)S(1)}, bf16[256,256]{1,0:T(8,128)(2,1)S(1)}, u32[]{:S(2)}, u32[]{:S(2)}) %collective-permute-start.21) | collective-permute-done | bytes 131104 | tf_op jit(solution)/shard_map/ppermute | solution.py:23
  71.1 1.6 %collective-permute-start.22 = (bf16[256,256]{1,0:T(8,128)(2,1)S(1)}, bf16[256,256]{1,0:T(8,128)(2,1)S(1)}, u32[]{:S(2)}, u32[]{:S(2)}) collective-permute-start(bf16[256,256]{1,0:T(8,128)(2,1)S(1)} %fusion.1), channel_id=1, source_target_pairs={{0,16},{4,20},{8,24},{12,28},{16,0},{20,4},{24,8},{28,12},{1,17},{... | collective-permute-start | bytes 393224 | tf_op jit(solution)/shard_map/ppermute | solution.py:23
  72.7 0.5 collective-permute-start.29
  73.8 4.7 %collective-permute-done.22 = bf16[256,256]{1,0:T(8,128)(2,1)S(1)} collective-permute-done((bf16[256,256]{1,0:T(8,128)(2,1)S(1)}, bf16[256,256]{1,0:T(8,128)(2,1)S(1)}, u32[]{:S(2)}, u32[]{:S(2)}) %collective-permute-start.22) | collective-permute-done | bytes 131104 | tf_op jit(solution)/shard_map/ppermute | solution.py:23
  78.7 0.8 collective-permute-start.23
  79.7 4.0 %collective-permute-done.23 = bf16[256,256]{1,0:T(8,128)(2,1)S(1)} collective-permute-done((bf16[256,256]{1,0:T(8,128)(2,1)S(1)}, bf16[256,256]{1,0:T(8,128)(2,1)S(1)}, u32[]{:S(2)}, u32[]{:S(2)}) %collective-permute-start.23) | collective-permute-done | bytes 131104 | tf_op jit(solution)/shard_map/ppermute | solution.py:23
  84.0 1.4 %collective-permute-done.24 = bf16[512,256]{1,0:T(8,128)(2,1)S(1)} collective-permute-done((bf16[512,256]{1,0:T(8,128)(2,1)S(1)}, bf16[512,256]{1,0:T(8,128)(2,1)S(1)}, u32[]{:S(2)}, u32[]{:S(2)}) %collective-permute-start.24) | collective-permute-done | bytes 262176 | tf_op jit(solution)/shard_map/ppermute | solution.py:23
  85.5 12.6 %shard_map.66 = f32[1,256]{1,0:T(1,128)} custom-call(bf16[1024,256]{1,0:T(8,128)(2,1)S(1)} %bitcast.63, bf16[1024,256]{1,0:T(8,128)(2,1)S(1)} %bitcast.64, bf16[1024,256]{1,0:T(8,128)(2,1)S(1)} %bitcast.65, bf16[1024,256]{1,0:T(8,128)(2,1)S(1)} %bitcast.66), custom_call_target="tpu_custom_call" | custom-call | tf_op jit(solution)/shard_map/pallas_call | solution.py:112
  (97 shorter events, 5.4 us)
Async XLA Ops:
  1.6 3.1 %copy-start.1 = (bf16[128,1024]{1,0:T(8,128)(2,1)S(1)}, bf16[128,1024]{1,0:T(8,128)(2,1)}, u32[]{:S(2)}) copy-start(bf16[128,1024]{1,0:T(8,128)(2,1)} %param.5) | copy-start | bytes 786436
  1.7 3.1 %copy-start.2 = (bf16[128,1024]{1,0:T(8,128)(2,1)S(1)}, bf16[128,1024]{1,0:T(8,128)(2,1)}, u32[]{:S(2)}) copy-start(bf16[128,1024]{1,0:T(8,128)(2,1)} %param.6) | copy-start | bytes 786436
  1.7 9.9 %collective-permute-start.1 = (bf16[128,1024]{1,0:T(8,128)(2,1)S(1)}, bf16[128,1024]{1,0:T(8,128)(2,1)S(1)}, u32[]{:S(2)}, u32[]{:S(2)}) collective-permute-start(bf16[128,1024]{1,0:T(8,128)(2,1)S(1)} %pad_maximum_fusion.5), channel_id=1, source_target_pairs={{0,4},{4,0},{8,12},{12,8},{16,20},{20,16},{24,28},{28,24},{1,5},{5... | collective-permute-start | bytes 786440 | tf_op jit(solution)/shard_map/ppermute | solution.py:23
  4.7 12.8 %copy-start.3 = (bf16[128,4096]{1,0:T(8,128)(2,1)S(1)}, bf16[128,4096]{1,0:T(8,128)(2,1)}, u32[]{:S(2)}) copy-start(bf16[128,4096]{1,0:T(8,128)(2,1)} %param.4) | copy-start | bytes 3145732
  4.8 7.8 %collective-permute-start.2 = (bf16[2,128,512]{2,1,0:T(8,128)(2,1)S(1)}, bf16[2,128,512]{2,1,0:T(8,128)(2,1)S(1)}, u32[]{:S(2)}, u32[]{:S(2)}) collective-permute-start(bf16[2,128,512]{2,1,0:T(8,128)(2,1)S(1)} %get-tuple-element.36), channel_id=1, source_target_pairs={{0,2},{1,3},{2,0},{3,1},{4,6},{5,7},{6,4},{7,5},{8,10},{9,11},{10,... | collective-permute-start | bytes 786440 | tf_op jit(solution)/shard_map/ppermute | solution.py:23
  6.3 0.7 copy-start.4
  7.0 4.5 %collective-permute-start = (s32[1,256]{1,0:T(1,128)S(1)}, s32[1,256]{1,0:T(1,128)S(1)}, u32[]{:S(2)}, u32[]{:S(2)}) collective-permute-start(s32[1,256]{1,0:T(1,128)S(1)} %get-tuple-element.55), channel_id=1, source_target_pairs={{0,16},{4,20},{8,24},{12,28},{16,0},{20,4},{24,8},{28,12},{1,17},{... | collective-permute-start | bytes 3080 | tf_op jit(solution)/shard_map/ppermute | solution.py:23
  12.6 13.3 %collective-permute-start.4 = (bf16[2,128,512]{2,1,0:T(8,128)(2,1)S(1)}, bf16[2,128,512]{2,1,0:T(8,128)(2,1)S(1)}, u32[]{:S(2)}, u32[]{:S(2)}) collective-permute-start(bf16[2,128,512]{2,1,0:T(8,128)(2,1)S(1)} %collective-permute-done.2), channel_id=1, source_target_pairs={{0,4},{4,0},{8,12},{12,8},{16,20},{20,16},{24,28},{28,24},{1,5},{5... | collective-permute-start | bytes 786440 | tf_op jit(solution)/shard_map/ppermute | solution.py:23
  13.9 3.6 %collective-permute-start.6 = (s32[2,256]{1,0:T(2,128)S(1)}, s32[2,256]{1,0:T(2,128)S(1)}, u32[]{:S(2)}, u32[]{:S(2)}) collective-permute-start(s32[2,256]{1,0:T(2,128)S(1)} %add_bitcast_fusion), channel_id=1, source_target_pairs={{0,8},{4,12},{8,0},{12,4},{16,24},{20,28},{24,16},{28,20},{1,9},{5... | collective-permute-start | bytes 6152 | tf_op jit(solution)/shard_map/ppermute | solution.py:23
  15.5 10.4 %collective-permute-start.3 = (bf16[2,128,512]{2,1,0:T(8,128)(2,1)S(1)}, bf16[2,128,512]{2,1,0:T(8,128)(2,1)S(1)}, u32[]{:S(2)}, u32[]{:S(2)}) collective-permute-start(bf16[2,128,512]{2,1,0:T(8,128)(2,1)S(1)} %get-tuple-element.15), channel_id=1, source_target_pairs={{0,4},{4,0},{8,12},{12,8},{16,20},{20,16},{24,28},{28,24},{1,5},{5... | collective-permute-start | bytes 786440 | tf_op jit(solution)/shard_map/ppermute | solution.py:23
  18.5 7.2 %collective-permute-start.7 = (bf16[128,512]{1,0:T(8,128)(2,1)S(1)}, bf16[128,512]{1,0:T(8,128)(2,1)S(1)}, u32[]{:S(2)}, u32[]{:S(2)}) collective-permute-start(bf16[128,512]{1,0:T(8,128)(2,1)S(1)} %get-tuple-element.18), channel_id=1, source_target_pairs={{0,2},{1,3},{2,0},{3,1},{4,6},{5,7},{6,4},{7,5},{8,10},{9,11},{10,... | collective-permute-start | bytes 393224 | tf_op jit(solution)/shard_map/ppermute | solution.py:23
  20.1 5.7 %collective-permute-start.8 = (bf16[128,512]{1,0:T(8,128)(2,1)S(1)}, bf16[128,512]{1,0:T(8,128)(2,1)S(1)}, u32[]{:S(2)}, u32[]{:S(2)}) collective-permute-start(bf16[128,512]{1,0:T(8,128)(2,1)S(1)} %get-tuple-element.19), channel_id=1, source_target_pairs={{0,2},{1,3},{2,0},{3,1},{4,6},{5,7},{6,4},{7,5},{8,10},{9,11},{10,... | collective-permute-start | bytes 393224 | tf_op jit(solution)/shard_map/ppermute | solution.py:23
  20.7 4.6 %collective-permute-start.13 = (s32[2,256]{1,0:T(2,128)S(1)}, s32[2,256]{1,0:T(2,128)S(1)}, u32[]{:S(2)}, u32[]{:S(2)}) collective-permute-start(s32[2,256]{1,0:T(2,128)S(1)} %pad_add_fusion.1), channel_id=1, source_target_pairs={{0,4},{4,0},{8,12},{12,8},{16,20},{20,16},{24,28},{28,24},{1,5},{5... | collective-permute-start | bytes 6152 | tf_op jit(solution)/shard_map/ppermute | solution.py:23
  25.8 7.8 %collective-permute-start.9 = (bf16[512,512]{1,0:T(8,128)(2,1)S(1)}, bf16[512,512]{1,0:T(8,128)(2,1)S(1)}, u32[]{:S(2)}, u32[]{:S(2)}) collective-permute-start(bf16[512,512]{1,0:T(8,128)(2,1)S(1)} %constant_dynamic-update-slice_fusion.4.refs_2_), channel_id=1, source_target_pairs={{0,1},{1,0},{2,3},{3,2},{4,5},{5,4},{6,7},{7,6},{8,9},{9,8},{10,11... | collective-permute-start | bytes 1572872 | tf_op jit(solution)/shard_map/ppermute | solution.py:23
  26.0 7.6 %collective-permute-start.5 = (bf16[2,512,256]{2,1,0:T(8,128)(2,1)S(1)}, bf16[2,512,256]{2,1,0:T(8,128)(2,1)S(1)}, u32[]{:S(2)}, u32[]{:S(2)}) collective-permute-start(bf16[2,512,256]{2,1,0:T(8,128)(2,1)S(1)} %get-tuple-element.24), channel_id=1, source_target_pairs={{0,1},{1,0},{2,3},{3,2},{4,5},{5,4},{6,7},{7,6},{8,9},{9,8},{10,11... | collective-permute-start | bytes 1572872 | tf_op jit(solution)/shard_map/ppermute | solution.py:23
  26.6 5.5 %collective-permute-start.14 = (bf16[128,512]{1,0:T(8,128)(2,1)S(1)}, bf16[128,512]{1,0:T(8,128)(2,1)S(1)}, u32[]{:S(2)}, u32[]{:S(2)}) collective-permute-start(bf16[128,512]{1,0:T(8,128)(2,1)S(1)} %pad_maximum_fusion.13), channel_id=1, source_target_pairs={{0,4},{4,0},{8,12},{12,8},{16,20},{20,16},{24,28},{28,24},{1,5},{5... | collective-permute-start | bytes 393224 | tf_op jit(solution)/shard_map/ppermute | solution.py:23
  28.4 8.4 %collective-permute-start.12 = (bf16[128,512]{1,0:T(8,128)(2,1)S(1)}, bf16[128,512]{1,0:T(8,128)(2,1)S(1)}, u32[]{:S(2)}, u32[]{:S(2)}) collective-permute-start(bf16[128,512]{1,0:T(8,128)(2,1)S(1)} %pad_maximum_fusion.12), channel_id=1, source_target_pairs={{0,2},{1,3},{2,0},{3,1},{4,6},{5,7},{6,4},{7,5},{8,10},{9,11},{10,... | collective-permute-start | bytes 393224 | tf_op jit(solution)/shard_map/ppermute | solution.py:23
  32.1 5.0 %collective-permute-start.15 = (bf16[128,512]{1,0:T(8,128)(2,1)S(1)}, bf16[128,512]{1,0:T(8,128)(2,1)S(1)}, u32[]{:S(2)}, u32[]{:S(2)}) collective-permute-start(bf16[128,512]{1,0:T(8,128)(2,1)S(1)} %collective-permute-done.14), channel_id=1, source_target_pairs={{0,2},{1,3},{2,0},{3,1},{4,6},{5,7},{6,4},{7,5},{8,10},{9,11},{10,... | collective-permute-start | bytes 393224 | tf_op jit(solution)/shard_map/ppermute | solution.py:23
  34.1 6.4 %collective-permute-start.10 = (f16[272,256]{1,0:T(8,128)(2,1)S(1)}, f16[272,256]{1,0:T(8,128)(2,1)S(1)}, u32[]{:S(2)}, u32[]{:S(2)}) collective-permute-start(f16[272,256]{1,0:T(8,128)(2,1)S(1)} %convert_element_type.81), channel_id=1, source_target_pairs={{0,8},{4,12},{8,0},{12,4},{16,24},{20,28},{24,16},{28,20},{1,9},{5... | collective-permute-start | bytes 417800 | tf_op jit(solution)/shard_map/ppermute | solution.py:23
  36.3 5.8 %collective-permute-start.11 = (f16[272,256]{1,0:T(8,128)(2,1)S(1)}, f16[272,256]{1,0:T(8,128)(2,1)S(1)}, u32[]{:S(2)}, u32[]{:S(2)}) collective-permute-start(f16[272,256]{1,0:T(8,128)(2,1)S(1)} %convert_element_type.82), channel_id=1, source_target_pairs={{0,8},{4,12},{8,0},{12,4},{16,24},{20,28},{24,16},{28,20},{1,9},{5... | collective-permute-start | bytes 417800 | tf_op jit(solution)/shard_map/ppermute | solution.py:23
  42.0 2.0 %collective-permute-start.16 = (bf16[512,512]{1,0:T(8,128)(2,1)S(1)}, bf16[512,512]{1,0:T(8,128)(2,1)S(1)}, u32[]{:S(2)}, u32[]{:S(2)}) collective-permute-start(bf16[512,512]{1,0:T(8,128)(2,1)S(1)} %pad_maximum_fusion.refs_2_), channel_id=1, source_target_pairs={{0,1},{1,0},{2,3},{3,2},{4,5},{5,4},{6,7},{7,6},{8,9},{9,8},{10,11... | collective-permute-start | bytes 1572872 | tf_op jit(solution)/shard_map/ppermute | solution.py:23
  42.8 14.4 %collective-permute-start.17 = (f16[528,256]{1,0:T(8,128)(2,1)S(1)}, f16[528,256]{1,0:T(8,128)(2,1)S(1)}, u32[]{:S(2)}, u32[]{:S(2)}) collective-permute-start(f16[528,256]{1,0:T(8,128)(2,1)S(1)} %convert_element_type.87), channel_id=1, source_target_pairs={{0,8},{4,12},{8,0},{12,4},{16,24},{20,28},{24,16},{28,20},{1,9},{5... | collective-permute-start | bytes 811016 | tf_op jit(solution)/shard_map/ppermute | solution.py:23
  44.6 13.1 %collective-permute-start.18 = (f16[272,256]{1,0:T(8,128)(2,1)S(1)}, f16[272,256]{1,0:T(8,128)(2,1)S(1)}, u32[]{:S(2)}, u32[]{:S(2)}) collective-permute-start(f16[272,256]{1,0:T(8,128)(2,1)S(1)} %convert_element_type.91), channel_id=1, source_target_pairs={{0,16},{4,20},{8,24},{12,28},{16,0},{20,4},{24,8},{28,12},{1,17},{... | collective-permute-start | bytes 417800 | tf_op jit(solution)/shard_map/ppermute | solution.py:23
  47.8 12.6 %collective-permute-start.19 = (f16[272,256]{1,0:T(8,128)(2,1)S(1)}, f16[272,256]{1,0:T(8,128)(2,1)S(1)}, u32[]{:S(2)}, u32[]{:S(2)}) collective-permute-start(f16[272,256]{1,0:T(8,128)(2,1)S(1)} %convert_element_type.93), channel_id=1, source_target_pairs={{0,16},{4,20},{8,24},{12,28},{16,0},{20,4},{24,8},{28,12},{1,17},{... | collective-permute-start | bytes 417800 | tf_op jit(solution)/shard_map/ppermute | solution.py:23
  60.5 5.0 %collective-permute-start.20 = (bf16[256,256]{1,0:T(8,128)(2,1)S(1)}, bf16[256,256]{1,0:T(8,128)(2,1)S(1)}, u32[]{:S(2)}, u32[]{:S(2)}) collective-permute-start(bf16[256,256]{1,0:T(8,128)(2,1)S(1)} %shard_map.65), channel_id=1, source_target_pairs={{0,4},{4,0},{8,12},{12,8},{16,20},{20,16},{24,28},{28,24},{1,5},{5... | collective-permute-start | bytes 393224 | tf_op jit(solution)/shard_map/ppermute | solution.py:23
  62.0 5.1 %collective-permute-start.25 = (bf16[256,256]{1,0:T(8,128)(2,1)S(1)}, bf16[256,256]{1,0:T(8,128)(2,1)S(1)}, u32[]{:S(2)}, u32[]{:S(2)}) collective-permute-start(bf16[256,256]{1,0:T(8,128)(2,1)S(1)} %shard_map.65), channel_id=1, source_target_pairs={{0,2},{1,3},{2,0},{3,1},{4,6},{5,7},{6,4},{7,5},{8,10},{9,11},{10,... | collective-permute-start | bytes 393224 | tf_op jit(solution)/shard_map/ppermute | solution.py:23
  65.9 5.0 %collective-permute-start.21 = (bf16[256,256]{1,0:T(8,128)(2,1)S(1)}, bf16[256,256]{1,0:T(8,128)(2,1)S(1)}, u32[]{:S(2)}, u32[]{:S(2)}) collective-permute-start(bf16[256,256]{1,0:T(8,128)(2,1)S(1)} %fusion), channel_id=1, source_target_pairs={{0,8},{4,12},{8,0},{12,4},{16,24},{20,28},{24,16},{28,20},{1,9},{5... | collective-permute-start | bytes 393224 | tf_op jit(solution)/shard_map/ppermute | solution.py:23
  66.2 7.1 %collective-permute-start.27 = (bf16[256,256]{1,0:T(8,128)(2,1)S(1)}, bf16[256,256]{1,0:T(8,128)(2,1)S(1)}, u32[]{:S(2)}, u32[]{:S(2)}) collective-permute-start(bf16[256,256]{1,0:T(8,128)(2,1)S(1)} %fusion), channel_id=1, source_target_pairs={{0,2},{1,3},{2,0},{3,1},{4,6},{5,7},{6,4},{7,5},{8,10},{9,11},{10,... | collective-permute-start | bytes 393224 | tf_op jit(solution)/shard_map/ppermute | solution.py:23
  67.2 6.4 %collective-permute-start.26 = (bf16[512,256]{1,0:T(8,128)(2,1)S(1)}, bf16[512,256]{1,0:T(8,128)(2,1)S(1)}, u32[]{:S(2)}, u32[]{:S(2)}) collective-permute-start(bf16[512,256]{1,0:T(8,128)(2,1)S(1)} %get-tuple-element.46), channel_id=1, source_target_pairs={{0,1},{1,0},{2,3},{3,2},{4,5},{5,4},{6,7},{7,6},{8,9},{9,8},{10,11... | collective-permute-start | bytes 786440 | tf_op jit(solution)/shard_map/ppermute | solution.py:23
  71.1 7.3 %collective-permute-start.22 = (bf16[256,256]{1,0:T(8,128)(2,1)S(1)}, bf16[256,256]{1,0:T(8,128)(2,1)S(1)}, u32[]{:S(2)}, u32[]{:S(2)}) collective-permute-start(bf16[256,256]{1,0:T(8,128)(2,1)S(1)} %fusion.1), channel_id=1, source_target_pairs={{0,16},{4,20},{8,24},{12,28},{16,0},{20,4},{24,8},{28,12},{1,17},{... | collective-permute-start | bytes 393224 | tf_op jit(solution)/shard_map/ppermute | solution.py:23
  72.7 6.7 %collective-permute-start.29 = (bf16[256,256]{1,0:T(8,128)(2,1)S(1)}, bf16[256,256]{1,0:T(8,128)(2,1)S(1)}, u32[]{:S(2)}, u32[]{:S(2)}) collective-permute-start(bf16[256,256]{1,0:T(8,128)(2,1)S(1)} %fusion.1), channel_id=1, source_target_pairs={{0,2},{1,3},{2,0},{3,1},{4,6},{5,7},{6,4},{7,5},{8,10},{9,11},{10,... | collective-permute-start | bytes 393224 | tf_op jit(solution)/shard_map/ppermute | solution.py:23
  73.4 6.2 %collective-permute-start.28 = (bf16[512,256]{1,0:T(8,128)(2,1)S(1)}, bf16[512,256]{1,0:T(8,128)(2,1)S(1)}, u32[]{:S(2)}, u32[]{:S(2)}) collective-permute-start(bf16[512,256]{1,0:T(8,128)(2,1)S(1)} %get-tuple-element.42), channel_id=1, source_target_pairs={{0,1},{1,0},{2,3},{3,2},{4,5},{5,4},{6,7},{7,6},{8,9},{9,8},{10,11... | collective-permute-start | bytes 786440 | tf_op jit(solution)/shard_map/ppermute | solution.py:23
  78.7 5.0 %collective-permute-start.23 = (bf16[256,256]{1,0:T(8,128)(2,1)S(1)}, bf16[256,256]{1,0:T(8,128)(2,1)S(1)}, u32[]{:S(2)}, u32[]{:S(2)}) collective-permute-start(bf16[256,256]{1,0:T(8,128)(2,1)S(1)} %fusion.2), channel_id=1, source_target_pairs={{0,2},{1,3},{2,0},{3,1},{4,6},{5,7},{6,4},{7,5},{8,10},{9,11},{10,... | collective-permute-start | bytes 393224 | tf_op jit(solution)/shard_map/ppermute | solution.py:23
  79.5 4.4 %collective-permute-start.30 = (bf16[512,256]{1,0:T(8,128)(2,1)S(1)}, bf16[512,256]{1,0:T(8,128)(2,1)S(1)}, u32[]{:S(2)}, u32[]{:S(2)}) collective-permute-start(bf16[512,256]{1,0:T(8,128)(2,1)S(1)} %get-tuple-element.38), channel_id=1, source_target_pairs={{0,1},{1,0},{2,3},{3,2},{4,5},{5,4},{6,7},{7,6},{8,9},{9,8},{10,11... | collective-permute-start | bytes 786440 | tf_op jit(solution)/shard_map/ppermute | solution.py:23
  83.8 1.6 %collective-permute-start.24 = (bf16[512,256]{1,0:T(8,128)(2,1)S(1)}, bf16[512,256]{1,0:T(8,128)(2,1)S(1)}, u32[]{:S(2)}, u32[]{:S(2)}) collective-permute-start(bf16[512,256]{1,0:T(8,128)(2,1)S(1)} %get-tuple-element.50), channel_id=1, source_target_pairs={{0,1},{1,0},{2,3},{3,2},{4,5},{5,4},{6,7},{7,6},{8,9},{9,8},{10,11... | collective-permute-start | bytes 786440 | tf_op jit(solution)/shard_map/ppermute | solution.py:23
  85.5 12.6 %copy-start = (bf16[2,512,256]{2,1,0:T(8,128)(2,1)}, bf16[2,512,256]{2,1,0:T(8,128)(2,1)S(1)}, u32[]{:S(2)}) copy-start(bf16[2,512,256]{2,1,0:T(8,128)(2,1)S(1)} %pad_maximum_fusion.1) | copy-start | bytes 1572868

commit v7 on v6

v7 whole, which is shorter than its diff:
```python
import functools

import jax
import jax.numpy as jnp
from jax import lax
from jax.experimental import pallas as pl
from jax.experimental.pallas import tpu as pltpu
from jax.sharding import PartitionSpec as P

ridge = 0.1
f32, bf16, f16 = jnp.float32, jnp.bfloat16, jnp.float16
step, height, lanes = 8, 32, 128
top, tag_rows = 14.0, 16
column_dims = (((0,), (0,)), ((), ()))


def bits_of(count):
    return count.bit_length() - 1


def exchange(block, axis, delta):
    count = lax.axis_size(axis)
    return lax.ppermute(block, axis, [(i, i ^ delta) for i in range(count)])


def reversed_bits(value, bits):
    out = 0
    for t in range(bits):
        out = out | ((value >> t) & 1) << (bits - 1 - t)
    return out


def pick(blocks, lists):
    out = []
    for block, listed in zip(blocks, lists):
        index = lax.broadcasted_iota(jnp.int32, (block.shape[1], listed.shape[0]), 0)
        one_hot = (index == listed).astype(bf16)
        out.append(jnp.dot(block, one_hot, preferred_element_type=f32).astype(bf16))
    return jnp.concatenate(out, axis=1)


def split3(v):
    a = v.astype(bf16)
    rest = v - a.astype(f32)
    b = rest.astype(bf16)
    c = (rest - b.astype(f32)).astype(bf16)
    return a, b, c


def eliminate(block, first):
    width = block.shape[1]
    lane = lax.broadcasted_iota(jnp.int32, (1, width), 1)
    on_diagonal = lax.broadcasted_iota(jnp.int32, (step, width), 1) - lax.broadcasted_iota(
        jnp.int32, (step, width), 0
    )
    done, scaled, diagonal = [], [], 0.0
    for corner in range(0, block.shape[0], step):
        below = lax.broadcasted_iota(jnp.int32, (block.shape[0], 1), 0)
        start = first + corner
        columns = [jnp.sum(jnp.where(lane == start + j, block, 0.0), axis=1, keepdims=True) for j in range(step)]
        heads, inverses = [], []
        for j in range(step):
            head = columns[j][j : j + 1, :]
            inverse = 1.0 / head
            factor = jnp.where(below > j, columns[j] * inverse, 0.0)
            block = block - factor * block[j : j + 1, :]
            for c in range(j + 1, step):
                columns[c] = columns[c] - factor * columns[c][j : j + 1, :]
            heads.append(head)
            inverses.append(inverse)
        heads = jnp.concatenate(heads, axis=0)
        diagonal = diagonal + jnp.sum(jnp.where(on_diagonal == start, heads, 0.0), axis=0, keepdims=True)
        done.append(block[:step])
        scaled.append(block[:step] * jnp.concatenate(inverses, axis=0))
        block = block[step:]
    return jnp.concatenate(done, axis=0), jnp.concatenate(scaled, axis=0), diagonal


def outer(scaled, rows):
    u1, u2, u3 = split3(rows)
    v1, v2, v3 = split3(scaled)
    left = jnp.concatenate([v1, v1, v2, v2, v1, v3], axis=0)
    right = jnp.concatenate([u1, u2, u1, u2, u3, u1], axis=0)
    return lax.dot_general(left, right, column_dims, preferred_element_type=f32)


def pivots_kernel(sets, late, *refs):
    grams, refs = refs[:sets], refs[sets:]
    if late:
        place_ref, cand_ref, refs = refs[0], refs[1], refs[2:]
    total_ref, work, diagonals = refs[0], refs[1:-1], refs[-1]
    n = grams[0].shape[0]
    for gram, matrix in zip(grams, work):
        matrix[...] = gram[...]
    if late:
        product = lax.dot_general(cand_ref[...], cand_ref[...], column_dims, preferred_element_type=f32)
        last = work[-1]
        last[...] = jnp.where(place_ref[0] & 1 == 0, last[...], shifted(product, cand_ref.shape[0]))
    diagonals[...] = jnp.zeros_like(diagonals)
    for base in range(0, n, lanes):

        def panel(k, carry, base=base):
            first = pl.multiple_of(k * height, height)
            parts = [eliminate(matrix[pl.ds(base + first, height), base:], first) for matrix in work]
            for q, (done, scaled, diagonal) in enumerate(parts):
                diagonals[q : q + 1, base:] += diagonal
                work[q][base:, base:] -= outer(scaled, done)
            return carry

        lax.fori_loop(0, min(lanes, n - base) // height, panel, 0)
    total_ref[...] = jnp.sum(0.5 * jnp.log(diagonals[...]), axis=0, keepdims=True)


def shifted(product, rows):
    n = product.shape[0]
    diagonal = lax.broadcasted_iota(jnp.int32, (n, n), 0) == lax.broadcasted_iota(jnp.int32, (n, n), 1)
    return product * f32(1 / rows) + jnp.where(diagonal, f32(ridge), f32(0))


def gram_of(blocks):
    product = sum(lax.dot_general(b, b, column_dims, preferred_element_type=f32) for b in blocks)
    return shifted(product, sum(b.shape[0] for b in blocks))


def log_pivots(grams, place=None, cand=None):
    sets, n = len(grams), grams[0].shape[0]
    operands, specs = list(grams), [pl.BlockSpec(memory_space=pltpu.VMEM)] * sets
    if cand is not None:
        operands += [place[None], cand]
        specs += [pl.BlockSpec(memory_space=pltpu.SMEM), pl.BlockSpec(memory_space=pltpu.VMEM)]
    return pl.pallas_call(
        functools.partial(pivots_kernel, sets, cand is not None),
        out_shape=jax.ShapeDtypeStruct((1, n), f32),
        in_specs=specs,
        out_specs=pl.BlockSpec(memory_space=pltpu.VMEM),
        scratch_shapes=[pltpu.VMEM((n, n), f32)] * sets + [pltpu.VMEM((sets, n), f32)],
        compiler_params=pltpu.CompilerParams(vmem_limit_bytes=40 << 20),
    )(*operands)


def half_of(block, upper):
    size = block.shape[-1] // 2
    return lax.dynamic_slice_in_dim(block, upper * size, size, axis=block.ndim - 1)


def sketch_kernel(mode, columns, starts, dots, plain, *refs):
    refs, out_ref = refs[:-1], refs[-1]
    mixes, refs = refs[:dots], refs[dots:]
    views = [ref.at[:, start : start + columns] for ref, start in zip(refs, starts)]
    points, terms, coded = views[:dots], views[dots : dots + plain], views[dots + plain :]
    size = {"code": out_ref.shape[0] - tag_rows, "keep": out_ref.shape[0], "multiply": 2 * out_ref.shape[0]}[mode] // 2
    totals = []
    for i in range(2):
        own, total = pl.ds(i * size, size), 0.0
        for mix_ref, points_ref in zip(mixes, points):
            total += lax.dot_general(mix_ref[i], points_ref[...], column_dims, preferred_element_type=f32)
        for term in terms:
            total += term[own, :]
        for codes in coded:
            total += codes[own, :] * jnp.exp2(codes[2 * size : 2 * size + 1, :] - top)
        totals.append(total)
    if mode == "code":
        largest = jnp.maximum(*[jnp.max(jnp.abs(t), axis=(0, 1), keepdims=True) for t in totals])
        exponent = jnp.ceil(jnp.log2(jnp.maximum(largest, f32(1e-30))))
        totals = [total * jnp.exp2(top - exponent) for total in totals]
        out_ref[2 * size :, :] = jnp.broadcast_to(exponent, (tag_rows, columns))
    if mode == "multiply":
        out_ref[...] = (totals[0] * totals[1]).astype(bf16)
    else:
        for i in range(2):
            out_ref[i * size : (i + 1) * size, :] = totals[i]


def sketch(mode, block, mixes, plain=()):
    columns, points, coded = block
    size = mixes[0].shape[2]
    rows, kind = {"code": (2 * size + tag_rows, f32), "keep": (2 * size, f32), "multiply": (size, bf16)}[mode]
    terms = list(points) + list(plain) + list(coded)
    operands = list(mixes[: len(points)]) + [array for array, _ in terms]
    return pl.pallas_call(
        functools.partial(sketch_kernel, mode, columns, [start for _, start in terms], len(points), len(plain)),
        out_shape=jax.ShapeDtypeStruct((rows, columns), kind),
        in_specs=[pl.BlockSpec(memory_space=pltpu.VMEM)] * len(operands),
        out_specs=pl.BlockSpec(memory_space=pltpu.VMEM),
        compiler_params=pltpu.CompilerParams(vmem_limit_bytes=48 << 20),
    )(*operands)


def halves(block):
    size = block[0] // 2
    return [[size] + [[(a, first + shift) for a, first in terms] for terms in block[1:]] for shift in (0, size)]


def local(orbitals, w_first, w_second, pivots):
    here, place = lax.axis_index("grid"), lax.axis_index("band")
    groups = lax.axis_size("grid")
    grid_bits, band_bits = bits_of(groups), bits_of(lax.axis_size("band"))
    order = pivots[0]
    kept = order.shape[1]
    width = orbitals.shape[1] // groups

    parts = 2 if grid_bits > 1 else 1
    count = groups // 2 // parts
    places = [[reversed_bits(p * count + i, grid_bits - 1) for i in range(count)] for p in range(parts)]

    def blocks_of(p, side):
        return [
            lax.dynamic_slice_in_dim(orbitals, (here ^ 2 * k + side) * width, width, axis=1) for k in places[p]
        ]

    raw = exchange(jnp.concatenate(blocks_of(parts - 1, 1), axis=1), "grid", 1)

    mixing = [jnp.stack([w_first, w_second])]
    for t in reversed(range(1, band_bits)):
        upper = place >> t & 1
        got = [exchange(half_of(m, 1 - upper), "band", 1 << t) for m in mixing]
        mixing = [half_of(m, upper) for m in mixing] + got
    near = mixing[0]

    orders = order[:1]
    for t in reversed(range(2, grid_bits)):
        orders = jnp.stack([orders, exchange(orders, "grid", 1 << t)], axis=1).reshape(-1, kept)
    if parts > 1:
        listed = jnp.concatenate([orders[k >> 1] for k in places[0]])
        size, span = near.shape[1:]
        digits = jnp.stack([listed >> 8, listed & 255]).astype(bf16)
        digits = jnp.pad(digits, ((0, 0), (0, -listed.shape[0] % (16 * span)))).reshape(2, -1, span)
        near = exchange(jnp.concatenate([near, digits], axis=1), "grid", 1)
        near, digits = near[:, :size], near[:, size:].reshape(2, -1)[:, : listed.shape[0]].astype(jnp.int32)
        far_lists = (digits[0] * 256 + digits[1]).reshape(-1, kept)
        orders = jnp.stack([orders, exchange(orders, "grid", 2)], axis=1).reshape(-1, kept)
    else:
        near = exchange(near, "grid", 1)
    near = [near] + [exchange(m, "grid", 1) for m in mixing[1:]]

    def over_bands(block):
        blocks = [block]
        for t in reversed(range(1, band_bits)):
            blocks = blocks + [exchange(m, "band", 1 << t) for m in blocks]
        return blocks

    def lists_of(p):
        return [orders[k] for k in places[p]]

    def gather(own, far):
        return jnp.concatenate(over_bands(own) + over_bands(far), axis=0)

    def over_cores(rows):
        return [(rows, 0), (exchange(rows, "band", 1), 0)]

    picked = {}
    for p in reversed(range(parts)):
        own = pick(blocks_of(p, 0), lists_of(p))
        if p == parts - 1:
            far = pick([raw[:, i * width : (i + 1) * width] for i in range(count)], lists_of(p))
            if parts > 1:
                orders, far_lists, _, _ = lax.optimization_barrier((orders, far_lists, own, far))
        else:
            far = exchange(pick(blocks_of(p, 1), far_lists), "grid", 1)
        picked[p] = own, far

    go = [count * kept, over_cores(gather(*picked[parts - 1])), []]
    mixing = jnp.concatenate(mixing + near, axis=1)
    mixes = [half_of(mixing, place & 1), exchange(half_of(mixing, 1 - (place & 1)), "band", 1)]

    def swap(block, bit):
        return exchange(sketch("code", block, mixes).astype(f16), "grid", 1 << bit)

    if parts > 1:
        stay = None
        for t in range(1, grid_bits):
            pieces = halves(go) if t < grid_bits - 1 else [go]
            got = [swap(piece, t) for piece in reversed(pieces)]
            if stay is None:
                got[0], rows = lax.optimization_barrier((got[0], gather(*picked[0])))
                stay = [count * kept, over_cores(rows), []]
            if len(pieces) > 1:
                stay, go = halves(stay)
                for block, codes in zip((go, stay), got):
                    block[2].append((codes.astype(f32), 0))
        held = sketch("keep", stay, mixes)
        chosen = sketch("multiply", [kept, [], [(got[0].astype(f32), 0)]], mixes, [(held, 0)])
    else:
        chosen = sketch("multiply", go, mixes)

    def in_order(block, got, t):
        upper = place >> t & 1 == 1
        count = 1 << (band_bits - 1 - t)
        share = block.reshape((count, -1) + block.shape[1:])
        other = got.reshape(share.shape)
        low, high = jnp.where(upper, other, share), jnp.where(upper, share, other)
        return jnp.concatenate([low, high], axis=1).reshape((-1,) + block.shape[1:])

    def over_higher(block):
        for t in reversed(range(1, band_bits)):
            block = in_order(block, exchange(block, "band", 1 << t), t)
        return block

    rounds = grid_bits + 1
    paired = rounds - 2 + rounds % 2
    index = lax.broadcasted_iota(jnp.int32, (kept, kept), 0)
    even = place & 1 == 0
    shared, grams = [], []
    for section in range(rounds):
        if section:
            got = exchange(chosen, "grid", 1 << section - 1)
            upper = here >> section - 1 & 1
            mine = (index == order[section] - upper * kept).astype(bf16)
            other = (index == order[section] - (1 - upper) * kept).astype(bf16)
            chosen = jnp.dot(chosen, mine, preferred_element_type=f32) + jnp.dot(got, other, preferred_element_type=f32)
            chosen = chosen.astype(bf16)
        if section == rounds - 1:
            final = over_higher(chosen)
        else:
            block = chosen
            if shared:
                block, shared[-1] = lax.optimization_barrier((block, shared[-1]))
            shared.append(over_higher(block))
            if section < paired and section % 2:
                low, high = shared[-2:]
                got = exchange(jnp.where(even, high, low), "band", 1)
                grams.append(gram_of([jnp.where(even, low, high), got]))
    cands = in_order(final, exchange(final, "band", 1), 0)
    if rounds % 2:
        odd = log_pivots([gram_of([cands])])
        quality = jnp.where(even, 0.0, odd) + (log_pivots(grams) if grams else 0.0)
    else:
        last = gram_of([shared[-1], exchange(shared[-1], "band", 1)])
        quality = log_pivots(grams + [last], place, cands)
    return cands, quality + exchange(quality, "band", 1)


def solution(mesh):
    in_specs = (
        P(("band", "grid"), None),
        P(("band", "grid"), None),
        P(("band", "grid"), None),
        P("grid", None, None),
    )
    out_specs = (P(), P("grid", None))
    return jax.shard_map(local, mesh=mesh, in_specs=in_specs, out_specs=out_specs, check_vma=False)
```

time: 98.2 us -> 93.1 us (0.948)
  Pallas kernels: 15.8 us -> 11.6 us
  starting transfers between devices: 31.8 us -> 28.4 us
  other arithmetic: 0.97 us -> 2.28 us
  matrix products: 3.16 us -> 4.25 us
    pallas_call x8 -> x6, Pallas kernels: 15.8 us -> 11.6 us  [the longest x1 9.11 us: log_pivots(): pl.pallas_call(functools.partial(pivots_kernel, sets, cand is not None),...]
    ppermute x31 -> x28, starting transfers between devices: 31.8 us -> 28.4 us  [exchange(): return lax.ppermute(block, axis, [(i, i ^ delta) for i in range(count)])]
    dot_general x0 -> x4, matrix products: none -> 1.08 us  [gram_of(): lax.dot_general(b, b, column_dims, preferred_element_type=f32)]
    ppermute x31 -> x28, waiting for transfers between devices: 43.3 us -> 44 us  [exchange(): return lax.ppermute(block, axis, [(i, i ^ delta) for i in range(count)])]
  transfers between devices with their start and end apart: 31 -> 28, of which waited for: 16 -> 17; matrix products, arithmetic and copies ran while one was open for 4% -> 7% of each run, Pallas kernels for 3% -> 3%
where the time goes in v7:
time: 93.1 us; the launch traced here: 92.9 us
  waiting for transfers between devices  44 us (47%)
  starting transfers between devices  28.4 us (31%)
  Pallas kernels  11.6 us (12%)
  matrix products  4.25 us (5%)
  other arithmetic  2.28 us (2%)
  local copies, waits for them, and re-layouts  1.21 us (1%)
  between operations  1.18 us (1%)
    ppermute x28, waiting for transfers between devices, exchange(): return lax.ppermute(block, axis, [(i, i ^ delta) for i in range(count)])  44 us
    ppermute x28, starting transfers between devices, exchange(): return lax.ppermute(block, axis, [(i, i ^ delta) for i in range(count)])  28.4 us
    pallas_call x1, Pallas kernels, log_pivots(): pl.pallas_call(functools.partial(pivots_kernel, sets, cand is not None),...  9.11 us
    pallas_call x5, Pallas kernels, sketch(): pl.pallas_call(functools.partial(sketch_kernel, mode, columns, [start for...  2.5 us
    dot_general x8, matrix products, pick(): out.append(jnp.dot(block, one_hot, preferred_element_type=f32).astype(bf16))  1.98 us
  transfers between devices with their start and end apart: 28, of which 17 were waited for; matrix products, arithmetic and copies ran while one was open for 7% of the time, Pallas kernels for 3%

profile of v7, /device:TPU:0, one launch (start us, length us, event | category | flops | bytes accessed | tf_op | source)
XLA Modules:
  0.0 92.9 jit_solution(1720759951677057973)
XLA Ops:
  0.7 0.8 slice_subtract_fusion
  1.5 4.1 %collective-permute-start.1 = (s32[1,256]{1,0:T(1,128)S(1)}, s32[1,256]{1,0:T(1,128)S(1)}, u32[]{:S(2)}, u32[]{:S(2)}) collective-permute-start(s32[1,256]{1,0:T(1,128)S(1)} %get-tuple-element.35), channel_id=1, source_target_pairs={{0,16},{4,20},{8,24},{12,28},{16,0},{20,4},{24,8},{28,12},{1,17},{... | collective-permute-start | bytes 3080 | tf_op jit(solution)/shard_map/ppermute | solution.py:23
  5.6 1.0 %constant_dynamic-slice_fusion.1 = (bf16[128,512]{1,0:T(8,128)(2,1)S(1)}, bf16[128,512]{1,0:T(8,128)(2,1)S(1)}) fusion(bf16[128,4096]{1,0:T(8,128)(2,1)} %param.4, s32[]{:T(128)S(6)} %select_n.135, s32[]{:T(128)S(6)} %select_n.136), kind=kLoop, calls=%fused_computation.104 | loop fusion | bytes 524296 | tf_op jit(solution)/shard_map/dynamic_slice | solution.py:208
  6.6 1.6 %collective-permute-start.7 = (bf16[128,1024]{1,0:T(8,128)(2,1)S(1)}, bf16[128,1024]{1,0:T(8,128)(2,1)S(1)}, u32[]{:S(2)}, u32[]{:S(2)}) collective-permute-start(bf16[128,1024]{1,0:T(8,128)(2,1)S(1)} %pad_maximum_fusion.5), channel_id=1, source_target_pairs={{0,4},{4,0},{8,12},{12,8},{16,20},{20,16},{24,28},{28,24},{1,5},{5... | collective-permute-start | bytes 786440 | tf_op jit(solution)/shard_map/ppermute | solution.py:23
  8.3 1.6 %collective-permute-start = (bf16[2,128,512]{2,1,0:T(8,128)(2,1)S(1)}, bf16[2,128,512]{2,1,0:T(8,128)(2,1)S(1)}, u32[]{:S(2)}, u32[]{:S(2)}) collective-permute-start(bf16[2,128,512]{2,1,0:T(8,128)(2,1)S(1)} %get-tuple-element.23), channel_id=1, source_target_pairs={{0,2},{1,3},{2,0},{3,1},{4,6},{5,7},{6,4},{7,5},{8,10},{9,11},{10,... | collective-permute-start | bytes 786440 | tf_op jit(solution)/shard_map/ppermute | solution.py:23
  9.8 1.6 %collective-permute-start.5 = (s32[2,256]{1,0:T(2,128)S(1)}, s32[2,256]{1,0:T(2,128)S(1)}, u32[]{:S(2)}, u32[]{:S(2)}) collective-permute-start(s32[2,256]{1,0:T(2,128)S(1)} %get-tuple-element.49), channel_id=1, source_target_pairs={{0,8},{4,12},{8,0},{12,4},{16,24},{20,28},{24,16},{28,20},{1,9},{5... | collective-permute-start | bytes 6152 | tf_op jit(solution)/shard_map/ppermute | solution.py:23
  11.5 0.6 collective-permute-start.2
  12.1 1.4 %collective-permute-done.5 = s32[2,256]{1,0:T(2,128)S(1)} collective-permute-done((s32[2,256]{1,0:T(2,128)S(1)}, s32[2,256]{1,0:T(2,128)S(1)}, u32[]{:S(2)}, u32[]{:S(2)}) %collective-permute-start.5) | collective-permute-done | bytes 2080 | tf_op jit(solution)/shard_map/ppermute | solution.py:23
  14.0 0.6 collective-permute-start.6
  14.6 1.3 %collective-permute-done.7 = bf16[128,1024]{1,0:T(8,128)(2,1)S(1)} collective-permute-done((bf16[128,1024]{1,0:T(8,128)(2,1)S(1)}, bf16[128,1024]{1,0:T(8,128)(2,1)S(1)}, u32[]{:S(2)}, u32[]{:S(2)}) %collective-permute-start.7) | collective-permute-done | bytes 262176 | tf_op jit(solution)/shard_map/ppermute | solution.py:23
  16.4 1.6 %collective-permute-start.8 = (bf16[128,512]{1,0:T(8,128)(2,1)S(1)}, bf16[128,512]{1,0:T(8,128)(2,1)S(1)}, u32[]{:S(2)}, u32[]{:S(2)}) collective-permute-start(bf16[128,512]{1,0:T(8,128)(2,1)S(1)} %pad_maximum_fusion.8), channel_id=1, source_target_pairs={{0,2},{1,3},{2,0},{3,1},{4,6},{5,7},{6,4},{7,5},{8,10},{9,11},{10,... | collective-permute-start | bytes 393224 | tf_op jit(solution)/shard_map/ppermute | solution.py:23
  18.0 1.5 %collective-permute-start.3 = (bf16[2,128,512]{2,1,0:T(8,128)(2,1)S(1)}, bf16[2,128,512]{2,1,0:T(8,128)(2,1)S(1)}, u32[]{:S(2)}, u32[]{:S(2)}) collective-permute-start(bf16[2,128,512]{2,1,0:T(8,128)(2,1)S(1)} %collective-permute-done), channel_id=1, source_target_pairs={{0,4},{4,0},{8,12},{12,8},{16,20},{20,16},{24,28},{28,24},{1,5},{5... | collective-permute-start | bytes 786440 | tf_op jit(solution)/shard_map/ppermute | solution.py:23
  19.5 2.7 %collective-permute-done.2 = bf16[2,144,512]{2,1,0:T(8,128)(2,1)S(1)} collective-permute-done((bf16[2,144,512]{2,1,0:T(8,128)(2,1)S(1)}, bf16[2,144,512]{2,1,0:T(8,128)(2,1)S(1)}, u32[]{:S(2)}, u32[]{:S(2)}) %collective-permute-start.2) | collective-permute-done | bytes 294944 | tf_op jit(solution)/shard_map/ppermute | solution.py:23
  23.0 3.4 %collective-permute-done.3 = bf16[2,128,512]{2,1,0:T(8,128)(2,1)S(1)} collective-permute-done((bf16[2,128,512]{2,1,0:T(8,128)(2,1)S(1)}, bf16[2,128,512]{2,1,0:T(8,128)(2,1)S(1)}, u32[]{:S(2)}, u32[]{:S(2)}) %collective-permute-start.3) | collective-permute-done | bytes 262176 | tf_op jit(solution)/shard_map/ppermute | solution.py:23
  26.7 1.6 %collective-permute-start.12 = (bf16[128,512]{1,0:T(8,128)(2,1)S(1)}, bf16[128,512]{1,0:T(8,128)(2,1)S(1)}, u32[]{:S(2)}, u32[]{:S(2)}) collective-permute-start(bf16[128,512]{1,0:T(8,128)(2,1)S(1)} %pad_maximum_fusion.10), channel_id=1, source_target_pairs={{0,4},{4,0},{8,12},{12,8},{16,20},{20,16},{24,28},{28,24},{1,5},{5... | collective-permute-start | bytes 393224 | tf_op jit(solution)/shard_map/ppermute | solution.py:23
  28.8 0.6 shard_map.59
  29.5 1.6 %collective-permute-start.10 = (f16[528,256]{1,0:T(8,128)(2,1)S(1)}, f16[528,256]{1,0:T(8,128)(2,1)S(1)}, u32[]{:S(2)}, u32[]{:S(2)}) collective-permute-start(f16[528,256]{1,0:T(8,128)(2,1)S(1)} %convert_element_type.75), channel_id=1, source_target_pairs={{0,8},{4,12},{8,0},{12,4},{16,24},{20,28},{24,16},{28,20},{1,9},{5... | collective-permute-start | bytes 811016 | tf_op jit(solution)/shard_map/ppermute | solution.py:23
  31.1 1.6 %collective-permute-start.11 = (bf16[128,512]{1,0:T(8,128)(2,1)S(1)}, bf16[128,512]{1,0:T(8,128)(2,1)S(1)}, u32[]{:S(2)}, u32[]{:S(2)}) collective-permute-start(bf16[128,512]{1,0:T(8,128)(2,1)S(1)} %pad_maximum_fusion.9), channel_id=1, source_target_pairs={{0,2},{1,3},{2,0},{3,1},{4,6},{5,7},{6,4},{7,5},{8,10},{9,11},{10,... | collective-permute-start | bytes 393224 | tf_op jit(solution)/shard_map/ppermute | solution.py:23
  32.7 1.4 %collective-permute-start.13 = (bf16[128,512]{1,0:T(8,128)(2,1)S(1)}, bf16[128,512]{1,0:T(8,128)(2,1)S(1)}, u32[]{:S(2)}, u32[]{:S(2)}) collective-permute-start(bf16[128,512]{1,0:T(8,128)(2,1)S(1)} %collective-permute-done.12), channel_id=1, source_target_pairs={{0,2},{1,3},{2,0},{3,1},{4,6},{5,7},{6,4},{7,5},{8,10},{9,11},{10,... | collective-permute-start | bytes 393224 | tf_op jit(solution)/shard_map/ppermute | solution.py:23
  34.1 3.5 %collective-permute-done.11 = bf16[128,512]{1,0:T(8,128)(2,1)S(1)} collective-permute-done((bf16[128,512]{1,0:T(8,128)(2,1)S(1)}, bf16[128,512]{1,0:T(8,128)(2,1)S(1)}, u32[]{:S(2)}, u32[]{:S(2)}) %collective-permute-start.11) | collective-permute-done | bytes 131104 | tf_op jit(solution)/shard_map/ppermute | solution.py:23
  37.6 1.8 %collective-permute-done.13 = bf16[128,512]{1,0:T(8,128)(2,1)S(1)} collective-permute-done((bf16[128,512]{1,0:T(8,128)(2,1)S(1)}, bf16[128,512]{1,0:T(8,128)(2,1)S(1)}, u32[]{:S(2)}, u32[]{:S(2)}) %collective-permute-start.13) | collective-permute-done | bytes 131104 | tf_op jit(solution)/shard_map/ppermute | solution.py:23
  39.5 0.7 shard_map.60
  40.2 0.5 collective-permute-start.15
  40.7 0.6 collective-permute-done.14.refs_3_
  41.4 0.7 shard_map.62
  42.1 0.4 collective-permute-start.16
  42.5 9.8 %collective-permute-done.15 = f16[528,256]{1,0:T(8,128)(2,1)S(1)} collective-permute-done((f16[528,256]{1,0:T(8,128)(2,1)S(1)}, f16[528,256]{1,0:T(8,128)(2,1)S(1)}, u32[]{:S(2)}, u32[]{:S(2)}) %collective-permute-start.15) | collective-permute-done | bytes 270368 | tf_op jit(solution)/shard_map/ppermute | solution.py:23
  52.4 0.5 shard_map.61.refs_0_
  52.8 4.5 %collective-permute-done.16 = f16[528,256]{1,0:T(8,128)(2,1)S(1)} collective-permute-done((f16[528,256]{1,0:T(8,128)(2,1)S(1)}, f16[528,256]{1,0:T(8,128)(2,1)S(1)}, u32[]{:S(2)}, u32[]{:S(2)}) %collective-permute-start.16) | collective-permute-done | bytes 270368 | tf_op jit(solution)/shard_map/ppermute | solution.py:23
  57.5 1.3 %collective-permute-start.17 = (bf16[256,256]{1,0:T(8,128)(2,1)S(1)}, bf16[256,256]{1,0:T(8,128)(2,1)S(1)}, u32[]{:S(2)}, u32[]{:S(2)}) collective-permute-start(bf16[256,256]{1,0:T(8,128)(2,1)S(1)} %shard_map.63), channel_id=1, source_target_pairs={{0,4},{4,0},{8,12},{12,8},{16,20},{20,16},{24,28},{28,24},{1,5},{5... | collective-permute-start | bytes 393224 | tf_op jit(solution)/shard_map/ppermute | solution.py:23
  58.8 1.5 %collective-permute-start.22 = (bf16[256,256]{1,0:T(8,128)(2,1)S(1)}, bf16[256,256]{1,0:T(8,128)(2,1)S(1)}, u32[]{:S(2)}, u32[]{:S(2)}) collective-permute-start(bf16[256,256]{1,0:T(8,128)(2,1)S(1)} %shard_map.63), channel_id=1, source_target_pairs={{0,2},{1,3},{2,0},{3,1},{4,6},{5,7},{6,4},{7,5},{8,10},{9,11},{10,... | collective-permute-start | bytes 393224 | tf_op jit(solution)/shard_map/ppermute | solution.py:23
  60.3 2.3 %collective-permute-done.17 = bf16[256,256]{1,0:T(8,128)(2,1)S(1)} collective-permute-done((bf16[256,256]{1,0:T(8,128)(2,1)S(1)}, bf16[256,256]{1,0:T(8,128)(2,1)S(1)}, u32[]{:S(2)}, u32[]{:S(2)}) %collective-permute-start.17) | collective-permute-done | bytes 131104 | tf_op jit(solution)/shard_map/ppermute | solution.py:23
  63.0 0.7 collective-permute-done.22
  63.8 1.6 %collective-permute-start.23 = (bf16[256,256]{1,0:T(8,128)(2,1)S(1)}, bf16[256,256]{1,0:T(8,128)(2,1)S(1)}, u32[]{:S(2)}, u32[]{:S(2)}) collective-permute-start(bf16[256,256]{1,0:T(8,128)(2,1)S(1)} %fusion.4), channel_id=1, source_target_pairs={{0,2},{1,3},{2,0},{3,1},{4,6},{5,7},{6,4},{7,5},{8,10},{9,11},{10,... | collective-permute-start | bytes 393224 | tf_op jit(solution)/shard_map/ppermute | solution.py:23
  65.6 2.4 %collective-permute-done.18 = bf16[256,256]{1,0:T(8,128)(2,1)S(1)} collective-permute-done((bf16[256,256]{1,0:T(8,128)(2,1)S(1)}, bf16[256,256]{1,0:T(8,128)(2,1)S(1)}, u32[]{:S(2)}, u32[]{:S(2)}) %collective-permute-start.18) | collective-permute-done | bytes 131104 | tf_op jit(solution)/shard_map/ppermute | solution.py:23
  68.3 0.6 collective-permute-done.23
  68.9 0.3 fusion.9
  69.2 1.6 %collective-permute-start.25 = (bf16[256,256]{1,0:T(8,128)(2,1)S(1)}, bf16[256,256]{1,0:T(8,128)(2,1)S(1)}, u32[]{:S(2)}, u32[]{:S(2)}) collective-permute-start(bf16[256,256]{1,0:T(8,128)(2,1)S(1)} %fusion.5), channel_id=1, source_target_pairs={{0,2},{1,3},{2,0},{3,1},{4,6},{5,7},{6,4},{7,5},{8,10},{9,11},{10,... | collective-permute-start | bytes 393224 | tf_op jit(solution)/shard_map/ppermute | solution.py:23
  71.0 4.0 %collective-permute-done.19 = bf16[256,256]{1,0:T(8,128)(2,1)S(1)} collective-permute-done((bf16[256,256]{1,0:T(8,128)(2,1)S(1)}, bf16[256,256]{1,0:T(8,128)(2,1)S(1)}, u32[]{:S(2)}, u32[]{:S(2)}) %collective-permute-start.19) | collective-permute-done | bytes 131104 | tf_op jit(solution)/shard_map/ppermute | solution.py:23
  75.2 1.6 %collective-permute-start.20 = (bf16[256,256]{1,0:T(8,128)(2,1)S(1)}, bf16[256,256]{1,0:T(8,128)(2,1)S(1)}, u32[]{:S(2)}, u32[]{:S(2)}) collective-permute-start(bf16[256,256]{1,0:T(8,128)(2,1)S(1)} %fusion.6), channel_id=1, source_target_pairs={{0,2},{1,3},{2,0},{3,1},{4,6},{5,7},{6,4},{7,5},{8,10},{9,11},{10,... | collective-permute-start | bytes 393224 | tf_op jit(solution)/shard_map/ppermute | solution.py:23
  76.9 0.3 fusion.49
  77.1 3.1 %collective-permute-done.20 = bf16[256,256]{1,0:T(8,128)(2,1)S(1)} collective-permute-done((bf16[256,256]{1,0:T(8,128)(2,1)S(1)}, bf16[256,256]{1,0:T(8,128)(2,1)S(1)}, u32[]{:S(2)}, u32[]{:S(2)}) %collective-permute-start.20) | collective-permute-done | bytes 131104 | tf_op jit(solution)/shard_map/ppermute | solution.py:23
  80.4 0.3 fusion.2.refs_0_
  80.6 0.3 fusion.3.refs_1_
  80.9 0.9 %collective-permute-done.21 = bf16[512,256]{1,0:T(8,128)(2,1)S(1)} collective-permute-done((bf16[512,256]{1,0:T(8,128)(2,1)S(1)}, bf16[512,256]{1,0:T(8,128)(2,1)S(1)}, u32[]{:S(2)}, u32[]{:S(2)}) %collective-permute-start.21) | collective-permute-done | bytes 262176 | tf_op jit(solution)/shard_map/ppermute | solution.py:23
  82.0 9.1 %shard_map.64 = f32[1,256]{1,0:T(1,128)S(1)} custom-call(f32[256,256]{1,0:T(8,128)S(1)} %fusion.2.refs_0_, f32[256,256]{1,0:T(8,128)S(1)} %fusion.3.refs_1_, s32[1]{0:T(128)} %bitcast.34.refs_2_, bf16[1024,256]{1,0:T(8,128)(2,1)S(1)} %bitcast.73), custom_call_target="tpu_custom_call" | custom-call | tf_op jit(solution)/shard_map/pallas_call | solution.py:131
  91.3 1.0 %collective-permute-done.27 = f32[1,256]{1,0:T(1,128)S(1)} collective-permute-done((f32[1,256]{1,0:T(1,128)S(1)}, f32[1,256]{1,0:T(1,128)S(1)}, u32[]{:S(2)}, u32[]{:S(2)}) %collective-permute-start.27) | collective-permute-done | bytes 1056 | tf_op jit(solution)/shard_map/ppermute | solution.py:23
  92.3 0.6 add.90
  (85 shorter events, 5.1 us)
Async XLA Ops:
  0.6 7.6 %copy-start.2 = (bf16[128,1024]{1,0:T(8,128)(2,1)S(1)}, bf16[128,1024]{1,0:T(8,128)(2,1)}, u32[]{:S(2)}) copy-start(bf16[128,1024]{1,0:T(8,128)(2,1)} %param.6) | copy-start | bytes 786436
  0.6 7.6 %copy-start.1 = (bf16[128,1024]{1,0:T(8,128)(2,1)S(1)}, bf16[128,1024]{1,0:T(8,128)(2,1)}, u32[]{:S(2)}) copy-start(bf16[128,1024]{1,0:T(8,128)(2,1)} %param.5) | copy-start | bytes 786436
  1.5 8.3 %collective-permute-start.1 = (s32[1,256]{1,0:T(1,128)S(1)}, s32[1,256]{1,0:T(1,128)S(1)}, u32[]{:S(2)}, u32[]{:S(2)}) collective-permute-start(s32[1,256]{1,0:T(1,128)S(1)} %get-tuple-element.35), channel_id=1, source_target_pairs={{0,16},{4,20},{8,24},{12,28},{16,0},{20,4},{24,8},{28,12},{1,17},{... | collective-permute-start | bytes 3080 | tf_op jit(solution)/shard_map/ppermute | solution.py:23
  6.6 6.9 %copy-start.3 = (bf16[128,4096]{1,0:T(8,128)(2,1)S(1)}, bf16[128,4096]{1,0:T(8,128)(2,1)}, u32[]{:S(2)}) copy-start(bf16[128,4096]{1,0:T(8,128)(2,1)} %param.4) | copy-start | bytes 3145732
  6.6 9.3 %collective-permute-start.7 = (bf16[128,1024]{1,0:T(8,128)(2,1)S(1)}, bf16[128,1024]{1,0:T(8,128)(2,1)S(1)}, u32[]{:S(2)}, u32[]{:S(2)}) collective-permute-start(bf16[128,1024]{1,0:T(8,128)(2,1)S(1)} %pad_maximum_fusion.5), channel_id=1, source_target_pairs={{0,4},{4,0},{8,12},{12,8},{16,20},{20,16},{24,28},{28,24},{1,5},{5... | collective-permute-start | bytes 786440 | tf_op jit(solution)/shard_map/ppermute | solution.py:23
  8.3 9.8 %collective-permute-start = (bf16[2,128,512]{2,1,0:T(8,128)(2,1)S(1)}, bf16[2,128,512]{2,1,0:T(8,128)(2,1)S(1)}, u32[]{:S(2)}, u32[]{:S(2)}) collective-permute-start(bf16[2,128,512]{2,1,0:T(8,128)(2,1)S(1)} %get-tuple-element.23), channel_id=1, source_target_pairs={{0,2},{1,3},{2,0},{3,1},{4,6},{5,7},{6,4},{7,5},{8,10},{9,11},{10,... | collective-permute-start | bytes 786440 | tf_op jit(solution)/shard_map/ppermute | solution.py:23
  9.8 3.7 %collective-permute-start.5 = (s32[2,256]{1,0:T(2,128)S(1)}, s32[2,256]{1,0:T(2,128)S(1)}, u32[]{:S(2)}, u32[]{:S(2)}) collective-permute-start(s32[2,256]{1,0:T(2,128)S(1)} %get-tuple-element.49), channel_id=1, source_target_pairs={{0,8},{4,12},{8,0},{12,4},{16,24},{20,28},{24,16},{28,20},{1,9},{5... | collective-permute-start | bytes 6152 | tf_op jit(solution)/shard_map/ppermute | solution.py:23
  11.5 10.7 %collective-permute-start.2 = (bf16[2,144,512]{2,1,0:T(8,128)(2,1)S(1)}, bf16[2,144,512]{2,1,0:T(8,128)(2,1)S(1)}, u32[]{:S(2)}, u32[]{:S(2)}) collective-permute-start(bf16[2,144,512]{2,1,0:T(8,128)(2,1)S(1)} %pad_maximum_fusion.4), channel_id=1, source_target_pairs={{0,4},{4,0},{8,12},{12,8},{16,20},{20,16},{24,28},{28,24},{1,5},{5... | collective-permute-start | bytes 884744 | tf_op jit(solution)/shard_map/ppermute | solution.py:23
  14.0 8.8 %collective-permute-start.6 = (bf16[128,512]{1,0:T(8,128)(2,1)S(1)}, bf16[128,512]{1,0:T(8,128)(2,1)S(1)}, u32[]{:S(2)}, u32[]{:S(2)}) collective-permute-start(bf16[128,512]{1,0:T(8,128)(2,1)S(1)} %pad_maximum_fusion.7), channel_id=1, source_target_pairs={{0,2},{1,3},{2,0},{3,1},{4,6},{5,7},{6,4},{7,5},{8,10},{9,11},{10,... | collective-permute-start | bytes 393224 | tf_op jit(solution)/shard_map/ppermute | solution.py:23
  16.4 6.5 %collective-permute-start.8 = (bf16[128,512]{1,0:T(8,128)(2,1)S(1)}, bf16[128,512]{1,0:T(8,128)(2,1)S(1)}, u32[]{:S(2)}, u32[]{:S(2)}) collective-permute-start(bf16[128,512]{1,0:T(8,128)(2,1)S(1)} %pad_maximum_fusion.8), channel_id=1, source_target_pairs={{0,2},{1,3},{2,0},{3,1},{4,6},{5,7},{6,4},{7,5},{8,10},{9,11},{10,... | collective-permute-start | bytes 393224 | tf_op jit(solution)/shard_map/ppermute | solution.py:23
  18.0 8.4 %collective-permute-start.3 = (bf16[2,128,512]{2,1,0:T(8,128)(2,1)S(1)}, bf16[2,128,512]{2,1,0:T(8,128)(2,1)S(1)}, u32[]{:S(2)}, u32[]{:S(2)}) collective-permute-start(bf16[2,128,512]{2,1,0:T(8,128)(2,1)S(1)} %collective-permute-done), channel_id=1, source_target_pairs={{0,4},{4,0},{8,12},{12,8},{16,20},{20,16},{24,28},{28,24},{1,5},{5... | collective-permute-start | bytes 786440 | tf_op jit(solution)/shard_map/ppermute | solution.py:23
  23.0 5.8 %collective-permute-start.9 = (bf16[512,512]{1,0:T(8,128)(2,1)S(1)}, bf16[512,512]{1,0:T(8,128)(2,1)S(1)}, u32[]{:S(2)}, u32[]{:S(2)}) collective-permute-start(bf16[512,512]{1,0:T(8,128)(2,1)S(1)} %pad_maximum_fusion.1.refs_2_), channel_id=1, source_target_pairs={{0,1},{1,0},{2,3},{3,2},{4,5},{5,4},{6,7},{7,6},{8,9},{9,8},{10,11... | collective-permute-start | bytes 1572872 | tf_op jit(solution)/shard_map/ppermute | solution.py:23
  26.6 2.2 %collective-permute-start.4 = (bf16[2,512,256]{2,1,0:T(8,128)(2,1)S(1)}, bf16[2,512,256]{2,1,0:T(8,128)(2,1)S(1)}, u32[]{:S(2)}, u32[]{:S(2)}) collective-permute-start(bf16[2,512,256]{2,1,0:T(8,128)(2,1)S(1)} %get-tuple-element.18), channel_id=1, source_target_pairs={{0,1},{1,0},{2,3},{3,2},{4,5},{5,4},{6,7},{7,6},{8,9},{9,8},{10,11... | collective-permute-start | bytes 1572872 | tf_op jit(solution)/shard_map/ppermute | solution.py:23
  26.7 6.0 %collective-permute-start.12 = (bf16[128,512]{1,0:T(8,128)(2,1)S(1)}, bf16[128,512]{1,0:T(8,128)(2,1)S(1)}, u32[]{:S(2)}, u32[]{:S(2)}) collective-permute-start(bf16[128,512]{1,0:T(8,128)(2,1)S(1)} %pad_maximum_fusion.10), channel_id=1, source_target_pairs={{0,4},{4,0},{8,12},{12,8},{16,20},{20,16},{24,28},{28,24},{1,5},{5... | collective-permute-start | bytes 393224 | tf_op jit(solution)/shard_map/ppermute | solution.py:23
  29.5 9.9 %collective-permute-start.10 = (f16[528,256]{1,0:T(8,128)(2,1)S(1)}, f16[528,256]{1,0:T(8,128)(2,1)S(1)}, u32[]{:S(2)}, u32[]{:S(2)}) collective-permute-start(f16[528,256]{1,0:T(8,128)(2,1)S(1)} %convert_element_type.75), channel_id=1, source_target_pairs={{0,8},{4,12},{8,0},{12,4},{16,24},{20,28},{24,16},{28,20},{1,9},{5... | collective-permute-start | bytes 811016 | tf_op jit(solution)/shard_map/ppermute | solution.py:23
  31.1 6.4 %collective-permute-start.11 = (bf16[128,512]{1,0:T(8,128)(2,1)S(1)}, bf16[128,512]{1,0:T(8,128)(2,1)S(1)}, u32[]{:S(2)}, u32[]{:S(2)}) collective-permute-start(bf16[128,512]{1,0:T(8,128)(2,1)S(1)} %pad_maximum_fusion.9), channel_id=1, source_target_pairs={{0,2},{1,3},{2,0},{3,1},{4,6},{5,7},{6,4},{7,5},{8,10},{9,11},{10,... | collective-permute-start | bytes 393224 | tf_op jit(solution)/shard_map/ppermute | solution.py:23
  32.7 6.6 %collective-permute-start.13 = (bf16[128,512]{1,0:T(8,128)(2,1)S(1)}, bf16[128,512]{1,0:T(8,128)(2,1)S(1)}, u32[]{:S(2)}, u32[]{:S(2)}) collective-permute-start(bf16[128,512]{1,0:T(8,128)(2,1)S(1)} %collective-permute-done.12), channel_id=1, source_target_pairs={{0,2},{1,3},{2,0},{3,1},{4,6},{5,7},{6,4},{7,5},{8,10},{9,11},{10,... | collective-permute-start | bytes 393224 | tf_op jit(solution)/shard_map/ppermute | solution.py:23
  39.4 2.0 %collective-permute-start.14 = (bf16[512,512]{1,0:T(8,128)(2,1)S(1)}, bf16[512,512]{1,0:T(8,128)(2,1)S(1)}, u32[]{:S(2)}, u32[]{:S(2)}) collective-permute-start(bf16[512,512]{1,0:T(8,128)(2,1)S(1)} %pad_maximum_fusion.2.refs_2_), channel_id=1, source_target_pairs={{0,1},{1,0},{2,3},{3,2},{4,5},{5,4},{6,7},{7,6},{8,9},{9,8},{10,11... | collective-permute-start | bytes 1572872 | tf_op jit(solution)/shard_map/ppermute | solution.py:23
  40.2 12.1 %collective-permute-start.15 = (f16[528,256]{1,0:T(8,128)(2,1)S(1)}, f16[528,256]{1,0:T(8,128)(2,1)S(1)}, u32[]{:S(2)}, u32[]{:S(2)}) collective-permute-start(f16[528,256]{1,0:T(8,128)(2,1)S(1)} %convert_element_type.81), channel_id=1, source_target_pairs={{0,8},{4,12},{8,0},{12,4},{16,24},{20,28},{24,16},{28,20},{1,9},{5... | collective-permute-start | bytes 811016 | tf_op jit(solution)/shard_map/ppermute | solution.py:23
  42.1 15.3 %collective-permute-start.16 = (f16[528,256]{1,0:T(8,128)(2,1)S(1)}, f16[528,256]{1,0:T(8,128)(2,1)S(1)}, u32[]{:S(2)}, u32[]{:S(2)}) collective-permute-start(f16[528,256]{1,0:T(8,128)(2,1)S(1)} %convert_element_type.84), channel_id=1, source_target_pairs={{0,16},{4,20},{8,24},{12,28},{16,0},{20,4},{24,8},{28,12},{1,17},{... | collective-permute-start | bytes 811016 | tf_op jit(solution)/shard_map/ppermute | solution.py:23
  57.5 5.0 %collective-permute-start.17 = (bf16[256,256]{1,0:T(8,128)(2,1)S(1)}, bf16[256,256]{1,0:T(8,128)(2,1)S(1)}, u32[]{:S(2)}, u32[]{:S(2)}) collective-permute-start(bf16[256,256]{1,0:T(8,128)(2,1)S(1)} %shard_map.63), channel_id=1, source_target_pairs={{0,4},{4,0},{8,12},{12,8},{16,20},{20,16},{24,28},{28,24},{1,5},{5... | collective-permute-start | bytes 393224 | tf_op jit(solution)/shard_map/ppermute | solution.py:23
  58.8 5.0 %collective-permute-start.22 = (bf16[256,256]{1,0:T(8,128)(2,1)S(1)}, bf16[256,256]{1,0:T(8,128)(2,1)S(1)}, u32[]{:S(2)}, u32[]{:S(2)}) collective-permute-start(bf16[256,256]{1,0:T(8,128)(2,1)S(1)} %shard_map.63), channel_id=1, source_target_pairs={{0,2},{1,3},{2,0},{3,1},{4,6},{5,7},{6,4},{7,5},{8,10},{9,11},{10,... | collective-permute-start | bytes 393224 | tf_op jit(solution)/shard_map/ppermute | solution.py:23
  62.9 5.0 %collective-permute-start.18 = (bf16[256,256]{1,0:T(8,128)(2,1)S(1)}, bf16[256,256]{1,0:T(8,128)(2,1)S(1)}, u32[]{:S(2)}, u32[]{:S(2)}) collective-permute-start(bf16[256,256]{1,0:T(8,128)(2,1)S(1)} %fusion.4), channel_id=1, source_target_pairs={{0,8},{4,12},{8,0},{12,4},{16,24},{20,28},{24,16},{28,20},{1,9},{5... | collective-permute-start | bytes 393224 | tf_op jit(solution)/shard_map/ppermute | solution.py:23
  63.8 5.0 %collective-permute-start.23 = (bf16[256,256]{1,0:T(8,128)(2,1)S(1)}, bf16[256,256]{1,0:T(8,128)(2,1)S(1)}, u32[]{:S(2)}, u32[]{:S(2)}) collective-permute-start(bf16[256,256]{1,0:T(8,128)(2,1)S(1)} %fusion.4), channel_id=1, source_target_pairs={{0,2},{1,3},{2,0},{3,1},{4,6},{5,7},{6,4},{7,5},{8,10},{9,11},{10,... | collective-permute-start | bytes 393224 | tf_op jit(solution)/shard_map/ppermute | solution.py:23
  68.2 6.8 %collective-permute-start.19 = (bf16[256,256]{1,0:T(8,128)(2,1)S(1)}, bf16[256,256]{1,0:T(8,128)(2,1)S(1)}, u32[]{:S(2)}, u32[]{:S(2)}) collective-permute-start(bf16[256,256]{1,0:T(8,128)(2,1)S(1)} %fusion.5), channel_id=1, source_target_pairs={{0,16},{4,20},{8,24},{12,28},{16,0},{20,4},{24,8},{28,12},{1,17},{... | collective-permute-start | bytes 393224 | tf_op jit(solution)/shard_map/ppermute | solution.py:23
  69.2 7.5 %collective-permute-start.25 = (bf16[256,256]{1,0:T(8,128)(2,1)S(1)}, bf16[256,256]{1,0:T(8,128)(2,1)S(1)}, u32[]{:S(2)}, u32[]{:S(2)}) collective-permute-start(bf16[256,256]{1,0:T(8,128)(2,1)S(1)} %fusion.5), channel_id=1, source_target_pairs={{0,2},{1,3},{2,0},{3,1},{4,6},{5,7},{6,4},{7,5},{8,10},{9,11},{10,... | collective-permute-start | bytes 393224 | tf_op jit(solution)/shard_map/ppermute | solution.py:23
  70.8 9.6 %collective-permute-start.24 = (bf16[512,256]{1,0:T(8,128)(2,1)S(1)}, bf16[512,256]{1,0:T(8,128)(2,1)S(1)}, u32[]{:S(2)}, u32[]{:S(2)}) collective-permute-start(bf16[512,256]{1,0:T(8,128)(2,1)S(1)} %broadcast_select_fusion), channel_id=1, source_target_pairs={{0,1},{1,0},{2,3},{3,2},{4,5},{5,4},{6,7},{7,6},{8,9},{9,8},{10,11... | collective-permute-start | bytes 786440 | tf_op jit(solution)/shard_map/ppermute | solution.py:23
  75.2 5.0 %collective-permute-start.20 = (bf16[256,256]{1,0:T(8,128)(2,1)S(1)}, bf16[256,256]{1,0:T(8,128)(2,1)S(1)}, u32[]{:S(2)}, u32[]{:S(2)}) collective-permute-start(bf16[256,256]{1,0:T(8,128)(2,1)S(1)} %fusion.6), channel_id=1, source_target_pairs={{0,2},{1,3},{2,0},{3,1},{4,6},{5,7},{6,4},{7,5},{8,10},{9,11},{10,... | collective-permute-start | bytes 393224 | tf_op jit(solution)/shard_map/ppermute | solution.py:23
  76.8 3.8 %collective-permute-start.26 = (bf16[512,256]{1,0:T(8,128)(2,1)S(1)}, bf16[512,256]{1,0:T(8,128)(2,1)S(1)}, u32[]{:S(2)}, u32[]{:S(2)}) collective-permute-start(bf16[512,256]{1,0:T(8,128)(2,1)S(1)} %maximum_bitcast_fusion.2), channel_id=1, source_target_pairs={{0,1},{1,0},{2,3},{3,2},{4,5},{5,4},{6,7},{7,6},{8,9},{9,8},{10,11... | collective-permute-start | bytes 786440 | tf_op jit(solution)/shard_map/ppermute | solution.py:23
  80.3 1.6 %collective-permute-start.21 = (bf16[512,256]{1,0:T(8,128)(2,1)S(1)}, bf16[512,256]{1,0:T(8,128)(2,1)S(1)}, u32[]{:S(2)}, u32[]{:S(2)}) collective-permute-start(bf16[512,256]{1,0:T(8,128)(2,1)S(1)} %get-tuple-element.30), channel_id=1, source_target_pairs={{0,1},{1,0},{2,3},{3,2},{4,5},{5,4},{6,7},{7,6},{8,9},{9,8},{10,11... | collective-permute-start | bytes 786440 | tf_op jit(solution)/shard_map/ppermute | solution.py:23
  82.0 10.9 %copy-start = (bf16[2,512,256]{2,1,0:T(8,128)(2,1)}, bf16[2,512,256]{2,1,0:T(8,128)(2,1)S(1)}, u32[]{:S(2)}) copy-start(bf16[2,512,256]{2,1,0:T(8,128)(2,1)S(1)} %pad_maximum_fusion.3) | copy-start | bytes 1572868
  91.1 1.2 %collective-permute-start.27 = (f32[1,256]{1,0:T(1,128)S(1)}, f32[1,256]{1,0:T(1,128)S(1)}, u32[]{:S(2)}, u32[]{:S(2)}) collective-permute-start(f32[1,256]{1,0:T(1,128)S(1)} %shard_map.64), channel_id=1, source_target_pairs={{0,1},{1,0},{2,3},{3,2},{4,5},{5,4},{6,7},{7,6},{8,9},{9,8},{10,11... | collective-permute-start | bytes 3080 | tf_op jit(solution)/shard_map/ppermute | solution.py:23

commit v8 on v7

--- a/solution.py
+++ b/solution.py
@@ -239,47 +239,46 @@
             blocks = blocks + [exchange(m, "band", 1 << t) for m in blocks]
         return blocks
 
-    def lists_of(p):
-        return [orders[k] for k in places[p]]
-
-    def gather(own, far):
-        return jnp.concatenate(over_bands(own) + over_bands(far), axis=0)
+    def joined(rows):
+        return jnp.concatenate(over_bands(rows), axis=0)
 
     def over_cores(rows):
-        return [(rows, 0), (exchange(rows, "band", 1), 0)]
-
-    picked = {}
-    for p in reversed(range(parts)):
-        own = pick(blocks_of(p, 0), lists_of(p))
-        if p == parts - 1:
-            far = pick([raw[:, i * width : (i + 1) * width] for i in range(count)], lists_of(p))
-            if parts > 1:
-                orders, far_lists, _, _ = lax.optimization_barrier((orders, far_lists, own, far))
-        else:
-            far = exchange(pick(blocks_of(p, 1), far_lists), "grid", 1)
-        picked[p] = own, far
-
-    go = [count * kept, over_cores(gather(*picked[parts - 1])), []]
-    mixing = jnp.concatenate(mixing + near, axis=1)
-    mixes = [half_of(mixing, place & 1), exchange(half_of(mixing, 1 - (place & 1)), "band", 1)]
-
-    def swap(block, bit):
-        return exchange(sketch("code", block, mixes).astype(f16), "grid", 1 << bit)
+        return [rows, exchange(rows, "band", 1)]
+
+    def shares(matrices):
+        whole = jnp.concatenate(matrices, axis=1)
+        return [half_of(whole, place & 1), exchange(half_of(whole, 1 - (place & 1)), "band", 1)]
+
+    own = pick([block for p in range(parts) for block in blocks_of(p, 0)], [orders[k] for p in places for k in p])
+    far = [None] * parts
+    far[-1] = pick([raw[:, i * width : (i + 1) * width] for i in range(count)], [orders[k] for k in places[-1]])
+    if parts > 1:
+        far[0] = exchange(pick(blocks_of(0, 1), far_lists), "grid", 1)
+    own = over_cores(joined(own))
+    mixes = shares(mixing) + shares(near)
+
+    def block_of(p, rows):
+        columns = count * kept
+        return [columns, [(array, p * columns) for array in own] + [(array, 0) for array in over_cores(rows)], []]
+
+    go = block_of(parts - 1, joined(far[-1]))
 
     if parts > 1:
         stay = None
         for t in range(1, grid_bits):
             pieces = halves(go) if t < grid_bits - 1 else [go]
-            got = [swap(piece, t) for piece in reversed(pieces)]
+            codes = [sketch("code", piece, mixes).astype(f16) for piece in reversed(pieces)]
+            got = exchange(codes[0], "grid", 1 << t)
             if stay is None:
-                got[0], rows = lax.optimization_barrier((got[0], gather(*picked[0])))
-                stay = [count * kept, over_cores(rows), []]
+                codes[1:], rows = lax.optimization_barrier((codes[1:], far[0]))
+                got, rows = lax.optimization_barrier((got, joined(rows)))
+                stay = block_of(0, rows)
             if len(pieces) > 1:
                 stay, go = halves(stay)
-                for block, codes in zip((go, stay), got):
-                    block[2].append((codes.astype(f32), 0))
+                go[2].append((got.astype(f32), 0))
+                stay[2].append((exchange(codes[1], "grid", 1 << t).astype(f32), 0))
         held = sketch("keep", stay, mixes)
-        chosen = sketch("multiply", [kept, [], [(got[0].astype(f32), 0)]], mixes, [(held, 0)])
+        chosen = sketch("multiply", [kept, [], [(got.astype(f32), 0)]], mixes, [(held, 0)])
     else:
         chosen = sketch("multiply", go, mixes)
 

time: 93.1 us -> 91.7 us (0.985)
  waiting for transfers between devices: 44 us -> 42.8 us
  local copies, waits for them, and re-layouts: 1.21 us -> 2.39 us
    unnamed x11 -> x15, local copies, waits for them, and re-layouts: 0.07 us -> 1.36 us
    ppermute x28 -> x29, waiting for transfers between devices: 44 us -> 42.8 us  [exchange(): return lax.ppermute(block, axis, [(i, i ^ delta) for i in range(count)])]
    ppermute x28 -> x29, starting transfers between devices: 28.4 us -> 27.8 us  [exchange(): return lax.ppermute(block, axis, [(i, i ^ delta) for i in range(count)])]
  transfers between devices with their start and end apart: 28 -> 29, of which waited for: 17 -> 18; matrix products, arithmetic and copies ran while one was open for 7% -> 6% of each run, Pallas kernels for 3% -> 3%
where the time goes in v8:
time: 91.7 us; the launch traced here: 91.6 us
  waiting for transfers between devices  42.8 us (47%)
  starting transfers between devices  27.8 us (30%)
  Pallas kernels  11.6 us (13%)
  matrix products  4.25 us (5%)
  local copies, waits for them, and re-layouts  2.39 us (3%)
  other arithmetic  1.43 us (2%)
  between operations  1.22 us (1%)
    ppermute x29, waiting for transfers between devices, exchange(): return lax.ppermute(block, axis, [(i, i ^ delta) for i in range(count)])  42.8 us
    ppermute x29, starting transfers between devices, exchange(): return lax.ppermute(block, axis, [(i, i ^ delta) for i in range(count)])  27.8 us
    pallas_call x1, Pallas kernels, log_pivots(): pl.pallas_call(functools.partial(pivots_kernel, sets, cand is not None),...  9.11 us
    pallas_call x5, Pallas kernels, sketch(): pl.pallas_call(functools.partial(sketch_kernel, mode, columns, [start for...  2.49 us
    dot_general x8, matrix products, pick(): out.append(jnp.dot(block, one_hot, preferred_element_type=f32).astype(bf16))  1.98 us
  transfers between devices with their start and end apart: 29, of which 18 were waited for; matrix products, arithmetic and copies ran while one was open for 6% of the time, Pallas kernels for 3%

profile of v8, /device:TPU:0, one launch (start us, length us, event | category | flops | bytes accessed | tf_op | source)
XLA Modules:
  0.0 91.6 jit_solution(15374447955930070525)
XLA Ops:
  0.7 0.7 copy-done.5
  1.3 4.1 %collective-permute-start.2 = (s32[1,256]{1,0:T(1,128)S(1)}, s32[1,256]{1,0:T(1,128)S(1)}, u32[]{:S(2)}, u32[]{:S(2)}) collective-permute-start(s32[1,256]{1,0:T(1,128)S(1)} %get-tuple-element.37), channel_id=1, source_target_pairs={{0,16},{4,20},{8,24},{12,28},{16,0},{20,4},{24,8},{28,12},{1,17},{... | collective-permute-start | bytes 3080 | tf_op jit(solution)/shard_map/ppermute | solution.py:23
  5.4 1.0 %constant_dynamic-slice_fusion.1 = (bf16[128,512]{1,0:T(8,128)(2,1)S(1)}, bf16[128,512]{1,0:T(8,128)(2,1)S(1)}) fusion(bf16[128,4096]{1,0:T(8,128)(2,1)} %param.4, s32[]{:T(128)S(6)} %select_n.139, s32[]{:T(128)S(6)} %select_n.140), kind=kLoop, calls=%fused_computation.112 | loop fusion | bytes 524296 | tf_op jit(solution)/shard_map/dynamic_slice | solution.py:208
  6.5 1.6 %collective-permute-start.9 = (bf16[128,1024]{1,0:T(8,128)(2,1)S(1)}, bf16[128,1024]{1,0:T(8,128)(2,1)S(1)}, u32[]{:S(2)}, u32[]{:S(2)}) collective-permute-start(bf16[128,1024]{1,0:T(8,128)(2,1)S(1)} %pad_maximum_fusion.4), channel_id=1, source_target_pairs={{0,4},{4,0},{8,12},{12,8},{16,20},{20,16},{24,28},{28,24},{1,5},{5... | collective-permute-start | bytes 786440 | tf_op jit(solution)/shard_map/ppermute | solution.py:23
  8.1 1.6 %collective-permute-start = (bf16[2,128,512]{2,1,0:T(8,128)(2,1)S(1)}, bf16[2,128,512]{2,1,0:T(8,128)(2,1)S(1)}, u32[]{:S(2)}, u32[]{:S(2)}) collective-permute-start(bf16[2,128,512]{2,1,0:T(8,128)(2,1)S(1)} %get-tuple-element.24), channel_id=1, source_target_pairs={{0,2},{1,3},{2,0},{3,1},{4,6},{5,7},{6,4},{7,5},{8,10},{9,11},{10,... | collective-permute-start | bytes 786440 | tf_op jit(solution)/shard_map/ppermute | solution.py:23
  9.7 1.6 %collective-permute-start.6 = (s32[2,256]{1,0:T(2,128)S(1)}, s32[2,256]{1,0:T(2,128)S(1)}, u32[]{:S(2)}, u32[]{:S(2)}) collective-permute-start(s32[2,256]{1,0:T(2,128)S(1)} %get-tuple-element.51), channel_id=1, source_target_pairs={{0,8},{4,12},{8,0},{12,4},{16,24},{20,28},{24,16},{28,20},{1,9},{5... | collective-permute-start | bytes 6152 | tf_op jit(solution)/shard_map/ppermute | solution.py:23
  11.4 1.0 %collective-permute-start.3 = (bf16[2,144,512]{2,1,0:T(8,128)(2,1)S(1)}, bf16[2,144,512]{2,1,0:T(8,128)(2,1)S(1)}, u32[]{:S(2)}, u32[]{:S(2)}) collective-permute-start(bf16[2,144,512]{2,1,0:T(8,128)(2,1)S(1)} %pad_maximum_fusion.2), channel_id=1, source_target_pairs={{0,4},{4,0},{8,12},{12,8},{16,20},{20,16},{24,28},{28,24},{1,5},{5... | collective-permute-start | bytes 884744 | tf_op jit(solution)/shard_map/ppermute | solution.py:23
  12.4 1.0 %collective-permute-done.6 = s32[2,256]{1,0:T(2,128)S(1)} collective-permute-done((s32[2,256]{1,0:T(2,128)S(1)}, s32[2,256]{1,0:T(2,128)S(1)}, u32[]{:S(2)}, u32[]{:S(2)}) %collective-permute-start.6) | collective-permute-done | bytes 2080 | tf_op jit(solution)/shard_map/ppermute | solution.py:23
  14.4 0.6 collective-permute-start.7
  15.0 0.8 collective-permute-done.9
  16.3 1.6 %collective-permute-start.10 = (bf16[128,512]{1,0:T(8,128)(2,1)S(1)}, bf16[128,512]{1,0:T(8,128)(2,1)S(1)}, u32[]{:S(2)}, u32[]{:S(2)}) collective-permute-start(bf16[128,512]{1,0:T(8,128)(2,1)S(1)} %pad_maximum_fusion.8), channel_id=1, source_target_pairs={{0,2},{1,3},{2,0},{3,1},{4,6},{5,7},{6,4},{7,5},{8,10},{9,11},{10,... | collective-permute-start | bytes 393224 | tf_op jit(solution)/shard_map/ppermute | solution.py:23
  18.0 1.6 %collective-permute-start.4 = (bf16[2,128,512]{2,1,0:T(8,128)(2,1)S(1)}, bf16[2,128,512]{2,1,0:T(8,128)(2,1)S(1)}, u32[]{:S(2)}, u32[]{:S(2)}) collective-permute-start(bf16[2,128,512]{2,1,0:T(8,128)(2,1)S(1)} %collective-permute-done), channel_id=1, source_target_pairs={{0,4},{4,0},{8,12},{12,8},{16,20},{20,16},{24,28},{28,24},{1,5},{5... | collective-permute-start | bytes 786440 | tf_op jit(solution)/shard_map/ppermute | solution.py:23
  19.6 3.1 %collective-permute-done.7 = bf16[128,1024]{1,0:T(8,128)(2,1)S(1)} collective-permute-done((bf16[128,1024]{1,0:T(8,128)(2,1)S(1)}, bf16[128,1024]{1,0:T(8,128)(2,1)S(1)}, u32[]{:S(2)}, u32[]{:S(2)}) %collective-permute-start.7) | collective-permute-done | bytes 262176 | tf_op jit(solution)/shard_map/ppermute | solution.py:23
  23.0 0.6 copy-done.1
  23.8 0.3 collective-permute-done.10
  24.1 0.3 collective-permute-start.11
  24.4 2.3 %collective-permute-done.4 = bf16[2,128,512]{2,1,0:T(8,128)(2,1)S(1)} collective-permute-done((bf16[2,128,512]{2,1,0:T(8,128)(2,1)S(1)}, bf16[2,128,512]{2,1,0:T(8,128)(2,1)S(1)}, u32[]{:S(2)}, u32[]{:S(2)}) %collective-permute-start.4) | collective-permute-done | bytes 262176 | tf_op jit(solution)/shard_map/ppermute | solution.py:23
  27.1 1.6 %collective-permute-start.13 = (bf16[128,512]{1,0:T(8,128)(2,1)S(1)}, bf16[128,512]{1,0:T(8,128)(2,1)S(1)}, u32[]{:S(2)}, u32[]{:S(2)}) collective-permute-start(bf16[128,512]{1,0:T(8,128)(2,1)S(1)} %pad_maximum_fusion.9), channel_id=1, source_target_pairs={{0,4},{4,0},{8,12},{12,8},{16,20},{20,16},{24,28},{28,24},{1,5},{5... | collective-permute-start | bytes 393224 | tf_op jit(solution)/shard_map/ppermute | solution.py:23
  28.7 0.7 shard_map.59
  29.4 1.6 %collective-permute-start.12 = (f16[528,256]{1,0:T(8,128)(2,1)S(1)}, f16[528,256]{1,0:T(8,128)(2,1)S(1)}, u32[]{:S(2)}, u32[]{:S(2)}) collective-permute-start(f16[528,256]{1,0:T(8,128)(2,1)S(1)} %convert_element_type.77), channel_id=1, source_target_pairs={{0,8},{4,12},{8,0},{12,4},{16,24},{20,28},{24,16},{28,20},{1,9},{5... | collective-permute-start | bytes 811016 | tf_op jit(solution)/shard_map/ppermute | solution.py:23
  31.1 0.6 shard_map.60
  31.8 1.3 %collective-permute-done.13 = bf16[128,512]{1,0:T(8,128)(2,1)S(1)} collective-permute-done((bf16[128,512]{1,0:T(8,128)(2,1)S(1)}, bf16[128,512]{1,0:T(8,128)(2,1)S(1)}, u32[]{:S(2)}, u32[]{:S(2)}) %collective-permute-start.13) | collective-permute-done | bytes 131104 | tf_op jit(solution)/shard_map/ppermute | solution.py:23
  33.1 1.0 %collective-permute-start.14 = (bf16[128,512]{1,0:T(8,128)(2,1)S(1)}, bf16[128,512]{1,0:T(8,128)(2,1)S(1)}, u32[]{:S(2)}, u32[]{:S(2)}) collective-permute-start(bf16[128,512]{1,0:T(8,128)(2,1)S(1)} %collective-permute-done.13), channel_id=1, source_target_pairs={{0,2},{1,3},{2,0},{3,1},{4,6},{5,7},{6,4},{7,5},{8,10},{9,11},{10,... | collective-permute-start | bytes 393224 | tf_op jit(solution)/shard_map/ppermute | solution.py:23
  34.1 4.1 %collective-permute-done.14 = bf16[128,512]{1,0:T(8,128)(2,1)S(1)} collective-permute-done((bf16[128,512]{1,0:T(8,128)(2,1)S(1)}, bf16[128,512]{1,0:T(8,128)(2,1)S(1)}, u32[]{:S(2)}, u32[]{:S(2)}) %collective-permute-start.14) | collective-permute-done | bytes 131104 | tf_op jit(solution)/shard_map/ppermute | solution.py:23
  38.3 1.6 %collective-permute-start.16 = (f16[528,256]{1,0:T(8,128)(2,1)S(1)}, f16[528,256]{1,0:T(8,128)(2,1)S(1)}, u32[]{:S(2)}, u32[]{:S(2)}) collective-permute-start(f16[528,256]{1,0:T(8,128)(2,1)S(1)} %convert_element_type.78), channel_id=1, source_target_pairs={{0,8},{4,12},{8,0},{12,4},{16,24},{20,28},{24,16},{28,20},{1,9},{5... | collective-permute-start | bytes 811016 | tf_op jit(solution)/shard_map/ppermute | solution.py:23
  40.0 0.7 shard_map.62
  40.7 0.4 collective-permute-start.17
  41.1 8.7 %collective-permute-done.16 = f16[528,256]{1,0:T(8,128)(2,1)S(1)} collective-permute-done((f16[528,256]{1,0:T(8,128)(2,1)S(1)}, f16[528,256]{1,0:T(8,128)(2,1)S(1)}, u32[]{:S(2)}, u32[]{:S(2)}) %collective-permute-start.16) | collective-permute-done | bytes 270368 | tf_op jit(solution)/shard_map/ppermute | solution.py:23
  49.8 0.5 shard_map.61.refs_0_
  50.3 5.7 %collective-permute-done.17 = f16[528,256]{1,0:T(8,128)(2,1)S(1)} collective-permute-done((f16[528,256]{1,0:T(8,128)(2,1)S(1)}, f16[528,256]{1,0:T(8,128)(2,1)S(1)}, u32[]{:S(2)}, u32[]{:S(2)}) %collective-permute-start.17) | collective-permute-done | bytes 270368 | tf_op jit(solution)/shard_map/ppermute | solution.py:23
  56.2 1.6 %collective-permute-start.18 = (bf16[256,256]{1,0:T(8,128)(2,1)S(1)}, bf16[256,256]{1,0:T(8,128)(2,1)S(1)}, u32[]{:S(2)}, u32[]{:S(2)}) collective-permute-start(bf16[256,256]{1,0:T(8,128)(2,1)S(1)} %shard_map.63), channel_id=1, source_target_pairs={{0,4},{4,0},{8,12},{12,8},{16,20},{20,16},{24,28},{28,24},{1,5},{5... | collective-permute-start | bytes 393224 | tf_op jit(solution)/shard_map/ppermute | solution.py:23
  57.8 1.0 %collective-permute-start.23 = (bf16[256,256]{1,0:T(8,128)(2,1)S(1)}, bf16[256,256]{1,0:T(8,128)(2,1)S(1)}, u32[]{:S(2)}, u32[]{:S(2)}) collective-permute-start(bf16[256,256]{1,0:T(8,128)(2,1)S(1)} %shard_map.63), channel_id=1, source_target_pairs={{0,2},{1,3},{2,0},{3,1},{4,6},{5,7},{6,4},{7,5},{8,10},{9,11},{10,... | collective-permute-start | bytes 393224 | tf_op jit(solution)/shard_map/ppermute | solution.py:23
  58.8 2.4 %collective-permute-done.18 = bf16[256,256]{1,0:T(8,128)(2,1)S(1)} collective-permute-done((bf16[256,256]{1,0:T(8,128)(2,1)S(1)}, bf16[256,256]{1,0:T(8,128)(2,1)S(1)}, u32[]{:S(2)}, u32[]{:S(2)}) %collective-permute-start.18) | collective-permute-done | bytes 131104 | tf_op jit(solution)/shard_map/ppermute | solution.py:23
  61.7 1.0 %collective-permute-done.23 = bf16[256,256]{1,0:T(8,128)(2,1)S(1)} collective-permute-done((bf16[256,256]{1,0:T(8,128)(2,1)S(1)}, bf16[256,256]{1,0:T(8,128)(2,1)S(1)}, u32[]{:S(2)}, u32[]{:S(2)}) %collective-permute-start.23) | collective-permute-done | bytes 131104 | tf_op jit(solution)/shard_map/ppermute | solution.py:23
  62.8 1.1 %collective-permute-start.24 = (bf16[256,256]{1,0:T(8,128)(2,1)S(1)}, bf16[256,256]{1,0:T(8,128)(2,1)S(1)}, u32[]{:S(2)}, u32[]{:S(2)}) collective-permute-start(bf16[256,256]{1,0:T(8,128)(2,1)S(1)} %fusion.4), channel_id=1, source_target_pairs={{0,2},{1,3},{2,0},{3,1},{4,6},{5,7},{6,4},{7,5},{8,10},{9,11},{10,... | collective-permute-start | bytes 393224 | tf_op jit(solution)/shard_map/ppermute | solution.py:23
  64.1 2.6 %collective-permute-done.19 = bf16[256,256]{1,0:T(8,128)(2,1)S(1)} collective-permute-done((bf16[256,256]{1,0:T(8,128)(2,1)S(1)}, bf16[256,256]{1,0:T(8,128)(2,1)S(1)}, u32[]{:S(2)}, u32[]{:S(2)}) %collective-permute-start.19) | collective-permute-done | bytes 131104 | tf_op jit(solution)/shard_map/ppermute | solution.py:23
  66.8 0.6 collective-permute-start.20
  67.4 1.0 %collective-permute-start.26 = (bf16[256,256]{1,0:T(8,128)(2,1)S(1)}, bf16[256,256]{1,0:T(8,128)(2,1)S(1)}, u32[]{:S(2)}, u32[]{:S(2)}) collective-permute-start(bf16[256,256]{1,0:T(8,128)(2,1)S(1)} %fusion.5), channel_id=1, source_target_pairs={{0,2},{1,3},{2,0},{3,1},{4,6},{5,7},{6,4},{7,5},{8,10},{9,11},{10,... | collective-permute-start | bytes 393224 | tf_op jit(solution)/shard_map/ppermute | solution.py:23
  68.7 0.3 collective-permute-done.24
  69.0 3.4 %collective-permute-done.26 = bf16[256,256]{1,0:T(8,128)(2,1)S(1)} collective-permute-done((bf16[256,256]{1,0:T(8,128)(2,1)S(1)}, bf16[256,256]{1,0:T(8,128)(2,1)S(1)}, u32[]{:S(2)}, u32[]{:S(2)}) %collective-permute-start.26) | collective-permute-done | bytes 131104 | tf_op jit(solution)/shard_map/ppermute | solution.py:23
  72.8 0.9 collective-permute-done.20
  73.9 1.1 %collective-permute-start.21 = (bf16[256,256]{1,0:T(8,128)(2,1)S(1)}, bf16[256,256]{1,0:T(8,128)(2,1)S(1)}, u32[]{:S(2)}, u32[]{:S(2)}) collective-permute-start(bf16[256,256]{1,0:T(8,128)(2,1)S(1)} %fusion.6), channel_id=1, source_target_pairs={{0,2},{1,3},{2,0},{3,1},{4,6},{5,7},{6,4},{7,5},{8,10},{9,11},{10,... | collective-permute-start | bytes 393224 | tf_op jit(solution)/shard_map/ppermute | solution.py:23
  75.1 0.5 collective-permute-start.25
  75.8 3.1 %collective-permute-done.21 = bf16[256,256]{1,0:T(8,128)(2,1)S(1)} collective-permute-done((bf16[256,256]{1,0:T(8,128)(2,1)S(1)}, bf16[256,256]{1,0:T(8,128)(2,1)S(1)}, u32[]{:S(2)}, u32[]{:S(2)}) %collective-permute-start.21) | collective-permute-done | bytes 131104 | tf_op jit(solution)/shard_map/ppermute | solution.py:23
  79.6 0.9 %collective-permute-done.22 = bf16[512,256]{1,0:T(8,128)(2,1)S(1)} collective-permute-done((bf16[512,256]{1,0:T(8,128)(2,1)S(1)}, bf16[512,256]{1,0:T(8,128)(2,1)S(1)}, u32[]{:S(2)}, u32[]{:S(2)}) %collective-permute-start.22) | collective-permute-done | bytes 262176 | tf_op jit(solution)/shard_map/ppermute | solution.py:23
  80.7 9.1 %shard_map.64 = f32[1,256]{1,0:T(1,128)S(1)} custom-call(f32[256,256]{1,0:T(8,128)S(1)} %fusion.2.refs_0_, f32[256,256]{1,0:T(8,128)S(1)} %fusion.3.refs_1_, s32[1]{0:T(128)} %bitcast.34.refs_2_, bf16[1024,256]{1,0:T(8,128)(2,1)S(1)} %bitcast.73), custom_call_target="tpu_custom_call" | custom-call | tf_op jit(solution)/shard_map/pallas_call | solution.py:131
  90.0 1.0 %collective-permute-done.28 = f32[1,256]{1,0:T(1,128)S(1)} collective-permute-done((f32[1,256]{1,0:T(1,128)S(1)}, f32[1,256]{1,0:T(1,128)S(1)}, u32[]{:S(2)}, u32[]{:S(2)}) %collective-permute-start.28) | collective-permute-done | bytes 1056 | tf_op jit(solution)/shard_map/ppermute | solution.py:23
  91.0 0.6 add.88
  (90 shorter events, 6.0 us)
Async XLA Ops:
  0.6 0.7 copy-start.5
  1.3 8.3 %collective-permute-start.2 = (s32[1,256]{1,0:T(1,128)S(1)}, s32[1,256]{1,0:T(1,128)S(1)}, u32[]{:S(2)}, u32[]{:S(2)}) collective-permute-start(s32[1,256]{1,0:T(1,128)S(1)} %get-tuple-element.37), channel_id=1, source_target_pairs={{0,16},{4,20},{8,24},{12,28},{16,0},{20,4},{24,8},{28,12},{1,17},{... | collective-permute-start | bytes 3080 | tf_op jit(solution)/shard_map/ppermute | solution.py:23
  6.4 1.7 %copy-start.2 = (bf16[128,1024]{1,0:T(8,128)(2,1)S(1)}, bf16[128,1024]{1,0:T(8,128)(2,1)}, u32[]{:S(2)}) copy-start(bf16[128,1024]{1,0:T(8,128)(2,1)} %param.5) | copy-start | bytes 786436
  6.4 1.6 %copy-start.3 = (bf16[128,1024]{1,0:T(8,128)(2,1)S(1)}, bf16[128,1024]{1,0:T(8,128)(2,1)}, u32[]{:S(2)}) copy-start(bf16[128,1024]{1,0:T(8,128)(2,1)} %param.6) | copy-start | bytes 786436
  6.5 6.9 %copy-start.4 = (bf16[128,4096]{1,0:T(8,128)(2,1)S(1)}, bf16[128,4096]{1,0:T(8,128)(2,1)}, u32[]{:S(2)}) copy-start(bf16[128,4096]{1,0:T(8,128)(2,1)} %param.4) | copy-start | bytes 3145732
  6.5 9.3 %collective-permute-start.9 = (bf16[128,1024]{1,0:T(8,128)(2,1)S(1)}, bf16[128,1024]{1,0:T(8,128)(2,1)S(1)}, u32[]{:S(2)}, u32[]{:S(2)}) collective-permute-start(bf16[128,1024]{1,0:T(8,128)(2,1)S(1)} %pad_maximum_fusion.4), channel_id=1, source_target_pairs={{0,4},{4,0},{8,12},{12,8},{16,20},{20,16},{24,28},{28,24},{1,5},{5... | collective-permute-start | bytes 786440 | tf_op jit(solution)/shard_map/ppermute | solution.py:23
  8.1 9.7 %collective-permute-start = (bf16[2,128,512]{2,1,0:T(8,128)(2,1)S(1)}, bf16[2,128,512]{2,1,0:T(8,128)(2,1)S(1)}, u32[]{:S(2)}, u32[]{:S(2)}) collective-permute-start(bf16[2,128,512]{2,1,0:T(8,128)(2,1)S(1)} %get-tuple-element.24), channel_id=1, source_target_pairs={{0,2},{1,3},{2,0},{3,1},{4,6},{5,7},{6,4},{7,5},{8,10},{9,11},{10,... | collective-permute-start | bytes 786440 | tf_op jit(solution)/shard_map/ppermute | solution.py:23
  9.7 3.7 %collective-permute-start.6 = (s32[2,256]{1,0:T(2,128)S(1)}, s32[2,256]{1,0:T(2,128)S(1)}, u32[]{:S(2)}, u32[]{:S(2)}) collective-permute-start(s32[2,256]{1,0:T(2,128)S(1)} %get-tuple-element.51), channel_id=1, source_target_pairs={{0,8},{4,12},{8,0},{12,4},{16,24},{20,28},{24,16},{28,20},{1,9},{5... | collective-permute-start | bytes 6152 | tf_op jit(solution)/shard_map/ppermute | solution.py:23
  11.4 11.4 %collective-permute-start.3 = (bf16[2,144,512]{2,1,0:T(8,128)(2,1)S(1)}, bf16[2,144,512]{2,1,0:T(8,128)(2,1)S(1)}, u32[]{:S(2)}, u32[]{:S(2)}) collective-permute-start(bf16[2,144,512]{2,1,0:T(8,128)(2,1)S(1)} %pad_maximum_fusion.2), channel_id=1, source_target_pairs={{0,4},{4,0},{8,12},{12,8},{16,20},{20,16},{24,28},{28,24},{1,5},{5... | collective-permute-start | bytes 884744 | tf_op jit(solution)/shard_map/ppermute | solution.py:23
  14.4 8.3 %collective-permute-start.7 = (bf16[128,1024]{1,0:T(8,128)(2,1)S(1)}, bf16[128,1024]{1,0:T(8,128)(2,1)S(1)}, u32[]{:S(2)}, u32[]{:S(2)}) collective-permute-start(bf16[128,1024]{1,0:T(8,128)(2,1)S(1)} %pad_maximum_fusion.3), channel_id=1, source_target_pairs={{0,2},{1,3},{2,0},{3,1},{4,6},{5,7},{6,4},{7,5},{8,10},{9,11},{10,... | collective-permute-start | bytes 786440 | tf_op jit(solution)/shard_map/ppermute | solution.py:23
  16.3 7.8 %collective-permute-start.10 = (bf16[128,512]{1,0:T(8,128)(2,1)S(1)}, bf16[128,512]{1,0:T(8,128)(2,1)S(1)}, u32[]{:S(2)}, u32[]{:S(2)}) collective-permute-start(bf16[128,512]{1,0:T(8,128)(2,1)S(1)} %pad_maximum_fusion.8), channel_id=1, source_target_pairs={{0,2},{1,3},{2,0},{3,1},{4,6},{5,7},{6,4},{7,5},{8,10},{9,11},{10,... | collective-permute-start | bytes 393224 | tf_op jit(solution)/shard_map/ppermute | solution.py:23
  17.9 10.8 %collective-permute-start.1 = (bf16[2,256,256]{2,1,0:T(8,128)(2,1)S(1)}, bf16[2,256,256]{2,1,0:T(8,128)(2,1)S(1)}, u32[]{:S(2)}, u32[]{:S(2)}) collective-permute-start(bf16[2,256,256]{2,1,0:T(8,128)(2,1)S(1)} %get-tuple-element.22), channel_id=1, source_target_pairs={{0,1},{1,0},{2,3},{3,2},{4,5},{5,4},{6,7},{7,6},{8,9},{9,8},{10,11... | collective-permute-start | bytes 786440 | tf_op jit(solution)/shard_map/ppermute | solution.py:23
  18.0 8.7 %collective-permute-start.4 = (bf16[2,128,512]{2,1,0:T(8,128)(2,1)S(1)}, bf16[2,128,512]{2,1,0:T(8,128)(2,1)S(1)}, u32[]{:S(2)}, u32[]{:S(2)}) collective-permute-start(bf16[2,128,512]{2,1,0:T(8,128)(2,1)S(1)} %collective-permute-done), channel_id=1, source_target_pairs={{0,4},{4,0},{8,12},{12,8},{16,20},{20,16},{24,28},{28,24},{1,5},{5... | collective-permute-start | bytes 786440 | tf_op jit(solution)/shard_map/ppermute | solution.py:23
  22.8 6.0 %collective-permute-start.8 = (bf16[256,1024]{1,0:T(8,128)(2,1)S(1)}, bf16[256,1024]{1,0:T(8,128)(2,1)S(1)}, u32[]{:S(2)}, u32[]{:S(2)}) collective-permute-start(bf16[256,1024]{1,0:T(8,128)(2,1)S(1)} %pad_maximum_fusion.refs_4_), channel_id=1, source_target_pairs={{0,1},{1,0},{2,3},{3,2},{4,5},{5,4},{6,7},{7,6},{8,9},{9,8},{10,11... | collective-permute-start | bytes 1572872 | tf_op jit(solution)/shard_map/ppermute | solution.py:23
  22.8 0.7 copy-start.1
  23.8 2.9 %slice-start = ((bf16[2,144,512]{2,1,0:T(8,128)(2,1)}), bf16[2,128,512]{2,1,0:T(8,128)(2,1)S(1)}, s32[]{:S(2)}) async-start(bf16[2,144,512]{2,1,0:T(8,128)(2,1)} %copy-done.1), calls=%async_computation | async-start | bytes 524288 | tf_op jit(solution)/shard_map/slice | solution.py:229
  24.1 4.6 %collective-permute-start.11 = (bf16[256,512]{1,0:T(8,128)(2,1)S(1)}, bf16[256,512]{1,0:T(8,128)(2,1)S(1)}, u32[]{:S(2)}, u32[]{:S(2)}) collective-permute-start(bf16[256,512]{1,0:T(8,128)(2,1)S(1)} %pad_maximum_fusion.5.refs_6_), channel_id=1, source_target_pairs={{0,1},{1,0},{2,3},{3,2},{4,5},{5,4},{6,7},{7,6},{8,9},{9,8},{10,11... | collective-permute-start | bytes 786440 | tf_op jit(solution)/shard_map/ppermute | solution.py:23
  26.8 1.9 %collective-permute-start.5 = (bf16[2,256,256]{2,1,0:T(8,128)(2,1)S(1)}, bf16[2,256,256]{2,1,0:T(8,128)(2,1)S(1)}, u32[]{:S(2)}, u32[]{:S(2)}) collective-permute-start(bf16[2,256,256]{2,1,0:T(8,128)(2,1)S(1)} %get-tuple-element.20), channel_id=1, source_target_pairs={{0,1},{1,0},{2,3},{3,2},{4,5},{5,4},{6,7},{7,6},{8,9},{9,8},{10,11... | collective-permute-start | bytes 786440 | tf_op jit(solution)/shard_map/ppermute | solution.py:23
  27.1 6.0 %collective-permute-start.13 = (bf16[128,512]{1,0:T(8,128)(2,1)S(1)}, bf16[128,512]{1,0:T(8,128)(2,1)S(1)}, u32[]{:S(2)}, u32[]{:S(2)}) collective-permute-start(bf16[128,512]{1,0:T(8,128)(2,1)S(1)} %pad_maximum_fusion.9), channel_id=1, source_target_pairs={{0,4},{4,0},{8,12},{12,8},{16,20},{20,16},{24,28},{28,24},{1,5},{5... | collective-permute-start | bytes 393224 | tf_op jit(solution)/shard_map/ppermute | solution.py:23
  29.4 8.8 %collective-permute-start.12 = (f16[528,256]{1,0:T(8,128)(2,1)S(1)}, f16[528,256]{1,0:T(8,128)(2,1)S(1)}, u32[]{:S(2)}, u32[]{:S(2)}) collective-permute-start(f16[528,256]{1,0:T(8,128)(2,1)S(1)} %convert_element_type.77), channel_id=1, source_target_pairs={{0,8},{4,12},{8,0},{12,4},{16,24},{20,28},{24,16},{28,20},{1,9},{5... | collective-permute-start | bytes 811016 | tf_op jit(solution)/shard_map/ppermute | solution.py:23
  33.1 5.1 %collective-permute-start.14 = (bf16[128,512]{1,0:T(8,128)(2,1)S(1)}, bf16[128,512]{1,0:T(8,128)(2,1)S(1)}, u32[]{:S(2)}, u32[]{:S(2)}) collective-permute-start(bf16[128,512]{1,0:T(8,128)(2,1)S(1)} %collective-permute-done.13), channel_id=1, source_target_pairs={{0,2},{1,3},{2,0},{3,1},{4,6},{5,7},{6,4},{7,5},{8,10},{9,11},{10,... | collective-permute-start | bytes 393224 | tf_op jit(solution)/shard_map/ppermute | solution.py:23
  38.2 1.8 %collective-permute-start.15 = (bf16[256,512]{1,0:T(8,128)(2,1)S(1)}, bf16[256,512]{1,0:T(8,128)(2,1)S(1)}, u32[]{:S(2)}, u32[]{:S(2)}) collective-permute-start(bf16[256,512]{1,0:T(8,128)(2,1)S(1)} %pad_maximum_fusion.6.refs_6_), channel_id=1, source_target_pairs={{0,1},{1,0},{2,3},{3,2},{4,5},{5,4},{6,7},{7,6},{8,9},{9,8},{10,11... | collective-permute-start | bytes 786440 | tf_op jit(solution)/shard_map/ppermute | solution.py:23
  38.3 11.5 %collective-permute-start.16 = (f16[528,256]{1,0:T(8,128)(2,1)S(1)}, f16[528,256]{1,0:T(8,128)(2,1)S(1)}, u32[]{:S(2)}, u32[]{:S(2)}) collective-permute-start(f16[528,256]{1,0:T(8,128)(2,1)S(1)} %convert_element_type.78), channel_id=1, source_target_pairs={{0,8},{4,12},{8,0},{12,4},{16,24},{20,28},{24,16},{28,20},{1,9},{5... | collective-permute-start | bytes 811016 | tf_op jit(solution)/shard_map/ppermute | solution.py:23
  40.7 15.4 %collective-permute-start.17 = (f16[528,256]{1,0:T(8,128)(2,1)S(1)}, f16[528,256]{1,0:T(8,128)(2,1)S(1)}, u32[]{:S(2)}, u32[]{:S(2)}) collective-permute-start(f16[528,256]{1,0:T(8,128)(2,1)S(1)} %convert_element_type.84), channel_id=1, source_target_pairs={{0,16},{4,20},{8,24},{12,28},{16,0},{20,4},{24,8},{28,12},{1,17},{... | collective-permute-start | bytes 811016 | tf_op jit(solution)/shard_map/ppermute | solution.py:23
  56.2 5.0 %collective-permute-start.18 = (bf16[256,256]{1,0:T(8,128)(2,1)S(1)}, bf16[256,256]{1,0:T(8,128)(2,1)S(1)}, u32[]{:S(2)}, u32[]{:S(2)}) collective-permute-start(bf16[256,256]{1,0:T(8,128)(2,1)S(1)} %shard_map.63), channel_id=1, source_target_pairs={{0,4},{4,0},{8,12},{12,8},{16,20},{20,16},{24,28},{28,24},{1,5},{5... | collective-permute-start | bytes 393224 | tf_op jit(solution)/shard_map/ppermute | solution.py:23
  57.8 5.0 %collective-permute-start.23 = (bf16[256,256]{1,0:T(8,128)(2,1)S(1)}, bf16[256,256]{1,0:T(8,128)(2,1)S(1)}, u32[]{:S(2)}, u32[]{:S(2)}) collective-permute-start(bf16[256,256]{1,0:T(8,128)(2,1)S(1)} %shard_map.63), channel_id=1, source_target_pairs={{0,2},{1,3},{2,0},{3,1},{4,6},{5,7},{6,4},{7,5},{8,10},{9,11},{10,... | collective-permute-start | bytes 393224 | tf_op jit(solution)/shard_map/ppermute | solution.py:23
  61.6 5.0 %collective-permute-start.19 = (bf16[256,256]{1,0:T(8,128)(2,1)S(1)}, bf16[256,256]{1,0:T(8,128)(2,1)S(1)}, u32[]{:S(2)}, u32[]{:S(2)}) collective-permute-start(bf16[256,256]{1,0:T(8,128)(2,1)S(1)} %fusion.4), channel_id=1, source_target_pairs={{0,8},{4,12},{8,0},{12,4},{16,24},{20,28},{24,16},{28,20},{1,9},{5... | collective-permute-start | bytes 393224 | tf_op jit(solution)/shard_map/ppermute | solution.py:23
  62.8 6.2 %collective-permute-start.24 = (bf16[256,256]{1,0:T(8,128)(2,1)S(1)}, bf16[256,256]{1,0:T(8,128)(2,1)S(1)}, u32[]{:S(2)}, u32[]{:S(2)}) collective-permute-start(bf16[256,256]{1,0:T(8,128)(2,1)S(1)} %fusion.4), channel_id=1, source_target_pairs={{0,2},{1,3},{2,0},{3,1},{4,6},{5,7},{6,4},{7,5},{8,10},{9,11},{10,... | collective-permute-start | bytes 393224 | tf_op jit(solution)/shard_map/ppermute | solution.py:23
  66.8 6.8 %collective-permute-start.20 = (bf16[256,256]{1,0:T(8,128)(2,1)S(1)}, bf16[256,256]{1,0:T(8,128)(2,1)S(1)}, u32[]{:S(2)}, u32[]{:S(2)}) collective-permute-start(bf16[256,256]{1,0:T(8,128)(2,1)S(1)} %fusion.5), channel_id=1, source_target_pairs={{0,16},{4,20},{8,24},{12,28},{16,0},{20,4},{24,8},{28,12},{1,17},{... | collective-permute-start | bytes 393224 | tf_op jit(solution)/shard_map/ppermute | solution.py:23
  67.4 5.0 %collective-permute-start.26 = (bf16[256,256]{1,0:T(8,128)(2,1)S(1)}, bf16[256,256]{1,0:T(8,128)(2,1)S(1)}, u32[]{:S(2)}, u32[]{:S(2)}) collective-permute-start(bf16[256,256]{1,0:T(8,128)(2,1)S(1)} %fusion.5), channel_id=1, source_target_pairs={{0,2},{1,3},{2,0},{3,1},{4,6},{5,7},{6,4},{7,5},{8,10},{9,11},{10,... | collective-permute-start | bytes 393224 | tf_op jit(solution)/shard_map/ppermute | solution.py:23
  73.9 5.0 %collective-permute-start.21 = (bf16[256,256]{1,0:T(8,128)(2,1)S(1)}, bf16[256,256]{1,0:T(8,128)(2,1)S(1)}, u32[]{:S(2)}, u32[]{:S(2)}) collective-permute-start(bf16[256,256]{1,0:T(8,128)(2,1)S(1)} %fusion.6), channel_id=1, source_target_pairs={{0,2},{1,3},{2,0},{3,1},{4,6},{5,7},{6,4},{7,5},{8,10},{9,11},{10,... | collective-permute-start | bytes 393224 | tf_op jit(solution)/shard_map/ppermute | solution.py:23
  75.0 4.1 %collective-permute-start.27 = (bf16[512,256]{1,0:T(8,128)(2,1)S(1)}, bf16[512,256]{1,0:T(8,128)(2,1)S(1)}, u32[]{:S(2)}, u32[]{:S(2)}) collective-permute-start(bf16[512,256]{1,0:T(8,128)(2,1)S(1)} %maximum_bitcast_fusion.2), channel_id=1, source_target_pairs={{0,1},{1,0},{2,3},{3,2},{4,5},{5,4},{6,7},{7,6},{8,9},{9,8},{10,11... | collective-permute-start | bytes 786440 | tf_op jit(solution)/shard_map/ppermute | solution.py:23
  75.1 4.3 %collective-permute-start.25 = (bf16[512,256]{1,0:T(8,128)(2,1)S(1)}, bf16[512,256]{1,0:T(8,128)(2,1)S(1)}, u32[]{:S(2)}, u32[]{:S(2)}) collective-permute-start(bf16[512,256]{1,0:T(8,128)(2,1)S(1)} %broadcast_select_fusion), channel_id=1, source_target_pairs={{0,1},{1,0},{2,3},{3,2},{4,5},{5,4},{6,7},{7,6},{8,9},{9,8},{10,11... | collective-permute-start | bytes 786440 | tf_op jit(solution)/shard_map/ppermute | solution.py:23
  79.0 1.6 %collective-permute-start.22 = (bf16[512,256]{1,0:T(8,128)(2,1)S(1)}, bf16[512,256]{1,0:T(8,128)(2,1)S(1)}, u32[]{:S(2)}, u32[]{:S(2)}) collective-permute-start(bf16[512,256]{1,0:T(8,128)(2,1)S(1)} %get-tuple-element.32), channel_id=1, source_target_pairs={{0,1},{1,0},{2,3},{3,2},{4,5},{5,4},{6,7},{7,6},{8,9},{9,8},{10,11... | collective-permute-start | bytes 786440 | tf_op jit(solution)/shard_map/ppermute | solution.py:23
  80.7 9.1 %copy-start = (bf16[2,512,256]{2,1,0:T(8,128)(2,1)}, bf16[2,512,256]{2,1,0:T(8,128)(2,1)S(1)}, u32[]{:S(2)}) copy-start(bf16[2,512,256]{2,1,0:T(8,128)(2,1)S(1)} %pad_maximum_fusion.1) | copy-start | bytes 1572868
  89.8 1.2 %collective-permute-start.28 = (f32[1,256]{1,0:T(1,128)S(1)}, f32[1,256]{1,0:T(1,128)S(1)}, u32[]{:S(2)}, u32[]{:S(2)}) collective-permute-start(f32[1,256]{1,0:T(1,128)S(1)} %shard_map.64), channel_id=1, source_target_pairs={{0,1},{1,0},{2,3},{3,2},{4,5},{5,4},{6,7},{7,6},{8,9},{9,8},{10,11... | collective-permute-start | bytes 3080 | tf_op jit(solution)/shard_map/ppermute | solution.py:23

commit v9 on v8

--- a/solution.py
+++ b/solution.py
@@ -48,7 +48,7 @@
 
 
 def eliminate(block, first):
-    width = block.shape[1]
+    width = min(lanes, block.shape[1])
     lane = lax.broadcasted_iota(jnp.int32, (1, width), 1)
     on_diagonal = lax.broadcasted_iota(jnp.int32, (step, width), 1) - lax.broadcasted_iota(
         jnp.int32, (step, width), 0
@@ -57,7 +57,8 @@
     for corner in range(0, block.shape[0], step):
         below = lax.broadcasted_iota(jnp.int32, (block.shape[0], 1), 0)
         start = first + corner
-        columns = [jnp.sum(jnp.where(lane == start + j, block, 0.0), axis=1, keepdims=True) for j in range(step)]
+        near = block[:, :width]
+        columns = [jnp.sum(jnp.where(lane == start + j, near, 0.0), axis=1, keepdims=True) for j in range(step)]
         heads, inverses = [], []
         for j in range(step):
             head = columns[j][j : j + 1, :]
@@ -103,7 +104,7 @@
             first = pl.multiple_of(k * height, height)
             parts = [eliminate(matrix[pl.ds(base + first, height), base:], first) for matrix in work]
             for q, (done, scaled, diagonal) in enumerate(parts):
-                diagonals[q : q + 1, base:] += diagonal
+                diagonals[q : q + 1, base : base + diagonal.shape[1]] += diagonal
                 work[q][base:, base:] -= outer(scaled, done)
             return carry
 
@@ -208,7 +209,9 @@
             lax.dynamic_slice_in_dim(orbitals, (here ^ 2 * k + side) * width, width, axis=1) for k in places[p]
         ]
 
-    raw = exchange(jnp.concatenate(blocks_of(parts - 1, 1), axis=1), "grid", 1)
+    raw = jnp.concatenate(blocks_of(parts - 1, 1), axis=1)
+    raw, orders = lax.optimization_barrier((raw, order[:1]))
+    raw = exchange(raw, "grid", 1)
 
     mixing = [jnp.stack([w_first, w_second])]
     for t in reversed(range(1, band_bits)):
@@ -217,7 +220,6 @@
         mixing = [half_of(m, upper) for m in mixing] + got
     near = mixing[0]
 
-    orders = order[:1]
     for t in reversed(range(2, grid_bits)):
         orders = jnp.stack([orders, exchange(orders, "grid", 1 << t)], axis=1).reshape(-1, kept)
     if parts > 1:

time: 91.7 us -> 90.9 us (level)
  transfers between devices with their start and end apart: 29 -> 29, of which waited for: 18 -> 18; matrix products, arithmetic and copies ran while one was open for 6% -> 5% of each run, Pallas kernels for 3% -> 3%
where the time goes in v9:
time: 90.9 us; the launch traced here: 90.7 us
  waiting for transfers between devices  43.2 us (48%)
  starting transfers between devices  27.4 us (30%)
  Pallas kernels  11.5 us (13%)
  matrix products  4.24 us (5%)
  local copies, waits for them, and re-layouts  1.73 us (2%)
  other arithmetic  1.45 us (2%)
  between operations  1.27 us (1%)
    ppermute x29, waiting for transfers between devices, exchange(): return lax.ppermute(block, axis, [(i, i ^ delta) for i in range(count)])  43.2 us
    ppermute x29, starting transfers between devices, exchange(): return lax.ppermute(block, axis, [(i, i ^ delta) for i in range(count)])  27.4 us
    pallas_call x1, Pallas kernels, log_pivots(): pl.pallas_call(functools.partial(pivots_kernel, sets, cand is not None),...  9 us
    pallas_call x5, Pallas kernels, sketch(): pl.pallas_call(functools.partial(sketch_kernel, mode, columns, [start for...  2.5 us
    dot_general x8, matrix products, pick(): out.append(jnp.dot(block, one_hot, preferred_element_type=f32).astype(bf16))  1.98 us
  transfers between devices with their start and end apart: 29, of which 18 were waited for; matrix products, arithmetic and copies ran while one was open for 5% of the time, Pallas kernels for 3%

profile of v9, /device:TPU:0, one launch (start us, length us, event | category | flops | bytes accessed | tf_op | source)
XLA Modules:
  0.0 90.7 jit_solution(11361012791695873468)
XLA Ops:
  0.7 1.0 %constant_dynamic-slice_fusion.1 = (bf16[128,512]{1,0:T(8,128)(2,1)S(1)}, bf16[128,512]{1,0:T(8,128)(2,1)S(1)}) fusion(bf16[128,4096]{1,0:T(8,128)(2,1)} %param.4, s32[]{:T(128)S(6)} %select_n.135, s32[]{:T(128)S(6)} %select_n.136), kind=kLoop, calls=%fused_computation.118 | loop fusion | bytes 524296 | tf_op jit(solution)/shard_map/dynamic_slice | solution.py:209
  1.8 4.1 %collective-permute-start.2 = (s32[1,256]{1,0:T(1,128)S(1)}, s32[1,256]{1,0:T(1,128)S(1)}, u32[]{:S(2)}, u32[]{:S(2)}) collective-permute-start(s32[1,256]{1,0:T(1,128)S(1)} %get-tuple-element.11), channel_id=1, source_target_pairs={{0,16},{4,20},{8,24},{12,28},{16,0},{20,4},{24,8},{28,12},{1,17},{... | collective-permute-start | bytes 3080 | tf_op jit(solution)/shard_map/ppermute | solution.py:23
  5.9 1.5 %collective-permute-start.9 = (bf16[128,1024]{1,0:T(8,128)(2,1)S(1)}, bf16[128,1024]{1,0:T(8,128)(2,1)S(1)}, u32[]{:S(2)}, u32[]{:S(2)}) collective-permute-start(bf16[128,1024]{1,0:T(8,128)(2,1)S(1)} %pad_maximum_fusion.3), channel_id=1, source_target_pairs={{0,4},{4,0},{8,12},{12,8},{16,20},{20,16},{24,28},{28,24},{1,5},{5... | collective-permute-start | bytes 786440 | tf_op jit(solution)/shard_map/ppermute | solution.py:23
  7.4 1.6 %collective-permute-start = (bf16[2,128,512]{2,1,0:T(8,128)(2,1)S(1)}, bf16[2,128,512]{2,1,0:T(8,128)(2,1)S(1)}, u32[]{:S(2)}, u32[]{:S(2)}) collective-permute-start(bf16[2,128,512]{2,1,0:T(8,128)(2,1)S(1)} %get-tuple-element.28), channel_id=1, source_target_pairs={{0,2},{1,3},{2,0},{3,1},{4,6},{5,7},{6,4},{7,5},{8,10},{9,11},{10,... | collective-permute-start | bytes 786440 | tf_op jit(solution)/shard_map/ppermute | solution.py:23
  9.0 1.6 %collective-permute-start.6 = (s32[2,256]{1,0:T(2,128)S(1)}, s32[2,256]{1,0:T(2,128)S(1)}, u32[]{:S(2)}, u32[]{:S(2)}) collective-permute-start(s32[2,256]{1,0:T(2,128)S(1)} %get-tuple-element.54), channel_id=1, source_target_pairs={{0,8},{4,12},{8,0},{12,4},{16,24},{20,28},{24,16},{28,20},{1,9},{5... | collective-permute-start | bytes 6152 | tf_op jit(solution)/shard_map/ppermute | solution.py:23
  10.7 0.6 collective-permute-start.3
  11.3 1.3 %collective-permute-done.6 = s32[2,256]{1,0:T(2,128)S(1)} collective-permute-done((s32[2,256]{1,0:T(2,128)S(1)}, s32[2,256]{1,0:T(2,128)S(1)}, u32[]{:S(2)}, u32[]{:S(2)}) %collective-permute-start.6) | collective-permute-done | bytes 2080 | tf_op jit(solution)/shard_map/ppermute | solution.py:23
  13.8 0.6 collective-permute-start.7
  14.4 0.7 collective-permute-done.9
  15.6 1.6 %collective-permute-start.10 = (bf16[128,512]{1,0:T(8,128)(2,1)S(1)}, bf16[128,512]{1,0:T(8,128)(2,1)S(1)}, u32[]{:S(2)}, u32[]{:S(2)}) collective-permute-start(bf16[128,512]{1,0:T(8,128)(2,1)S(1)} %pad_maximum_fusion.8), channel_id=1, source_target_pairs={{0,2},{1,3},{2,0},{3,1},{4,6},{5,7},{6,4},{7,5},{8,10},{9,11},{10,... | collective-permute-start | bytes 393224 | tf_op jit(solution)/shard_map/ppermute | solution.py:23
  17.3 1.6 %collective-permute-start.4 = (bf16[2,128,512]{2,1,0:T(8,128)(2,1)S(1)}, bf16[2,128,512]{2,1,0:T(8,128)(2,1)S(1)}, u32[]{:S(2)}, u32[]{:S(2)}) collective-permute-start(bf16[2,128,512]{2,1,0:T(8,128)(2,1)S(1)} %collective-permute-done), channel_id=1, source_target_pairs={{0,4},{4,0},{8,12},{12,8},{16,20},{20,16},{24,28},{28,24},{1,5},{5... | collective-permute-start | bytes 786440 | tf_op jit(solution)/shard_map/ppermute | solution.py:23
  18.9 3.1 %collective-permute-done.7 = bf16[128,1024]{1,0:T(8,128)(2,1)S(1)} collective-permute-done((bf16[128,1024]{1,0:T(8,128)(2,1)S(1)}, bf16[128,1024]{1,0:T(8,128)(2,1)S(1)}, u32[]{:S(2)}, u32[]{:S(2)}) %collective-permute-start.7) | collective-permute-done | bytes 262176 | tf_op jit(solution)/shard_map/ppermute | solution.py:23
  22.3 0.6 copy-done.1
  23.1 0.3 collective-permute-done.10
  23.4 0.3 collective-permute-start.11
  23.7 2.3 %collective-permute-done.4 = bf16[2,128,512]{2,1,0:T(8,128)(2,1)S(1)} collective-permute-done((bf16[2,128,512]{2,1,0:T(8,128)(2,1)S(1)}, bf16[2,128,512]{2,1,0:T(8,128)(2,1)S(1)}, u32[]{:S(2)}, u32[]{:S(2)}) %collective-permute-start.4) | collective-permute-done | bytes 262176 | tf_op jit(solution)/shard_map/ppermute | solution.py:23
  26.4 1.6 %collective-permute-start.13 = (bf16[128,512]{1,0:T(8,128)(2,1)S(1)}, bf16[128,512]{1,0:T(8,128)(2,1)S(1)}, u32[]{:S(2)}, u32[]{:S(2)}) collective-permute-start(bf16[128,512]{1,0:T(8,128)(2,1)S(1)} %pad_maximum_fusion.9), channel_id=1, source_target_pairs={{0,4},{4,0},{8,12},{12,8},{16,20},{20,16},{24,28},{28,24},{1,5},{5... | collective-permute-start | bytes 393224 | tf_op jit(solution)/shard_map/ppermute | solution.py:23
  28.0 0.7 shard_map.59
  28.7 1.6 %collective-permute-start.12 = (f16[528,256]{1,0:T(8,128)(2,1)S(1)}, f16[528,256]{1,0:T(8,128)(2,1)S(1)}, u32[]{:S(2)}, u32[]{:S(2)}) collective-permute-start(f16[528,256]{1,0:T(8,128)(2,1)S(1)} %convert_element_type.77), channel_id=1, source_target_pairs={{0,8},{4,12},{8,0},{12,4},{16,24},{20,28},{24,16},{28,20},{1,9},{5... | collective-permute-start | bytes 811016 | tf_op jit(solution)/shard_map/ppermute | solution.py:23
  30.4 0.6 shard_map.60
  31.1 1.3 %collective-permute-done.13 = bf16[128,512]{1,0:T(8,128)(2,1)S(1)} collective-permute-done((bf16[128,512]{1,0:T(8,128)(2,1)S(1)}, bf16[128,512]{1,0:T(8,128)(2,1)S(1)}, u32[]{:S(2)}, u32[]{:S(2)}) %collective-permute-start.13) | collective-permute-done | bytes 131104 | tf_op jit(solution)/shard_map/ppermute | solution.py:23
  32.4 1.0 %collective-permute-start.14 = (bf16[128,512]{1,0:T(8,128)(2,1)S(1)}, bf16[128,512]{1,0:T(8,128)(2,1)S(1)}, u32[]{:S(2)}, u32[]{:S(2)}) collective-permute-start(bf16[128,512]{1,0:T(8,128)(2,1)S(1)} %collective-permute-done.13), channel_id=1, source_target_pairs={{0,2},{1,3},{2,0},{3,1},{4,6},{5,7},{6,4},{7,5},{8,10},{9,11},{10,... | collective-permute-start | bytes 393224 | tf_op jit(solution)/shard_map/ppermute | solution.py:23
  33.4 4.1 %collective-permute-done.14 = bf16[128,512]{1,0:T(8,128)(2,1)S(1)} collective-permute-done((bf16[128,512]{1,0:T(8,128)(2,1)S(1)}, bf16[128,512]{1,0:T(8,128)(2,1)S(1)}, u32[]{:S(2)}, u32[]{:S(2)}) %collective-permute-start.14) | collective-permute-done | bytes 131104 | tf_op jit(solution)/shard_map/ppermute | solution.py:23
  37.6 1.6 %collective-permute-start.16 = (f16[528,256]{1,0:T(8,128)(2,1)S(1)}, f16[528,256]{1,0:T(8,128)(2,1)S(1)}, u32[]{:S(2)}, u32[]{:S(2)}) collective-permute-start(f16[528,256]{1,0:T(8,128)(2,1)S(1)} %convert_element_type.78), channel_id=1, source_target_pairs={{0,8},{4,12},{8,0},{12,4},{16,24},{20,28},{24,16},{28,20},{1,9},{5... | collective-permute-start | bytes 811016 | tf_op jit(solution)/shard_map/ppermute | solution.py:23
  39.3 0.7 shard_map.62
  40.0 0.6 collective-permute-start.17
  40.6 8.7 %collective-permute-done.16 = f16[528,256]{1,0:T(8,128)(2,1)S(1)} collective-permute-done((f16[528,256]{1,0:T(8,128)(2,1)S(1)}, f16[528,256]{1,0:T(8,128)(2,1)S(1)}, u32[]{:S(2)}, u32[]{:S(2)}) %collective-permute-start.16) | collective-permute-done | bytes 270368 | tf_op jit(solution)/shard_map/ppermute | solution.py:23
  49.3 0.5 shard_map.61.refs_0_
  49.8 5.5 %collective-permute-done.17 = f16[528,256]{1,0:T(8,128)(2,1)S(1)} collective-permute-done((f16[528,256]{1,0:T(8,128)(2,1)S(1)}, f16[528,256]{1,0:T(8,128)(2,1)S(1)}, u32[]{:S(2)}, u32[]{:S(2)}) %collective-permute-start.17) | collective-permute-done | bytes 270368 | tf_op jit(solution)/shard_map/ppermute | solution.py:23
  55.5 1.6 %collective-permute-start.18 = (bf16[256,256]{1,0:T(8,128)(2,1)S(1)}, bf16[256,256]{1,0:T(8,128)(2,1)S(1)}, u32[]{:S(2)}, u32[]{:S(2)}) collective-permute-start(bf16[256,256]{1,0:T(8,128)(2,1)S(1)} %shard_map.63), channel_id=1, source_target_pairs={{0,4},{4,0},{8,12},{12,8},{16,20},{20,16},{24,28},{28,24},{1,5},{5... | collective-permute-start | bytes 393224 | tf_op jit(solution)/shard_map/ppermute | solution.py:23
  57.1 1.0 %collective-permute-start.23 = (bf16[256,256]{1,0:T(8,128)(2,1)S(1)}, bf16[256,256]{1,0:T(8,128)(2,1)S(1)}, u32[]{:S(2)}, u32[]{:S(2)}) collective-permute-start(bf16[256,256]{1,0:T(8,128)(2,1)S(1)} %shard_map.63), channel_id=1, source_target_pairs={{0,2},{1,3},{2,0},{3,1},{4,6},{5,7},{6,4},{7,5},{8,10},{9,11},{10,... | collective-permute-start | bytes 393224 | tf_op jit(solution)/shard_map/ppermute | solution.py:23
  58.1 2.4 %collective-permute-done.18 = bf16[256,256]{1,0:T(8,128)(2,1)S(1)} collective-permute-done((bf16[256,256]{1,0:T(8,128)(2,1)S(1)}, bf16[256,256]{1,0:T(8,128)(2,1)S(1)}, u32[]{:S(2)}, u32[]{:S(2)}) %collective-permute-start.18) | collective-permute-done | bytes 131104 | tf_op jit(solution)/shard_map/ppermute | solution.py:23
  61.0 1.0 %collective-permute-done.23 = bf16[256,256]{1,0:T(8,128)(2,1)S(1)} collective-permute-done((bf16[256,256]{1,0:T(8,128)(2,1)S(1)}, bf16[256,256]{1,0:T(8,128)(2,1)S(1)}, u32[]{:S(2)}, u32[]{:S(2)}) %collective-permute-start.23) | collective-permute-done | bytes 131104 | tf_op jit(solution)/shard_map/ppermute | solution.py:23
  62.1 1.1 %collective-permute-start.24 = (bf16[256,256]{1,0:T(8,128)(2,1)S(1)}, bf16[256,256]{1,0:T(8,128)(2,1)S(1)}, u32[]{:S(2)}, u32[]{:S(2)}) collective-permute-start(bf16[256,256]{1,0:T(8,128)(2,1)S(1)} %fusion.4), channel_id=1, source_target_pairs={{0,2},{1,3},{2,0},{3,1},{4,6},{5,7},{6,4},{7,5},{8,10},{9,11},{10,... | collective-permute-start | bytes 393224 | tf_op jit(solution)/shard_map/ppermute | solution.py:23
  63.4 2.6 %collective-permute-done.19 = bf16[256,256]{1,0:T(8,128)(2,1)S(1)} collective-permute-done((bf16[256,256]{1,0:T(8,128)(2,1)S(1)}, bf16[256,256]{1,0:T(8,128)(2,1)S(1)}, u32[]{:S(2)}, u32[]{:S(2)}) %collective-permute-start.19) | collective-permute-done | bytes 131104 | tf_op jit(solution)/shard_map/ppermute | solution.py:23
  66.2 1.4 %collective-permute-start.26 = (bf16[256,256]{1,0:T(8,128)(2,1)S(1)}, bf16[256,256]{1,0:T(8,128)(2,1)S(1)}, u32[]{:S(2)}, u32[]{:S(2)}) collective-permute-start(bf16[256,256]{1,0:T(8,128)(2,1)S(1)} %fusion.5), channel_id=1, source_target_pairs={{0,2},{1,3},{2,0},{3,1},{4,6},{5,7},{6,4},{7,5},{8,10},{9,11},{10,... | collective-permute-start | bytes 393224 | tf_op jit(solution)/shard_map/ppermute | solution.py:23
  67.8 0.5 collective-permute-done.24
  68.3 3.0 %collective-permute-done.26 = bf16[256,256]{1,0:T(8,128)(2,1)S(1)} collective-permute-done((bf16[256,256]{1,0:T(8,128)(2,1)S(1)}, bf16[256,256]{1,0:T(8,128)(2,1)S(1)}, u32[]{:S(2)}, u32[]{:S(2)}) %collective-permute-start.26) | collective-permute-done | bytes 131104 | tf_op jit(solution)/shard_map/ppermute | solution.py:23
  71.4 0.3 fusion.13
  71.7 1.3 %collective-permute-done.20 = bf16[256,256]{1,0:T(8,128)(2,1)S(1)} collective-permute-done((bf16[256,256]{1,0:T(8,128)(2,1)S(1)}, bf16[256,256]{1,0:T(8,128)(2,1)S(1)}, u32[]{:S(2)}, u32[]{:S(2)}) %collective-permute-start.20) | collective-permute-done | bytes 131104 | tf_op jit(solution)/shard_map/ppermute | solution.py:23
  73.1 1.1 %collective-permute-start.21 = (bf16[256,256]{1,0:T(8,128)(2,1)S(1)}, bf16[256,256]{1,0:T(8,128)(2,1)S(1)}, u32[]{:S(2)}, u32[]{:S(2)}) collective-permute-start(bf16[256,256]{1,0:T(8,128)(2,1)S(1)} %fusion.6), channel_id=1, source_target_pairs={{0,2},{1,3},{2,0},{3,1},{4,6},{5,7},{6,4},{7,5},{8,10},{9,11},{10,... | collective-permute-start | bytes 393224 | tf_op jit(solution)/shard_map/ppermute | solution.py:23
  74.3 0.5 collective-permute-start.25
  75.1 3.1 %collective-permute-done.21 = bf16[256,256]{1,0:T(8,128)(2,1)S(1)} collective-permute-done((bf16[256,256]{1,0:T(8,128)(2,1)S(1)}, bf16[256,256]{1,0:T(8,128)(2,1)S(1)}, u32[]{:S(2)}, u32[]{:S(2)}) %collective-permute-start.21) | collective-permute-done | bytes 131104 | tf_op jit(solution)/shard_map/ppermute | solution.py:23
  78.3 0.3 fusion.3.refs_1_
  78.9 0.9 %collective-permute-done.22 = bf16[512,256]{1,0:T(8,128)(2,1)S(1)} collective-permute-done((bf16[512,256]{1,0:T(8,128)(2,1)S(1)}, bf16[512,256]{1,0:T(8,128)(2,1)S(1)}, u32[]{:S(2)}, u32[]{:S(2)}) %collective-permute-start.22) | collective-permute-done | bytes 262176 | tf_op jit(solution)/shard_map/ppermute | solution.py:23
  79.9 9.0 %shard_map.64 = f32[1,256]{1,0:T(1,128)S(1)} custom-call(f32[256,256]{1,0:T(8,128)S(1)} %fusion.2.refs_0_, f32[256,256]{1,0:T(8,128)S(1)} %fusion.3.refs_1_, s32[1]{0:T(128)} %bitcast.34.refs_2_, bf16[1024,256]{1,0:T(8,128)(2,1)S(1)} %bitcast.73), custom_call_target="tpu_custom_call" | custom-call | tf_op jit(solution)/shard_map/pallas_call | solution.py:132
  89.2 1.0 %collective-permute-done.28 = f32[1,256]{1,0:T(1,128)S(1)} collective-permute-done((f32[1,256]{1,0:T(1,128)S(1)}, f32[1,256]{1,0:T(1,128)S(1)}, u32[]{:S(2)}, u32[]{:S(2)}) %collective-permute-start.28) | collective-permute-done | bytes 1056 | tf_op jit(solution)/shard_map/ppermute | solution.py:23
  90.2 0.6 add.88
  (93 shorter events, 5.6 us)
Async XLA Ops:
  0.7 1.1 %copy-start.5 = (s32[1,4,256]{2,1,0:T(4,128)S(1)}, s32[1,4,256]{2,1,0:T(4,128)}, u32[]{:S(2)}) copy-start(s32[1,4,256]{2,1,0:T(4,128)} %param.7) | copy-start | bytes 12292
  1.7 5.7 %copy-start.2 = (bf16[128,1024]{1,0:T(8,128)(2,1)S(1)}, bf16[128,1024]{1,0:T(8,128)(2,1)}, u32[]{:S(2)}) copy-start(bf16[128,1024]{1,0:T(8,128)(2,1)} %param.5) | copy-start | bytes 786436
  1.7 5.7 %copy-start.3 = (bf16[128,1024]{1,0:T(8,128)(2,1)S(1)}, bf16[128,1024]{1,0:T(8,128)(2,1)}, u32[]{:S(2)}) copy-start(bf16[128,1024]{1,0:T(8,128)(2,1)} %param.6) | copy-start | bytes 786436
  1.7 11.0 %copy-start.4 = (bf16[128,4096]{1,0:T(8,128)(2,1)S(1)}, bf16[128,4096]{1,0:T(8,128)(2,1)}, u32[]{:S(2)}) copy-start(bf16[128,4096]{1,0:T(8,128)(2,1)} %param.4) | copy-start | bytes 3145732
  1.8 7.2 %collective-permute-start.2 = (s32[1,256]{1,0:T(1,128)S(1)}, s32[1,256]{1,0:T(1,128)S(1)}, u32[]{:S(2)}, u32[]{:S(2)}) collective-permute-start(s32[1,256]{1,0:T(1,128)S(1)} %get-tuple-element.11), channel_id=1, source_target_pairs={{0,16},{4,20},{8,24},{12,28},{16,0},{20,4},{24,8},{28,12},{1,17},{... | collective-permute-start | bytes 3080 | tf_op jit(solution)/shard_map/ppermute | solution.py:23
  5.9 9.2 %collective-permute-start.9 = (bf16[128,1024]{1,0:T(8,128)(2,1)S(1)}, bf16[128,1024]{1,0:T(8,128)(2,1)S(1)}, u32[]{:S(2)}, u32[]{:S(2)}) collective-permute-start(bf16[128,1024]{1,0:T(8,128)(2,1)S(1)} %pad_maximum_fusion.3), channel_id=1, source_target_pairs={{0,4},{4,0},{8,12},{12,8},{16,20},{20,16},{24,28},{28,24},{1,5},{5... | collective-permute-start | bytes 786440 | tf_op jit(solution)/shard_map/ppermute | solution.py:23
  7.4 9.7 %collective-permute-start = (bf16[2,128,512]{2,1,0:T(8,128)(2,1)S(1)}, bf16[2,128,512]{2,1,0:T(8,128)(2,1)S(1)}, u32[]{:S(2)}, u32[]{:S(2)}) collective-permute-start(bf16[2,128,512]{2,1,0:T(8,128)(2,1)S(1)} %get-tuple-element.28), channel_id=1, source_target_pairs={{0,2},{1,3},{2,0},{3,1},{4,6},{5,7},{6,4},{7,5},{8,10},{9,11},{10,... | collective-permute-start | bytes 786440 | tf_op jit(solution)/shard_map/ppermute | solution.py:23
  9.0 3.7 %collective-permute-start.6 = (s32[2,256]{1,0:T(2,128)S(1)}, s32[2,256]{1,0:T(2,128)S(1)}, u32[]{:S(2)}, u32[]{:S(2)}) collective-permute-start(s32[2,256]{1,0:T(2,128)S(1)} %get-tuple-element.54), channel_id=1, source_target_pairs={{0,8},{4,12},{8,0},{12,4},{16,24},{20,28},{24,16},{28,20},{1,9},{5... | collective-permute-start | bytes 6152 | tf_op jit(solution)/shard_map/ppermute | solution.py:23
  10.7 11.4 %collective-permute-start.3 = (bf16[2,144,512]{2,1,0:T(8,128)(2,1)S(1)}, bf16[2,144,512]{2,1,0:T(8,128)(2,1)S(1)}, u32[]{:S(2)}, u32[]{:S(2)}) collective-permute-start(bf16[2,144,512]{2,1,0:T(8,128)(2,1)S(1)} %pad_maximum_fusion.2), channel_id=1, source_target_pairs={{0,4},{4,0},{8,12},{12,8},{16,20},{20,16},{24,28},{28,24},{1,5},{5... | collective-permute-start | bytes 884744 | tf_op jit(solution)/shard_map/ppermute | solution.py:23
  13.8 8.2 %collective-permute-start.7 = (bf16[128,1024]{1,0:T(8,128)(2,1)S(1)}, bf16[128,1024]{1,0:T(8,128)(2,1)S(1)}, u32[]{:S(2)}, u32[]{:S(2)}) collective-permute-start(bf16[128,1024]{1,0:T(8,128)(2,1)S(1)} %pad_maximum_fusion.4), channel_id=1, source_target_pairs={{0,2},{1,3},{2,0},{3,1},{4,6},{5,7},{6,4},{7,5},{8,10},{9,11},{10,... | collective-permute-start | bytes 786440 | tf_op jit(solution)/shard_map/ppermute | solution.py:23
  15.6 7.8 %collective-permute-start.10 = (bf16[128,512]{1,0:T(8,128)(2,1)S(1)}, bf16[128,512]{1,0:T(8,128)(2,1)S(1)}, u32[]{:S(2)}, u32[]{:S(2)}) collective-permute-start(bf16[128,512]{1,0:T(8,128)(2,1)S(1)} %pad_maximum_fusion.8), channel_id=1, source_target_pairs={{0,2},{1,3},{2,0},{3,1},{4,6},{5,7},{6,4},{7,5},{8,10},{9,11},{10,... | collective-permute-start | bytes 393224 | tf_op jit(solution)/shard_map/ppermute | solution.py:23
  17.2 10.8 %collective-permute-start.1 = (bf16[2,256,256]{2,1,0:T(8,128)(2,1)S(1)}, bf16[2,256,256]{2,1,0:T(8,128)(2,1)S(1)}, u32[]{:S(2)}, u32[]{:S(2)}) collective-permute-start(bf16[2,256,256]{2,1,0:T(8,128)(2,1)S(1)} %get-tuple-element.26), channel_id=1, source_target_pairs={{0,1},{1,0},{2,3},{3,2},{4,5},{5,4},{6,7},{7,6},{8,9},{9,8},{10,11... | collective-permute-start | bytes 786440 | tf_op jit(solution)/shard_map/ppermute | solution.py:23
  17.3 8.7 %collective-permute-start.4 = (bf16[2,128,512]{2,1,0:T(8,128)(2,1)S(1)}, bf16[2,128,512]{2,1,0:T(8,128)(2,1)S(1)}, u32[]{:S(2)}, u32[]{:S(2)}) collective-permute-start(bf16[2,128,512]{2,1,0:T(8,128)(2,1)S(1)} %collective-permute-done), channel_id=1, source_target_pairs={{0,4},{4,0},{8,12},{12,8},{16,20},{20,16},{24,28},{28,24},{1,5},{5... | collective-permute-start | bytes 786440 | tf_op jit(solution)/shard_map/ppermute | solution.py:23
  22.1 6.0 %collective-permute-start.8 = (bf16[256,1024]{1,0:T(8,128)(2,1)S(1)}, bf16[256,1024]{1,0:T(8,128)(2,1)S(1)}, u32[]{:S(2)}, u32[]{:S(2)}) collective-permute-start(bf16[256,1024]{1,0:T(8,128)(2,1)S(1)} %pad_maximum_fusion.refs_4_), channel_id=1, source_target_pairs={{0,1},{1,0},{2,3},{3,2},{4,5},{5,4},{6,7},{7,6},{8,9},{9,8},{10,11... | collective-permute-start | bytes 1572872 | tf_op jit(solution)/shard_map/ppermute | solution.py:23
  22.1 0.7 copy-start.1
  23.1 2.9 %slice-start = ((bf16[2,144,512]{2,1,0:T(8,128)(2,1)}), bf16[2,128,512]{2,1,0:T(8,128)(2,1)S(1)}, s32[]{:S(2)}) async-start(bf16[2,144,512]{2,1,0:T(8,128)(2,1)} %copy-done.1), calls=%async_computation | async-start | bytes 524288 | tf_op jit(solution)/shard_map/slice | solution.py:231
  23.4 4.6 %collective-permute-start.11 = (bf16[256,512]{1,0:T(8,128)(2,1)S(1)}, bf16[256,512]{1,0:T(8,128)(2,1)S(1)}, u32[]{:S(2)}, u32[]{:S(2)}) collective-permute-start(bf16[256,512]{1,0:T(8,128)(2,1)S(1)} %pad_maximum_fusion.5.refs_6_), channel_id=1, source_target_pairs={{0,1},{1,0},{2,3},{3,2},{4,5},{5,4},{6,7},{7,6},{8,9},{9,8},{10,11... | collective-permute-start | bytes 786440 | tf_op jit(solution)/shard_map/ppermute | solution.py:23
  26.1 1.9 %collective-permute-start.5 = (bf16[2,256,256]{2,1,0:T(8,128)(2,1)S(1)}, bf16[2,256,256]{2,1,0:T(8,128)(2,1)S(1)}, u32[]{:S(2)}, u32[]{:S(2)}) collective-permute-start(bf16[2,256,256]{2,1,0:T(8,128)(2,1)S(1)} %get-tuple-element.24), channel_id=1, source_target_pairs={{0,1},{1,0},{2,3},{3,2},{4,5},{5,4},{6,7},{7,6},{8,9},{9,8},{10,11... | collective-permute-start | bytes 786440 | tf_op jit(solution)/shard_map/ppermute | solution.py:23
  26.4 6.0 %collective-permute-start.13 = (bf16[128,512]{1,0:T(8,128)(2,1)S(1)}, bf16[128,512]{1,0:T(8,128)(2,1)S(1)}, u32[]{:S(2)}, u32[]{:S(2)}) collective-permute-start(bf16[128,512]{1,0:T(8,128)(2,1)S(1)} %pad_maximum_fusion.9), channel_id=1, source_target_pairs={{0,4},{4,0},{8,12},{12,8},{16,20},{20,16},{24,28},{28,24},{1,5},{5... | collective-permute-start | bytes 393224 | tf_op jit(solution)/shard_map/ppermute | solution.py:23
  28.7 8.8 %collective-permute-start.12 = (f16[528,256]{1,0:T(8,128)(2,1)S(1)}, f16[528,256]{1,0:T(8,128)(2,1)S(1)}, u32[]{:S(2)}, u32[]{:S(2)}) collective-permute-start(f16[528,256]{1,0:T(8,128)(2,1)S(1)} %convert_element_type.77), channel_id=1, source_target_pairs={{0,8},{4,12},{8,0},{12,4},{16,24},{20,28},{24,16},{28,20},{1,9},{5... | collective-permute-start | bytes 811016 | tf_op jit(solution)/shard_map/ppermute | solution.py:23
  32.4 5.1 %collective-permute-start.14 = (bf16[128,512]{1,0:T(8,128)(2,1)S(1)}, bf16[128,512]{1,0:T(8,128)(2,1)S(1)}, u32[]{:S(2)}, u32[]{:S(2)}) collective-permute-start(bf16[128,512]{1,0:T(8,128)(2,1)S(1)} %collective-permute-done.13), channel_id=1, source_target_pairs={{0,2},{1,3},{2,0},{3,1},{4,6},{5,7},{6,4},{7,5},{8,10},{9,11},{10,... | collective-permute-start | bytes 393224 | tf_op jit(solution)/shard_map/ppermute | solution.py:23
  37.5 1.8 %collective-permute-start.15 = (bf16[256,512]{1,0:T(8,128)(2,1)S(1)}, bf16[256,512]{1,0:T(8,128)(2,1)S(1)}, u32[]{:S(2)}, u32[]{:S(2)}) collective-permute-start(bf16[256,512]{1,0:T(8,128)(2,1)S(1)} %pad_maximum_fusion.6.refs_6_), channel_id=1, source_target_pairs={{0,1},{1,0},{2,3},{3,2},{4,5},{5,4},{6,7},{7,6},{8,9},{9,8},{10,11... | collective-permute-start | bytes 786440 | tf_op jit(solution)/shard_map/ppermute | solution.py:23
  37.6 11.7 %collective-permute-start.16 = (f16[528,256]{1,0:T(8,128)(2,1)S(1)}, f16[528,256]{1,0:T(8,128)(2,1)S(1)}, u32[]{:S(2)}, u32[]{:S(2)}) collective-permute-start(f16[528,256]{1,0:T(8,128)(2,1)S(1)} %convert_element_type.78), channel_id=1, source_target_pairs={{0,8},{4,12},{8,0},{12,4},{16,24},{20,28},{24,16},{28,20},{1,9},{5... | collective-permute-start | bytes 811016 | tf_op jit(solution)/shard_map/ppermute | solution.py:23
  40.0 15.4 %collective-permute-start.17 = (f16[528,256]{1,0:T(8,128)(2,1)S(1)}, f16[528,256]{1,0:T(8,128)(2,1)S(1)}, u32[]{:S(2)}, u32[]{:S(2)}) collective-permute-start(f16[528,256]{1,0:T(8,128)(2,1)S(1)} %convert_element_type.84), channel_id=1, source_target_pairs={{0,16},{4,20},{8,24},{12,28},{16,0},{20,4},{24,8},{28,12},{1,17},{... | collective-permute-start | bytes 811016 | tf_op jit(solution)/shard_map/ppermute | solution.py:23
  55.5 5.0 %collective-permute-start.18 = (bf16[256,256]{1,0:T(8,128)(2,1)S(1)}, bf16[256,256]{1,0:T(8,128)(2,1)S(1)}, u32[]{:S(2)}, u32[]{:S(2)}) collective-permute-start(bf16[256,256]{1,0:T(8,128)(2,1)S(1)} %shard_map.63), channel_id=1, source_target_pairs={{0,4},{4,0},{8,12},{12,8},{16,20},{20,16},{24,28},{28,24},{1,5},{5... | collective-permute-start | bytes 393224 | tf_op jit(solution)/shard_map/ppermute | solution.py:23
  57.1 5.0 %collective-permute-start.23 = (bf16[256,256]{1,0:T(8,128)(2,1)S(1)}, bf16[256,256]{1,0:T(8,128)(2,1)S(1)}, u32[]{:S(2)}, u32[]{:S(2)}) collective-permute-start(bf16[256,256]{1,0:T(8,128)(2,1)S(1)} %shard_map.63), channel_id=1, source_target_pairs={{0,2},{1,3},{2,0},{3,1},{4,6},{5,7},{6,4},{7,5},{8,10},{9,11},{10,... | collective-permute-start | bytes 393224 | tf_op jit(solution)/shard_map/ppermute | solution.py:23
  60.9 5.0 %collective-permute-start.19 = (bf16[256,256]{1,0:T(8,128)(2,1)S(1)}, bf16[256,256]{1,0:T(8,128)(2,1)S(1)}, u32[]{:S(2)}, u32[]{:S(2)}) collective-permute-start(bf16[256,256]{1,0:T(8,128)(2,1)S(1)} %fusion.4), channel_id=1, source_target_pairs={{0,8},{4,12},{8,0},{12,4},{16,24},{20,28},{24,16},{28,20},{1,9},{5... | collective-permute-start | bytes 393224 | tf_op jit(solution)/shard_map/ppermute | solution.py:23
  62.1 6.2 %collective-permute-start.24 = (bf16[256,256]{1,0:T(8,128)(2,1)S(1)}, bf16[256,256]{1,0:T(8,128)(2,1)S(1)}, u32[]{:S(2)}, u32[]{:S(2)}) collective-permute-start(bf16[256,256]{1,0:T(8,128)(2,1)S(1)} %fusion.4), channel_id=1, source_target_pairs={{0,2},{1,3},{2,0},{3,1},{4,6},{5,7},{6,4},{7,5},{8,10},{9,11},{10,... | collective-permute-start | bytes 393224 | tf_op jit(solution)/shard_map/ppermute | solution.py:23
  66.2 6.8 %collective-permute-start.20 = (bf16[256,256]{1,0:T(8,128)(2,1)S(1)}, bf16[256,256]{1,0:T(8,128)(2,1)S(1)}, u32[]{:S(2)}, u32[]{:S(2)}) collective-permute-start(bf16[256,256]{1,0:T(8,128)(2,1)S(1)} %fusion.5), channel_id=1, source_target_pairs={{0,16},{4,20},{8,24},{12,28},{16,0},{20,4},{24,8},{28,12},{1,17},{... | collective-permute-start | bytes 393224 | tf_op jit(solution)/shard_map/ppermute | solution.py:23
  66.2 5.0 %collective-permute-start.26 = (bf16[256,256]{1,0:T(8,128)(2,1)S(1)}, bf16[256,256]{1,0:T(8,128)(2,1)S(1)}, u32[]{:S(2)}, u32[]{:S(2)}) collective-permute-start(bf16[256,256]{1,0:T(8,128)(2,1)S(1)} %fusion.5), channel_id=1, source_target_pairs={{0,2},{1,3},{2,0},{3,1},{4,6},{5,7},{6,4},{7,5},{8,10},{9,11},{10,... | collective-permute-start | bytes 393224 | tf_op jit(solution)/shard_map/ppermute | solution.py:23
  73.1 5.0 %collective-permute-start.21 = (bf16[256,256]{1,0:T(8,128)(2,1)S(1)}, bf16[256,256]{1,0:T(8,128)(2,1)S(1)}, u32[]{:S(2)}, u32[]{:S(2)}) collective-permute-start(bf16[256,256]{1,0:T(8,128)(2,1)S(1)} %fusion.6), channel_id=1, source_target_pairs={{0,2},{1,3},{2,0},{3,1},{4,6},{5,7},{6,4},{7,5},{8,10},{9,11},{10,... | collective-permute-start | bytes 393224 | tf_op jit(solution)/shard_map/ppermute | solution.py:23
  74.3 4.1 %collective-permute-start.27 = (bf16[512,256]{1,0:T(8,128)(2,1)S(1)}, bf16[512,256]{1,0:T(8,128)(2,1)S(1)}, u32[]{:S(2)}, u32[]{:S(2)}) collective-permute-start(bf16[512,256]{1,0:T(8,128)(2,1)S(1)} %maximum_bitcast_fusion.2), channel_id=1, source_target_pairs={{0,1},{1,0},{2,3},{3,2},{4,5},{5,4},{6,7},{7,6},{8,9},{9,8},{10,11... | collective-permute-start | bytes 786440 | tf_op jit(solution)/shard_map/ppermute | solution.py:23
  74.3 4.3 %collective-permute-start.25 = (bf16[512,256]{1,0:T(8,128)(2,1)S(1)}, bf16[512,256]{1,0:T(8,128)(2,1)S(1)}, u32[]{:S(2)}, u32[]{:S(2)}) collective-permute-start(bf16[512,256]{1,0:T(8,128)(2,1)S(1)} %broadcast_select_fusion), channel_id=1, source_target_pairs={{0,1},{1,0},{2,3},{3,2},{4,5},{5,4},{6,7},{7,6},{8,9},{9,8},{10,11... | collective-permute-start | bytes 786440 | tf_op jit(solution)/shard_map/ppermute | solution.py:23
  78.2 1.6 %collective-permute-start.22 = (bf16[512,256]{1,0:T(8,128)(2,1)S(1)}, bf16[512,256]{1,0:T(8,128)(2,1)S(1)}, u32[]{:S(2)}, u32[]{:S(2)}) collective-permute-start(bf16[512,256]{1,0:T(8,128)(2,1)S(1)} %get-tuple-element.36), channel_id=1, source_target_pairs={{0,1},{1,0},{2,3},{3,2},{4,5},{5,4},{6,7},{7,6},{8,9},{9,8},{10,11... | collective-permute-start | bytes 786440 | tf_op jit(solution)/shard_map/ppermute | solution.py:23
  79.9 9.0 %copy-start = (bf16[2,512,256]{2,1,0:T(8,128)(2,1)}, bf16[2,512,256]{2,1,0:T(8,128)(2,1)S(1)}, u32[]{:S(2)}) copy-start(bf16[2,512,256]{2,1,0:T(8,128)(2,1)S(1)} %pad_maximum_fusion.1) | copy-start | bytes 1572868
  89.0 1.2 %collective-permute-start.28 = (f32[1,256]{1,0:T(1,128)S(1)}, f32[1,256]{1,0:T(1,128)S(1)}, u32[]{:S(2)}, u32[]{:S(2)}) collective-permute-start(f32[1,256]{1,0:T(1,128)S(1)} %shard_map.64), channel_id=1, source_target_pairs={{0,1},{1,0},{2,3},{3,2},{4,5},{5,4},{6,7},{7,6},{8,9},{9,8},{10,11... | collective-permute-start | bytes 3080 | tf_op jit(solution)/shard_map/ppermute | solution.py:23

commit v10 on v9

--- a/solution.py
+++ b/solution.py
@@ -9,7 +9,7 @@
 
 ridge = 0.1
 f32, bf16, f16 = jnp.float32, jnp.bfloat16, jnp.float16
-step, height, lanes = 8, 32, 128
+step, height, lanes = 8, 64, 128
 top, tag_rows = 14.0, 16
 column_dims = (((0,), (0,)), ((), ()))
 
@@ -255,7 +255,9 @@
     far = [None] * parts
     far[-1] = pick([raw[:, i * width : (i + 1) * width] for i in range(count)], [orders[k] for k in places[-1]])
     if parts > 1:
-        far[0] = exchange(pick(blocks_of(0, 1), far_lists), "grid", 1)
+        far[0] = pick(blocks_of(0, 1), far_lists)
+        far[0], near = lax.optimization_barrier((far[0], near))
+        far[0] = exchange(far[0], "grid", 1)
     own = over_cores(joined(own))
     mixes = shares(mixing) + shares(near)
 

time: 90.9 us -> 90.4 us (level)
  no operation moved by 1% of the time
where the time goes in v10:
time: 90.4 us; the launch traced here: 90.2 us
  waiting for transfers between devices  43.5 us (48%)
  starting transfers between devices  27.2 us (30%)
  Pallas kernels  11.3 us (12%)
  matrix products  4.24 us (5%)
  other arithmetic  1.41 us (2%)
  local copies, waits for them, and re-layouts  1.31 us (1%)
  between operations  1.29 us (1%)
    ppermute x29, waiting for transfers between devices, exchange(): return lax.ppermute(block, axis, [(i, i ^ delta) for i in range(count)])  43.5 us
    ppermute x29, starting transfers between devices, exchange(): return lax.ppermute(block, axis, [(i, i ^ delta) for i in range(count)])  27.2 us
    pallas_call x1, Pallas kernels, log_pivots(): pl.pallas_call(functools.partial(pivots_kernel, sets, cand is not None),...  8.8 us
    pallas_call x5, Pallas kernels, sketch(): pl.pallas_call(functools.partial(sketch_kernel, mode, columns, [start for...  2.5 us
    dot_general x8, matrix products, pick(): out.append(jnp.dot(block, one_hot, preferred_element_type=f32).astype(bf16))  1.98 us
  transfers between devices with their start and end apart: 29, of which 18 were waited for; matrix products, arithmetic and copies ran while one was open for 5% of the time, Pallas kernels for 3%

profile of v10, /device:TPU:0, one launch (start us, length us, event | category | flops | bytes accessed | tf_op | source)
XLA Modules:
  0.0 90.2 jit_solution(10501367554832550952)
XLA Ops:
  0.7 1.0 %constant_dynamic-slice_fusion.3 = (bf16[128,512]{1,0:T(8,128)(2,1)S(1)}, bf16[128,512]{1,0:T(8,128)(2,1)S(1)}) fusion(bf16[128,4096]{1,0:T(8,128)(2,1)} %param.4, s32[]{:T(128)S(6)} %select_n.136, s32[]{:T(128)S(6)} %select_n.137), kind=kLoop, calls=%fused_computation.115 | loop fusion | bytes 524296 | tf_op jit(solution)/shard_map/dynamic_slice | solution.py:209
  1.8 4.1 %collective-permute-start.2 = (s32[1,256]{1,0:T(1,128)S(1)}, s32[1,256]{1,0:T(1,128)S(1)}, u32[]{:S(2)}, u32[]{:S(2)}) collective-permute-start(s32[1,256]{1,0:T(1,128)S(1)} %get-tuple-element.14), channel_id=1, source_target_pairs={{0,16},{4,20},{8,24},{12,28},{16,0},{20,4},{24,8},{28,12},{1,17},{... | collective-permute-start | bytes 3080 | tf_op jit(solution)/shard_map/ppermute | solution.py:23
  5.9 1.5 %collective-permute-start.9 = (bf16[128,1024]{1,0:T(8,128)(2,1)S(1)}, bf16[128,1024]{1,0:T(8,128)(2,1)S(1)}, u32[]{:S(2)}, u32[]{:S(2)}) collective-permute-start(bf16[128,1024]{1,0:T(8,128)(2,1)S(1)} %pad_maximum_fusion.3), channel_id=1, source_target_pairs={{0,4},{4,0},{8,12},{12,8},{16,20},{20,16},{24,28},{28,24},{1,5},{5... | collective-permute-start | bytes 786440 | tf_op jit(solution)/shard_map/ppermute | solution.py:23
  7.4 1.6 %collective-permute-start = (bf16[2,128,512]{2,1,0:T(8,128)(2,1)S(1)}, bf16[2,128,512]{2,1,0:T(8,128)(2,1)S(1)}, u32[]{:S(2)}, u32[]{:S(2)}) collective-permute-start(bf16[2,128,512]{2,1,0:T(8,128)(2,1)S(1)} %get-tuple-element.34), channel_id=1, source_target_pairs={{0,2},{1,3},{2,0},{3,1},{4,6},{5,7},{6,4},{7,5},{8,10},{9,11},{10,... | collective-permute-start | bytes 786440 | tf_op jit(solution)/shard_map/ppermute | solution.py:23
  9.0 1.6 %collective-permute-start.6 = (s32[2,256]{1,0:T(2,128)S(1)}, s32[2,256]{1,0:T(2,128)S(1)}, u32[]{:S(2)}, u32[]{:S(2)}) collective-permute-start(s32[2,256]{1,0:T(2,128)S(1)} %get-tuple-element.58), channel_id=1, source_target_pairs={{0,8},{4,12},{8,0},{12,4},{16,24},{20,28},{24,16},{28,20},{1,9},{5... | collective-permute-start | bytes 6152 | tf_op jit(solution)/shard_map/ppermute | solution.py:23
  10.7 0.6 collective-permute-start.3
  11.3 1.3 %collective-permute-done.6 = s32[2,256]{1,0:T(2,128)S(1)} collective-permute-done((s32[2,256]{1,0:T(2,128)S(1)}, s32[2,256]{1,0:T(2,128)S(1)}, u32[]{:S(2)}, u32[]{:S(2)}) %collective-permute-start.6) | collective-permute-done | bytes 2080 | tf_op jit(solution)/shard_map/ppermute | solution.py:23
  13.8 0.6 collective-permute-start.7
  14.4 0.7 collective-permute-done.9
  15.6 1.6 %collective-permute-start.10 = (bf16[128,512]{1,0:T(8,128)(2,1)S(1)}, bf16[128,512]{1,0:T(8,128)(2,1)S(1)}, u32[]{:S(2)}, u32[]{:S(2)}) collective-permute-start(bf16[128,512]{1,0:T(8,128)(2,1)S(1)} %pad_maximum_fusion.9), channel_id=1, source_target_pairs={{0,2},{1,3},{2,0},{3,1},{4,6},{5,7},{6,4},{7,5},{8,10},{9,11},{10,... | collective-permute-start | bytes 393224 | tf_op jit(solution)/shard_map/ppermute | solution.py:23
  17.3 1.6 %collective-permute-start.4 = (bf16[2,128,512]{2,1,0:T(8,128)(2,1)S(1)}, bf16[2,128,512]{2,1,0:T(8,128)(2,1)S(1)}, u32[]{:S(2)}, u32[]{:S(2)}) collective-permute-start(bf16[2,128,512]{2,1,0:T(8,128)(2,1)S(1)} %collective-permute-done), channel_id=1, source_target_pairs={{0,4},{4,0},{8,12},{12,8},{16,20},{20,16},{24,28},{28,24},{1,5},{5... | collective-permute-start | bytes 786440 | tf_op jit(solution)/shard_map/ppermute | solution.py:23
  18.9 3.1 %collective-permute-done.7 = bf16[128,1024]{1,0:T(8,128)(2,1)S(1)} collective-permute-done((bf16[128,1024]{1,0:T(8,128)(2,1)S(1)}, bf16[128,1024]{1,0:T(8,128)(2,1)S(1)}, u32[]{:S(2)}, u32[]{:S(2)}) %collective-permute-start.7) | collective-permute-done | bytes 262176 | tf_op jit(solution)/shard_map/ppermute | solution.py:23
  22.9 0.5 collective-permute-done.10
  23.5 2.5 %collective-permute-done.4 = bf16[2,128,512]{2,1,0:T(8,128)(2,1)S(1)} collective-permute-done((bf16[2,128,512]{2,1,0:T(8,128)(2,1)S(1)}, bf16[2,128,512]{2,1,0:T(8,128)(2,1)S(1)}, u32[]{:S(2)}, u32[]{:S(2)}) %collective-permute-start.4) | collective-permute-done | bytes 262176 | tf_op jit(solution)/shard_map/ppermute | solution.py:23
  26.2 1.6 %collective-permute-start.13 = (bf16[128,512]{1,0:T(8,128)(2,1)S(1)}, bf16[128,512]{1,0:T(8,128)(2,1)S(1)}, u32[]{:S(2)}, u32[]{:S(2)}) collective-permute-start(bf16[128,512]{1,0:T(8,128)(2,1)S(1)} %pad_maximum_fusion.8), channel_id=1, source_target_pairs={{0,4},{4,0},{8,12},{12,8},{16,20},{20,16},{24,28},{28,24},{1,5},{5... | collective-permute-start | bytes 393224 | tf_op jit(solution)/shard_map/ppermute | solution.py:23
  27.8 0.7 shard_map.59
  28.5 1.6 %collective-permute-start.12 = (f16[528,256]{1,0:T(8,128)(2,1)S(1)}, f16[528,256]{1,0:T(8,128)(2,1)S(1)}, u32[]{:S(2)}, u32[]{:S(2)}) collective-permute-start(f16[528,256]{1,0:T(8,128)(2,1)S(1)} %convert_element_type.80), channel_id=1, source_target_pairs={{0,8},{4,12},{8,0},{12,4},{16,24},{20,28},{24,16},{28,20},{1,9},{5... | collective-permute-start | bytes 811016 | tf_op jit(solution)/shard_map/ppermute | solution.py:23
  30.2 0.6 shard_map.60
  30.9 1.3 %collective-permute-done.13 = bf16[128,512]{1,0:T(8,128)(2,1)S(1)} collective-permute-done((bf16[128,512]{1,0:T(8,128)(2,1)S(1)}, bf16[128,512]{1,0:T(8,128)(2,1)S(1)}, u32[]{:S(2)}, u32[]{:S(2)}) %collective-permute-start.13) | collective-permute-done | bytes 131104 | tf_op jit(solution)/shard_map/ppermute | solution.py:23
  32.1 1.0 %collective-permute-start.14 = (bf16[128,512]{1,0:T(8,128)(2,1)S(1)}, bf16[128,512]{1,0:T(8,128)(2,1)S(1)}, u32[]{:S(2)}, u32[]{:S(2)}) collective-permute-start(bf16[128,512]{1,0:T(8,128)(2,1)S(1)} %collective-permute-done.13), channel_id=1, source_target_pairs={{0,2},{1,3},{2,0},{3,1},{4,6},{5,7},{6,4},{7,5},{8,10},{9,11},{10,... | collective-permute-start | bytes 393224 | tf_op jit(solution)/shard_map/ppermute | solution.py:23
  33.2 4.0 %collective-permute-done.14 = bf16[128,512]{1,0:T(8,128)(2,1)S(1)} collective-permute-done((bf16[128,512]{1,0:T(8,128)(2,1)S(1)}, bf16[128,512]{1,0:T(8,128)(2,1)S(1)}, u32[]{:S(2)}, u32[]{:S(2)}) %collective-permute-start.14) | collective-permute-done | bytes 131104 | tf_op jit(solution)/shard_map/ppermute | solution.py:23
  37.3 1.6 %collective-permute-start.16 = (f16[528,256]{1,0:T(8,128)(2,1)S(1)}, f16[528,256]{1,0:T(8,128)(2,1)S(1)}, u32[]{:S(2)}, u32[]{:S(2)}) collective-permute-start(f16[528,256]{1,0:T(8,128)(2,1)S(1)} %convert_element_type.81), channel_id=1, source_target_pairs={{0,8},{4,12},{8,0},{12,4},{16,24},{20,28},{24,16},{28,20},{1,9},{5... | collective-permute-start | bytes 811016 | tf_op jit(solution)/shard_map/ppermute | solution.py:23
  39.0 0.7 shard_map.62
  39.7 0.6 collective-permute-start.17
  40.3 8.7 %collective-permute-done.16 = f16[528,256]{1,0:T(8,128)(2,1)S(1)} collective-permute-done((f16[528,256]{1,0:T(8,128)(2,1)S(1)}, f16[528,256]{1,0:T(8,128)(2,1)S(1)}, u32[]{:S(2)}, u32[]{:S(2)}) %collective-permute-start.16) | collective-permute-done | bytes 270368 | tf_op jit(solution)/shard_map/ppermute | solution.py:23
  49.0 0.5 shard_map.61.refs_0_
  49.5 5.5 %collective-permute-done.17 = f16[528,256]{1,0:T(8,128)(2,1)S(1)} collective-permute-done((f16[528,256]{1,0:T(8,128)(2,1)S(1)}, f16[528,256]{1,0:T(8,128)(2,1)S(1)}, u32[]{:S(2)}, u32[]{:S(2)}) %collective-permute-start.17) | collective-permute-done | bytes 270368 | tf_op jit(solution)/shard_map/ppermute | solution.py:23
  55.2 1.6 %collective-permute-start.18 = (bf16[256,256]{1,0:T(8,128)(2,1)S(1)}, bf16[256,256]{1,0:T(8,128)(2,1)S(1)}, u32[]{:S(2)}, u32[]{:S(2)}) collective-permute-start(bf16[256,256]{1,0:T(8,128)(2,1)S(1)} %shard_map.63), channel_id=1, source_target_pairs={{0,4},{4,0},{8,12},{12,8},{16,20},{20,16},{24,28},{28,24},{1,5},{5... | collective-permute-start | bytes 393224 | tf_op jit(solution)/shard_map/ppermute | solution.py:23
  56.7 1.0 %collective-permute-start.23 = (bf16[256,256]{1,0:T(8,128)(2,1)S(1)}, bf16[256,256]{1,0:T(8,128)(2,1)S(1)}, u32[]{:S(2)}, u32[]{:S(2)}) collective-permute-start(bf16[256,256]{1,0:T(8,128)(2,1)S(1)} %shard_map.63), channel_id=1, source_target_pairs={{0,2},{1,3},{2,0},{3,1},{4,6},{5,7},{6,4},{7,5},{8,10},{9,11},{10,... | collective-permute-start | bytes 393224 | tf_op jit(solution)/shard_map/ppermute | solution.py:23
  57.8 2.4 %collective-permute-done.18 = bf16[256,256]{1,0:T(8,128)(2,1)S(1)} collective-permute-done((bf16[256,256]{1,0:T(8,128)(2,1)S(1)}, bf16[256,256]{1,0:T(8,128)(2,1)S(1)}, u32[]{:S(2)}, u32[]{:S(2)}) %collective-permute-start.18) | collective-permute-done | bytes 131104 | tf_op jit(solution)/shard_map/ppermute | solution.py:23
  60.7 1.0 %collective-permute-done.23 = bf16[256,256]{1,0:T(8,128)(2,1)S(1)} collective-permute-done((bf16[256,256]{1,0:T(8,128)(2,1)S(1)}, bf16[256,256]{1,0:T(8,128)(2,1)S(1)}, u32[]{:S(2)}, u32[]{:S(2)}) %collective-permute-start.23) | collective-permute-done | bytes 131104 | tf_op jit(solution)/shard_map/ppermute | solution.py:23
  61.8 1.1 %collective-permute-start.24 = (bf16[256,256]{1,0:T(8,128)(2,1)S(1)}, bf16[256,256]{1,0:T(8,128)(2,1)S(1)}, u32[]{:S(2)}, u32[]{:S(2)}) collective-permute-start(bf16[256,256]{1,0:T(8,128)(2,1)S(1)} %fusion.4), channel_id=1, source_target_pairs={{0,2},{1,3},{2,0},{3,1},{4,6},{5,7},{6,4},{7,5},{8,10},{9,11},{10,... | collective-permute-start | bytes 393224 | tf_op jit(solution)/shard_map/ppermute | solution.py:23
  63.1 2.6 %collective-permute-done.19 = bf16[256,256]{1,0:T(8,128)(2,1)S(1)} collective-permute-done((bf16[256,256]{1,0:T(8,128)(2,1)S(1)}, bf16[256,256]{1,0:T(8,128)(2,1)S(1)}, u32[]{:S(2)}, u32[]{:S(2)}) %collective-permute-start.19) | collective-permute-done | bytes 131104 | tf_op jit(solution)/shard_map/ppermute | solution.py:23
  65.9 1.4 %collective-permute-start.26 = (bf16[256,256]{1,0:T(8,128)(2,1)S(1)}, bf16[256,256]{1,0:T(8,128)(2,1)S(1)}, u32[]{:S(2)}, u32[]{:S(2)}) collective-permute-start(bf16[256,256]{1,0:T(8,128)(2,1)S(1)} %fusion.5), channel_id=1, source_target_pairs={{0,2},{1,3},{2,0},{3,1},{4,6},{5,7},{6,4},{7,5},{8,10},{9,11},{10,... | collective-permute-start | bytes 393224 | tf_op jit(solution)/shard_map/ppermute | solution.py:23
  67.5 0.5 collective-permute-done.24
  68.0 3.0 %collective-permute-done.26 = bf16[256,256]{1,0:T(8,128)(2,1)S(1)} collective-permute-done((bf16[256,256]{1,0:T(8,128)(2,1)S(1)}, bf16[256,256]{1,0:T(8,128)(2,1)S(1)}, u32[]{:S(2)}, u32[]{:S(2)}) %collective-permute-start.26) | collective-permute-done | bytes 131104 | tf_op jit(solution)/shard_map/ppermute | solution.py:23
  71.1 0.3 fusion.11
  71.3 1.3 %collective-permute-done.20 = bf16[256,256]{1,0:T(8,128)(2,1)S(1)} collective-permute-done((bf16[256,256]{1,0:T(8,128)(2,1)S(1)}, bf16[256,256]{1,0:T(8,128)(2,1)S(1)}, u32[]{:S(2)}, u32[]{:S(2)}) %collective-permute-start.20) | collective-permute-done | bytes 131104 | tf_op jit(solution)/shard_map/ppermute | solution.py:23
  72.8 1.1 %collective-permute-start.21 = (bf16[256,256]{1,0:T(8,128)(2,1)S(1)}, bf16[256,256]{1,0:T(8,128)(2,1)S(1)}, u32[]{:S(2)}, u32[]{:S(2)}) collective-permute-start(bf16[256,256]{1,0:T(8,128)(2,1)S(1)} %fusion.6), channel_id=1, source_target_pairs={{0,2},{1,3},{2,0},{3,1},{4,6},{5,7},{6,4},{7,5},{8,10},{9,11},{10,... | collective-permute-start | bytes 393224 | tf_op jit(solution)/shard_map/ppermute | solution.py:23
  74.0 0.5 collective-permute-start.25
  74.5 0.3 fusion.50
  74.8 3.1 %collective-permute-done.21 = bf16[256,256]{1,0:T(8,128)(2,1)S(1)} collective-permute-done((bf16[256,256]{1,0:T(8,128)(2,1)S(1)}, bf16[256,256]{1,0:T(8,128)(2,1)S(1)}, u32[]{:S(2)}, u32[]{:S(2)}) %collective-permute-start.21) | collective-permute-done | bytes 131104 | tf_op jit(solution)/shard_map/ppermute | solution.py:23
  78.0 0.3 fusion.3.refs_1_
  78.3 0.3 fusion.2.refs_0_
  78.6 1.0 %collective-permute-done.22 = bf16[512,256]{1,0:T(8,128)(2,1)S(1)} collective-permute-done((bf16[512,256]{1,0:T(8,128)(2,1)S(1)}, bf16[512,256]{1,0:T(8,128)(2,1)S(1)}, u32[]{:S(2)}, u32[]{:S(2)}) %collective-permute-start.22) | collective-permute-done | bytes 262176 | tf_op jit(solution)/shard_map/ppermute | solution.py:23
  79.6 8.8 %shard_map.64 = f32[1,256]{1,0:T(1,128)S(1)} custom-call(f32[256,256]{1,0:T(8,128)S(1)} %fusion.2.refs_0_, f32[256,256]{1,0:T(8,128)S(1)} %fusion.3.refs_1_, s32[1]{0:T(128)} %bitcast.34.refs_2_, bf16[1024,256]{1,0:T(8,128)(2,1)S(1)} %bitcast.73), custom_call_target="tpu_custom_call" | custom-call | tf_op jit(solution)/shard_map/pallas_call | solution.py:132
  88.6 1.0 %collective-permute-done.28 = f32[1,256]{1,0:T(1,128)S(1)} collective-permute-done((f32[1,256]{1,0:T(1,128)S(1)}, f32[1,256]{1,0:T(1,128)S(1)}, u32[]{:S(2)}, u32[]{:S(2)}) %collective-permute-start.28) | collective-permute-done | bytes 1056 | tf_op jit(solution)/shard_map/ppermute | solution.py:23
  89.6 0.6 add.88
  (95 shorter events, 5.3 us)
Async XLA Ops:
  0.7 1.1 %copy-start.5 = (s32[1,4,256]{2,1,0:T(4,128)S(1)}, s32[1,4,256]{2,1,0:T(4,128)}, u32[]{:S(2)}) copy-start(s32[1,4,256]{2,1,0:T(4,128)} %param.7) | copy-start | bytes 12292
  1.7 5.7 %copy-start.2 = (bf16[128,1024]{1,0:T(8,128)(2,1)S(1)}, bf16[128,1024]{1,0:T(8,128)(2,1)}, u32[]{:S(2)}) copy-start(bf16[128,1024]{1,0:T(8,128)(2,1)} %param.5) | copy-start | bytes 786436
  1.7 5.7 %copy-start.3 = (bf16[128,1024]{1,0:T(8,128)(2,1)S(1)}, bf16[128,1024]{1,0:T(8,128)(2,1)}, u32[]{:S(2)}) copy-start(bf16[128,1024]{1,0:T(8,128)(2,1)} %param.6) | copy-start | bytes 786436
  1.7 11.0 %copy-start.4 = (bf16[128,4096]{1,0:T(8,128)(2,1)S(1)}, bf16[128,4096]{1,0:T(8,128)(2,1)}, u32[]{:S(2)}) copy-start(bf16[128,4096]{1,0:T(8,128)(2,1)} %param.4) | copy-start | bytes 3145732
  1.8 7.2 %collective-permute-start.2 = (s32[1,256]{1,0:T(1,128)S(1)}, s32[1,256]{1,0:T(1,128)S(1)}, u32[]{:S(2)}, u32[]{:S(2)}) collective-permute-start(s32[1,256]{1,0:T(1,128)S(1)} %get-tuple-element.14), channel_id=1, source_target_pairs={{0,16},{4,20},{8,24},{12,28},{16,0},{20,4},{24,8},{28,12},{1,17},{... | collective-permute-start | bytes 3080 | tf_op jit(solution)/shard_map/ppermute | solution.py:23
  5.9 9.2 %collective-permute-start.9 = (bf16[128,1024]{1,0:T(8,128)(2,1)S(1)}, bf16[128,1024]{1,0:T(8,128)(2,1)S(1)}, u32[]{:S(2)}, u32[]{:S(2)}) collective-permute-start(bf16[128,1024]{1,0:T(8,128)(2,1)S(1)} %pad_maximum_fusion.3), channel_id=1, source_target_pairs={{0,4},{4,0},{8,12},{12,8},{16,20},{20,16},{24,28},{28,24},{1,5},{5... | collective-permute-start | bytes 786440 | tf_op jit(solution)/shard_map/ppermute | solution.py:23
  7.4 9.7 %collective-permute-start = (bf16[2,128,512]{2,1,0:T(8,128)(2,1)S(1)}, bf16[2,128,512]{2,1,0:T(8,128)(2,1)S(1)}, u32[]{:S(2)}, u32[]{:S(2)}) collective-permute-start(bf16[2,128,512]{2,1,0:T(8,128)(2,1)S(1)} %get-tuple-element.34), channel_id=1, source_target_pairs={{0,2},{1,3},{2,0},{3,1},{4,6},{5,7},{6,4},{7,5},{8,10},{9,11},{10,... | collective-permute-start | bytes 786440 | tf_op jit(solution)/shard_map/ppermute | solution.py:23
  9.0 3.7 %collective-permute-start.6 = (s32[2,256]{1,0:T(2,128)S(1)}, s32[2,256]{1,0:T(2,128)S(1)}, u32[]{:S(2)}, u32[]{:S(2)}) collective-permute-start(s32[2,256]{1,0:T(2,128)S(1)} %get-tuple-element.58), channel_id=1, source_target_pairs={{0,8},{4,12},{8,0},{12,4},{16,24},{20,28},{24,16},{28,20},{1,9},{5... | collective-permute-start | bytes 6152 | tf_op jit(solution)/shard_map/ppermute | solution.py:23
  10.7 11.4 %collective-permute-start.3 = (bf16[2,144,512]{2,1,0:T(8,128)(2,1)S(1)}, bf16[2,144,512]{2,1,0:T(8,128)(2,1)S(1)}, u32[]{:S(2)}, u32[]{:S(2)}) collective-permute-start(bf16[2,144,512]{2,1,0:T(8,128)(2,1)S(1)} %pad_maximum_fusion.2), channel_id=1, source_target_pairs={{0,4},{4,0},{8,12},{12,8},{16,20},{20,16},{24,28},{28,24},{1,5},{5... | collective-permute-start | bytes 884744 | tf_op jit(solution)/shard_map/ppermute | solution.py:23
  13.8 8.2 %collective-permute-start.7 = (bf16[128,1024]{1,0:T(8,128)(2,1)S(1)}, bf16[128,1024]{1,0:T(8,128)(2,1)S(1)}, u32[]{:S(2)}, u32[]{:S(2)}) collective-permute-start(bf16[128,1024]{1,0:T(8,128)(2,1)S(1)} %pad_maximum_fusion.4), channel_id=1, source_target_pairs={{0,2},{1,3},{2,0},{3,1},{4,6},{5,7},{6,4},{7,5},{8,10},{9,11},{10,... | collective-permute-start | bytes 786440 | tf_op jit(solution)/shard_map/ppermute | solution.py:23
  15.6 7.8 %collective-permute-start.10 = (bf16[128,512]{1,0:T(8,128)(2,1)S(1)}, bf16[128,512]{1,0:T(8,128)(2,1)S(1)}, u32[]{:S(2)}, u32[]{:S(2)}) collective-permute-start(bf16[128,512]{1,0:T(8,128)(2,1)S(1)} %pad_maximum_fusion.9), channel_id=1, source_target_pairs={{0,2},{1,3},{2,0},{3,1},{4,6},{5,7},{6,4},{7,5},{8,10},{9,11},{10,... | collective-permute-start | bytes 393224 | tf_op jit(solution)/shard_map/ppermute | solution.py:23
  17.2 10.6 %collective-permute-start.1 = (bf16[2,256,256]{2,1,0:T(8,128)(2,1)S(1)}, bf16[2,256,256]{2,1,0:T(8,128)(2,1)S(1)}, u32[]{:S(2)}, u32[]{:S(2)}) collective-permute-start(bf16[2,256,256]{2,1,0:T(8,128)(2,1)S(1)} %get-tuple-element.32), channel_id=1, source_target_pairs={{0,1},{1,0},{2,3},{3,2},{4,5},{5,4},{6,7},{7,6},{8,9},{9,8},{10,11... | collective-permute-start | bytes 786440 | tf_op jit(solution)/shard_map/ppermute | solution.py:23
  17.3 8.7 %collective-permute-start.4 = (bf16[2,128,512]{2,1,0:T(8,128)(2,1)S(1)}, bf16[2,128,512]{2,1,0:T(8,128)(2,1)S(1)}, u32[]{:S(2)}, u32[]{:S(2)}) collective-permute-start(bf16[2,128,512]{2,1,0:T(8,128)(2,1)S(1)} %collective-permute-done), channel_id=1, source_target_pairs={{0,4},{4,0},{8,12},{12,8},{16,20},{20,16},{24,28},{28,24},{1,5},{5... | collective-permute-start | bytes 786440 | tf_op jit(solution)/shard_map/ppermute | solution.py:23
  22.1 5.7 %collective-permute-start.8 = (bf16[256,1024]{1,0:T(8,128)(2,1)S(1)}, bf16[256,1024]{1,0:T(8,128)(2,1)S(1)}, u32[]{:S(2)}, u32[]{:S(2)}) collective-permute-start(bf16[256,1024]{1,0:T(8,128)(2,1)S(1)} %pad_maximum_fusion.refs_4_), channel_id=1, source_target_pairs={{0,1},{1,0},{2,3},{3,2},{4,5},{5,4},{6,7},{7,6},{8,9},{9,8},{10,11... | collective-permute-start | bytes 1572872 | tf_op jit(solution)/shard_map/ppermute | solution.py:23
  22.1 0.7 copy-start.1
  22.9 3.1 %slice-start = ((bf16[2,144,512]{2,1,0:T(8,128)(2,1)}), bf16[2,128,512]{2,1,0:T(8,128)(2,1)S(1)}, s32[]{:S(2)}) async-start(bf16[2,144,512]{2,1,0:T(8,128)(2,1)} %copy-done.1), calls=%async_computation | async-start | bytes 524288 | tf_op jit(solution)/shard_map/slice | solution.py:231
  23.4 4.4 %collective-permute-start.11 = (bf16[256,512]{1,0:T(8,128)(2,1)S(1)}, bf16[256,512]{1,0:T(8,128)(2,1)S(1)}, u32[]{:S(2)}, u32[]{:S(2)}) collective-permute-start(bf16[256,512]{1,0:T(8,128)(2,1)S(1)} %pad_maximum_fusion.5.refs_6_), channel_id=1, source_target_pairs={{0,1},{1,0},{2,3},{3,2},{4,5},{5,4},{6,7},{7,6},{8,9},{9,8},{10,11... | collective-permute-start | bytes 786440 | tf_op jit(solution)/shard_map/ppermute | solution.py:23
  26.1 1.7 %collective-permute-start.5 = (bf16[2,256,256]{2,1,0:T(8,128)(2,1)S(1)}, bf16[2,256,256]{2,1,0:T(8,128)(2,1)S(1)}, u32[]{:S(2)}, u32[]{:S(2)}) collective-permute-start(bf16[2,256,256]{2,1,0:T(8,128)(2,1)S(1)} %get-tuple-element.30), channel_id=1, source_target_pairs={{0,1},{1,0},{2,3},{3,2},{4,5},{5,4},{6,7},{7,6},{8,9},{9,8},{10,11... | collective-permute-start | bytes 786440 | tf_op jit(solution)/shard_map/ppermute | solution.py:23
  26.2 5.9 %collective-permute-start.13 = (bf16[128,512]{1,0:T(8,128)(2,1)S(1)}, bf16[128,512]{1,0:T(8,128)(2,1)S(1)}, u32[]{:S(2)}, u32[]{:S(2)}) collective-permute-start(bf16[128,512]{1,0:T(8,128)(2,1)S(1)} %pad_maximum_fusion.8), channel_id=1, source_target_pairs={{0,4},{4,0},{8,12},{12,8},{16,20},{20,16},{24,28},{28,24},{1,5},{5... | collective-permute-start | bytes 393224 | tf_op jit(solution)/shard_map/ppermute | solution.py:23
  28.5 8.7 %collective-permute-start.12 = (f16[528,256]{1,0:T(8,128)(2,1)S(1)}, f16[528,256]{1,0:T(8,128)(2,1)S(1)}, u32[]{:S(2)}, u32[]{:S(2)}) collective-permute-start(f16[528,256]{1,0:T(8,128)(2,1)S(1)} %convert_element_type.80), channel_id=1, source_target_pairs={{0,8},{4,12},{8,0},{12,4},{16,24},{20,28},{24,16},{28,20},{1,9},{5... | collective-permute-start | bytes 811016 | tf_op jit(solution)/shard_map/ppermute | solution.py:23
  32.1 5.1 %collective-permute-start.14 = (bf16[128,512]{1,0:T(8,128)(2,1)S(1)}, bf16[128,512]{1,0:T(8,128)(2,1)S(1)}, u32[]{:S(2)}, u32[]{:S(2)}) collective-permute-start(bf16[128,512]{1,0:T(8,128)(2,1)S(1)} %collective-permute-done.13), channel_id=1, source_target_pairs={{0,2},{1,3},{2,0},{3,1},{4,6},{5,7},{6,4},{7,5},{8,10},{9,11},{10,... | collective-permute-start | bytes 393224 | tf_op jit(solution)/shard_map/ppermute | solution.py:23
  37.2 1.8 %collective-permute-start.15 = (bf16[256,512]{1,0:T(8,128)(2,1)S(1)}, bf16[256,512]{1,0:T(8,128)(2,1)S(1)}, u32[]{:S(2)}, u32[]{:S(2)}) collective-permute-start(bf16[256,512]{1,0:T(8,128)(2,1)S(1)} %pad_maximum_fusion.6.refs_6_), channel_id=1, source_target_pairs={{0,1},{1,0},{2,3},{3,2},{4,5},{5,4},{6,7},{7,6},{8,9},{9,8},{10,11... | collective-permute-start | bytes 786440 | tf_op jit(solution)/shard_map/ppermute | solution.py:23
  37.3 11.7 %collective-permute-start.16 = (f16[528,256]{1,0:T(8,128)(2,1)S(1)}, f16[528,256]{1,0:T(8,128)(2,1)S(1)}, u32[]{:S(2)}, u32[]{:S(2)}) collective-permute-start(f16[528,256]{1,0:T(8,128)(2,1)S(1)} %convert_element_type.81), channel_id=1, source_target_pairs={{0,8},{4,12},{8,0},{12,4},{16,24},{20,28},{24,16},{28,20},{1,9},{5... | collective-permute-start | bytes 811016 | tf_op jit(solution)/shard_map/ppermute | solution.py:23
  39.7 15.4 %collective-permute-start.17 = (f16[528,256]{1,0:T(8,128)(2,1)S(1)}, f16[528,256]{1,0:T(8,128)(2,1)S(1)}, u32[]{:S(2)}, u32[]{:S(2)}) collective-permute-start(f16[528,256]{1,0:T(8,128)(2,1)S(1)} %convert_element_type.84), channel_id=1, source_target_pairs={{0,16},{4,20},{8,24},{12,28},{16,0},{20,4},{24,8},{28,12},{1,17},{... | collective-permute-start | bytes 811016 | tf_op jit(solution)/shard_map/ppermute | solution.py:23
  55.2 5.0 %collective-permute-start.18 = (bf16[256,256]{1,0:T(8,128)(2,1)S(1)}, bf16[256,256]{1,0:T(8,128)(2,1)S(1)}, u32[]{:S(2)}, u32[]{:S(2)}) collective-permute-start(bf16[256,256]{1,0:T(8,128)(2,1)S(1)} %shard_map.63), channel_id=1, source_target_pairs={{0,4},{4,0},{8,12},{12,8},{16,20},{20,16},{24,28},{28,24},{1,5},{5... | collective-permute-start | bytes 393224 | tf_op jit(solution)/shard_map/ppermute | solution.py:23
  56.7 5.0 %collective-permute-start.23 = (bf16[256,256]{1,0:T(8,128)(2,1)S(1)}, bf16[256,256]{1,0:T(8,128)(2,1)S(1)}, u32[]{:S(2)}, u32[]{:S(2)}) collective-permute-start(bf16[256,256]{1,0:T(8,128)(2,1)S(1)} %shard_map.63), channel_id=1, source_target_pairs={{0,2},{1,3},{2,0},{3,1},{4,6},{5,7},{6,4},{7,5},{8,10},{9,11},{10,... | collective-permute-start | bytes 393224 | tf_op jit(solution)/shard_map/ppermute | solution.py:23
  60.6 5.0 %collective-permute-start.19 = (bf16[256,256]{1,0:T(8,128)(2,1)S(1)}, bf16[256,256]{1,0:T(8,128)(2,1)S(1)}, u32[]{:S(2)}, u32[]{:S(2)}) collective-permute-start(bf16[256,256]{1,0:T(8,128)(2,1)S(1)} %fusion.4), channel_id=1, source_target_pairs={{0,8},{4,12},{8,0},{12,4},{16,24},{20,28},{24,16},{28,20},{1,9},{5... | collective-permute-start | bytes 393224 | tf_op jit(solution)/shard_map/ppermute | solution.py:23
  61.8 6.2 %collective-permute-start.24 = (bf16[256,256]{1,0:T(8,128)(2,1)S(1)}, bf16[256,256]{1,0:T(8,128)(2,1)S(1)}, u32[]{:S(2)}, u32[]{:S(2)}) collective-permute-start(bf16[256,256]{1,0:T(8,128)(2,1)S(1)} %fusion.4), channel_id=1, source_target_pairs={{0,2},{1,3},{2,0},{3,1},{4,6},{5,7},{6,4},{7,5},{8,10},{9,11},{10,... | collective-permute-start | bytes 393224 | tf_op jit(solution)/shard_map/ppermute | solution.py:23
  65.8 6.8 %collective-permute-start.20 = (bf16[256,256]{1,0:T(8,128)(2,1)S(1)}, bf16[256,256]{1,0:T(8,128)(2,1)S(1)}, u32[]{:S(2)}, u32[]{:S(2)}) collective-permute-start(bf16[256,256]{1,0:T(8,128)(2,1)S(1)} %fusion.5), channel_id=1, source_target_pairs={{0,16},{4,20},{8,24},{12,28},{16,0},{20,4},{24,8},{28,12},{1,17},{... | collective-permute-start | bytes 393224 | tf_op jit(solution)/shard_map/ppermute | solution.py:23
  65.9 5.0 %collective-permute-start.26 = (bf16[256,256]{1,0:T(8,128)(2,1)S(1)}, bf16[256,256]{1,0:T(8,128)(2,1)S(1)}, u32[]{:S(2)}, u32[]{:S(2)}) collective-permute-start(bf16[256,256]{1,0:T(8,128)(2,1)S(1)} %fusion.5), channel_id=1, source_target_pairs={{0,2},{1,3},{2,0},{3,1},{4,6},{5,7},{6,4},{7,5},{8,10},{9,11},{10,... | collective-permute-start | bytes 393224 | tf_op jit(solution)/shard_map/ppermute | solution.py:23
  72.8 5.0 %collective-permute-start.21 = (bf16[256,256]{1,0:T(8,128)(2,1)S(1)}, bf16[256,256]{1,0:T(8,128)(2,1)S(1)}, u32[]{:S(2)}, u32[]{:S(2)}) collective-permute-start(bf16[256,256]{1,0:T(8,128)(2,1)S(1)} %fusion.6), channel_id=1, source_target_pairs={{0,2},{1,3},{2,0},{3,1},{4,6},{5,7},{6,4},{7,5},{8,10},{9,11},{10,... | collective-permute-start | bytes 393224 | tf_op jit(solution)/shard_map/ppermute | solution.py:23
  74.0 4.1 %collective-permute-start.27 = (bf16[512,256]{1,0:T(8,128)(2,1)S(1)}, bf16[512,256]{1,0:T(8,128)(2,1)S(1)}, u32[]{:S(2)}, u32[]{:S(2)}) collective-permute-start(bf16[512,256]{1,0:T(8,128)(2,1)S(1)} %maximum_bitcast_fusion.2), channel_id=1, source_target_pairs={{0,1},{1,0},{2,3},{3,2},{4,5},{5,4},{6,7},{7,6},{8,9},{9,8},{10,11... | collective-permute-start | bytes 786440 | tf_op jit(solution)/shard_map/ppermute | solution.py:23
  74.0 4.3 %collective-permute-start.25 = (bf16[512,256]{1,0:T(8,128)(2,1)S(1)}, bf16[512,256]{1,0:T(8,128)(2,1)S(1)}, u32[]{:S(2)}, u32[]{:S(2)}) collective-permute-start(bf16[512,256]{1,0:T(8,128)(2,1)S(1)} %broadcast_select_fusion), channel_id=1, source_target_pairs={{0,1},{1,0},{2,3},{3,2},{4,5},{5,4},{6,7},{7,6},{8,9},{9,8},{10,11... | collective-permute-start | bytes 786440 | tf_op jit(solution)/shard_map/ppermute | solution.py:23
  77.9 1.6 %collective-permute-start.22 = (bf16[512,256]{1,0:T(8,128)(2,1)S(1)}, bf16[512,256]{1,0:T(8,128)(2,1)S(1)}, u32[]{:S(2)}, u32[]{:S(2)}) collective-permute-start(bf16[512,256]{1,0:T(8,128)(2,1)S(1)} %get-tuple-element.42), channel_id=1, source_target_pairs={{0,1},{1,0},{2,3},{3,2},{4,5},{5,4},{6,7},{7,6},{8,9},{9,8},{10,11... | collective-permute-start | bytes 786440 | tf_op jit(solution)/shard_map/ppermute | solution.py:23
  79.6 8.8 %copy-start = (bf16[2,512,256]{2,1,0:T(8,128)(2,1)}, bf16[2,512,256]{2,1,0:T(8,128)(2,1)S(1)}, u32[]{:S(2)}) copy-start(bf16[2,512,256]{2,1,0:T(8,128)(2,1)S(1)} %pad_maximum_fusion.1) | copy-start | bytes 1572868
  88.4 1.2 %collective-permute-start.28 = (f32[1,256]{1,0:T(1,128)S(1)}, f32[1,256]{1,0:T(1,128)S(1)}, u32[]{:S(2)}, u32[]{:S(2)}) collective-permute-start(f32[1,256]{1,0:T(1,128)S(1)} %shard_map.64), channel_id=1, source_target_pairs={{0,1},{1,0},{2,3},{3,2},{4,5},{5,4},{6,7},{7,6},{8,9},{9,8},{10,11... | collective-permute-start | bytes 3080 | tf_op jit(solution)/shard_map/ppermute | solution.py:23

commit v11 on v10

--- a/solution.py
+++ b/solution.py
@@ -88,15 +88,18 @@
 def pivots_kernel(sets, late, *refs):
     grams, refs = refs[:sets], refs[sets:]
     if late:
-        place_ref, cand_ref, refs = refs[0], refs[1], refs[2:]
+        place_ref, part_ref, cand_ref, refs = refs[0], refs[1], refs[2], refs[3:]
     total_ref, work, diagonals = refs[0], refs[1:-1], refs[-1]
     n = grams[0].shape[0]
     for gram, matrix in zip(grams, work):
         matrix[...] = gram[...]
     if late:
-        product = lax.dot_general(cand_ref[...], cand_ref[...], column_dims, preferred_element_type=f32)
+        product = 0.0
+        for half in (part_ref, cand_ref):
+            product += lax.dot_general(half[...], half[...], column_dims, preferred_element_type=f32)
         last = work[-1]
-        last[...] = jnp.where(place_ref[0] & 1 == 0, last[...], shifted(product, cand_ref.shape[0]))
+        product = shifted(product, 2 * cand_ref.shape[0])
+        last[...] = jnp.where(place_ref[0] & 1 == 0, last[...], product)
     diagonals[...] = jnp.zeros_like(diagonals)
     for base in range(0, n, lanes):
 
@@ -123,12 +126,12 @@
     return shifted(product, sum(b.shape[0] for b in blocks))
 
 
-def log_pivots(grams, place=None, cand=None):
+def log_pivots(grams, place=None, part=None, cand=None):
     sets, n = len(grams), grams[0].shape[0]
     operands, specs = list(grams), [pl.BlockSpec(memory_space=pltpu.VMEM)] * sets
     if cand is not None:
-        operands += [place[None], cand]
-        specs += [pl.BlockSpec(memory_space=pltpu.SMEM), pl.BlockSpec(memory_space=pltpu.VMEM)]
+        operands += [place[None], part, cand]
+        specs += [pl.BlockSpec(memory_space=pltpu.SMEM)] + [pl.BlockSpec(memory_space=pltpu.VMEM)] * 2
     return pl.pallas_call(
         functools.partial(pivots_kernel, sets, cand is not None),
         out_shape=jax.ShapeDtypeStruct((1, n), f32),
@@ -323,13 +326,14 @@
                 low, high = shared[-2:]
                 got = exchange(jnp.where(even, high, low), "band", 1)
                 grams.append(gram_of([jnp.where(even, low, high), got]))
-    cands = in_order(final, exchange(final, "band", 1), 0)
+    got = exchange(final, "band", 1)
+    cands = in_order(final, got, 0)
     if rounds % 2:
         odd = log_pivots([gram_of([cands])])
         quality = jnp.where(even, 0.0, odd) + (log_pivots(grams) if grams else 0.0)
     else:
         last = gram_of([shared[-1], exchange(shared[-1], "band", 1)])
-        quality = log_pivots(grams + [last], place, cands)
+        quality = log_pivots(grams + [last], place, final, got)
     return cands, quality + exchange(quality, "band", 1)
 
 

time: 90.4 us -> 90.3 us (level)
  transfers between devices with their start and end apart: 29 -> 29, of which waited for: 18 -> 18; matrix products, arithmetic and copies ran while one was open for 5% -> 6% of each run, Pallas kernels for 3% -> 3%
where the time goes in v11:
time: 90.3 us; the launch traced here: 90.1 us
  waiting for transfers between devices  42.6 us (47%)
  starting transfers between devices  27.2 us (30%)
  Pallas kernels  11.3 us (13%)
  matrix products  4.24 us (5%)
  other arithmetic  2.23 us (2%)
  local copies, waits for them, and re-layouts  1.3 us (1%)
  between operations  1.26 us (1%)
    ppermute x29, waiting for transfers between devices, exchange(): return lax.ppermute(block, axis, [(i, i ^ delta) for i in range(count)])  42.6 us
    ppermute x29, starting transfers between devices, exchange(): return lax.ppermute(block, axis, [(i, i ^ delta) for i in range(count)])  27.2 us
    pallas_call x1, Pallas kernels, log_pivots(): pl.pallas_call(functools.partial(pivots_kernel, sets, cand is not None),...  8.81 us
    pallas_call x5, Pallas kernels, sketch(): pl.pallas_call(functools.partial(sketch_kernel, mode, columns, [start for...  2.49 us
    dot_general x8, matrix products, pick(): out.append(jnp.dot(block, one_hot, preferred_element_type=f32).astype(bf16))  1.98 us
  transfers between devices with their start and end apart: 29, of which 18 were waited for; matrix products, arithmetic and copies ran while one was open for 6% of the time, Pallas kernels for 3%

profile of v11, /device:TPU:0, one launch (start us, length us, event | category | flops | bytes accessed | tf_op | source)
XLA Modules:
  0.0 90.1 jit_solution(6028882041757821312)
XLA Ops:
  0.7 1.0 %constant_dynamic-slice_fusion.3 = (bf16[128,512]{1,0:T(8,128)(2,1)S(1)}, bf16[128,512]{1,0:T(8,128)(2,1)S(1)}) fusion(bf16[128,4096]{1,0:T(8,128)(2,1)} %param.4, s32[]{:T(128)S(6)} %select_n.136, s32[]{:T(128)S(6)} %select_n.137), kind=kLoop, calls=%fused_computation.115 | loop fusion | bytes 524296 | tf_op jit(solution)/shard_map/dynamic_slice | solution.py:212
  1.8 4.1 %collective-permute-start.2 = (s32[1,256]{1,0:T(1,128)S(1)}, s32[1,256]{1,0:T(1,128)S(1)}, u32[]{:S(2)}, u32[]{:S(2)}) collective-permute-start(s32[1,256]{1,0:T(1,128)S(1)} %get-tuple-element.14), channel_id=1, source_target_pairs={{0,16},{4,20},{8,24},{12,28},{16,0},{20,4},{24,8},{28,12},{1,17},{... | collective-permute-start | bytes 3080 | tf_op jit(solution)/shard_map/ppermute | solution.py:23
  5.9 1.5 %collective-permute-start.9 = (bf16[128,1024]{1,0:T(8,128)(2,1)S(1)}, bf16[128,1024]{1,0:T(8,128)(2,1)S(1)}, u32[]{:S(2)}, u32[]{:S(2)}) collective-permute-start(bf16[128,1024]{1,0:T(8,128)(2,1)S(1)} %pad_maximum_fusion.3), channel_id=1, source_target_pairs={{0,4},{4,0},{8,12},{12,8},{16,20},{20,16},{24,28},{28,24},{1,5},{5... | collective-permute-start | bytes 786440 | tf_op jit(solution)/shard_map/ppermute | solution.py:23
  7.4 1.6 %collective-permute-start = (bf16[2,128,512]{2,1,0:T(8,128)(2,1)S(1)}, bf16[2,128,512]{2,1,0:T(8,128)(2,1)S(1)}, u32[]{:S(2)}, u32[]{:S(2)}) collective-permute-start(bf16[2,128,512]{2,1,0:T(8,128)(2,1)S(1)} %get-tuple-element.34), channel_id=1, source_target_pairs={{0,2},{1,3},{2,0},{3,1},{4,6},{5,7},{6,4},{7,5},{8,10},{9,11},{10,... | collective-permute-start | bytes 786440 | tf_op jit(solution)/shard_map/ppermute | solution.py:23
  9.0 1.6 %collective-permute-start.6 = (s32[2,256]{1,0:T(2,128)S(1)}, s32[2,256]{1,0:T(2,128)S(1)}, u32[]{:S(2)}, u32[]{:S(2)}) collective-permute-start(s32[2,256]{1,0:T(2,128)S(1)} %get-tuple-element.58), channel_id=1, source_target_pairs={{0,8},{4,12},{8,0},{12,4},{16,24},{20,28},{24,16},{28,20},{1,9},{5... | collective-permute-start | bytes 6152 | tf_op jit(solution)/shard_map/ppermute | solution.py:23
  10.7 0.6 collective-permute-start.3
  11.3 1.3 %collective-permute-done.6 = s32[2,256]{1,0:T(2,128)S(1)} collective-permute-done((s32[2,256]{1,0:T(2,128)S(1)}, s32[2,256]{1,0:T(2,128)S(1)}, u32[]{:S(2)}, u32[]{:S(2)}) %collective-permute-start.6) | collective-permute-done | bytes 2080 | tf_op jit(solution)/shard_map/ppermute | solution.py:23
  13.8 0.6 collective-permute-start.7
  14.4 0.7 collective-permute-done.9
  15.6 1.6 %collective-permute-start.10 = (bf16[128,512]{1,0:T(8,128)(2,1)S(1)}, bf16[128,512]{1,0:T(8,128)(2,1)S(1)}, u32[]{:S(2)}, u32[]{:S(2)}) collective-permute-start(bf16[128,512]{1,0:T(8,128)(2,1)S(1)} %pad_maximum_fusion.9), channel_id=1, source_target_pairs={{0,2},{1,3},{2,0},{3,1},{4,6},{5,7},{6,4},{7,5},{8,10},{9,11},{10,... | collective-permute-start | bytes 393224 | tf_op jit(solution)/shard_map/ppermute | solution.py:23
  17.3 1.6 %collective-permute-start.4 = (bf16[2,128,512]{2,1,0:T(8,128)(2,1)S(1)}, bf16[2,128,512]{2,1,0:T(8,128)(2,1)S(1)}, u32[]{:S(2)}, u32[]{:S(2)}) collective-permute-start(bf16[2,128,512]{2,1,0:T(8,128)(2,1)S(1)} %collective-permute-done), channel_id=1, source_target_pairs={{0,4},{4,0},{8,12},{12,8},{16,20},{20,16},{24,28},{28,24},{1,5},{5... | collective-permute-start | bytes 786440 | tf_op jit(solution)/shard_map/ppermute | solution.py:23
  18.9 3.1 %collective-permute-done.7 = bf16[128,1024]{1,0:T(8,128)(2,1)S(1)} collective-permute-done((bf16[128,1024]{1,0:T(8,128)(2,1)S(1)}, bf16[128,1024]{1,0:T(8,128)(2,1)S(1)}, u32[]{:S(2)}, u32[]{:S(2)}) %collective-permute-start.7) | collective-permute-done | bytes 262176 | tf_op jit(solution)/shard_map/ppermute | solution.py:23
  22.9 0.5 collective-permute-done.10
  23.5 2.5 %collective-permute-done.4 = bf16[2,128,512]{2,1,0:T(8,128)(2,1)S(1)} collective-permute-done((bf16[2,128,512]{2,1,0:T(8,128)(2,1)S(1)}, bf16[2,128,512]{2,1,0:T(8,128)(2,1)S(1)}, u32[]{:S(2)}, u32[]{:S(2)}) %collective-permute-start.4) | collective-permute-done | bytes 262176 | tf_op jit(solution)/shard_map/ppermute | solution.py:23
  26.2 1.6 %collective-permute-start.13 = (bf16[128,512]{1,0:T(8,128)(2,1)S(1)}, bf16[128,512]{1,0:T(8,128)(2,1)S(1)}, u32[]{:S(2)}, u32[]{:S(2)}) collective-permute-start(bf16[128,512]{1,0:T(8,128)(2,1)S(1)} %pad_maximum_fusion.8), channel_id=1, source_target_pairs={{0,4},{4,0},{8,12},{12,8},{16,20},{20,16},{24,28},{28,24},{1,5},{5... | collective-permute-start | bytes 393224 | tf_op jit(solution)/shard_map/ppermute | solution.py:23
  27.8 0.7 shard_map.59
  28.5 1.6 %collective-permute-start.12 = (f16[528,256]{1,0:T(8,128)(2,1)S(1)}, f16[528,256]{1,0:T(8,128)(2,1)S(1)}, u32[]{:S(2)}, u32[]{:S(2)}) collective-permute-start(f16[528,256]{1,0:T(8,128)(2,1)S(1)} %convert_element_type.80), channel_id=1, source_target_pairs={{0,8},{4,12},{8,0},{12,4},{16,24},{20,28},{24,16},{28,20},{1,9},{5... | collective-permute-start | bytes 811016 | tf_op jit(solution)/shard_map/ppermute | solution.py:23
  30.2 0.6 shard_map.60
  30.9 1.3 %collective-permute-done.13 = bf16[128,512]{1,0:T(8,128)(2,1)S(1)} collective-permute-done((bf16[128,512]{1,0:T(8,128)(2,1)S(1)}, bf16[128,512]{1,0:T(8,128)(2,1)S(1)}, u32[]{:S(2)}, u32[]{:S(2)}) %collective-permute-start.13) | collective-permute-done | bytes 131104 | tf_op jit(solution)/shard_map/ppermute | solution.py:23
  32.1 1.0 %collective-permute-start.14 = (bf16[128,512]{1,0:T(8,128)(2,1)S(1)}, bf16[128,512]{1,0:T(8,128)(2,1)S(1)}, u32[]{:S(2)}, u32[]{:S(2)}) collective-permute-start(bf16[128,512]{1,0:T(8,128)(2,1)S(1)} %collective-permute-done.13), channel_id=1, source_target_pairs={{0,2},{1,3},{2,0},{3,1},{4,6},{5,7},{6,4},{7,5},{8,10},{9,11},{10,... | collective-permute-start | bytes 393224 | tf_op jit(solution)/shard_map/ppermute | solution.py:23
  33.2 4.0 %collective-permute-done.14 = bf16[128,512]{1,0:T(8,128)(2,1)S(1)} collective-permute-done((bf16[128,512]{1,0:T(8,128)(2,1)S(1)}, bf16[128,512]{1,0:T(8,128)(2,1)S(1)}, u32[]{:S(2)}, u32[]{:S(2)}) %collective-permute-start.14) | collective-permute-done | bytes 131104 | tf_op jit(solution)/shard_map/ppermute | solution.py:23
  37.3 1.6 %collective-permute-start.16 = (f16[528,256]{1,0:T(8,128)(2,1)S(1)}, f16[528,256]{1,0:T(8,128)(2,1)S(1)}, u32[]{:S(2)}, u32[]{:S(2)}) collective-permute-start(f16[528,256]{1,0:T(8,128)(2,1)S(1)} %convert_element_type.81), channel_id=1, source_target_pairs={{0,8},{4,12},{8,0},{12,4},{16,24},{20,28},{24,16},{28,20},{1,9},{5... | collective-permute-start | bytes 811016 | tf_op jit(solution)/shard_map/ppermute | solution.py:23
  39.0 0.7 shard_map.62
  39.7 0.6 collective-permute-start.17
  40.3 8.7 %collective-permute-done.16 = f16[528,256]{1,0:T(8,128)(2,1)S(1)} collective-permute-done((f16[528,256]{1,0:T(8,128)(2,1)S(1)}, f16[528,256]{1,0:T(8,128)(2,1)S(1)}, u32[]{:S(2)}, u32[]{:S(2)}) %collective-permute-start.16) | collective-permute-done | bytes 270368 | tf_op jit(solution)/shard_map/ppermute | solution.py:23
  49.0 0.5 shard_map.61.refs_0_
  49.5 5.5 %collective-permute-done.17 = f16[528,256]{1,0:T(8,128)(2,1)S(1)} collective-permute-done((f16[528,256]{1,0:T(8,128)(2,1)S(1)}, f16[528,256]{1,0:T(8,128)(2,1)S(1)}, u32[]{:S(2)}, u32[]{:S(2)}) %collective-permute-start.17) | collective-permute-done | bytes 270368 | tf_op jit(solution)/shard_map/ppermute | solution.py:23
  55.2 1.6 %collective-permute-start.18 = (bf16[256,256]{1,0:T(8,128)(2,1)S(1)}, bf16[256,256]{1,0:T(8,128)(2,1)S(1)}, u32[]{:S(2)}, u32[]{:S(2)}) collective-permute-start(bf16[256,256]{1,0:T(8,128)(2,1)S(1)} %shard_map.63), channel_id=1, source_target_pairs={{0,4},{4,0},{8,12},{12,8},{16,20},{20,16},{24,28},{28,24},{1,5},{5... | collective-permute-start | bytes 393224 | tf_op jit(solution)/shard_map/ppermute | solution.py:23
  56.7 1.0 %collective-permute-start.23 = (bf16[256,256]{1,0:T(8,128)(2,1)S(1)}, bf16[256,256]{1,0:T(8,128)(2,1)S(1)}, u32[]{:S(2)}, u32[]{:S(2)}) collective-permute-start(bf16[256,256]{1,0:T(8,128)(2,1)S(1)} %shard_map.63), channel_id=1, source_target_pairs={{0,2},{1,3},{2,0},{3,1},{4,6},{5,7},{6,4},{7,5},{8,10},{9,11},{10,... | collective-permute-start | bytes 393224 | tf_op jit(solution)/shard_map/ppermute | solution.py:23
  57.8 2.4 %collective-permute-done.18 = bf16[256,256]{1,0:T(8,128)(2,1)S(1)} collective-permute-done((bf16[256,256]{1,0:T(8,128)(2,1)S(1)}, bf16[256,256]{1,0:T(8,128)(2,1)S(1)}, u32[]{:S(2)}, u32[]{:S(2)}) %collective-permute-start.18) | collective-permute-done | bytes 131104 | tf_op jit(solution)/shard_map/ppermute | solution.py:23
  60.7 1.0 %collective-permute-done.23 = bf16[256,256]{1,0:T(8,128)(2,1)S(1)} collective-permute-done((bf16[256,256]{1,0:T(8,128)(2,1)S(1)}, bf16[256,256]{1,0:T(8,128)(2,1)S(1)}, u32[]{:S(2)}, u32[]{:S(2)}) %collective-permute-start.23) | collective-permute-done | bytes 131104 | tf_op jit(solution)/shard_map/ppermute | solution.py:23
  61.8 1.1 %collective-permute-start.24 = (bf16[256,256]{1,0:T(8,128)(2,1)S(1)}, bf16[256,256]{1,0:T(8,128)(2,1)S(1)}, u32[]{:S(2)}, u32[]{:S(2)}) collective-permute-start(bf16[256,256]{1,0:T(8,128)(2,1)S(1)} %fusion.4), channel_id=1, source_target_pairs={{0,2},{1,3},{2,0},{3,1},{4,6},{5,7},{6,4},{7,5},{8,10},{9,11},{10,... | collective-permute-start | bytes 393224 | tf_op jit(solution)/shard_map/ppermute | solution.py:23
  63.1 2.6 %collective-permute-done.19 = bf16[256,256]{1,0:T(8,128)(2,1)S(1)} collective-permute-done((bf16[256,256]{1,0:T(8,128)(2,1)S(1)}, bf16[256,256]{1,0:T(8,128)(2,1)S(1)}, u32[]{:S(2)}, u32[]{:S(2)}) %collective-permute-start.19) | collective-permute-done | bytes 131104 | tf_op jit(solution)/shard_map/ppermute | solution.py:23
  65.9 1.4 %collective-permute-start.26 = (bf16[256,256]{1,0:T(8,128)(2,1)S(1)}, bf16[256,256]{1,0:T(8,128)(2,1)S(1)}, u32[]{:S(2)}, u32[]{:S(2)}) collective-permute-start(bf16[256,256]{1,0:T(8,128)(2,1)S(1)} %fusion.5), channel_id=1, source_target_pairs={{0,2},{1,3},{2,0},{3,1},{4,6},{5,7},{6,4},{7,5},{8,10},{9,11},{10,... | collective-permute-start | bytes 393224 | tf_op jit(solution)/shard_map/ppermute | solution.py:23
  67.5 0.5 collective-permute-done.24
  68.0 3.0 %collective-permute-done.26 = bf16[256,256]{1,0:T(8,128)(2,1)S(1)} collective-permute-done((bf16[256,256]{1,0:T(8,128)(2,1)S(1)}, bf16[256,256]{1,0:T(8,128)(2,1)S(1)}, u32[]{:S(2)}, u32[]{:S(2)}) %collective-permute-start.26) | collective-permute-done | bytes 131104 | tf_op jit(solution)/shard_map/ppermute | solution.py:23
  71.1 0.3 fusion.11
  71.3 1.3 %collective-permute-done.20 = bf16[256,256]{1,0:T(8,128)(2,1)S(1)} collective-permute-done((bf16[256,256]{1,0:T(8,128)(2,1)S(1)}, bf16[256,256]{1,0:T(8,128)(2,1)S(1)}, u32[]{:S(2)}, u32[]{:S(2)}) %collective-permute-start.20) | collective-permute-done | bytes 131104 | tf_op jit(solution)/shard_map/ppermute | solution.py:23
  72.8 1.1 %collective-permute-start.21 = (bf16[256,256]{1,0:T(8,128)(2,1)S(1)}, bf16[256,256]{1,0:T(8,128)(2,1)S(1)}, u32[]{:S(2)}, u32[]{:S(2)}) collective-permute-start(bf16[256,256]{1,0:T(8,128)(2,1)S(1)} %fusion.6), channel_id=1, source_target_pairs={{0,2},{1,3},{2,0},{3,1},{4,6},{5,7},{6,4},{7,5},{8,10},{9,11},{10,... | collective-permute-start | bytes 393224 | tf_op jit(solution)/shard_map/ppermute | solution.py:23
  74.0 0.5 collective-permute-start.25
  74.5 0.3 fusion.50
  74.8 3.1 %collective-permute-done.21 = bf16[256,256]{1,0:T(8,128)(2,1)S(1)} collective-permute-done((bf16[256,256]{1,0:T(8,128)(2,1)S(1)}, bf16[256,256]{1,0:T(8,128)(2,1)S(1)}, u32[]{:S(2)}, u32[]{:S(2)}) %collective-permute-start.21) | collective-permute-done | bytes 131104 | tf_op jit(solution)/shard_map/ppermute | solution.py:23
  78.0 0.3 fusion.3.refs_1_
  78.3 0.3 fusion.2.refs_0_
  78.6 1.0 %collective-permute-done.22.refs_4_ = bf16[512,256]{1,0:T(8,128)(2,1)S(1)} collective-permute-done((bf16[512,256]{1,0:T(8,128)(2,1)S(1)}, bf16[512,256]{1,0:T(8,128)(2,1)S(1)}, u32[]{:S(2)}, u32[]{:S(2)}) %collective-permute-start.22) | collective-permute-done | bytes 262176 | tf_op jit(solution)/shard_map/ppermute | solution.py:23
  79.5 8.8 %shard_map.64 = f32[1,256]{1,0:T(1,128)S(1)} custom-call(f32[256,256]{1,0:T(8,128)S(1)} %fusion.2.refs_0_, f32[256,256]{1,0:T(8,128)S(1)} %fusion.3.refs_1_, s32[1]{0:T(128)} %bitcast.34.refs_2_, bf16[512,256]{1,0:T(8,128)(2,1)S(1)} %get-tuple-element.42.refs_3_, bf16[512,256]{1,0:T(8,128)(2,1)S(1)} %collective-permute-done.22.refs_4_), custom_call_target="tpu_custom_call" | custom-call | tf_op jit(solution)/shard_map/pallas_call | solution.py:135
  88.6 0.8 pad_maximum_fusion.1
  89.6 0.6 add.88
  (93 shorter events, 5.3 us)
Async XLA Ops:
  0.7 1.1 %copy-start.4 = (s32[1,4,256]{2,1,0:T(4,128)S(1)}, s32[1,4,256]{2,1,0:T(4,128)}, u32[]{:S(2)}) copy-start(s32[1,4,256]{2,1,0:T(4,128)} %param.7) | copy-start | bytes 12292
  1.7 5.7 %copy-start.1 = (bf16[128,1024]{1,0:T(8,128)(2,1)S(1)}, bf16[128,1024]{1,0:T(8,128)(2,1)}, u32[]{:S(2)}) copy-start(bf16[128,1024]{1,0:T(8,128)(2,1)} %param.5) | copy-start | bytes 786436
  1.7 5.7 %copy-start.2 = (bf16[128,1024]{1,0:T(8,128)(2,1)S(1)}, bf16[128,1024]{1,0:T(8,128)(2,1)}, u32[]{:S(2)}) copy-start(bf16[128,1024]{1,0:T(8,128)(2,1)} %param.6) | copy-start | bytes 786436
  1.7 11.0 %copy-start.3 = (bf16[128,4096]{1,0:T(8,128)(2,1)S(1)}, bf16[128,4096]{1,0:T(8,128)(2,1)}, u32[]{:S(2)}) copy-start(bf16[128,4096]{1,0:T(8,128)(2,1)} %param.4) | copy-start | bytes 3145732
  1.8 7.2 %collective-permute-start.2 = (s32[1,256]{1,0:T(1,128)S(1)}, s32[1,256]{1,0:T(1,128)S(1)}, u32[]{:S(2)}, u32[]{:S(2)}) collective-permute-start(s32[1,256]{1,0:T(1,128)S(1)} %get-tuple-element.14), channel_id=1, source_target_pairs={{0,16},{4,20},{8,24},{12,28},{16,0},{20,4},{24,8},{28,12},{1,17},{... | collective-permute-start | bytes 3080 | tf_op jit(solution)/shard_map/ppermute | solution.py:23
  5.9 9.2 %collective-permute-start.9 = (bf16[128,1024]{1,0:T(8,128)(2,1)S(1)}, bf16[128,1024]{1,0:T(8,128)(2,1)S(1)}, u32[]{:S(2)}, u32[]{:S(2)}) collective-permute-start(bf16[128,1024]{1,0:T(8,128)(2,1)S(1)} %pad_maximum_fusion.3), channel_id=1, source_target_pairs={{0,4},{4,0},{8,12},{12,8},{16,20},{20,16},{24,28},{28,24},{1,5},{5... | collective-permute-start | bytes 786440 | tf_op jit(solution)/shard_map/ppermute | solution.py:23
  7.4 9.8 %collective-permute-start = (bf16[2,128,512]{2,1,0:T(8,128)(2,1)S(1)}, bf16[2,128,512]{2,1,0:T(8,128)(2,1)S(1)}, u32[]{:S(2)}, u32[]{:S(2)}) collective-permute-start(bf16[2,128,512]{2,1,0:T(8,128)(2,1)S(1)} %get-tuple-element.34), channel_id=1, source_target_pairs={{0,2},{1,3},{2,0},{3,1},{4,6},{5,7},{6,4},{7,5},{8,10},{9,11},{10,... | collective-permute-start | bytes 786440 | tf_op jit(solution)/shard_map/ppermute | solution.py:23
  9.0 3.7 %collective-permute-start.6 = (s32[2,256]{1,0:T(2,128)S(1)}, s32[2,256]{1,0:T(2,128)S(1)}, u32[]{:S(2)}, u32[]{:S(2)}) collective-permute-start(s32[2,256]{1,0:T(2,128)S(1)} %get-tuple-element.58), channel_id=1, source_target_pairs={{0,8},{4,12},{8,0},{12,4},{16,24},{20,28},{24,16},{28,20},{1,9},{5... | collective-permute-start | bytes 6152 | tf_op jit(solution)/shard_map/ppermute | solution.py:23
  10.7 11.4 %collective-permute-start.3 = (bf16[2,144,512]{2,1,0:T(8,128)(2,1)S(1)}, bf16[2,144,512]{2,1,0:T(8,128)(2,1)S(1)}, u32[]{:S(2)}, u32[]{:S(2)}) collective-permute-start(bf16[2,144,512]{2,1,0:T(8,128)(2,1)S(1)} %pad_maximum_fusion.2), channel_id=1, source_target_pairs={{0,4},{4,0},{8,12},{12,8},{16,20},{20,16},{24,28},{28,24},{1,5},{5... | collective-permute-start | bytes 884744 | tf_op jit(solution)/shard_map/ppermute | solution.py:23
  13.8 8.2 %collective-permute-start.7 = (bf16[128,1024]{1,0:T(8,128)(2,1)S(1)}, bf16[128,1024]{1,0:T(8,128)(2,1)S(1)}, u32[]{:S(2)}, u32[]{:S(2)}) collective-permute-start(bf16[128,1024]{1,0:T(8,128)(2,1)S(1)} %pad_maximum_fusion.4), channel_id=1, source_target_pairs={{0,2},{1,3},{2,0},{3,1},{4,6},{5,7},{6,4},{7,5},{8,10},{9,11},{10,... | collective-permute-start | bytes 786440 | tf_op jit(solution)/shard_map/ppermute | solution.py:23
  15.6 7.8 %collective-permute-start.10 = (bf16[128,512]{1,0:T(8,128)(2,1)S(1)}, bf16[128,512]{1,0:T(8,128)(2,1)S(1)}, u32[]{:S(2)}, u32[]{:S(2)}) collective-permute-start(bf16[128,512]{1,0:T(8,128)(2,1)S(1)} %pad_maximum_fusion.9), channel_id=1, source_target_pairs={{0,2},{1,3},{2,0},{3,1},{4,6},{5,7},{6,4},{7,5},{8,10},{9,11},{10,... | collective-permute-start | bytes 393224 | tf_op jit(solution)/shard_map/ppermute | solution.py:23
  17.2 10.6 %collective-permute-start.1 = (bf16[2,256,256]{2,1,0:T(8,128)(2,1)S(1)}, bf16[2,256,256]{2,1,0:T(8,128)(2,1)S(1)}, u32[]{:S(2)}, u32[]{:S(2)}) collective-permute-start(bf16[2,256,256]{2,1,0:T(8,128)(2,1)S(1)} %get-tuple-element.32), channel_id=1, source_target_pairs={{0,1},{1,0},{2,3},{3,2},{4,5},{5,4},{6,7},{7,6},{8,9},{9,8},{10,11... | collective-permute-start | bytes 786440 | tf_op jit(solution)/shard_map/ppermute | solution.py:23
  17.3 8.7 %collective-permute-start.4 = (bf16[2,128,512]{2,1,0:T(8,128)(2,1)S(1)}, bf16[2,128,512]{2,1,0:T(8,128)(2,1)S(1)}, u32[]{:S(2)}, u32[]{:S(2)}) collective-permute-start(bf16[2,128,512]{2,1,0:T(8,128)(2,1)S(1)} %collective-permute-done), channel_id=1, source_target_pairs={{0,4},{4,0},{8,12},{12,8},{16,20},{20,16},{24,28},{28,24},{1,5},{5... | collective-permute-start | bytes 786440 | tf_op jit(solution)/shard_map/ppermute | solution.py:23
  22.1 5.7 %collective-permute-start.8 = (bf16[256,1024]{1,0:T(8,128)(2,1)S(1)}, bf16[256,1024]{1,0:T(8,128)(2,1)S(1)}, u32[]{:S(2)}, u32[]{:S(2)}) collective-permute-start(bf16[256,1024]{1,0:T(8,128)(2,1)S(1)} %pad_maximum_fusion.refs_4_), channel_id=1, source_target_pairs={{0,1},{1,0},{2,3},{3,2},{4,5},{5,4},{6,7},{7,6},{8,9},{9,8},{10,11... | collective-permute-start | bytes 1572872 | tf_op jit(solution)/shard_map/ppermute | solution.py:23
  22.1 0.7 copy-start
  22.9 3.1 %slice-start = ((bf16[2,144,512]{2,1,0:T(8,128)(2,1)}), bf16[2,128,512]{2,1,0:T(8,128)(2,1)S(1)}, s32[]{:S(2)}) async-start(bf16[2,144,512]{2,1,0:T(8,128)(2,1)} %copy-done), calls=%async_computation | async-start | bytes 524288 | tf_op jit(solution)/shard_map/slice | solution.py:234
  23.4 4.4 %collective-permute-start.11 = (bf16[256,512]{1,0:T(8,128)(2,1)S(1)}, bf16[256,512]{1,0:T(8,128)(2,1)S(1)}, u32[]{:S(2)}, u32[]{:S(2)}) collective-permute-start(bf16[256,512]{1,0:T(8,128)(2,1)S(1)} %pad_maximum_fusion.5.refs_6_), channel_id=1, source_target_pairs={{0,1},{1,0},{2,3},{3,2},{4,5},{5,4},{6,7},{7,6},{8,9},{9,8},{10,11... | collective-permute-start | bytes 786440 | tf_op jit(solution)/shard_map/ppermute | solution.py:23
  26.1 1.7 %collective-permute-start.5 = (bf16[2,256,256]{2,1,0:T(8,128)(2,1)S(1)}, bf16[2,256,256]{2,1,0:T(8,128)(2,1)S(1)}, u32[]{:S(2)}, u32[]{:S(2)}) collective-permute-start(bf16[2,256,256]{2,1,0:T(8,128)(2,1)S(1)} %get-tuple-element.30), channel_id=1, source_target_pairs={{0,1},{1,0},{2,3},{3,2},{4,5},{5,4},{6,7},{7,6},{8,9},{9,8},{10,11... | collective-permute-start | bytes 786440 | tf_op jit(solution)/shard_map/ppermute | solution.py:23
  26.2 5.9 %collective-permute-start.13 = (bf16[128,512]{1,0:T(8,128)(2,1)S(1)}, bf16[128,512]{1,0:T(8,128)(2,1)S(1)}, u32[]{:S(2)}, u32[]{:S(2)}) collective-permute-start(bf16[128,512]{1,0:T(8,128)(2,1)S(1)} %pad_maximum_fusion.8), channel_id=1, source_target_pairs={{0,4},{4,0},{8,12},{12,8},{16,20},{20,16},{24,28},{28,24},{1,5},{5... | collective-permute-start | bytes 393224 | tf_op jit(solution)/shard_map/ppermute | solution.py:23
  28.5 8.7 %collective-permute-start.12 = (f16[528,256]{1,0:T(8,128)(2,1)S(1)}, f16[528,256]{1,0:T(8,128)(2,1)S(1)}, u32[]{:S(2)}, u32[]{:S(2)}) collective-permute-start(f16[528,256]{1,0:T(8,128)(2,1)S(1)} %convert_element_type.80), channel_id=1, source_target_pairs={{0,8},{4,12},{8,0},{12,4},{16,24},{20,28},{24,16},{28,20},{1,9},{5... | collective-permute-start | bytes 811016 | tf_op jit(solution)/shard_map/ppermute | solution.py:23
  32.1 5.1 %collective-permute-start.14 = (bf16[128,512]{1,0:T(8,128)(2,1)S(1)}, bf16[128,512]{1,0:T(8,128)(2,1)S(1)}, u32[]{:S(2)}, u32[]{:S(2)}) collective-permute-start(bf16[128,512]{1,0:T(8,128)(2,1)S(1)} %collective-permute-done.13), channel_id=1, source_target_pairs={{0,2},{1,3},{2,0},{3,1},{4,6},{5,7},{6,4},{7,5},{8,10},{9,11},{10,... | collective-permute-start | bytes 393224 | tf_op jit(solution)/shard_map/ppermute | solution.py:23
  37.2 1.8 %collective-permute-start.15 = (bf16[256,512]{1,0:T(8,128)(2,1)S(1)}, bf16[256,512]{1,0:T(8,128)(2,1)S(1)}, u32[]{:S(2)}, u32[]{:S(2)}) collective-permute-start(bf16[256,512]{1,0:T(8,128)(2,1)S(1)} %pad_maximum_fusion.6.refs_6_), channel_id=1, source_target_pairs={{0,1},{1,0},{2,3},{3,2},{4,5},{5,4},{6,7},{7,6},{8,9},{9,8},{10,11... | collective-permute-start | bytes 786440 | tf_op jit(solution)/shard_map/ppermute | solution.py:23
  37.3 11.7 %collective-permute-start.16 = (f16[528,256]{1,0:T(8,128)(2,1)S(1)}, f16[528,256]{1,0:T(8,128)(2,1)S(1)}, u32[]{:S(2)}, u32[]{:S(2)}) collective-permute-start(f16[528,256]{1,0:T(8,128)(2,1)S(1)} %convert_element_type.81), channel_id=1, source_target_pairs={{0,8},{4,12},{8,0},{12,4},{16,24},{20,28},{24,16},{28,20},{1,9},{5... | collective-permute-start | bytes 811016 | tf_op jit(solution)/shard_map/ppermute | solution.py:23
  39.7 15.4 %collective-permute-start.17 = (f16[528,256]{1,0:T(8,128)(2,1)S(1)}, f16[528,256]{1,0:T(8,128)(2,1)S(1)}, u32[]{:S(2)}, u32[]{:S(2)}) collective-permute-start(f16[528,256]{1,0:T(8,128)(2,1)S(1)} %convert_element_type.84), channel_id=1, source_target_pairs={{0,16},{4,20},{8,24},{12,28},{16,0},{20,4},{24,8},{28,12},{1,17},{... | collective-permute-start | bytes 811016 | tf_op jit(solution)/shard_map/ppermute | solution.py:23
  55.2 5.0 %collective-permute-start.18 = (bf16[256,256]{1,0:T(8,128)(2,1)S(1)}, bf16[256,256]{1,0:T(8,128)(2,1)S(1)}, u32[]{:S(2)}, u32[]{:S(2)}) collective-permute-start(bf16[256,256]{1,0:T(8,128)(2,1)S(1)} %shard_map.63), channel_id=1, source_target_pairs={{0,4},{4,0},{8,12},{12,8},{16,20},{20,16},{24,28},{28,24},{1,5},{5... | collective-permute-start | bytes 393224 | tf_op jit(solution)/shard_map/ppermute | solution.py:23
  56.7 5.0 %collective-permute-start.23 = (bf16[256,256]{1,0:T(8,128)(2,1)S(1)}, bf16[256,256]{1,0:T(8,128)(2,1)S(1)}, u32[]{:S(2)}, u32[]{:S(2)}) collective-permute-start(bf16[256,256]{1,0:T(8,128)(2,1)S(1)} %shard_map.63), channel_id=1, source_target_pairs={{0,2},{1,3},{2,0},{3,1},{4,6},{5,7},{6,4},{7,5},{8,10},{9,11},{10,... | collective-permute-start | bytes 393224 | tf_op jit(solution)/shard_map/ppermute | solution.py:23
  60.6 5.0 %collective-permute-start.19 = (bf16[256,256]{1,0:T(8,128)(2,1)S(1)}, bf16[256,256]{1,0:T(8,128)(2,1)S(1)}, u32[]{:S(2)}, u32[]{:S(2)}) collective-permute-start(bf16[256,256]{1,0:T(8,128)(2,1)S(1)} %fusion.4), channel_id=1, source_target_pairs={{0,8},{4,12},{8,0},{12,4},{16,24},{20,28},{24,16},{28,20},{1,9},{5... | collective-permute-start | bytes 393224 | tf_op jit(solution)/shard_map/ppermute | solution.py:23
  61.8 6.2 %collective-permute-start.24 = (bf16[256,256]{1,0:T(8,128)(2,1)S(1)}, bf16[256,256]{1,0:T(8,128)(2,1)S(1)}, u32[]{:S(2)}, u32[]{:S(2)}) collective-permute-start(bf16[256,256]{1,0:T(8,128)(2,1)S(1)} %fusion.4), channel_id=1, source_target_pairs={{0,2},{1,3},{2,0},{3,1},{4,6},{5,7},{6,4},{7,5},{8,10},{9,11},{10,... | collective-permute-start | bytes 393224 | tf_op jit(solution)/shard_map/ppermute | solution.py:23
  65.8 6.8 %collective-permute-start.20 = (bf16[256,256]{1,0:T(8,128)(2,1)S(1)}, bf16[256,256]{1,0:T(8,128)(2,1)S(1)}, u32[]{:S(2)}, u32[]{:S(2)}) collective-permute-start(bf16[256,256]{1,0:T(8,128)(2,1)S(1)} %fusion.5), channel_id=1, source_target_pairs={{0,16},{4,20},{8,24},{12,28},{16,0},{20,4},{24,8},{28,12},{1,17},{... | collective-permute-start | bytes 393224 | tf_op jit(solution)/shard_map/ppermute | solution.py:23
  65.9 5.0 %collective-permute-start.26 = (bf16[256,256]{1,0:T(8,128)(2,1)S(1)}, bf16[256,256]{1,0:T(8,128)(2,1)S(1)}, u32[]{:S(2)}, u32[]{:S(2)}) collective-permute-start(bf16[256,256]{1,0:T(8,128)(2,1)S(1)} %fusion.5), channel_id=1, source_target_pairs={{0,2},{1,3},{2,0},{3,1},{4,6},{5,7},{6,4},{7,5},{8,10},{9,11},{10,... | collective-permute-start | bytes 393224 | tf_op jit(solution)/shard_map/ppermute | solution.py:23
  72.8 5.0 %collective-permute-start.21 = (bf16[256,256]{1,0:T(8,128)(2,1)S(1)}, bf16[256,256]{1,0:T(8,128)(2,1)S(1)}, u32[]{:S(2)}, u32[]{:S(2)}) collective-permute-start(bf16[256,256]{1,0:T(8,128)(2,1)S(1)} %fusion.6), channel_id=1, source_target_pairs={{0,2},{1,3},{2,0},{3,1},{4,6},{5,7},{6,4},{7,5},{8,10},{9,11},{10,... | collective-permute-start | bytes 393224 | tf_op jit(solution)/shard_map/ppermute | solution.py:23
  73.9 4.1 %collective-permute-start.27 = (bf16[512,256]{1,0:T(8,128)(2,1)S(1)}, bf16[512,256]{1,0:T(8,128)(2,1)S(1)}, u32[]{:S(2)}, u32[]{:S(2)}) collective-permute-start(bf16[512,256]{1,0:T(8,128)(2,1)S(1)} %maximum_bitcast_fusion.2), channel_id=1, source_target_pairs={{0,1},{1,0},{2,3},{3,2},{4,5},{5,4},{6,7},{7,6},{8,9},{9,8},{10,11... | collective-permute-start | bytes 786440 | tf_op jit(solution)/shard_map/ppermute | solution.py:23
  74.0 4.3 %collective-permute-start.25 = (bf16[512,256]{1,0:T(8,128)(2,1)S(1)}, bf16[512,256]{1,0:T(8,128)(2,1)S(1)}, u32[]{:S(2)}, u32[]{:S(2)}) collective-permute-start(bf16[512,256]{1,0:T(8,128)(2,1)S(1)} %broadcast_select_fusion), channel_id=1, source_target_pairs={{0,1},{1,0},{2,3},{3,2},{4,5},{5,4},{6,7},{7,6},{8,9},{9,8},{10,11... | collective-permute-start | bytes 786440 | tf_op jit(solution)/shard_map/ppermute | solution.py:23
  77.9 1.6 %collective-permute-start.22 = (bf16[512,256]{1,0:T(8,128)(2,1)S(1)}, bf16[512,256]{1,0:T(8,128)(2,1)S(1)}, u32[]{:S(2)}, u32[]{:S(2)}) collective-permute-start(bf16[512,256]{1,0:T(8,128)(2,1)S(1)} %get-tuple-element.42.refs_3_), channel_id=1, source_target_pairs={{0,1},{1,0},{2,3},{3,2},{4,5},{5,4},{6,7},{7,6},{8,9},{9,8},{10,11... | collective-permute-start | bytes 786440 | tf_op jit(solution)/shard_map/ppermute | solution.py:23
  88.3 1.2 %collective-permute-start.28 = (f32[1,256]{1,0:T(1,128)S(1)}, f32[1,256]{1,0:T(1,128)S(1)}, u32[]{:S(2)}, u32[]{:S(2)}) collective-permute-start(f32[1,256]{1,0:T(1,128)S(1)} %shard_map.64), channel_id=1, source_target_pairs={{0,1},{1,0},{2,3},{3,2},{4,5},{5,4},{6,7},{7,6},{8,9},{9,8},{10,11... | collective-permute-start | bytes 3080 | tf_op jit(solution)/shard_map/ppermute | solution.py:23

commit v12 on v11

--- a/solution.py
+++ b/solution.py
@@ -321,7 +321,7 @@
             block = chosen
             if shared:
                 block, shared[-1] = lax.optimization_barrier((block, shared[-1]))
-            shared.append(over_higher(block))
+            shared.append(joined(block))
             if section < paired and section % 2:
                 low, high = shared[-2:]
                 got = exchange(jnp.where(even, high, low), "band", 1)

time: 90.3 us -> 90.7 us (level)
  waiting for transfers between devices: 42.6 us -> 43.9 us
    ppermute x29, waiting for transfers between devices: 42.6 us -> 43.9 us  [exchange(): return lax.ppermute(block, axis, [(i, i ^ delta) for i in range(count)])]
  transfers between devices with their start and end apart: 29 -> 29, of which waited for: 18 -> 18; matrix products, arithmetic and copies ran while one was open for 6% -> 7% of each run, Pallas kernels for 3% -> 3%
where the time goes in v12:
time: 90.7 us; the launch traced here: 90.6 us
  waiting for transfers between devices  43.9 us (48%)
  starting transfers between devices  26.5 us (29%)
  Pallas kernels  11.3 us (12%)
  matrix products  4.23 us (5%)
  other arithmetic  2.12 us (2%)
  local copies, waits for them, and re-layouts  1.34 us (1%)
  between operations  1.27 us (1%)
    ppermute x29, waiting for transfers between devices, exchange(): return lax.ppermute(block, axis, [(i, i ^ delta) for i in range(count)])  43.9 us
    ppermute x29, starting transfers between devices, exchange(): return lax.ppermute(block, axis, [(i, i ^ delta) for i in range(count)])  26.5 us
    pallas_call x1, Pallas kernels, log_pivots(): pl.pallas_call(functools.partial(pivots_kernel, sets, cand is not None),...  8.8 us
    pallas_call x5, Pallas kernels, sketch(): pl.pallas_call(functools.partial(sketch_kernel, mode, columns, [start for...  2.49 us
    dot_general x8, matrix products, pick(): out.append(jnp.dot(block, one_hot, preferred_element_type=f32).astype(bf16))  1.98 us
  transfers between devices with their start and end apart: 29, of which 18 were waited for; matrix products, arithmetic and copies ran while one was open for 7% of the time, Pallas kernels for 3%

profile of v12, /device:TPU:0, one launch (start us, length us, event | category | flops | bytes accessed | tf_op | source)
XLA Modules:
  0.0 90.6 jit_solution(16213390817155147589)
XLA Ops:
  0.7 1.0 %constant_dynamic-slice_fusion.3 = (bf16[128,512]{1,0:T(8,128)(2,1)S(1)}, bf16[128,512]{1,0:T(8,128)(2,1)S(1)}) fusion(bf16[128,4096]{1,0:T(8,128)(2,1)} %param.4, s32[]{:T(128)S(6)} %select_n.94, s32[]{:T(128)S(6)} %select_n.95), kind=kLoop, calls=%fused_computation.110 | loop fusion | bytes 524296 | tf_op jit(solution)/shard_map/dynamic_slice | solution.py:212
  1.8 4.1 %collective-permute-start.2 = (s32[1,256]{1,0:T(1,128)S(1)}, s32[1,256]{1,0:T(1,128)S(1)}, u32[]{:S(2)}, u32[]{:S(2)}) collective-permute-start(s32[1,256]{1,0:T(1,128)S(1)} %get-tuple-element.14), channel_id=1, source_target_pairs={{0,16},{4,20},{8,24},{12,28},{16,0},{20,4},{24,8},{28,12},{1,17},{... | collective-permute-start | bytes 3080 | tf_op jit(solution)/shard_map/ppermute | solution.py:23
  5.9 1.5 %collective-permute-start.9 = (bf16[128,1024]{1,0:T(8,128)(2,1)S(1)}, bf16[128,1024]{1,0:T(8,128)(2,1)S(1)}, u32[]{:S(2)}, u32[]{:S(2)}) collective-permute-start(bf16[128,1024]{1,0:T(8,128)(2,1)S(1)} %pad_maximum_fusion.3), channel_id=1, source_target_pairs={{0,4},{4,0},{8,12},{12,8},{16,20},{20,16},{24,28},{28,24},{1,5},{5... | collective-permute-start | bytes 786440 | tf_op jit(solution)/shard_map/ppermute | solution.py:23
  7.4 1.6 %collective-permute-start = (bf16[2,128,512]{2,1,0:T(8,128)(2,1)S(1)}, bf16[2,128,512]{2,1,0:T(8,128)(2,1)S(1)}, u32[]{:S(2)}, u32[]{:S(2)}) collective-permute-start(bf16[2,128,512]{2,1,0:T(8,128)(2,1)S(1)} %get-tuple-element.34), channel_id=1, source_target_pairs={{0,2},{1,3},{2,0},{3,1},{4,6},{5,7},{6,4},{7,5},{8,10},{9,11},{10,... | collective-permute-start | bytes 786440 | tf_op jit(solution)/shard_map/ppermute | solution.py:23
  9.0 1.6 %collective-permute-start.6 = (s32[2,256]{1,0:T(2,128)S(1)}, s32[2,256]{1,0:T(2,128)S(1)}, u32[]{:S(2)}, u32[]{:S(2)}) collective-permute-start(s32[2,256]{1,0:T(2,128)S(1)} %get-tuple-element.52), channel_id=1, source_target_pairs={{0,8},{4,12},{8,0},{12,4},{16,24},{20,28},{24,16},{28,20},{1,9},{5... | collective-permute-start | bytes 6152 | tf_op jit(solution)/shard_map/ppermute | solution.py:23
  10.7 0.6 collective-permute-start.3
  11.3 1.3 %collective-permute-done.6 = s32[2,256]{1,0:T(2,128)S(1)} collective-permute-done((s32[2,256]{1,0:T(2,128)S(1)}, s32[2,256]{1,0:T(2,128)S(1)}, u32[]{:S(2)}, u32[]{:S(2)}) %collective-permute-start.6) | collective-permute-done | bytes 2080 | tf_op jit(solution)/shard_map/ppermute | solution.py:23
  13.5 0.2 convolution_convert_fusion.5
  13.8 0.6 collective-permute-start.7
  14.4 0.7 collective-permute-done.9
  15.6 1.6 %collective-permute-start.10 = (bf16[128,512]{1,0:T(8,128)(2,1)S(1)}, bf16[128,512]{1,0:T(8,128)(2,1)S(1)}, u32[]{:S(2)}, u32[]{:S(2)}) collective-permute-start(bf16[128,512]{1,0:T(8,128)(2,1)S(1)} %pad_maximum_fusion.10), channel_id=1, source_target_pairs={{0,2},{1,3},{2,0},{3,1},{4,6},{5,7},{6,4},{7,5},{8,10},{9,11},{10,... | collective-permute-start | bytes 393224 | tf_op jit(solution)/shard_map/ppermute | solution.py:23
  17.3 1.6 %collective-permute-start.4 = (bf16[2,128,512]{2,1,0:T(8,128)(2,1)S(1)}, bf16[2,128,512]{2,1,0:T(8,128)(2,1)S(1)}, u32[]{:S(2)}, u32[]{:S(2)}) collective-permute-start(bf16[2,128,512]{2,1,0:T(8,128)(2,1)S(1)} %collective-permute-done), channel_id=1, source_target_pairs={{0,4},{4,0},{8,12},{12,8},{16,20},{20,16},{24,28},{28,24},{1,5},{5... | collective-permute-start | bytes 786440 | tf_op jit(solution)/shard_map/ppermute | solution.py:23
  18.9 3.1 %collective-permute-done.7 = bf16[128,1024]{1,0:T(8,128)(2,1)S(1)} collective-permute-done((bf16[128,1024]{1,0:T(8,128)(2,1)S(1)}, bf16[128,1024]{1,0:T(8,128)(2,1)S(1)}, u32[]{:S(2)}, u32[]{:S(2)}) %collective-permute-start.7) | collective-permute-done | bytes 262176 | tf_op jit(solution)/shard_map/ppermute | solution.py:23
  22.9 0.5 collective-permute-done.10
  23.5 2.5 %collective-permute-done.4 = bf16[2,128,512]{2,1,0:T(8,128)(2,1)S(1)} collective-permute-done((bf16[2,128,512]{2,1,0:T(8,128)(2,1)S(1)}, bf16[2,128,512]{2,1,0:T(8,128)(2,1)S(1)}, u32[]{:S(2)}, u32[]{:S(2)}) %collective-permute-start.4) | collective-permute-done | bytes 262176 | tf_op jit(solution)/shard_map/ppermute | solution.py:23
  26.2 1.6 %collective-permute-start.13 = (bf16[128,512]{1,0:T(8,128)(2,1)S(1)}, bf16[128,512]{1,0:T(8,128)(2,1)S(1)}, u32[]{:S(2)}, u32[]{:S(2)}) collective-permute-start(bf16[128,512]{1,0:T(8,128)(2,1)S(1)} %pad_maximum_fusion.9), channel_id=1, source_target_pairs={{0,4},{4,0},{8,12},{12,8},{16,20},{20,16},{24,28},{28,24},{1,5},{5... | collective-permute-start | bytes 393224 | tf_op jit(solution)/shard_map/ppermute | solution.py:23
  27.8 0.7 shard_map.59
  28.5 1.6 %collective-permute-start.12 = (f16[528,256]{1,0:T(8,128)(2,1)S(1)}, f16[528,256]{1,0:T(8,128)(2,1)S(1)}, u32[]{:S(2)}, u32[]{:S(2)}) collective-permute-start(f16[528,256]{1,0:T(8,128)(2,1)S(1)} %convert_element_type.80), channel_id=1, source_target_pairs={{0,8},{4,12},{8,0},{12,4},{16,24},{20,28},{24,16},{28,20},{1,9},{5... | collective-permute-start | bytes 811016 | tf_op jit(solution)/shard_map/ppermute | solution.py:23
  30.2 0.6 shard_map.60
  30.9 1.3 %collective-permute-done.13 = bf16[128,512]{1,0:T(8,128)(2,1)S(1)} collective-permute-done((bf16[128,512]{1,0:T(8,128)(2,1)S(1)}, bf16[128,512]{1,0:T(8,128)(2,1)S(1)}, u32[]{:S(2)}, u32[]{:S(2)}) %collective-permute-start.13) | collective-permute-done | bytes 131104 | tf_op jit(solution)/shard_map/ppermute | solution.py:23
  32.1 1.0 %collective-permute-start.14 = (bf16[128,512]{1,0:T(8,128)(2,1)S(1)}, bf16[128,512]{1,0:T(8,128)(2,1)S(1)}, u32[]{:S(2)}, u32[]{:S(2)}) collective-permute-start(bf16[128,512]{1,0:T(8,128)(2,1)S(1)} %collective-permute-done.13), channel_id=1, source_target_pairs={{0,2},{1,3},{2,0},{3,1},{4,6},{5,7},{6,4},{7,5},{8,10},{9,11},{10,... | collective-permute-start | bytes 393224 | tf_op jit(solution)/shard_map/ppermute | solution.py:23
  33.2 4.0 %collective-permute-done.14 = bf16[128,512]{1,0:T(8,128)(2,1)S(1)} collective-permute-done((bf16[128,512]{1,0:T(8,128)(2,1)S(1)}, bf16[128,512]{1,0:T(8,128)(2,1)S(1)}, u32[]{:S(2)}, u32[]{:S(2)}) %collective-permute-start.14) | collective-permute-done | bytes 131104 | tf_op jit(solution)/shard_map/ppermute | solution.py:23
  37.3 1.6 %collective-permute-start.16 = (f16[528,256]{1,0:T(8,128)(2,1)S(1)}, f16[528,256]{1,0:T(8,128)(2,1)S(1)}, u32[]{:S(2)}, u32[]{:S(2)}) collective-permute-start(f16[528,256]{1,0:T(8,128)(2,1)S(1)} %convert_element_type.81), channel_id=1, source_target_pairs={{0,8},{4,12},{8,0},{12,4},{16,24},{20,28},{24,16},{28,20},{1,9},{5... | collective-permute-start | bytes 811016 | tf_op jit(solution)/shard_map/ppermute | solution.py:23
  39.0 0.7 shard_map.62
  39.7 0.6 collective-permute-start.17
  40.3 8.7 %collective-permute-done.16 = f16[528,256]{1,0:T(8,128)(2,1)S(1)} collective-permute-done((f16[528,256]{1,0:T(8,128)(2,1)S(1)}, f16[528,256]{1,0:T(8,128)(2,1)S(1)}, u32[]{:S(2)}, u32[]{:S(2)}) %collective-permute-start.16) | collective-permute-done | bytes 270368 | tf_op jit(solution)/shard_map/ppermute | solution.py:23
  49.0 0.5 shard_map.61.refs_0_
  49.5 5.5 %collective-permute-done.17 = f16[528,256]{1,0:T(8,128)(2,1)S(1)} collective-permute-done((f16[528,256]{1,0:T(8,128)(2,1)S(1)}, f16[528,256]{1,0:T(8,128)(2,1)S(1)}, u32[]{:S(2)}, u32[]{:S(2)}) %collective-permute-start.17) | collective-permute-done | bytes 270368 | tf_op jit(solution)/shard_map/ppermute | solution.py:23
  55.2 1.6 %collective-permute-start.18 = (bf16[256,256]{1,0:T(8,128)(2,1)S(1)}, bf16[256,256]{1,0:T(8,128)(2,1)S(1)}, u32[]{:S(2)}, u32[]{:S(2)}) collective-permute-start(bf16[256,256]{1,0:T(8,128)(2,1)S(1)} %shard_map.63), channel_id=1, source_target_pairs={{0,4},{4,0},{8,12},{12,8},{16,20},{20,16},{24,28},{28,24},{1,5},{5... | collective-permute-start | bytes 393224 | tf_op jit(solution)/shard_map/ppermute | solution.py:23
  56.7 1.0 %collective-permute-start.23 = (bf16[256,256]{1,0:T(8,128)(2,1)S(1)}, bf16[256,256]{1,0:T(8,128)(2,1)S(1)}, u32[]{:S(2)}, u32[]{:S(2)}) collective-permute-start(bf16[256,256]{1,0:T(8,128)(2,1)S(1)} %shard_map.63), channel_id=1, source_target_pairs={{0,2},{1,3},{2,0},{3,1},{4,6},{5,7},{6,4},{7,5},{8,10},{9,11},{10,... | collective-permute-start | bytes 393224 | tf_op jit(solution)/shard_map/ppermute | solution.py:23
  57.8 2.4 %collective-permute-done.18 = bf16[256,256]{1,0:T(8,128)(2,1)S(1)} collective-permute-done((bf16[256,256]{1,0:T(8,128)(2,1)S(1)}, bf16[256,256]{1,0:T(8,128)(2,1)S(1)}, u32[]{:S(2)}, u32[]{:S(2)}) %collective-permute-start.18) | collective-permute-done | bytes 131104 | tf_op jit(solution)/shard_map/ppermute | solution.py:23
  60.7 1.0 %collective-permute-done.23 = bf16[256,256]{1,0:T(8,128)(2,1)S(1)} collective-permute-done((bf16[256,256]{1,0:T(8,128)(2,1)S(1)}, bf16[256,256]{1,0:T(8,128)(2,1)S(1)}, u32[]{:S(2)}, u32[]{:S(2)}) %collective-permute-start.23) | collective-permute-done | bytes 131104 | tf_op jit(solution)/shard_map/ppermute | solution.py:23
  61.7 1.1 %collective-permute-start.24 = (bf16[256,256]{1,0:T(8,128)(2,1)S(1)}, bf16[256,256]{1,0:T(8,128)(2,1)S(1)}, u32[]{:S(2)}, u32[]{:S(2)}) collective-permute-start(bf16[256,256]{1,0:T(8,128)(2,1)S(1)} %fusion.4), channel_id=1, source_target_pairs={{0,2},{1,3},{2,0},{3,1},{4,6},{5,7},{6,4},{7,5},{8,10},{9,11},{10,... | collective-permute-start | bytes 393224 | tf_op jit(solution)/shard_map/ppermute | solution.py:23
  63.1 2.6 %collective-permute-done.19 = bf16[256,256]{1,0:T(8,128)(2,1)S(1)} collective-permute-done((bf16[256,256]{1,0:T(8,128)(2,1)S(1)}, bf16[256,256]{1,0:T(8,128)(2,1)S(1)}, u32[]{:S(2)}, u32[]{:S(2)}) %collective-permute-start.19) | collective-permute-done | bytes 131104 | tf_op jit(solution)/shard_map/ppermute | solution.py:23
  65.9 1.1 %collective-permute-done.24 = bf16[256,256]{1,0:T(8,128)(2,1)S(1)} collective-permute-done((bf16[256,256]{1,0:T(8,128)(2,1)S(1)}, bf16[256,256]{1,0:T(8,128)(2,1)S(1)}, u32[]{:S(2)}, u32[]{:S(2)}) %collective-permute-start.24) | collective-permute-done | bytes 131104 | tf_op jit(solution)/shard_map/ppermute | solution.py:23
  67.0 1.1 %collective-permute-start.26 = (bf16[256,256]{1,0:T(8,128)(2,1)S(1)}, bf16[256,256]{1,0:T(8,128)(2,1)S(1)}, u32[]{:S(2)}, u32[]{:S(2)}) collective-permute-start(bf16[256,256]{1,0:T(8,128)(2,1)S(1)} %fusion.5), channel_id=1, source_target_pairs={{0,2},{1,3},{2,0},{3,1},{4,6},{5,7},{6,4},{7,5},{8,10},{9,11},{10,... | collective-permute-start | bytes 393224 | tf_op jit(solution)/shard_map/ppermute | solution.py:23
  68.5 3.6 %collective-permute-done.26 = bf16[256,256]{1,0:T(8,128)(2,1)S(1)} collective-permute-done((bf16[256,256]{1,0:T(8,128)(2,1)S(1)}, bf16[256,256]{1,0:T(8,128)(2,1)S(1)}, u32[]{:S(2)}, u32[]{:S(2)}) %collective-permute-start.26) | collective-permute-done | bytes 131104 | tf_op jit(solution)/shard_map/ppermute | solution.py:23
  72.2 0.5 collective-permute-done.20
  72.8 1.1 %collective-permute-start.21 = (bf16[256,256]{1,0:T(8,128)(2,1)S(1)}, bf16[256,256]{1,0:T(8,128)(2,1)S(1)}, u32[]{:S(2)}, u32[]{:S(2)}) collective-permute-start(bf16[256,256]{1,0:T(8,128)(2,1)S(1)} %fusion.6), channel_id=1, source_target_pairs={{0,2},{1,3},{2,0},{3,1},{4,6},{5,7},{6,4},{7,5},{8,10},{9,11},{10,... | collective-permute-start | bytes 393224 | tf_op jit(solution)/shard_map/ppermute | solution.py:23
  73.9 0.3 fusion.52
  74.2 0.3 fusion.2.refs_0_
  74.5 3.9 %collective-permute-done.21 = bf16[256,256]{1,0:T(8,128)(2,1)S(1)} collective-permute-done((bf16[256,256]{1,0:T(8,128)(2,1)S(1)}, bf16[256,256]{1,0:T(8,128)(2,1)S(1)}, u32[]{:S(2)}, u32[]{:S(2)}) %collective-permute-start.21) | collective-permute-done | bytes 131104 | tf_op jit(solution)/shard_map/ppermute | solution.py:23
  78.5 0.3 fusion.53
  78.8 0.3 fusion.3.refs_1_
  79.0 1.0 %collective-permute-done.22.refs_4_ = bf16[512,256]{1,0:T(8,128)(2,1)S(1)} collective-permute-done((bf16[512,256]{1,0:T(8,128)(2,1)S(1)}, bf16[512,256]{1,0:T(8,128)(2,1)S(1)}, u32[]{:S(2)}, u32[]{:S(2)}) %collective-permute-start.22) | collective-permute-done | bytes 262176 | tf_op jit(solution)/shard_map/ppermute | solution.py:23
  80.0 8.8 %shard_map.64 = f32[1,256]{1,0:T(1,128)S(1)} custom-call(f32[256,256]{1,0:T(8,128)S(1)} %fusion.2.refs_0_, f32[256,256]{1,0:T(8,128)S(1)} %fusion.3.refs_1_, s32[1]{0:T(128)} %bitcast.25.refs_2_, bf16[512,256]{1,0:T(8,128)(2,1)S(1)} %get-tuple-element.36.refs_3_, bf16[512,256]{1,0:T(8,128)(2,1)S(1)} %collective-permute-done.22.refs_4_), custom_call_target="tpu_custom_call" | custom-call | tf_op jit(solution)/shard_map/pallas_call | solution.py:135
  89.1 0.8 pad_maximum_fusion.1
  90.0 0.6 add.88
  (94 shorter events, 5.1 us)
Async XLA Ops:
  0.7 1.1 %copy-start.4 = (s32[1,4,256]{2,1,0:T(4,128)S(1)}, s32[1,4,256]{2,1,0:T(4,128)}, u32[]{:S(2)}) copy-start(s32[1,4,256]{2,1,0:T(4,128)} %param.7) | copy-start | bytes 12292
  1.7 5.7 %copy-start.1 = (bf16[128,1024]{1,0:T(8,128)(2,1)S(1)}, bf16[128,1024]{1,0:T(8,128)(2,1)}, u32[]{:S(2)}) copy-start(bf16[128,1024]{1,0:T(8,128)(2,1)} %param.5) | copy-start | bytes 786436
  1.7 5.7 %copy-start.2 = (bf16[128,1024]{1,0:T(8,128)(2,1)S(1)}, bf16[128,1024]{1,0:T(8,128)(2,1)}, u32[]{:S(2)}) copy-start(bf16[128,1024]{1,0:T(8,128)(2,1)} %param.6) | copy-start | bytes 786436
  1.7 11.0 %copy-start.3 = (bf16[128,4096]{1,0:T(8,128)(2,1)S(1)}, bf16[128,4096]{1,0:T(8,128)(2,1)}, u32[]{:S(2)}) copy-start(bf16[128,4096]{1,0:T(8,128)(2,1)} %param.4) | copy-start | bytes 3145732
  1.8 7.2 %collective-permute-start.2 = (s32[1,256]{1,0:T(1,128)S(1)}, s32[1,256]{1,0:T(1,128)S(1)}, u32[]{:S(2)}, u32[]{:S(2)}) collective-permute-start(s32[1,256]{1,0:T(1,128)S(1)} %get-tuple-element.14), channel_id=1, source_target_pairs={{0,16},{4,20},{8,24},{12,28},{16,0},{20,4},{24,8},{28,12},{1,17},{... | collective-permute-start | bytes 3080 | tf_op jit(solution)/shard_map/ppermute | solution.py:23
  5.9 9.2 %collective-permute-start.9 = (bf16[128,1024]{1,0:T(8,128)(2,1)S(1)}, bf16[128,1024]{1,0:T(8,128)(2,1)S(1)}, u32[]{:S(2)}, u32[]{:S(2)}) collective-permute-start(bf16[128,1024]{1,0:T(8,128)(2,1)S(1)} %pad_maximum_fusion.3), channel_id=1, source_target_pairs={{0,4},{4,0},{8,12},{12,8},{16,20},{20,16},{24,28},{28,24},{1,5},{5... | collective-permute-start | bytes 786440 | tf_op jit(solution)/shard_map/ppermute | solution.py:23
  7.4 9.8 %collective-permute-start = (bf16[2,128,512]{2,1,0:T(8,128)(2,1)S(1)}, bf16[2,128,512]{2,1,0:T(8,128)(2,1)S(1)}, u32[]{:S(2)}, u32[]{:S(2)}) collective-permute-start(bf16[2,128,512]{2,1,0:T(8,128)(2,1)S(1)} %get-tuple-element.34), channel_id=1, source_target_pairs={{0,2},{1,3},{2,0},{3,1},{4,6},{5,7},{6,4},{7,5},{8,10},{9,11},{10,... | collective-permute-start | bytes 786440 | tf_op jit(solution)/shard_map/ppermute | solution.py:23
  9.0 3.7 %collective-permute-start.6 = (s32[2,256]{1,0:T(2,128)S(1)}, s32[2,256]{1,0:T(2,128)S(1)}, u32[]{:S(2)}, u32[]{:S(2)}) collective-permute-start(s32[2,256]{1,0:T(2,128)S(1)} %get-tuple-element.52), channel_id=1, source_target_pairs={{0,8},{4,12},{8,0},{12,4},{16,24},{20,28},{24,16},{28,20},{1,9},{5... | collective-permute-start | bytes 6152 | tf_op jit(solution)/shard_map/ppermute | solution.py:23
  10.7 11.4 %collective-permute-start.3 = (bf16[2,144,512]{2,1,0:T(8,128)(2,1)S(1)}, bf16[2,144,512]{2,1,0:T(8,128)(2,1)S(1)}, u32[]{:S(2)}, u32[]{:S(2)}) collective-permute-start(bf16[2,144,512]{2,1,0:T(8,128)(2,1)S(1)} %pad_maximum_fusion.2), channel_id=1, source_target_pairs={{0,4},{4,0},{8,12},{12,8},{16,20},{20,16},{24,28},{28,24},{1,5},{5... | collective-permute-start | bytes 884744 | tf_op jit(solution)/shard_map/ppermute | solution.py:23
  13.8 8.2 %collective-permute-start.7 = (bf16[128,1024]{1,0:T(8,128)(2,1)S(1)}, bf16[128,1024]{1,0:T(8,128)(2,1)S(1)}, u32[]{:S(2)}, u32[]{:S(2)}) collective-permute-start(bf16[128,1024]{1,0:T(8,128)(2,1)S(1)} %pad_maximum_fusion.4), channel_id=1, source_target_pairs={{0,2},{1,3},{2,0},{3,1},{4,6},{5,7},{6,4},{7,5},{8,10},{9,11},{10,... | collective-permute-start | bytes 786440 | tf_op jit(solution)/shard_map/ppermute | solution.py:23
  15.6 7.8 %collective-permute-start.10 = (bf16[128,512]{1,0:T(8,128)(2,1)S(1)}, bf16[128,512]{1,0:T(8,128)(2,1)S(1)}, u32[]{:S(2)}, u32[]{:S(2)}) collective-permute-start(bf16[128,512]{1,0:T(8,128)(2,1)S(1)} %pad_maximum_fusion.10), channel_id=1, source_target_pairs={{0,2},{1,3},{2,0},{3,1},{4,6},{5,7},{6,4},{7,5},{8,10},{9,11},{10,... | collective-permute-start | bytes 393224 | tf_op jit(solution)/shard_map/ppermute | solution.py:23
  17.2 10.6 %collective-permute-start.1 = (bf16[2,256,256]{2,1,0:T(8,128)(2,1)S(1)}, bf16[2,256,256]{2,1,0:T(8,128)(2,1)S(1)}, u32[]{:S(2)}, u32[]{:S(2)}) collective-permute-start(bf16[2,256,256]{2,1,0:T(8,128)(2,1)S(1)} %get-tuple-element.32), channel_id=1, source_target_pairs={{0,1},{1,0},{2,3},{3,2},{4,5},{5,4},{6,7},{7,6},{8,9},{9,8},{10,11... | collective-permute-start | bytes 786440 | tf_op jit(solution)/shard_map/ppermute | solution.py:23
  17.3 8.7 %collective-permute-start.4 = (bf16[2,128,512]{2,1,0:T(8,128)(2,1)S(1)}, bf16[2,128,512]{2,1,0:T(8,128)(2,1)S(1)}, u32[]{:S(2)}, u32[]{:S(2)}) collective-permute-start(bf16[2,128,512]{2,1,0:T(8,128)(2,1)S(1)} %collective-permute-done), channel_id=1, source_target_pairs={{0,4},{4,0},{8,12},{12,8},{16,20},{20,16},{24,28},{28,24},{1,5},{5... | collective-permute-start | bytes 786440 | tf_op jit(solution)/shard_map/ppermute | solution.py:23
  22.1 5.7 %collective-permute-start.8 = (bf16[256,1024]{1,0:T(8,128)(2,1)S(1)}, bf16[256,1024]{1,0:T(8,128)(2,1)S(1)}, u32[]{:S(2)}, u32[]{:S(2)}) collective-permute-start(bf16[256,1024]{1,0:T(8,128)(2,1)S(1)} %pad_maximum_fusion.refs_4_), channel_id=1, source_target_pairs={{0,1},{1,0},{2,3},{3,2},{4,5},{5,4},{6,7},{7,6},{8,9},{9,8},{10,11... | collective-permute-start | bytes 1572872 | tf_op jit(solution)/shard_map/ppermute | solution.py:23
  22.1 0.7 copy-start
  22.9 3.1 %slice-start = ((bf16[2,144,512]{2,1,0:T(8,128)(2,1)}), bf16[2,128,512]{2,1,0:T(8,128)(2,1)S(1)}, s32[]{:S(2)}) async-start(bf16[2,144,512]{2,1,0:T(8,128)(2,1)} %copy-done), calls=%async_computation | async-start | bytes 524288 | tf_op jit(solution)/shard_map/slice | solution.py:234
  23.4 4.4 %collective-permute-start.11 = (bf16[256,512]{1,0:T(8,128)(2,1)S(1)}, bf16[256,512]{1,0:T(8,128)(2,1)S(1)}, u32[]{:S(2)}, u32[]{:S(2)}) collective-permute-start(bf16[256,512]{1,0:T(8,128)(2,1)S(1)} %pad_maximum_fusion.5.refs_6_), channel_id=1, source_target_pairs={{0,1},{1,0},{2,3},{3,2},{4,5},{5,4},{6,7},{7,6},{8,9},{9,8},{10,11... | collective-permute-start | bytes 786440 | tf_op jit(solution)/shard_map/ppermute | solution.py:23
  26.1 1.7 %collective-permute-start.5 = (bf16[2,256,256]{2,1,0:T(8,128)(2,1)S(1)}, bf16[2,256,256]{2,1,0:T(8,128)(2,1)S(1)}, u32[]{:S(2)}, u32[]{:S(2)}) collective-permute-start(bf16[2,256,256]{2,1,0:T(8,128)(2,1)S(1)} %get-tuple-element.30), channel_id=1, source_target_pairs={{0,1},{1,0},{2,3},{3,2},{4,5},{5,4},{6,7},{7,6},{8,9},{9,8},{10,11... | collective-permute-start | bytes 786440 | tf_op jit(solution)/shard_map/ppermute | solution.py:23
  26.2 5.9 %collective-permute-start.13 = (bf16[128,512]{1,0:T(8,128)(2,1)S(1)}, bf16[128,512]{1,0:T(8,128)(2,1)S(1)}, u32[]{:S(2)}, u32[]{:S(2)}) collective-permute-start(bf16[128,512]{1,0:T(8,128)(2,1)S(1)} %pad_maximum_fusion.9), channel_id=1, source_target_pairs={{0,4},{4,0},{8,12},{12,8},{16,20},{20,16},{24,28},{28,24},{1,5},{5... | collective-permute-start | bytes 393224 | tf_op jit(solution)/shard_map/ppermute | solution.py:23
  28.5 8.7 %collective-permute-start.12 = (f16[528,256]{1,0:T(8,128)(2,1)S(1)}, f16[528,256]{1,0:T(8,128)(2,1)S(1)}, u32[]{:S(2)}, u32[]{:S(2)}) collective-permute-start(f16[528,256]{1,0:T(8,128)(2,1)S(1)} %convert_element_type.80), channel_id=1, source_target_pairs={{0,8},{4,12},{8,0},{12,4},{16,24},{20,28},{24,16},{28,20},{1,9},{5... | collective-permute-start | bytes 811016 | tf_op jit(solution)/shard_map/ppermute | solution.py:23
  32.1 5.1 %collective-permute-start.14 = (bf16[128,512]{1,0:T(8,128)(2,1)S(1)}, bf16[128,512]{1,0:T(8,128)(2,1)S(1)}, u32[]{:S(2)}, u32[]{:S(2)}) collective-permute-start(bf16[128,512]{1,0:T(8,128)(2,1)S(1)} %collective-permute-done.13), channel_id=1, source_target_pairs={{0,2},{1,3},{2,0},{3,1},{4,6},{5,7},{6,4},{7,5},{8,10},{9,11},{10,... | collective-permute-start | bytes 393224 | tf_op jit(solution)/shard_map/ppermute | solution.py:23
  37.2 1.8 %collective-permute-start.15 = (bf16[256,512]{1,0:T(8,128)(2,1)S(1)}, bf16[256,512]{1,0:T(8,128)(2,1)S(1)}, u32[]{:S(2)}, u32[]{:S(2)}) collective-permute-start(bf16[256,512]{1,0:T(8,128)(2,1)S(1)} %pad_maximum_fusion.6.refs_6_), channel_id=1, source_target_pairs={{0,1},{1,0},{2,3},{3,2},{4,5},{5,4},{6,7},{7,6},{8,9},{9,8},{10,11... | collective-permute-start | bytes 786440 | tf_op jit(solution)/shard_map/ppermute | solution.py:23
  37.3 11.7 %collective-permute-start.16 = (f16[528,256]{1,0:T(8,128)(2,1)S(1)}, f16[528,256]{1,0:T(8,128)(2,1)S(1)}, u32[]{:S(2)}, u32[]{:S(2)}) collective-permute-start(f16[528,256]{1,0:T(8,128)(2,1)S(1)} %convert_element_type.81), channel_id=1, source_target_pairs={{0,8},{4,12},{8,0},{12,4},{16,24},{20,28},{24,16},{28,20},{1,9},{5... | collective-permute-start | bytes 811016 | tf_op jit(solution)/shard_map/ppermute | solution.py:23
  39.7 15.4 %collective-permute-start.17 = (f16[528,256]{1,0:T(8,128)(2,1)S(1)}, f16[528,256]{1,0:T(8,128)(2,1)S(1)}, u32[]{:S(2)}, u32[]{:S(2)}) collective-permute-start(f16[528,256]{1,0:T(8,128)(2,1)S(1)} %convert_element_type.84), channel_id=1, source_target_pairs={{0,16},{4,20},{8,24},{12,28},{16,0},{20,4},{24,8},{28,12},{1,17},{... | collective-permute-start | bytes 811016 | tf_op jit(solution)/shard_map/ppermute | solution.py:23
  55.2 5.0 %collective-permute-start.18 = (bf16[256,256]{1,0:T(8,128)(2,1)S(1)}, bf16[256,256]{1,0:T(8,128)(2,1)S(1)}, u32[]{:S(2)}, u32[]{:S(2)}) collective-permute-start(bf16[256,256]{1,0:T(8,128)(2,1)S(1)} %shard_map.63), channel_id=1, source_target_pairs={{0,4},{4,0},{8,12},{12,8},{16,20},{20,16},{24,28},{28,24},{1,5},{5... | collective-permute-start | bytes 393224 | tf_op jit(solution)/shard_map/ppermute | solution.py:23
  56.7 5.0 %collective-permute-start.23 = (bf16[256,256]{1,0:T(8,128)(2,1)S(1)}, bf16[256,256]{1,0:T(8,128)(2,1)S(1)}, u32[]{:S(2)}, u32[]{:S(2)}) collective-permute-start(bf16[256,256]{1,0:T(8,128)(2,1)S(1)} %shard_map.63), channel_id=1, source_target_pairs={{0,2},{1,3},{2,0},{3,1},{4,6},{5,7},{6,4},{7,5},{8,10},{9,11},{10,... | collective-permute-start | bytes 393224 | tf_op jit(solution)/shard_map/ppermute | solution.py:23
  60.6 5.0 %collective-permute-start.19 = (bf16[256,256]{1,0:T(8,128)(2,1)S(1)}, bf16[256,256]{1,0:T(8,128)(2,1)S(1)}, u32[]{:S(2)}, u32[]{:S(2)}) collective-permute-start(bf16[256,256]{1,0:T(8,128)(2,1)S(1)} %fusion.4), channel_id=1, source_target_pairs={{0,8},{4,12},{8,0},{12,4},{16,24},{20,28},{24,16},{28,20},{1,9},{5... | collective-permute-start | bytes 393224 | tf_op jit(solution)/shard_map/ppermute | solution.py:23
  61.7 5.3 %collective-permute-start.24 = (bf16[256,256]{1,0:T(8,128)(2,1)S(1)}, bf16[256,256]{1,0:T(8,128)(2,1)S(1)}, u32[]{:S(2)}, u32[]{:S(2)}) collective-permute-start(bf16[256,256]{1,0:T(8,128)(2,1)S(1)} %fusion.4), channel_id=1, source_target_pairs={{0,2},{1,3},{2,0},{3,1},{4,6},{5,7},{6,4},{7,5},{8,10},{9,11},{10,... | collective-permute-start | bytes 393224 | tf_op jit(solution)/shard_map/ppermute | solution.py:23
  65.8 6.8 %collective-permute-start.20 = (bf16[256,256]{1,0:T(8,128)(2,1)S(1)}, bf16[256,256]{1,0:T(8,128)(2,1)S(1)}, u32[]{:S(2)}, u32[]{:S(2)}) collective-permute-start(bf16[256,256]{1,0:T(8,128)(2,1)S(1)} %fusion.5), channel_id=1, source_target_pairs={{0,16},{4,20},{8,24},{12,28},{16,0},{20,4},{24,8},{28,12},{1,17},{... | collective-permute-start | bytes 393224 | tf_op jit(solution)/shard_map/ppermute | solution.py:23
  67.0 5.0 %collective-permute-start.26 = (bf16[256,256]{1,0:T(8,128)(2,1)S(1)}, bf16[256,256]{1,0:T(8,128)(2,1)S(1)}, u32[]{:S(2)}, u32[]{:S(2)}) collective-permute-start(bf16[256,256]{1,0:T(8,128)(2,1)S(1)} %fusion.5), channel_id=1, source_target_pairs={{0,2},{1,3},{2,0},{3,1},{4,6},{5,7},{6,4},{7,5},{8,10},{9,11},{10,... | collective-permute-start | bytes 393224 | tf_op jit(solution)/shard_map/ppermute | solution.py:23
  68.2 5.8 %collective-permute-start.25 = (bf16[512,256]{1,0:T(8,128)(2,1)S(1)}, bf16[512,256]{1,0:T(8,128)(2,1)S(1)}, u32[]{:S(2)}, u32[]{:S(2)}) collective-permute-start(bf16[512,256]{1,0:T(8,128)(2,1)S(1)} %broadcast_select_fusion), channel_id=1, source_target_pairs={{0,1},{1,0},{2,3},{3,2},{4,5},{5,4},{6,7},{7,6},{8,9},{9,8},{10,11... | collective-permute-start | bytes 786440 | tf_op jit(solution)/shard_map/ppermute | solution.py:23
  72.1 6.4 %collective-permute-start.27 = (bf16[512,256]{1,0:T(8,128)(2,1)S(1)}, bf16[512,256]{1,0:T(8,128)(2,1)S(1)}, u32[]{:S(2)}, u32[]{:S(2)}) collective-permute-start(bf16[512,256]{1,0:T(8,128)(2,1)S(1)} %constant_dynamic-update-slice_fusion.6), channel_id=1, source_target_pairs={{0,1},{1,0},{2,3},{3,2},{4,5},{5,4},{6,7},{7,6},{8,9},{9,8},{10,11... | collective-permute-start | bytes 786440 | tf_op jit(solution)/shard_map/ppermute | solution.py:23
  72.8 5.5 %collective-permute-start.21 = (bf16[256,256]{1,0:T(8,128)(2,1)S(1)}, bf16[256,256]{1,0:T(8,128)(2,1)S(1)}, u32[]{:S(2)}, u32[]{:S(2)}) collective-permute-start(bf16[256,256]{1,0:T(8,128)(2,1)S(1)} %fusion.6), channel_id=1, source_target_pairs={{0,2},{1,3},{2,0},{3,1},{4,6},{5,7},{6,4},{7,5},{8,10},{9,11},{10,... | collective-permute-start | bytes 393224 | tf_op jit(solution)/shard_map/ppermute | solution.py:23
  78.4 1.6 %collective-permute-start.22 = (bf16[512,256]{1,0:T(8,128)(2,1)S(1)}, bf16[512,256]{1,0:T(8,128)(2,1)S(1)}, u32[]{:S(2)}, u32[]{:S(2)}) collective-permute-start(bf16[512,256]{1,0:T(8,128)(2,1)S(1)} %get-tuple-element.36.refs_3_), channel_id=1, source_target_pairs={{0,1},{1,0},{2,3},{3,2},{4,5},{5,4},{6,7},{7,6},{8,9},{9,8},{10,11... | collective-permute-start | bytes 786440 | tf_op jit(solution)/shard_map/ppermute | solution.py:23
  88.8 1.2 %collective-permute-start.28 = (f32[1,256]{1,0:T(1,128)S(1)}, f32[1,256]{1,0:T(1,128)S(1)}, u32[]{:S(2)}, u32[]{:S(2)}) collective-permute-start(f32[1,256]{1,0:T(1,128)S(1)} %shard_map.64), channel_id=1, source_target_pairs={{0,1},{1,0},{2,3},{3,2},{4,5},{5,4},{6,7},{7,6},{8,9},{9,8},{10,11... | collective-permute-start | bytes 3080 | tf_op jit(solution)/shard_map/ppermute | solution.py:23
